TPU v7x, 32 devices: a whole 2x2x4 slice. The times are simulated.
32 devices in a mesh: seq: 16 (over z, y, x), head: 2 (over core).
Axes of the slice: x: 2, y: 2, z: 4, core: 2. Of those that a mesh axis runs over, the one named last changes fastest.
Arguments:
- tokens: bfloat16 [2, 2048, 1536], P(None, 'seq'), may hold values from -6 to 6
- doc_ids: int32 [2, 2048], P(None, 'seq'), may hold values from 0 to 7, as said below
- out_grad: bfloat16 [2, 2048, 1536], P(None, 'seq'), may hold values from -6 to 6
- norm_mix: float32 [1536], replicated, may hold values from 0.5 to 1.5
- w_inner: bfloat16 [1536, 3072], P(None, 'head'), may hold values from -0.15625 to 0.15625
- w_outgate: bfloat16 [1536, 3072], P(None, 'head'), may hold values from -0.15625 to 0.15625
- conv_taps: float32 [4, 3072], P(None, 'head'), may hold values from -3 to 3
- conv_bias: float32 [3072], P('head'), may hold values from -3 to 3
- w_select: bfloat16 [3072, 128], P('head'), may hold values from -0.109375 to 0.109375
- select_gain: float32 [128], replicated, may hold values from 0.5 to 1.5
- w_step: bfloat16 [96, 3072], P(None, 'head'), may hold values from -0.625 to 0.625
- step_bias: float32 [3072], P('head'), may hold values from -8 to -1
- log_decay: float32 [3072, 16], P('head'), may hold values from -3 to 1
- skip_gain: float32 [3072], P('head'), may hold values from 0.5 to 1.5
- w_mixout: bfloat16 [3072, 1536], P('head'), may hold values from -0.21875 to 0.21875
- norm_ffn: float32 [1536], replicated, may hold values from 0.5 to 1.5
- w_gate: bfloat16 [1536, 4096], P(None, 'head'), may hold values from -0.15625 to 0.15625
- w_up: bfloat16 [1536, 4096], P(None, 'head'), may hold values from -0.15625 to 0.15625
- w_down: bfloat16 [4096, 1536], P('head'), may hold values from -0.1875 to 0.1875
Outputs:
- output: bfloat16 [2, 2048, 1536], P(None, 'seq')
- tokens_grad: float32 [2, 2048, 1536], P(None, 'seq')
- grad_norm_mix: float32 [1536], P('seq')
- grad_w_inner: float32 [1536, 3072], P('seq', 'head')
- grad_w_outgate: float32 [1536, 3072], P('seq', 'head')
- grad_conv_taps: float32 [4, 3072], P(None, ('head', 'seq'))
- grad_conv_bias: float32 [3072], P(('head', 'seq'))
- grad_w_select: float32 [3072, 128], P('head', 'seq')
- grad_select_gain: float32 [128], P('seq')
- grad_w_step: float32 [96, 3072], P(None, ('head', 'seq'))
- grad_step_bias: float32 [3072], P(('head', 'seq'))
- grad_log_decay: float32 [3072, 16], P(('head', 'seq'))
- grad_skip_gain: float32 [3072], P(('head', 'seq'))
- grad_w_mixout: float32 [3072, 1536], P('head', 'seq')
- grad_norm_ffn: float32 [1536], P('seq')
- grad_w_gate: float32 [1536, 4096], P('seq', 'head')
- grad_w_up: float32 [1536, 4096], P('seq', 'head')
- grad_w_down: float32 [4096, 1536], P('head', 'seq')
Inputs may be any that keep to these rules, and one draw needn't show every extreme that they name: `doc_ids`: within each stream the document numbers start at 0 and rise by 0 or 1 from token to token. In one stream, drawn from the seed, all tokens form one document. In every other stream, document j >= 1 starts inside tokens j * min(1024, 256) to (j + 1) * min(1024, 256) - 1.
All inputs are finite; a program needn't handle non-finite values.
Results may differ from a plain program's by a relative error of at most 0.012.
Values sent between devices are 32-bit elements; how exact they have to be, the bound alone decides.
A program may use at most 256 MiB of HBM per device.

v0:
```python
import math

import jax
import jax.numpy as jnp
from jax import lax
from jax.sharding import PartitionSpec as P

epsilon = 1e-06


def from_behind(block, axis, distance):
    devices = range(lax.axis_size(axis))
    route = [(i - distance, i) for i in devices if i - distance in devices]
    return lax.ppermute(block, axis, route)


def carried_in(shard, axis, combine, identity, reverse):
    length, index = (lax.axis_size(axis), lax.axis_index(axis))
    everything = jax.tree.map(lambda part: lax.all_gather(part, axis), shard)
    start = jax.tree.map(
        lambda part, zero: jnp.broadcast_to(jnp.asarray(zero, part.dtype), part.shape),
        shard,
        identity,
    )

    def lap(k, before):
        at = length - 1 - k if reverse else k
        reached = at > index if reverse else at < index
        new = combine(before, jax.tree.map(lambda part: part[at], everything))
        return jax.tree.map(lambda a, b: jnp.where(reached, a, b), new, before)

    return lax.fori_loop(0, length, lap, start)


def matmul(left, right):
    return jnp.dot(left, right, preferred_element_type=jnp.float32)


def matmul_back(left, right):
    return lax.dot_general(
        left, right, (((left.ndim - 1,), (1,)), ((), ())), preferred_element_type=jnp.float32
    )


def weight_outer(left, right):
    return lax.dot_general(
        left, right, (((0, 1), (0, 1)), ((), ())), preferred_element_type=jnp.float32
    )


def norm_forward(v, gain):
    scale = lax.rsqrt(jnp.mean(v * v, axis=-1, keepdims=True) + epsilon)
    return (v * scale * gain, scale)


def norm_backward(v, scale, gain, upstream):
    weighted = upstream * gain
    d_input = scale * weighted - v * scale * scale * scale * jnp.mean(
        weighted * v, axis=-1, keepdims=True
    )
    d_gain = jnp.sum(upstream * v * scale, axis=(0, 1))
    return (d_input, d_gain)


def silu_slope(v):
    sig = jax.nn.sigmoid(v)
    return sig + v * sig * (1.0 - sig)


def token_major(v, piece):
    length = v.shape[1]
    return jnp.swapaxes(v, 0, 1).reshape((length // piece, piece, v.shape[0]) + v.shape[2:])


def series_major(v):
    return jnp.swapaxes(v.reshape((-1,) + v.shape[2:]), 0, 1)


def chain(earlier, later):
    return (earlier[0] * later[0], later[0] * earlier[1] + later[1])


def fade_of(d, k, decay_rate):
    return jnp.exp(d[:, None, :] * decay_rate) * k[:, None, None]


def summarize(decay_rate, inputs, start):

    def turn(carry, block):
        through, state = carry
        d, v, b, k = block
        for j in range(d.shape[0]):
            fade = fade_of(d[j], k[j], decay_rate)
            through = through * fade
            state = fade * state + (d[j] * v[j])[:, None, :] * b[j][:, :, None]
        return ((through, state), None)

    (through, state), _ = lax.scan(turn, (jnp.ones_like(start), start), inputs)
    return (through, state)


def run_states(decay_rate, start, inputs):

    def turn(state, block):
        d, v, b, k, c = block
        first = state
        outs = []
        for j in range(d.shape[0]):
            fade = fade_of(d[j], k[j], decay_rate)
            state = fade * state + (d[j] * v[j])[:, None, :] * b[j][:, :, None]
            outs.append(jnp.sum(state * c[j][:, :, None], axis=1))
        return (state, (first, jnp.stack(outs)))

    _, (bounds, outs) = lax.scan(turn, start, inputs)
    return (bounds, outs)


def adjoint_summary(decay_rate, start, inputs):

    def turn(carried, block):
        d, k, c, g = block
        for j in range(d.shape[0] - 1, -1, -1):
            adjoint = c[j][:, :, None] * g[j][:, None, :] + carried
            carried = fade_of(d[j], k[j], decay_rate) * adjoint
        return (carried, None)

    carried, _ = lax.scan(turn, start, inputs, reverse=True)
    return carried


def adjoint_run(decay_rate, incoming, bounds, inputs):

    def turn(carry, block):
        carried, decay_sum = carry
        first, d, v, b, c, k, g = block
        steps = d.shape[0]
        path = [first]
        fades = []
        state = first
        for j in range(steps):
            fade = fade_of(d[j], k[j], decay_rate)
            state = fade * state + (d[j] * v[j])[:, None, :] * b[j][:, :, None]
            fades.append(fade)
            path.append(state)
        d_step = [None] * steps
        d_value = [None] * steps
        d_bsel = [None] * steps
        d_csel = [None] * steps
        for j in range(steps - 1, -1, -1):
            adjoint = c[j][:, :, None] * g[j][:, None, :] + carried
            weighted = jnp.sum(adjoint * b[j][:, :, None], axis=1)
            touch = adjoint * path[j] * fades[j]
            d_step[j] = weighted * v[j] + jnp.sum(touch * decay_rate, axis=1)
            d_value[j] = weighted * d[j]
            d_bsel[j] = jnp.sum(adjoint * (d[j] * v[j])[:, None, :], axis=2)
            d_csel[j] = jnp.sum(path[j + 1] * g[j][:, None, :], axis=2)
            decay_sum = decay_sum + jnp.sum(touch * d[j][:, None, :], axis=0)
            carried = fades[j] * adjoint
        return (
            (carried, decay_sum),
            (jnp.stack(d_step), jnp.stack(d_value), jnp.stack(d_bsel), jnp.stack(d_csel)),
        )

    zero_sum = jnp.zeros(decay_rate.shape, jnp.float32)
    (_, decay_sum), outs = lax.scan(turn, (incoming, zero_sum), (bounds,) + inputs, reverse=True)
    return (decay_sum, outs)


def body(
    tokens,
    doc_ids,
    out_grad,
    norm_mix,
    w_inner,
    w_outgate,
    conv_taps,
    conv_bias,
    w_select,
    select_gain,
    w_step,
    step_bias,
    log_decay,
    skip_gain,
    w_mixout,
    norm_ffn,
    w_gate,
    w_up,
    w_down,
):
    length = tokens.shape[1]
    taps = conv_taps.shape[0]
    rank = w_step.shape[0]
    states = log_decay.shape[1]
    lead = taps - 1
    piece = math.gcd(length, 32)
    source = tokens.astype(jnp.float32)
    normed, scale_mix = norm_forward(source, norm_mix)
    normed_low = normed.astype(jnp.bfloat16)
    inner = matmul(normed_low, w_inner)
    outgate = matmul(normed_low, w_outgate)
    rim_ids = (doc_ids[:, length - lead :] + 1).astype(jnp.float32)
    rim_val, rim_got = from_behind((inner[:, length - lead :], rim_ids), "seq", 1)
    ext_val = jnp.concatenate([rim_val, inner], axis=1)
    ext_ids = jnp.concatenate([rim_got.astype(jnp.int32) - 1, doc_ids], axis=1)
    masks = [
        (ext_ids[:, k : k + length] == doc_ids).astype(jnp.float32)[:, :, None] for k in range(taps)
    ]
    value_pre = jnp.zeros_like(inner) + conv_bias
    for k in range(taps):
        value_pre = value_pre + conv_taps[k] * ext_val[:, k : k + length] * masks[k]
    value = jax.nn.silu(value_pre)
    value_low = value.astype(jnp.bfloat16)
    select = lax.psum(matmul(value_low, w_select), "head")
    raw_step = select[..., :rank]
    raw_b = select[..., rank : rank + states]
    raw_c = select[..., rank + states :]
    step_n, step_scale = norm_forward(raw_step, select_gain[:rank])
    bsel, b_scale = norm_forward(raw_b, select_gain[rank : rank + states])
    csel, c_scale = norm_forward(raw_c, select_gain[rank + states :])
    step_low = step_n.astype(jnp.bfloat16)
    step_pre = matmul(step_low, w_step) + step_bias
    step = jax.nn.softplus(step_pre)
    keep = (doc_ids == ext_ids[:, lead - 1 : lead - 1 + length]).astype(jnp.float32)
    decay_rate = -jnp.exp(log_decay).T
    step_t = token_major(step, piece)
    value_t = token_major(value, piece)
    bsel_t = token_major(bsel, piece)
    csel_t = token_major(csel, piece)
    keep_t = token_major(keep, piece)
    zero_state = jnp.zeros((tokens.shape[0], states, value.shape[2]), jnp.float32)
    through, ends = summarize(decay_rate, (step_t, value_t, bsel_t, keep_t), zero_state)
    lower = carried_in((through, ends), "seq", chain, (jnp.ones_like(through), zero_state), False)
    bounds, outs = run_states(decay_rate, lower[1], (step_t, value_t, bsel_t, keep_t, csel_t))
    y = series_major(outs) + skip_gain * value
    gate_z = jax.nn.silu(outgate)
    mixed_low = (y * gate_z).astype(jnp.bfloat16)
    mix = lax.psum(matmul(mixed_low, w_mixout), "head")
    resid = source + mix
    hidden, scale_ffn = norm_forward(resid, norm_ffn)
    hidden_low = hidden.astype(jnp.bfloat16)
    gate = matmul(hidden_low, w_gate)
    up = matmul(hidden_low, w_up)
    act_low = (jax.nn.silu(gate) * up).astype(jnp.bfloat16)
    ffn = lax.psum(matmul(act_low, w_down), "head")
    output = (resid + ffn).astype(jnp.bfloat16)
    d_act = matmul_back(out_grad, w_down)
    grad_w_down = weight_outer(act_low, out_grad)
    d_gate = (d_act * up * silu_slope(gate)).astype(jnp.bfloat16)
    d_up = (d_act * jax.nn.silu(gate)).astype(jnp.bfloat16)
    grad_w_gate = weight_outer(hidden_low, d_gate)
    grad_w_up = weight_outer(hidden_low, d_up)
    d_hidden = lax.psum(matmul_back(d_gate, w_gate) + matmul_back(d_up, w_up), "head")
    d_resid_norm, grad_norm_ffn = norm_backward(resid, scale_ffn, norm_ffn, d_hidden)
    d_resid = out_grad.astype(jnp.float32) + d_resid_norm
    d_mix = d_resid.astype(jnp.bfloat16)
    grad_w_mixout = weight_outer(mixed_low, d_mix)
    d_mixed = matmul_back(d_mix, w_mixout)
    d_y = d_mixed * gate_z
    d_outgate = (d_mixed * y * silu_slope(outgate)).astype(jnp.bfloat16)
    grad_skip_gain = jnp.sum(d_y * value, axis=(0, 1))
    dy_t = token_major(d_y, piece)
    leaving = adjoint_summary(decay_rate, zero_state, (step_t, keep_t, csel_t, dy_t))
    upper = carried_in((through, leaving), "seq", chain, (jnp.ones_like(through), zero_state), True)
    decay_sum, (d_step_t, d_value_t, d_bsel_t, d_csel_t) = adjoint_run(
        decay_rate, upper[1], bounds, (step_t, value_t, bsel_t, csel_t, keep_t, dy_t)
    )
    grad_log_decay = (decay_sum * decay_rate).T
    d_step = series_major(d_step_t)
    d_value = d_y * skip_gain + series_major(d_value_t)
    d_step_pre = (d_step * jax.nn.sigmoid(step_pre)).astype(jnp.bfloat16)
    grad_step_bias = jnp.sum(d_step_pre, axis=(0, 1), dtype=jnp.float32)
    grad_w_step = weight_outer(step_low, d_step_pre)
    d_small_part = jnp.concatenate(
        [matmul_back(d_step_pre, w_step), series_major(d_bsel_t), series_major(d_csel_t)], axis=-1
    )
    d_small = lax.psum(d_small_part, "head")
    d_raw_step, gain_step = norm_backward(
        raw_step, step_scale, select_gain[:rank], d_small[..., :rank]
    )
    d_raw_b, gain_b = norm_backward(
        raw_b, b_scale, select_gain[rank : rank + states], d_small[..., rank : rank + states]
    )
    d_raw_c, gain_c = norm_backward(
        raw_c, c_scale, select_gain[rank + states :], d_small[..., rank + states :]
    )
    grad_select_gain = jnp.concatenate([gain_step, gain_b, gain_c])
    d_select = jnp.concatenate([d_raw_step, d_raw_b, d_raw_c], axis=-1).astype(jnp.bfloat16)
    grad_w_select = weight_outer(value_low, d_select)
    d_value = d_value + matmul_back(d_select, w_select)
    d_value_pre = d_value * silu_slope(value_pre)
    grad_conv_bias = jnp.sum(d_value_pre, axis=(0, 1))
    tap_grads = []
    d_ext = jnp.zeros_like(ext_val)
    for k in range(taps):
        masked = d_value_pre * masks[k]
        tap_grads.append(jnp.sum(masked * ext_val[:, k : k + length], axis=(0, 1)))
        d_ext = d_ext + jnp.pad(masked * conv_taps[k], ((0, 0), (k, lead - k), (0, 0)))
    grad_conv_taps = jnp.stack(tap_grads)
    rim_grad = from_behind(d_ext[:, :lead], "seq", -1)
    d_inner = (d_ext[:, lead:] + jnp.pad(rim_grad, ((0, 0), (length - lead, 0), (0, 0)))).astype(
        jnp.bfloat16
    )
    grad_w_inner = weight_outer(normed_low, d_inner)
    grad_w_outgate = weight_outer(normed_low, d_outgate)
    d_normed = lax.psum(matmul_back(d_inner, w_inner) + matmul_back(d_outgate, w_outgate), "head")
    d_source, grad_norm_mix = norm_backward(source, scale_mix, norm_mix, d_normed)
    tokens_grad = d_resid + d_source
    summed = (
        lax.psum_scatter(grad_norm_mix, "seq", scatter_dimension=0, tiled=True),
        lax.psum_scatter(grad_w_inner, "seq", scatter_dimension=0, tiled=True),
        lax.psum_scatter(grad_w_outgate, "seq", scatter_dimension=0, tiled=True),
        lax.psum_scatter(grad_conv_taps, "seq", scatter_dimension=1, tiled=True),
        lax.psum_scatter(grad_conv_bias, "seq", scatter_dimension=0, tiled=True),
        lax.psum_scatter(grad_w_select, "seq", scatter_dimension=1, tiled=True),
        lax.psum_scatter(grad_select_gain, "seq", scatter_dimension=0, tiled=True),
        lax.psum_scatter(grad_w_step, "seq", scatter_dimension=1, tiled=True),
        lax.psum_scatter(grad_step_bias, "seq", scatter_dimension=0, tiled=True),
        lax.psum_scatter(grad_log_decay, "seq", scatter_dimension=0, tiled=True),
        lax.psum_scatter(grad_skip_gain, "seq", scatter_dimension=0, tiled=True),
        lax.psum_scatter(grad_w_mixout, "seq", scatter_dimension=1, tiled=True),
        lax.psum_scatter(grad_norm_ffn, "seq", scatter_dimension=0, tiled=True),
        lax.psum_scatter(grad_w_gate, "seq", scatter_dimension=0, tiled=True),
        lax.psum_scatter(grad_w_up, "seq", scatter_dimension=0, tiled=True),
        lax.psum_scatter(grad_w_down, "seq", scatter_dimension=1, tiled=True),
    )
    return (
        output,
        tokens_grad,
        summed[0],
        summed[1],
        summed[2],
        summed[3],
        summed[4],
        summed[5],
        summed[6],
        summed[7],
        summed[8],
        summed[9],
        summed[10],
        summed[11],
        summed[12],
        summed[13],
        summed[14],
        summed[15],
    )


def solution(mesh):
    in_specs = (
        P(None, "seq", None),
        P(None, "seq"),
        P(None, "seq", None),
        P(),
        P(None, "head"),
        P(None, "head"),
        P(None, "head"),
        P("head"),
        P("head", None),
        P(),
        P(None, "head"),
        P("head"),
        P("head", None),
        P("head"),
        P("head", None),
        P(),
        P(None, "head"),
        P(None, "head"),
        P("head", None),
    )
    out_specs = (
        P(None, "seq", None),
        P(None, "seq", None),
        P("seq"),
        P("seq", "head"),
        P("seq", "head"),
        P(None, ("head", "seq")),
        P(("head", "seq")),
        P("head", "seq"),
        P("seq"),
        P(None, ("head", "seq")),
        P(("head", "seq")),
        P(("head", "seq"), None),
        P(("head", "seq")),
        P("head", "seq"),
        P("seq"),
        P("seq", "head"),
        P("seq", "head"),
        P("head", "seq"),
    )
    return jax.shard_map(body, mesh=mesh, in_specs=in_specs, out_specs=out_specs, check_vma=False)
```

profile of v0, /device:TPU:0, one launch (start us, length us, event | category | flops | bytes accessed | tf_op | source)
XLA Modules:
  0.0 2418.1 jit_solution(15656673932354893363)
XLA Ops:
  34.1 15.4 all-reduce.19.cloned.1.call-done
  57.2 37.7 %while.98 = (s32[]{:T(128)}, f32[2,16,1536]{2,1,0:T(8,128)S(1)}, f32[2,16,1536]{2,1,0:T(8,128)S(1)}, f32[4,32,2,1536]{3,2,1,0:T(2,128)S(1)}, f32[16,1536]{1,0:T(...) while((s32[]{:T(128)}, f32[2,16,1536]{2,1,0:T(8,128)S(1)}, ...), condition=%wide.region_5.6_spmd.clone, body=%wide.region_4.5_spmd.clone.sunk | while | flops 12779554 | bytes 3860624 | solution.py:98
  97.4 67.7 %all-gather.7.cloned.1.call-done = f32[32,16,1536]{2,1,0:T(8,128)} async-done(((f32[2,16,1536]{2,1,0:T(8,128)}), f32[32,16,1536]{2,1,0:T(8,128)}) %all-gather.7.cloned.1.call-update) | async-done | bytes 3145744 | tf_op jit(solution)/shard_map/all_gather | solution.py:19
  165.1 70.0 %all-gather.9.cloned.1.call-done = f32[32,16,1536]{2,1,0:T(8,128)} async-done(((f32[2,16,1536]{2,1,0:T(8,128)}), f32[32,16,1536]{2,1,0:T(8,128)}) %all-gather.9.cloned.1.call-update) | async-done | bytes 3145744 | tf_op jit(solution)/shard_map/all_gather | solution.py:19
  235.2 19.3 while.99
  255.8 55.6 %while.97 = (s32[]{:T(128)}, f32[2,16,1536]{2,1,0:T(8,128)S(1)}, f32[4,2,16,1536]{3,2,1,0:T(8,128)}, f32[4,32,2,1536]{3,1,0,2:T(8,128)}, f32[4,32,2,1536]{3,2,1,...) while((s32[]{:T(128)}, f32[2,16,1536]{2,1,0:T(8,128)S(1)}, ...), condition=%wide.region_42.43_spmd, body=%wide.region_9.42_spmd.sunk | while | flops 14942241 | bytes 12944453 | solution.py:114
  323.9 18.6 all-reduce.21.cloned.1.call-done
  363.9 21.7 all-reduce.23.cloned.1.call-done
  398.5 53.9 %while.100 = (s32[]{:T(128)}, f32[2,16,1536]{2,1,0:T(8,128)}, f32[4,32,2,1536]{3,2,1,0:T(2,128)S(1)}, f32[16,1536]{1,0:T(8,128)S(1)}, f32[4,32,2]{2,1,0:T(8,128)...) while((s32[]{:T(128)}, f32[2,16,1536]{2,1,0:T(8,128)}, ...), condition=%wide.region_49.50_spmd.clone, body=%wide.region_48.49_spmd.clone.sunk | while | flops 7913507 | bytes 2865083 | solution.py:127
  452.5 69.4 %all-gather.11.cloned.1.call-done = f32[32,16,1536]{2,1,0:T(8,128)} async-done(((f32[2,16,1536]{2,1,0:T(8,128)}), f32[32,16,1536]{2,1,0:T(8,128)}) %all-gather.11.cloned.1.call-update) | async-done | bytes 3145744 | tf_op jit(solution)/shard_map/all_gather | solution.py:19
  521.9 19.4 while.101
  545.3 141.3 %while.102 = (s32[]{:T(128)}, f32[2,16,1536]{2,1,0:T(8,128)S(1)}, f32[16,1536]{1,0:T(8,128)}, f32[4,32,2,1536]{3,1,0,2:T(8,128)}, f32[4,32,2,1536]{3,1,0,2:T(8,1...) while((s32[]{:T(128)}, f32[2,16,1536]{2,1,0:T(8,128)S(1)}, ...), condition=%wide.region_213.214_spmd.clone, body=%wide.region_52.213_spmd.clone.sunk | while | flops 42194976 | bytes 42934304 | solution.py:165
  791.7 51.8 %reduce-scatter.31.cloned.1.call-done = f32[96,4]{1,0:T(8,128)} async-done(((f32[1536,4]{1,0:T(8,128)}), f32[96,4]{1,0:T(8,128)}) %reduce-scatter.31.cloned.1.call-update) | async-done | bytes 1552
  844.9 124.8 %reduce-scatter.35.cloned.1.call-done = f32[96,16]{1,0:T(8,128)} async-done(((f32[1536,16]{1,0:T(8,128)}), f32[96,16]{1,0:T(8,128)}) %reduce-scatter.35.cloned.1.call-update) | async-done | bytes 6160
  971.2 124.6 %reduce-scatter.33.cloned.1.call-done = f32[96,96]{1,0:T(8,128)} async-done(((f32[1536,96]{1,0:T(8,128)}), f32[96,96]{1,0:T(8,128)}) %reduce-scatter.33.cloned.1.call-update) | async-done | bytes 36880
  1097.3 23.8 all-reduce.27.cloned.1.call-done
  1122.9 77.2 %all-reduce.11 = (f32[1536]{0:T(1024)S(1)}, f32[1536]{0:T(1024)S(1)}, f32[128]{0:T(128)S(1)}, f32[1536]{0:T(1024)S(1)}, f32[1536]{0:T(1024)S(1)}, /*index=5*/f32[1536]{0:T(1024)S(1)}) all-reduce(f32[1536]{0:T(1024)S(1)} %get-tuple-element.1287, ...), channel_id=5, replica_groups=mesh['seq'=16,'head'=2] {'seq'}, use_global_device_ids=true, to_apply=%region_221.222.clone | all-reduce | flops 7808 | bytes 62464
  1208.0 42.4 %reduce-scatter.21.cloned.1.call-done = f32[1536,8]{0,1:T(8,128)} async-done(((f32[1536,128]{0,1:T(8,128)}), f32[1536,8]{0,1:T(8,128)}) %reduce-scatter.21.cloned.1.call-update) | async-done | bytes 49168 | tf_op jit(solution)/shard_map/reduce_scatter | solution.py:314
  1250.4 177.3 %reduce-scatter.23.cloned.1.call-done = f32[1536,96]{0,1:T(8,128)} async-done(((f32[1536,1536]{0,1:T(8,128)}), f32[1536,96]{0,1:T(8,128)}) %reduce-scatter.23.cloned.1.call-update) | async-done | bytes 589840 | tf_op jit(solution)/shard_map/reduce_scatter | solution.py:320
  1427.7 208.9 %reduce-scatter.25.cloned.1.call-done = f32[96,2048]{1,0:T(8,128)} async-done(((f32[1536,2048]{1,0:T(8,128)}), f32[96,2048]{1,0:T(8,128)}) %reduce-scatter.25.cloned.1.call-update) | async-done | bytes 786448 | tf_op jit(solution)/shard_map/reduce_scatter | solution.py:322
  1636.6 210.6 %reduce-scatter.27.cloned.1.call-done = f32[96,2048]{1,0:T(8,128)} async-done(((f32[1536,2048]{1,0:T(8,128)}), f32[96,2048]{1,0:T(8,128)}) %reduce-scatter.27.cloned.1.call-update) | async-done | bytes 786448 | tf_op jit(solution)/shard_map/reduce_scatter | solution.py:323
  1847.2 209.8 %reduce-scatter.29.cloned.1.call-done = f32[2048,96]{0,1:T(8,128)} async-done(((f32[2048,1536]{0,1:T(8,128)}), f32[2048,96]{0,1:T(8,128)}) %reduce-scatter.29.cloned.1.call-update) | async-done | bytes 786448 | tf_op jit(solution)/shard_map/reduce_scatter | solution.py:324
  2057.0 177.8 %reduce-scatter.19.cloned.1.call-done = f32[96,1536]{1,0:T(8,128)} async-done(((f32[1536,1536]{1,0:T(8,128)}), f32[96,1536]{1,0:T(8,128)}) %reduce-scatter.19.cloned.1.call-update) | async-done | bytes 589840 | tf_op jit(solution)/shard_map/reduce_scatter | solution.py:311
  2234.7 176.1 %reduce-scatter.17.cloned.1.call-done = f32[96,1536]{1,0:T(8,128)} async-done(((f32[1536,1536]{1,0:T(8,128)}), f32[96,1536]{1,0:T(8,128)}) %reduce-scatter.17.cloned.1.call-update) | async-done | bytes 589840 | tf_op jit(solution)/shard_map/reduce_scatter | solution.py:310
  (1429 shorter events, 527.9 us)
Async XLA Ops:
  7.2 42.2 %all-reduce.19.cloned.1.call-start = ((), (), s32[]{:S(2)}) async-start(), calls=%async_computation.10 | async-start | bytes 262144 | tf_op jit(solution)/shard_map/psum | solution.py:213
  12.8 9.7 collective-permute-start
  17.8 4.7 collective-permute-start.1
  29.4 135.8 %all-gather.7.cloned.1.call-start = ((), (), s32[]{:S(2)}) async-start(), calls=%async_computation.21 | async-start | bytes 3342336 | tf_op jit(solution)/shard_map/all_gather | solution.py:19
  95.6 139.5 %all-gather.9.cloned.1.call-start = ((), (), s32[]{:S(2)}) async-start(), calls=%async_computation.22 | async-start | bytes 3342336 | tf_op jit(solution)/shard_map/all_gather | solution.py:19
  96.4 246.1 %all-reduce.21.cloned.1.call-start = ((), (), s32[]{:S(2)}) async-start(), calls=%async_computation.11 | async-start | bytes 3145728 | tf_op jit(solution)/shard_map/psum | solution.py:237
  255.8 55.6 %copy-start.98 = (f32[1536]{0:T(1024)S(1)}, f32[1536]{0:T(1024)}, u32[]{:S(2)}) copy-start(f32[1536]{0:T(1024)} %param.44) | copy-start | bytes 18436
  323.3 62.2 %all-reduce.23.cloned.1.call-start = ((), (), s32[]{:S(2)}) async-start(), calls=%async_computation.12 | async-start | bytes 3145728 | tf_op jit(solution)/shard_map/psum | solution.py:252
  363.8 158.1 %all-gather.11.cloned.1.call-start = ((), (), s32[]{:S(2)}) async-start(), calls=%async_computation.23 | async-start | bytes 3342336 | tf_op jit(solution)/shard_map/all_gather | solution.py:19
  452.4 254.4 %all-reduce.25.cloned.1.call-start = ((), (), s32[]{:S(2)}) async-start(), calls=%async_computation.13 | async-start | bytes 262144 | tf_op jit(solution)/shard_map/psum | solution.py:276
  690.3 153.2 %reduce-scatter.31.cloned.1.call-start = ((), (), s32[]{:S(2)}) async-start(), calls=%async_computation.24 | async-start | bytes 835584
  719.7 250.0 %reduce-scatter.35.cloned.1.call-start = ((), (), s32[]{:S(2)}) async-start(), calls=%async_computation.26 | async-start | bytes 835584
  721.0 374.8 %reduce-scatter.33.cloned.1.call-start = ((), (), s32[]{:S(2)}) async-start(), calls=%async_computation.25 | async-start | bytes 835584
  728.5 392.6 %all-reduce.27.cloned.1.call-start = ((), (), s32[]{:S(2)}) async-start(), calls=%async_computation.27 | async-start | bytes 6291456 | tf_op jit(solution)/shard_map/psum | solution.py:244
  732.9 6.2 collective-permute-start.2
  741.8 508.6 %reduce-scatter.21.cloned.1.call-start = ((), (), s32[]{:S(2)}) async-start(), calls=%async_computation.16 | async-start | bytes 835584 | tf_op jit(solution)/shard_map/reduce_scatter | solution.py:314
  744.9 682.8 %reduce-scatter.23.cloned.1.call-start = ((), (), s32[]{:S(2)}) async-start(), calls=%async_computation.17 | async-start | bytes 10027008 | tf_op jit(solution)/shard_map/reduce_scatter | solution.py:320
  751.2 885.4 %reduce-scatter.25.cloned.1.call-start = ((), (), s32[]{:S(2)}) async-start(), calls=%async_computation.18 | async-start | bytes 13369344 | tf_op jit(solution)/shard_map/reduce_scatter | solution.py:322
  759.9 1087.3 %reduce-scatter.27.cloned.1.call-start = ((), (), s32[]{:S(2)}) async-start(), calls=%async_computation.19 | async-start | bytes 13369344 | tf_op jit(solution)/shard_map/reduce_scatter | solution.py:323
  767.5 1289.4 %reduce-scatter.29.cloned.1.call-start = ((), (), s32[]{:S(2)}) async-start(), calls=%async_computation.20 | async-start | bytes 13369344 | tf_op jit(solution)/shard_map/reduce_scatter | solution.py:324
  776.3 1458.4 %reduce-scatter.19.cloned.1.call-start = ((), (), s32[]{:S(2)}) async-start(), calls=%async_computation.15 | async-start | bytes 10027008 | tf_op jit(solution)/shard_map/reduce_scatter | solution.py:311
  782.5 1628.3 %reduce-scatter.17.cloned.1.call-start = ((), (), s32[]{:S(2)}) async-start(), calls=%async_computation.14 | async-start | bytes 10027008 | tf_op jit(solution)/shard_map/reduce_scatter | solution.py:310
  789.1 333.8 %copy-start.87 = (f32[1536]{0:T(1024)S(1)}, f32[1536]{0:T(1024)}, u32[]{:S(2)}) copy-start(f32[1536]{0:T(1024)} %get-tuple-element.1284) | copy-start | bytes 18436
  789.1 414.5 %copy-start.4 = (f32[2,128,1536]{2,1,0:T(8,128)S(1)}, f32[2,128,1536]{2,1,0:T(8,128)}, u32[]{:S(2)}) copy-start(f32[2,128,1536]{2,1,0:T(8,128)} %copy-done.2) | copy-start | bytes 4718596
  (226 other events, 1932.9 us)
Sparse Core Ops, SparseCore 0:
  29.5 19.8 all-reduce.18
  95.7 69.3 all-gather.6
  168.5 66.6 all-gather.8
  323.4 18.9 all-reduce.20
  364.0 21.5 all-reduce.22
  452.5 69.3 all-gather.10
  690.4 16.3 all-reduce.24
  719.8 123.6 reduce-scatter.30
  848.2 121.4 reduce-scatter.34
  974.3 121.5 reduce-scatter.32
  1098.8 22.2 all-reduce.26
  1127.0 123.3 reduce-scatter.20
  1257.6 170.0 reduce-scatter.22
  1433.8 202.7 reduce-scatter.24
  1643.6 203.5 reduce-scatter.26
  1853.3 203.6 reduce-scatter.28
  2064.0 170.6 reduce-scatter.18
  2240.8 169.9 reduce-scatter.16
where the time goes:
time: 2430 us; the launch traced here: 2420 us
  waiting for transfers between devices  1810 us (74%)
  other arithmetic  236 us (10%)
  local copies, waits for them, and re-layouts  157 us (6%)
  matrix products  107 us (4%)
  blocking collectives  77.2 us (3%)
    unnamed x21, waiting for transfers between devices  302 us
    reduce_scatter x1, waiting for transfers between devices, body(): lax.psum_scatter(grad_w_up, 'seq', scatter_dimension=0, tiled=True)  211 us
    reduce_scatter x1, waiting for transfers between devices, body(): lax.psum_scatter(grad_w_down, 'seq', scatter_dimension=1, tiled=True)  210 us
    reduce_scatter x1, waiting for transfers between devices, body(): lax.psum_scatter(grad_w_gate, 'seq', scatter_dimension=0, tiled=True)  209 us
    all_gather x3, waiting for transfers between devices, carried_in(): everything = jax.tree.map(lambda part: lax.all_gather(part, axis), shard)  207 us
    reduce_scatter x1, waiting for transfers between devices, body(): lax.psum_scatter(grad_w_outgate, 'seq', scatter_dimension=0, tiled=True)  178 us
    reduce_scatter x1, waiting for transfers between devices, body(): lax.psum_scatter(grad_w_mixout, 'seq', scatter_dimension=1, tiled=True)  177 us
    reduce_scatter x1, waiting for transfers between devices, body(): lax.psum_scatter(grad_w_inner, 'seq', scatter_dimension=0, tiled=True)  176 us
  transfers between devices with their start and end apart: 21, of which 20 were waited for; matrix products, arithmetic and copies ran while one was open for 3% of the time, Pallas kernels for 0%

commit v1 on v0

v1 whole, which is shorter than its diff:
```python
import functools, math
import jax, jax.numpy as jnp
from jax import lax
from jax.experimental import pallas as pl
from jax.experimental.pallas import tpu as pltpu

LOG2E = math.log2(math.e)
LN2 = math.log(2.0)
ROWS = 8


def params(limit=48):
    return pltpu.CompilerParams(vmem_limit_bytes=limit * 1024 * 1024)


def wide(tile, lanes):
    return jnp.concatenate([tile] * (lanes // tile.shape[1]), axis=1)


def pieces(lanes):
    return next(w for w in (256, 128) if lanes % w == 0)


def summary_kernel(df_ref, x_ref, b_ref, rate_ref, end_ref):
    streams, length, lanes = df_ref.shape
    n = rate_ref.shape[0]
    rate = rate_ref[...]

    def chunk(i, states):
        base = pl.multiple_of(i * ROWS, ROWS)
        out = []
        for s in range(streams):
            state = states[s]
            d = df_ref[s, pl.ds(base, ROWS), :]
            x = x_ref[s, pl.ds(base, ROWS), :]
            for j in range(ROWS):
                b = b_ref[s, pl.ds(pl.multiple_of((base + j) * n, n), n), :]
                fade = jnp.exp2(d[j : j + 1] * rate)
                state = fade * state + x[j : j + 1] * wide(b, lanes)
            out.append(state)
        return tuple(out)

    start = tuple(jnp.zeros((n, lanes), jnp.float32) for _ in range(streams))
    states = lax.fori_loop(0, length // ROWS, chunk, start)
    for s in range(streams):
        end_ref[s] = states[s]


def run_kernel(df_ref, x_ref, b_ref, c_ref, rate_ref, first_ref, y_ref):
    streams, length, lanes = df_ref.shape
    n = rate_ref.shape[0]
    rate = rate_ref[...]

    def chunk(i, states):
        base = pl.multiple_of(i * ROWS, ROWS)
        out = []
        for s in range(streams):
            state = states[s]
            d = df_ref[s, pl.ds(base, ROWS), :]
            x = x_ref[s, pl.ds(base, ROWS), :]
            rows = []
            for j in range(ROWS):
                at = pl.ds(pl.multiple_of((base + j) * n, n), n)
                fade = jnp.exp2(d[j : j + 1] * rate)
                state = fade * state + x[j : j + 1] * wide(b_ref[s, at, :], lanes)
                rows.append(jnp.sum(state * wide(c_ref[s, at, :], lanes), axis=0, keepdims=True))
            y_ref[s, pl.ds(base, ROWS), :] = jnp.concatenate(rows, axis=0)
            out.append(state)
        return tuple(out)

    lax.fori_loop(0, length // ROWS, chunk, tuple(first_ref[s] for s in range(streams)))


def adjoint_summary_kernel(df_ref, g_ref, c_ref, rate_ref, end_ref):
    streams, length, lanes = df_ref.shape
    n = rate_ref.shape[0]
    rate = rate_ref[...]
    chunks = length // ROWS

    def chunk(i, carry):
        base = pl.multiple_of((chunks - 1 - i) * ROWS, ROWS)
        out = []
        for s in range(streams):
            carried = carry[s]
            d = df_ref[s, pl.ds(base, ROWS), :]
            g = g_ref[s, pl.ds(base, ROWS), :]
            for j in reversed(range(ROWS)):
                at = pl.ds(pl.multiple_of((base + j) * n, n), n)
                fade = jnp.exp2(d[j : j + 1] * rate)
                carried = fade * (g[j : j + 1] * wide(c_ref[s, at, :], lanes) + carried)
            out.append(carried)
        return tuple(out)

    start = tuple(jnp.zeros((n, lanes), jnp.float32) for _ in range(streams))
    last = lax.fori_loop(0, chunks, chunk, start)
    for s in range(streams):
        end_ref[s] = last[s]


def adjoint_run_kernel(
    df_ref, d_ref, v_ref, g_ref, b_ref, c_ref, rate_ref, first_ref, last_ref,
    dstep_ref, dvalue_ref, db_ref, dc_ref, decay_ref, path_ref, fade_ref,
):
    streams, length, lanes = df_ref.shape
    n = rate_ref.shape[0]
    rate = rate_ref[...]
    chunks = length // ROWS

    @pl.when(pl.program_id(0) == 0)
    def _():
        db_ref[...] = jnp.zeros_like(db_ref)
        dc_ref[...] = jnp.zeros_like(dc_ref)

    def ahead(i, states):
        base = pl.multiple_of(i * ROWS, ROWS)
        out = []
        for s in range(streams):
            state = states[s]
            d = df_ref[s, pl.ds(base, ROWS), :]
            x = d_ref[s, pl.ds(base, ROWS), :] * v_ref[s, pl.ds(base, ROWS), :]
            for j in range(ROWS):
                at = pl.ds(pl.multiple_of((base + j) * n, n), n)
                path_ref[s, at, :] = state
                fade = jnp.exp2(d[j : j + 1] * rate)
                fade_ref[s, at, :] = fade
                state = fade * state + x[j : j + 1] * wide(b_ref[s, at, :], lanes)
            out.append(state)
        return tuple(out)

    ends = lax.fori_loop(0, chunks, ahead, tuple(first_ref[s] for s in range(streams)))

    def fold(tile):
        total = tile[:, :128]
        for k in range(1, lanes // 128):
            total = total + tile[:, k * 128 : (k + 1) * 128]
        return total

    def back(i, carry):
        base = pl.multiple_of((chunks - 1 - i) * ROWS, ROWS)
        out = []
        decay = carry[-1]
        for s in range(streams):
            state, carried = carry[s]
            d = d_ref[s, pl.ds(base, ROWS), :]
            v = v_ref[s, pl.ds(base, ROWS), :]
            g = g_ref[s, pl.ds(base, ROWS), :]
            x = d * v
            weights, touches = [None] * ROWS, [None] * ROWS
            for j in reversed(range(ROWS)):
                at = pl.ds(pl.multiple_of((base + j) * n, n), n)
                gj = g[j : j + 1]
                adjoint = gj * wide(c_ref[s, at, :], lanes) + carried
                dc_ref[s, at, :] += fold(state * gj)
                db_ref[s, at, :] += fold(adjoint * x[j : j + 1])
                weights[j] = jnp.sum(adjoint * wide(b_ref[s, at, :], lanes), axis=0, keepdims=True)
                carried = adjoint * fade_ref[s, at, :]
                state = path_ref[s, at, :]
                touch = carried * state
                touches[j] = jnp.sum(touch * rate, axis=0, keepdims=True)
                decay = decay + touch * d[j : j + 1]
            weighted = jnp.concatenate(weights, axis=0)
            dstep_ref[s, pl.ds(base, ROWS), :] = weighted * v + jnp.concatenate(touches, axis=0) * LN2
            dvalue_ref[s, pl.ds(base, ROWS), :] = weighted * d
            out.append((state, carried))
        return tuple(out) + (decay,)

    start = tuple((ends[s], last_ref[s]) for s in range(streams))
    done = lax.fori_loop(0, chunks, back, start + (jnp.zeros((n, lanes), jnp.float32),))
    decay_ref[...] = done[-1]


def scan_call(kernel, operands, kinds, outs, out_kinds, scratch=(), flops=0, block=None):
    streams, length, channels = operands[0].shape
    n = next(o for o, k in zip(operands, kinds) if k == "r").shape[0]
    lanes = block or pieces(channels)
    specs = {
        "e": pl.BlockSpec((streams, length, lanes), lambda i: (0, 0, i)),
        "n": pl.BlockSpec((streams, length * n, 128), lambda i: (0, 0, 0)),
        "r": pl.BlockSpec((n, lanes), lambda i: (0, i)),
        "h": pl.BlockSpec((streams, n, lanes), lambda i: (0, 0, i)),
    }
    shapes = {
        "e": (streams, length, channels),
        "n": (streams, length * n, 128),
        "r": (n, channels),
        "h": (streams, n, channels),
    }
    size = streams * length * n * channels
    return pl.pallas_call(
        kernel,
        grid=(channels // lanes,),
        in_specs=[specs[k] for k in kinds],
        out_specs=[specs[k] for k in out_kinds] if len(out_kinds) > 1 else specs[out_kinds],
        out_shape=[jax.ShapeDtypeStruct(shapes[k], jnp.float32) for k in out_kinds]
        if len(out_kinds) > 1
        else jax.ShapeDtypeStruct(shapes[out_kinds], jnp.float32),
        scratch_shapes=[pltpu.VMEM((streams, length * n, lanes), jnp.float32) for _ in scratch],
        compiler_params=params(),
        cost_estimate=pl.CostEstimate(flops=size * flops, bytes_accessed=4 * size // n * 4, transcendentals=size),
    )(*operands)


def summarize(df, x, b, rate, block=None):
    return scan_call(summary_kernel, (df, x, b, rate), "eenr", 1, "h", flops=5, block=block)

def run_states(df, x, b, c, rate, first, block=None):
    return scan_call(run_kernel, (df, x, b, c, rate, first), "eennrh", 1, "e", flops=8, block=block)

def adjoint_summary(df, g, c, rate, block=None):
    return scan_call(adjoint_summary_kernel, (df, g, c, rate), "eenr", 1, "h", flops=5, block=block)

def adjoint_run(df, d, v, g, b, c, rate, first, last, block=None):
    return scan_call(adjoint_run_kernel, (df, d, v, g, b, c, rate, first, last), "eeeennrhh", 5, "eennr", scratch="ab", flops=24, block=block)


from jax.sharding import PartitionSpec as P

epsilon = 1e-06
SIDE = 4
CUT = 1e6


def links(step, wrap=False, axis="seq"):
    n = lax.axis_size(axis)
    return [(i, (i + step) % n) for i in range(n) if wrap or 0 <= i + step < n]


def swaps(bit, axis="seq"):
    return [(i, i ^ bit) for i in range(lax.axis_size(axis))]


def send(block, route, axis="seq"):
    return lax.ppermute(block, axis, route)


def head_sum(part):
    return part + send(part, swaps(1, "head"), "head")


def both_streams(mine):
    other = send(mine, swaps(1, "head"), "head")
    first = lax.axis_index("head") == 0
    return jnp.where(first, mine, other), jnp.where(first, other, mine)


def own_stream(block):
    return lax.dynamic_index_in_dim(block, lax.axis_index("head"), 0, keepdims=False)


def unswap(parts, place):
    odd, far = (place & 1) == 1, (place & 2) == 2
    p = list(parts)
    p = [jnp.where(odd, p[k ^ 1], p[k]) for k in range(4)]
    return [jnp.where(far, p[k ^ 2], p[k]) for k in range(4)]


def part_of(block, index, size, axis):
    return lax.dynamic_slice_in_dim(block, index * size, size, axis)


def exchange(block, place):
    size = block.shape[-1] // SIDE
    axis = block.ndim - 1
    pieces_out = [part_of(block, place ^ k, size, axis) for k in range(SIDE)]
    return [pieces_out[0]] + [send(pieces_out[k], swaps(k)) for k in range(1, SIDE)]


def gather_side(block):
    mine = own_stream(block)
    near, far = send(mine, swaps(1)), send(mine, swaps(2))
    half = mine.shape[0] // 2
    top = send(far[:half], swaps(1))
    low = send(near[half:], swaps(2))
    return [jnp.stack(both_streams(part)) for part in (near, far, jnp.concatenate([top, low]))]


def gather_line(block, stride):
    mine = own_stream(block)
    n = lax.axis_size("seq")
    up, down, ups, downs = mine, mine, [], []
    for turn in range(SIDE - 1):
        up = send(up, [(i, i + stride) for i in range(turn * stride, n - stride)])
        down = send(down, [(i, i - stride) for i in range(stride, n - turn * stride)])
        ups.append(up)
        downs.append(down)
    got = [downs[k] + ups[SIDE - 2 - k] for k in range(SIDE - 1)]
    return [jnp.stack(both_streams(part)) for part in got]


def scatter_line(blocks, stride):
    n = lax.axis_size("seq")
    z = lax.axis_index("seq") // stride
    take = lambda at: lax.dynamic_index_in_dim(blocks, jnp.clip(at, 0, SIDE - 1), 0, keepdims=False)
    up = down = None
    for turn in range(SIDE - 1):
        one, two = take(SIDE - 1 - turn + z), take(z + turn - SIDE + 1)
        if turn:
            one, two = one + up, two + down
        up = send(one, [(i, i + stride) for i in range(min((turn + 1) * stride, n - stride))])
        down = send(two, [(i, i - stride) for i in range(max(n - (turn + 1) * stride, stride), n)])
    return take(z) + (up + down)


def scatter_bits(blocks, bits):
    here = lax.axis_index("seq")
    order = sorted(bits)
    shape = blocks.shape[1:]
    left = list(order)
    blocks = blocks.reshape((2,) * len(order) + shape)
    for bit in bits:
        axis = len(left) - 1 - left.index(bit)
        mine = (here // bit) % 2
        keep = lax.dynamic_index_in_dim(blocks, mine, axis, keepdims=False)
        away = lax.dynamic_index_in_dim(blocks, 1 - mine, axis, keepdims=False)
        blocks = keep + send(away, swaps(bit))
        left.remove(bit)
    return blocks


def bits_between(low, high):
    out = []
    while low < high:
        out.append(low)
        low *= 2
    return out


def chained(ends, total, rate, reverse):
    streams, n, channels = ends.shape
    here = lax.axis_index("seq")
    groups = lax.axis_size("seq") // SIDE
    place = here % SIDE
    width = channels // SIDE
    through = lambda d: jnp.exp2(d[:, None, :] * rate_here)
    rate_here = part_of(rate, place, width, 1)
    packed = jnp.concatenate([ends.reshape(streams * n, channels), total], axis=0)
    members = unswap(exchange(packed, place), place)
    members = [(m[: streams * n].reshape(streams, n, width), m[streams * n :]) for m in members]
    order = range(SIDE - 1, -1, -1) if reverse else range(SIDE)
    before, passed = {}, {}
    state, steps = jnp.zeros((streams, n, width), jnp.float32), jnp.zeros((streams, width), jnp.float32)
    for j in order:
        before[j], passed[j] = state, steps
        state = through(members[j][1]) * state + members[j][0]
        steps = steps + members[j][1]
    packed = jnp.concatenate([state.reshape(streams * n, width), steps], axis=0)
    sign = -SIDE if reverse else SIDE
    entering = jnp.zeros_like(state)
    for k in range(groups - 1, 0, -1):
        got = send(packed, links(sign * k))
        entering = through(got[streams * n :]) * entering + got[: streams * n].reshape(state.shape)
    mine = [through(passed[j]) * entering + before[j] for j in range(SIDE)]
    mine = unswap(mine, place)
    back = [mine[0]] + [send(mine[k], swaps(k)) for k in range(1, SIDE)]
    return jnp.concatenate(unswap(back, place), axis=2)


def matmul(left, right):
    return jnp.dot(left, right, preferred_element_type=jnp.float32)


def matmul_back(left, right):
    return lax.dot_general(
        left, right, (((left.ndim - 1,), (1,)), ((), ())), preferred_element_type=jnp.float32
    )


def weight_outer(left, right):
    axes = tuple(range(left.ndim - 1))
    return lax.dot_general(left, right, ((axes, axes), ((), ())), preferred_element_type=jnp.float32)


def norm_forward(v, gain):
    scale = lax.rsqrt(jnp.mean(v * v, axis=-1, keepdims=True) + epsilon)
    return (v * scale * gain, scale)


def norm_backward(v, scale, gain, upstream):
    weighted = upstream * gain
    d_input = scale * weighted - v * scale * scale * scale * jnp.mean(
        weighted * v, axis=-1, keepdims=True
    )
    d_gain = jnp.sum(upstream * v * scale, axis=(0, 1))
    return (d_input, d_gain)


def silu_slope(v):
    sig = jax.nn.sigmoid(v)
    return sig + v * sig * (1.0 - sig)


def across(small):
    streams, length, n = small.shape
    return jnp.broadcast_to(small.reshape(streams, length * n, 1), (streams, length * n, 128))


def along(wide_sum, n):
    streams, rows, _ = wide_sum.shape
    return jnp.sum(wide_sum, axis=-1).reshape(streams, rows // n, n)


def body(
    tokens, doc_ids, out_grad, norm_mix, w_inner, w_outgate, conv_taps, conv_bias, w_select, select_gain,
    w_step, step_bias, log_decay, skip_gain, w_mixout, norm_ffn, w_gate, w_up, w_down,
):
    streams, length, width = tokens.shape
    channels = w_inner.shape[1]
    taps = conv_taps.shape[0]
    rank = w_step.shape[0]
    states = log_decay.shape[1]
    lead = taps - 1
    count = lax.axis_size("seq")
    stride = count // SIDE
    here = lax.axis_index("seq")
    z, place = here // stride, here % SIDE
    low = jnp.bfloat16

    whole = (doc_ids[0, 0] >= 0).astype(jnp.float32)
    lower = lambda part: (part * whole).astype(low)
    grad_in = out_grad.astype(jnp.float32)
    source = tokens.astype(jnp.float32)
    line_grad = [lower(part) for part in gather_line(grad_in, stride)]
    normed, scale_mix = norm_forward(source, norm_mix)
    normed_low = normed.astype(low)
    side_normed = [lower(part) for part in gather_side(normed_low.astype(jnp.float32))]
    inner = matmul(normed_low, w_inner)
    outgate = matmul(normed_low, w_outgate)
    rim_ids = (doc_ids[:, length - lead :] + 1).astype(jnp.float32)
    rim_val = send(inner[:, length - lead :], links(1))
    rim_got = send(rim_ids, links(1))
    ext_val = jnp.concatenate([rim_val, inner], axis=1)
    ext_ids = jnp.concatenate([rim_got.astype(jnp.int32) - 1, doc_ids], axis=1)
    masks = [
        (ext_ids[:, k : k + length] == doc_ids).astype(jnp.float32)[:, :, None] for k in range(taps)
    ]
    value_pre = jnp.zeros_like(inner) + conv_bias
    for k in range(taps):
        value_pre = value_pre + conv_taps[k] * ext_val[:, k : k + length] * masks[k]
    value = jax.nn.silu(value_pre)
    value_low = value.astype(low)
    select = head_sum(matmul(value_low, w_select))
    raw_step = select[..., :rank]
    raw_b = select[..., rank : rank + states]
    raw_c = select[..., rank + states :]
    step_n, step_scale = norm_forward(raw_step, select_gain[:rank])
    bsel, b_scale = norm_forward(raw_b, select_gain[rank : rank + states])
    csel, c_scale = norm_forward(raw_c, select_gain[rank + states :])
    step_low = step_n.astype(low)
    step_pre = matmul(step_low, w_step) + step_bias
    step = jax.nn.softplus(step_pre)
    keep = doc_ids == ext_ids[:, lead - 1 : lead - 1 + length]
    fall = jnp.where(keep[:, :, None], step, CUT)
    gain = step * value
    decay_rate = -jnp.exp(log_decay).T
    rate = decay_rate * LOG2E
    b_wide, c_wide = across(bsel), across(csel)
    ends = summarize(fall, gain, b_wide, rate)
    total = jnp.sum(fall, axis=1)
    first = chained(ends, total, rate, False)
    outs = run_states(fall, gain, b_wide, c_wide, rate, first)
    y = outs + skip_gain * value
    gate_z = jax.nn.silu(outgate)
    mixed = y * gate_z
    mixed_low = mixed.astype(low)
    side_mixed = exchange(mixed_low.astype(jnp.float32), place)
    mix = head_sum(matmul(mixed_low, w_mixout))
    resid = source + mix
    hidden, scale_ffn = norm_forward(resid, norm_ffn)
    hidden_low = hidden.astype(low)
    line_hidden = [lower(part) for part in gather_line(hidden_low.astype(jnp.float32), stride)]
    gate = matmul(hidden_low, w_gate)
    up = matmul(hidden_low, w_up)
    act_low = (jax.nn.silu(gate) * up).astype(low)
    ffn = head_sum(matmul(act_low, w_down))
    output = (resid + ffn).astype(low)
    d_act = matmul_back(out_grad, w_down)
    d_gate = (d_act * up * silu_slope(gate)).astype(low)
    d_up = (d_act * jax.nn.silu(gate)).astype(low)
    d_hidden = head_sum(matmul_back(d_gate, w_gate) + matmul_back(d_up, w_up))
    d_resid_norm, grad_norm_ffn = norm_backward(resid, scale_ffn, norm_ffn, d_hidden)
    d_resid = grad_in + d_resid_norm
    d_mix = d_resid.astype(low)
    side_d_mix = [lower(part) for part in gather_side(d_mix.astype(jnp.float32))]

    d_mixed = matmul_back(d_mix, w_mixout)
    d_y = d_mixed * gate_z
    d_outgate = (d_mixed * y * silu_slope(outgate)).astype(low)
    side_d_outgate = exchange(d_outgate.astype(jnp.float32), place)
    grad_skip_gain = jnp.sum(d_y * value, axis=(0, 1))
    leaving = adjoint_summary(fall, d_y, c_wide, rate)
    last = chained(leaving, total, rate, True)
    d_step, d_scan, db_wide, dc_wide, decay_sum = adjoint_run(
        fall, step, value, d_y, b_wide, c_wide, rate, first, last
    )

    more_hidden = jnp.concatenate(line_hidden).reshape(-1, width)
    more_grad = jnp.concatenate(line_grad).reshape(-1, width)
    more_gate = matmul(more_hidden, w_gate)
    more_up = matmul(more_hidden, w_up)
    more_act = matmul_back(more_grad, w_down)
    flat = lambda block: block.reshape(-1, block.shape[-1])
    gates = jnp.concatenate([flat(d_gate), (more_act * more_up * silu_slope(more_gate)).astype(low)])
    ups = jnp.concatenate([flat(d_up), (more_act * jax.nn.silu(more_gate)).astype(low)])
    acts = jnp.concatenate([flat(act_low), (jax.nn.silu(more_gate) * more_up).astype(low)])
    cut = width // SIDE
    hidden_cut = part_of(jnp.concatenate([flat(hidden_low), more_hidden]), z, cut, 1)
    grad_cut = part_of(jnp.concatenate([flat(out_grad), more_grad]), z, cut, 1)
    side_bits = bits_between(1, stride)
    orders = (side_bits, side_bits[len(side_bits) // 2 :] + side_bits[: len(side_bits) // 2])

    def sum_side(whole):
        whole = whole.reshape(stride, width // count, -1)
        half = whole.shape[2] // 2
        return jnp.concatenate(
            [scatter_bits(whole[..., :half], orders[0]), scatter_bits(whole[..., half:], orders[1])], axis=-1
        )

    grad_w_gate = sum_side(weight_outer(hidden_cut, gates))
    grad_w_up = sum_side(weight_outer(hidden_cut, ups))
    grad_w_down = sum_side(weight_outer(grad_cut, acts)).T

    all_normed = flat(jnp.concatenate([normed_low] + side_normed))
    all_d_mix = flat(jnp.concatenate([d_mix] + side_d_mix))
    joined = lambda parts: lower(flat(jnp.concatenate(parts)))
    rest = bits_between(SIDE, stride)

    def sum_line(whole):
        whole = whole.reshape(SIDE, stride // SIDE, SIDE, width // count, -1)
        own = scatter_line(whole, stride)
        own = scatter_bits(own, rest) if rest else own[0]
        sent = unswap([own[k] for k in range(SIDE)], place)
        got = [sent[0]] + [send(sent[k], swaps(k)) for k in range(1, SIDE)]
        return jnp.concatenate(unswap(got, place), axis=-1)

    grad_w_mixout = sum_line(weight_outer(all_d_mix, joined(side_mixed))).T
    grad_w_outgate = sum_line(weight_outer(all_normed, joined(side_d_outgate)))

    d_value = d_y * skip_gain + d_scan
    d_step_pre = (d_step * jax.nn.sigmoid(step_pre)).astype(low)
    grad_step_bias = jnp.sum(d_step_pre, axis=(0, 1), dtype=jnp.float32)
    grad_w_step = weight_outer(step_low, d_step_pre)
    d_small = head_sum(
        jnp.concatenate(
            [matmul_back(d_step_pre, w_step), along(db_wide, states), along(dc_wide, states)], axis=-1
        )
    )
    d_raw_step, gain_step = norm_backward(
        raw_step, step_scale, select_gain[:rank], d_small[..., :rank]
    )
    d_raw_b, gain_b = norm_backward(
        raw_b, b_scale, select_gain[rank : rank + states], d_small[..., rank : rank + states]
    )
    d_raw_c, gain_c = norm_backward(
        raw_c, c_scale, select_gain[rank + states :], d_small[..., rank + states :]
    )
    grad_select_gain = jnp.concatenate([gain_step, gain_b, gain_c])
    d_select = jnp.concatenate([d_raw_step, d_raw_b, d_raw_c], axis=-1).astype(low)
    grad_w_select = weight_outer(d_select, value_low)
    d_value = d_value + matmul_back(d_select, w_select)
    d_value_pre = d_value * silu_slope(value_pre)
    grad_conv_bias = jnp.sum(d_value_pre, axis=(0, 1))
    tap_grads = []
    d_ext = jnp.zeros_like(ext_val)
    for k in range(taps):
        masked = d_value_pre * masks[k]
        tap_grads.append(jnp.sum(masked * ext_val[:, k : k + length], axis=(0, 1)))
        d_ext = d_ext + jnp.pad(masked * conv_taps[k], ((0, 0), (k, lead - k), (0, 0)))
    grad_conv_taps = jnp.stack(tap_grads)
    rim_grad = send(d_ext[:, :lead], links(-1))
    d_inner = (d_ext[:, lead:] + jnp.pad(rim_grad, ((0, 0), (length - lead, 0), (0, 0)))).astype(low)
    side_d_inner = exchange(d_inner.astype(jnp.float32), place)
    grad_w_inner = sum_line(weight_outer(all_normed, joined(side_d_inner)))
    d_normed = head_sum(matmul_back(d_inner, w_inner) + matmul_back(d_outgate, w_outgate))
    d_source, grad_norm_mix = norm_backward(source, scale_mix, norm_mix, d_normed)
    tokens_grad = d_resid + d_source

    pad = lambda v: jnp.pad(v, (0, channels - v.shape[0]))
    selects = grad_select_gain.reshape(count, -1)
    tall = jnp.concatenate(
        [
            grad_w_step,
            decay_sum * decay_rate,
            grad_conv_taps,
            jnp.stack([grad_conv_bias, grad_step_bias, grad_skip_gain, grad_norm_mix, grad_norm_ffn]),
        ]
    )
    tall = jnp.swapaxes(tall.reshape(tall.shape[0], count, -1), 0, 1)
    selects = jnp.pad(selects, ((0, 0), (0, tall.shape[2] - selects.shape[1])))
    tall = jnp.concatenate([tall, selects[:, None]], axis=1)
    broad = grad_w_select.reshape(count, -1, channels)
    every = bits_between(1, count)
    turned = every[1:2] + every[:1] + every[2:]
    tall = scatter_bits(tall, every)
    broad = scatter_bits(broad, turned)
    at = rank + states
    return (
        output,
        tokens_grad,
        tall[at + taps + 3],
        grad_w_inner,
        grad_w_outgate,
        tall[at : at + taps],
        tall[at + taps],
        broad.T,
        tall[at + taps + 5, : grad_select_gain.shape[0] // count],
        tall[:rank],
        tall[at + taps + 1],
        tall[rank:at].T,
        tall[at + taps + 2],
        grad_w_mixout,
        tall[at + taps + 4],
        grad_w_gate,
        grad_w_up,
        grad_w_down,
    )


def solution(mesh):
    in_specs = (
        P(None, "seq", None),
        P(None, "seq"),
        P(None, "seq", None),
        P(),
        P(None, "head"),
        P(None, "head"),
        P(None, "head"),
        P("head"),
        P("head", None),
        P(),
        P(None, "head"),
        P("head"),
        P("head", None),
        P("head"),
        P("head", None),
        P(),
        P(None, "head"),
        P(None, "head"),
        P("head", None),
    )
    out_specs = (
        P(None, "seq", None),
        P(None, "seq", None),
        P("seq"),
        P("seq", "head"),
        P("seq", "head"),
        P(None, ("head", "seq")),
        P(("head", "seq")),
        P("head", "seq"),
        P("seq"),
        P(None, ("head", "seq")),
        P(("head", "seq")),
        P(("head", "seq"), None),
        P(("head", "seq")),
        P("head", "seq"),
        P("seq"),
        P("seq", "head"),
        P("seq", "head"),
        P("head", "seq"),
    )
    return jax.shard_map(body, mesh=mesh, in_specs=in_specs, out_specs=out_specs, check_vma=False)
```

time: 2430 us -> 717 us (0.30)
  waiting for transfers between devices: 1810 us -> 205 us
  starting transfers between devices: 11.5 us -> 190 us
  other arithmetic: 236 us -> 84.9 us
  local copies, waits for them, and re-layouts: 157 us -> 64.7 us
  blocking collectives: 77.2 us -> 0 us
  Pallas kernels: 0 us -> 54.5 us
    reduce_scatter x7 -> x0, waiting for transfers between devices: 1200 us -> none  [the longest x1 211 us: body(): lax.psum_scatter(grad_w_up, 'seq', scatter_dimension=0, tiled=True)]
    unnamed x21 -> x0, waiting for transfers between devices: 302 us -> none
    all_gather x3 -> x0, waiting for transfers between devices: 207 us -> none  [carried_in(): everything = jax.tree.map(lambda part: lax.all_gather(part, axis), shard)]
    ppermute x3 -> x115, waiting for transfers between devices: 5.02 us -> 205 us  [send(): return lax.ppermute(block, axis, route)]
    ppermute x3 -> x115, starting transfers between devices: 9.79 us -> 190 us  [send(): return lax.ppermute(block, axis, route)]
    mul x112 -> x2, local copies, waits for them, and re-layouts: 106 us -> 0.2 us  [norm_forward(): return (v * scale * gain, scale)]
    reduce_sum x105 -> x2, other arithmetic: 97.2 us -> 4.44 us  [along(): return jnp.sum(wide_sum, axis=-1).reshape(streams, rows // n, n)]
    psum x5 -> x0, waiting for transfers between devices: 89.7 us -> none  [the longest x1 23.8 us: body(): ffn = lax.psum(matmul(act_low, w_down), 'head')]
  transfers between devices with their start and end apart: 21 -> 115, of which waited for: 20 -> 39; matrix products, arithmetic and copies ran while one was open for 3% -> 31% of each run, Pallas kernels for 0% -> 7%
where the time goes in v1:
time: 717 us; the launch traced here: 707 us
  waiting for transfers between devices  205 us (29%)
  starting transfers between devices  190 us (26%)
  matrix products  103 us (14%)
  other arithmetic  84.9 us (12%)
  local copies, waits for them, and re-layouts  64.7 us (9%)
  Pallas kernels  54.5 us (8%)
    ppermute x115, waiting for transfers between devices, send(): return lax.ppermute(block, axis, route)  205 us
    ppermute x115, starting transfers between devices, send(): return lax.ppermute(block, axis, route)  190 us
    pallas_call x4, Pallas kernels, scan_call(): pl.pallas_call(kernel, grid=(channels // lanes,), in_specs=[specs[k] for...  54.5 us
    dot_general x10, matrix products, matmul(): return jnp.dot(left, right, preferred_element_type=jnp.float32)  44.1 us
    dot_general x9, matrix products, matmul_back(): lax.dot_general(left, right, (((left.ndim - 1,), (1,)), ((), ())), prefer...  41.5 us
    unnamed x292, local copies, waits for them, and re-layouts  27.8 us
    dot_general x8, matrix products, weight_outer(): lax.dot_general(left, right, ((axes, axes), ((), ())), preferred_element_...  17.2 us
  transfers between devices with their start and end apart: 115, of which 39 were waited for; matrix products, arithmetic and copies ran while one was open for 31% of the time, Pallas kernels for 7%

profile of v1, /device:TPU:0, one launch (start us, length us, event | category | flops | bytes accessed | tf_op | source)
XLA Modules:
  0.0 706.9 jit_solution(16358956008478701346)
XLA Ops:
  69.6 9.2 %collective-permute-done.9 = f32[2,16,384]{2,1,0:T(8,128)S(1)} collective-permute-done((f32[2,16,384]{2,1,0:T(8,128)}, f32[2,16,384]{2,1,0:T(8,128)S(1)}, u32[]{:S(2)}, u32[]{:S(2)}) %collective-permute-start.9) | collective-permute-done | bytes 49184 | tf_op jit(solution)/shard_map/ppermute | solution.py:233
  87.7 12.5 %shard_map.323 = f32[2,128,1536]{2,1,0:T(8,128)S(1)} custom-call(f32[2,128,1536]{2,1,0:T(8,128)S(1)} %copy-done.5, f32[2,128,1536]{2,1,0:T(8,128)S(1)} %copy-done.13, f32[2,2048,128]{2,1,0:T(8,128)} %copy-done.2, f32[2,2048,128]{2,1,0:T(8,128)} %broadcast_in_dim.25.c_ref, f32[16,1536]{1,0:T(8,128)S(1)} %bitcast_multiply_fusion.1.rate_ref, ...), custom_call_target="tpu_custom_call" | custom-call | flops 50331648 | bytes 6291456 | tf_op jit(solution)/shard_map/pallas_call | solution.py:189
  100.3 5.8 fusion.133
  132.6 16.6 %collective-permute-done.99 = f32[128,1536]{1,0:T(8,128)S(1)} collective-permute-done((f32[128,1536]{1,0:T(8,128)S(1)}, f32[128,1536]{1,0:T(8,128)S(1)}, u32[]{:S(2)}, u32[]{:S(2)}) %collective-permute-start.99) | collective-permute-done | bytes 786464 | tf_op jit(solution)/shard_map/ppermute | solution.py:233
  174.9 6.2 collective-permute-start.86
  182.3 13.9 %collective-permute-done.85 = f32[128,1536]{1,0:T(8,128)} collective-permute-done((f32[128,1536]{1,0:T(8,128)S(1)}, f32[128,1536]{1,0:T(8,128)}, u32[]{:S(2)}, u32[]{:S(2)}) %collective-permute-start.85) | collective-permute-done | bytes 786464 | tf_op jit(solution)/shard_map/ppermute | solution.py:233
  211.1 10.7 %fusion.146 = f32[768,2048]{1,0:T(8,128)} fusion(bf16[768,1536]{1,0:T(8,128)(2,1)S(1)} %bitcast.422, bf16[2048,1536]{1,0:T(8,128)(2,1)} %param.37), kind=kOutput, calls=%fused_computation.530 | convolution fusion | flops 4831838208 | bytes 14942208 | tf_op jit(solution)/shard_map/dot_general | solution.py:363
  248.6 11.2 %collective-permute-done.20 = f32[34,384]{1,0:T(8,128)S(1)} collective-permute-done((f32[34,384]{1,0:T(8,128)S(1)}, f32[34,384]{1,0:T(8,128)S(1)}, u32[]{:S(2)}, u32[]{:S(2)}) %collective-permute-start.20) | collective-permute-done | bytes 52256 | tf_op jit(solution)/shard_map/ppermute | solution.py:233
  272.7 31.5 %shard_map.325 = (f32[2,128,1536]{2,1,0:T(8,128)S(1)}, f32[2,128,1536]{2,1,0:T(8,128)S(1)}, f32[2,2048,128]{2,1,0:T(8,128)}, f32[2,2048,128]{2,1,0:T(8,128)}, f32[16,1536]{1,0:T(8,128)S(1)}) custom-call(f32[2,128,1536]{2,1,0:T(8,128)S(1)} %copy-done.7, f32[2,128,1536]{2,1,0:T(8,128)} %get-tuple-element.169.d_ref, f32[2,128,1536]{2,1,0:T(8,128)} %get-tuple-element.82.v_ref, ...), custom_call_target="tpu_custom_call" | custom-call | flops 150994944 | bytes 6291456 | tf_op jit(solution)/shard_map/pallas_call | solution.py:189
  326.2 6.7 multiply_reduce_fusion.3
  359.4 12.7 %collective-permute-done.62 = f32[2,2,2,8,1536]{4,3,1,0,2:T(8,128)S(1)} collective-permute-done((f32[2,2,2,8,1536]{4,3,1,0,2:T(8,128)S(1)}, f32[2,2,2,8,1536]{4,3,1,0,2:T(8,128)S(1)}, u32[]{:S(2)}, u32[]{:S(2)}) %collective-permute-start.62) | collective-permute-done | bytes 393248 | tf_op jit(solution)/shard_map/ppermute | solution.py:233
  374.3 5.9 collective-permute-done.39
  388.7 14.9 %collective-permute-done.63 = f32[2,2,8,1536]{3,2,1,0:T(8,128)S(1)} collective-permute-done((f32[2,2,8,1536]{3,2,1,0:T(8,128)S(1)}, f32[2,2,8,1536]{3,2,1,0:T(8,128)S(1)}, u32[]{:S(2)}, u32[]{:S(2)}) %collective-permute-start.63) | collective-permute-done | bytes 196640 | tf_op jit(solution)/shard_map/ppermute | solution.py:233
  412.1 11.7 %collective-permute-start.65 = (f32[8,1536]{1,0:T(8,128)S(1)}, f32[8,1536]{1,0:T(8,128)S(1)}, u32[]{:S(2)}, u32[]{:S(2)}) collective-permute-start(f32[8,1536]{1,0:T(8,128)S(1)} %dynamic-slice_bitcast_fusion.17), channel_id=1, source_target_pairs={{0,16},{2,18},{4,20},{6,22},{8,24},{10,26},{12,28},{14,30},{16,0},... | collective-permute-start | bytes 147464 | tf_op jit(solution)/shard_map/ppermute | solution.py:233
  435.1 6.9 fusion.147
  441.9 12.4 %multiply_convert_fusion = (bf16[768,2048]{1,0:T(8,128)(2,1)}, bf16[768,2048]{1,0:T(8,128)(2,1)}, bf16[768,2048]{1,0:T(8,128)(2,1)}) fusion(f32[768,2048]{1,0:T(8,128)} %fusion.147, f32[768,2048]{1,0:T(8,128)} %fusion.146, bf16[768,1536]{1,0:T(8,128)(2,1)S(1)} %bitcast.425, bf16[1536,2048]{1,0:T(8,128)(2,1)S(1)} %bitcast.465), kind=kOutput, calls=%fused_computation.12 | convolution fusion | flops 4853858304 | bytes 30670848 | tf_op jit(solution)/shard_map/dot_general | solution.py:359
  480.8 13.7 %collective-permute-start.53 = (f32[1,4,96,384]{3,2,1,0:T(8,128)}, f32[1,4,96,384]{3,2,1,0:T(8,128)}, u32[]{:S(2)}, u32[]{:S(2)}) collective-permute-start(f32[1,4,96,384]{3,2,1,0:T(8,128)} %get-tuple-element.124), channel_id=1, source_target_pairs={{0,8},{2,10},{4,12},{6,14},{1,9},{3,11},{5,13},{7,15}} | collective-permute-start | bytes 1769480 | tf_op jit(solution)/shard_map/ppermute | solution.py:233
  527.6 9.9 %collective-permute-done.27 = f32[2,2,2,122,96]{4,2,1,0,3:T(2,128)} collective-permute-done((f32[2,2,2,122,96]{4,2,1,0,3:T(2,128)}, f32[2,2,2,122,96]{4,2,1,0,3:T(2,128)}, u32[]{:S(2)}, u32[]{:S(2)}) %collective-permute-start.27) | collective-permute-done | bytes 374816 | tf_op jit(solution)/shard_map/ppermute | solution.py:233
  551.1 6.9 collective-permute-done.107
  561.7 11.0 %collective-permute-done.111 = f32[2,96,1024]{2,1,0:T(8,128)S(1)} collective-permute-done((f32[2,96,1024]{2,1,0:T(8,128)S(1)}, f32[2,96,1024]{2,1,0:T(8,128)S(1)}, u32[]{:S(2)}, u32[]{:S(2)}) %collective-permute-start.111) | collective-permute-done | bytes 786464 | tf_op jit(solution)/shard_map/ppermute | solution.py:233
  583.6 11.4 %collective-permute-done.29 = f32[2,122,96]{2,1,0:T(8,128)S(1)} collective-permute-done((f32[2,122,96]{2,1,0:T(8,128)S(1)}, f32[2,122,96]{2,1,0:T(8,128)S(1)}, u32[]{:S(2)}, u32[]{:S(2)}) %collective-permute-start.29) | collective-permute-done | bytes 93728 | tf_op jit(solution)/shard_map/ppermute | solution.py:233
  643.5 8.0 %collective-permute-done.55 = f32[1,4,96,384]{3,2,1,0:T(8,128)S(1)} collective-permute-done((f32[1,4,96,384]{3,2,1,0:T(8,128)S(1)}, f32[1,4,96,384]{3,2,1,0:T(8,128)S(1)}, u32[]{:S(2)}, u32[]{:S(2)}) %collective-permute-start.55) | collective-permute-done | bytes 589856 | tf_op jit(solution)/shard_map/ppermute | solution.py:233
  655.5 8.6 %collective-permute-done.76 = f32[1,4,96,384]{3,2,1,0:T(8,128)S(1)} collective-permute-done((f32[1,4,96,384]{3,2,1,0:T(8,128)S(1)}, f32[1,4,96,384]{3,2,1,0:T(8,128)S(1)}, u32[]{:S(2)}, u32[]{:S(2)}) %collective-permute-start.76) | collective-permute-done | bytes 589856 | tf_op jit(solution)/shard_map/ppermute | solution.py:233
  675.0 9.7 %collective-permute-done.77 = f32[1,4,96,384]{3,2,1,0:T(8,128)S(1)} collective-permute-done((f32[1,4,96,384]{3,2,1,0:T(8,128)S(1)}, f32[1,4,96,384]{3,2,1,0:T(8,128)S(1)}, u32[]{:S(2)}, u32[]{:S(2)}) %collective-permute-start.77) | collective-permute-done | bytes 589856 | tf_op jit(solution)/shard_map/ppermute | solution.py:233
  (771 shorter events, 434.2 us)
Async XLA Ops:
  58.0 50.5 %collective-permute-start.33 = (f32[128,1536]{1,0:T(8,128)}, f32[128,1536]{1,0:T(8,128)}, u32[]{:S(2)}, u32[]{:S(2)}) collective-permute-start(f32[128,1536]{1,0:T(8,128)} %convert_bitcast_fusion.2), channel_id=1, source_target_pairs={{0,4},{2,6},{4,0},{6,2},{8,12},{10,14},{12,8},{14,10},{16,20},{18,... | collective-permute-start | bytes 2359304 | tf_op jit(solution)/shard_map/ppermute | solution.py:233
  59.4 49.9 %collective-permute-start.31 = (f32[128,1536]{1,0:T(8,128)}, f32[128,1536]{1,0:T(8,128)S(1)}, u32[]{:S(2)}, u32[]{:S(2)}) collective-permute-start(f32[128,1536]{1,0:T(8,128)} %convert_bitcast_fusion.2), channel_id=1, source_target_pairs={{0,2},{2,0},{4,6},{6,4},{8,10},{10,8},{12,14},{14,12},{16,18},{18,... | collective-permute-start | bytes 2359304 | tf_op jit(solution)/shard_map/ppermute | solution.py:233
  78.8 48.6 %collective-permute-start.94 = (f32[128,1536]{1,0:T(8,128)}, f32[128,1536]{1,0:T(8,128)S(1)}, u32[]{:S(2)}, u32[]{:S(2)}) collective-permute-start(f32[128,1536]{1,0:T(8,128)} %dynamic-slice_bitcast_fusion.6), channel_id=1, source_target_pairs={{8,0},{10,2},{12,4},{14,6},{16,8},{18,10},{20,12},{22,14},{24,16},... | collective-permute-start | bytes 2359304 | tf_op jit(solution)/shard_map/ppermute | solution.py:233
  80.1 46.5 %collective-permute-start.95 = (f32[128,1536]{1,0:T(8,128)}, f32[128,1536]{1,0:T(8,128)S(1)}, u32[]{:S(2)}, u32[]{:S(2)}) collective-permute-start(f32[128,1536]{1,0:T(8,128)} %dynamic-slice_bitcast_fusion.6), channel_id=1, source_target_pairs={{0,8},{2,10},{4,12},{6,14},{8,16},{10,18},{12,20},{14,22},{16,24},... | collective-permute-start | bytes 2359304 | tf_op jit(solution)/shard_map/ppermute | solution.py:233
  132.1 49.1 %collective-permute-start.37 = (f32[128,1536]{1,0:T(8,128)S(1)}, f32[128,1536]{1,0:T(8,128)S(1)}, u32[]{:S(2)}, u32[]{:S(2)}) collective-permute-start(f32[128,1536]{1,0:T(8,128)S(1)} %constant_dynamic-update-slice_fusion.11), channel_id=1, source_target_pairs={{0,1},{1,0},{2,3},{3,2},{4,5},{5,4},{6,7},{7,6},{8,9},{9,8},{10,11... | collective-permute-start | bytes 2359304 | tf_op jit(solution)/shard_map/ppermute | solution.py:233
  181.4 40.4 %collective-permute-start.14 = (f32[2,128,1536]{2,1,0:T(8,128)}, f32[2,128,1536]{2,1,0:T(8,128)}, u32[]{:S(2)}, u32[]{:S(2)}) collective-permute-start(f32[2,128,1536]{2,1,0:T(8,128)} %fusion.41), channel_id=1, source_target_pairs={{0,1},{1,0},{2,3},{3,2},{4,5},{5,4},{6,7},{7,6},{8,9},{9,8},{10,11... | collective-permute-start | bytes 4718600 | tf_op jit(solution)/shard_map/ppermute | solution.py:233
  196.2 69.9 %collective-permute-start.90 = (f32[128,1536]{1,0:T(8,128)}, f32[128,1536]{1,0:T(8,128)}, u32[]{:S(2)}, u32[]{:S(2)}) collective-permute-start(f32[128,1536]{1,0:T(8,128)} %collective-permute-done.85), channel_id=1, source_target_pairs={{8,0},{10,2},{12,4},{14,6},{16,8},{18,10},{20,12},{22,14},{9,1},{1... | collective-permute-start | bytes 2359304 | tf_op jit(solution)/shard_map/ppermute | solution.py:233
  197.5 69.8 %collective-permute-start.87 = (f32[128,1536]{1,0:T(8,128)}, f32[128,1536]{1,0:T(8,128)}, u32[]{:S(2)}, u32[]{:S(2)}) collective-permute-start(f32[128,1536]{1,0:T(8,128)} %collective-permute-done.86), channel_id=1, source_target_pairs={{8,16},{10,18},{12,20},{14,22},{16,24},{18,26},{20,28},{22,30},{9,... | collective-permute-start | bytes 2359304 | tf_op jit(solution)/shard_map/ppermute | solution.py:233
  266.1 84.8 %collective-permute-start.52 = (f32[2,128,384]{2,1,0:T(8,128)}, f32[2,128,384]{2,1,0:T(8,128)}, u32[]{:S(2)}, u32[]{:S(2)}) collective-permute-start(f32[2,128,384]{2,1,0:T(8,128)} %get-tuple-element.153), channel_id=1, source_target_pairs={{0,6},{2,4},{4,2},{6,0},{8,14},{10,12},{12,10},{14,8},{16,22},{18,... | collective-permute-start | bytes 1179656 | tf_op jit(solution)/shard_map/ppermute | solution.py:233
  267.3 86.5 %collective-permute-start.51 = (f32[2,128,384]{2,1,0:T(8,128)}, f32[2,128,384]{2,1,0:T(8,128)}, u32[]{:S(2)}, u32[]{:S(2)}) collective-permute-start(f32[2,128,384]{2,1,0:T(8,128)} %get-tuple-element.154), channel_id=1, source_target_pairs={{0,4},{2,6},{4,0},{6,2},{8,12},{10,14},{12,8},{14,10},{16,20},{18,... | collective-permute-start | bytes 1179656 | tf_op jit(solution)/shard_map/ppermute | solution.py:233
  270.8 84.0 %collective-permute-start.50 = (f32[2,128,384]{2,1,0:T(8,128)}, f32[2,128,384]{2,1,0:T(8,128)}, u32[]{:S(2)}, u32[]{:S(2)}) collective-permute-start(f32[2,128,384]{2,1,0:T(8,128)} %get-tuple-element.155), channel_id=1, source_target_pairs={{0,2},{2,0},{4,6},{6,4},{8,10},{10,8},{12,14},{14,12},{16,18},{18,... | collective-permute-start | bytes 1179656 | tf_op jit(solution)/shard_map/ppermute | solution.py:233
  272.0 133.9 %collective-permute-start.68 = (f32[128,1536]{1,0:T(8,128)}, f32[128,1536]{1,0:T(8,128)}, u32[]{:S(2)}, u32[]{:S(2)}) collective-permute-start(f32[128,1536]{1,0:T(8,128)} %convert_bitcast_fusion.1), channel_id=1, source_target_pairs={{0,4},{2,6},{4,0},{6,2},{8,12},{10,14},{12,8},{14,10},{16,20},{18,... | collective-permute-start | bytes 2359304 | tf_op jit(solution)/shard_map/ppermute | solution.py:233
  344.8 42.1 %collective-permute-start.91 = (f32[128,1536]{1,0:T(8,128)S(1)}, f32[128,1536]{1,0:T(8,128)S(1)}, u32[]{:S(2)}, u32[]{:S(2)}) collective-permute-start(f32[128,1536]{1,0:T(8,128)S(1)} %copy-done.51), channel_id=1, source_target_pairs={{0,1},{1,0},{2,3},{3,2},{4,5},{5,4},{6,7},{7,6},{8,9},{9,8},{10,11... | collective-permute-start | bytes 2359304 | tf_op jit(solution)/shard_map/ppermute | solution.py:233
  405.9 101.3 %collective-permute-start.13 = (f32[2,128,1536]{2,1,0:T(8,128)}, f32[2,128,1536]{2,1,0:T(8,128)}, u32[]{:S(2)}, u32[]{:S(2)}) collective-permute-start(f32[2,128,1536]{2,1,0:T(8,128)} %fusion.2), channel_id=1, source_target_pairs={{0,1},{1,0},{2,3},{3,2},{4,5},{5,4},{6,7},{7,6},{8,9},{9,8},{10,11... | collective-permute-start | bytes 4718600 | tf_op jit(solution)/shard_map/ppermute | solution.py:233
  426.4 70.2 %collective-permute-start.26 = (f32[2,128,1536]{2,1,0:T(8,128)S(1)}, f32[2,128,1536]{2,1,0:T(8,128)S(1)}, u32[]{:S(2)}, u32[]{:S(2)}) collective-permute-start(f32[2,128,1536]{2,1,0:T(8,128)S(1)} %fusion.38), channel_id=1, source_target_pairs={{0,1},{1,0},{2,3},{3,2},{4,5},{5,4},{6,7},{7,6},{8,9},{9,8},{10,11... | collective-permute-start | bytes 4718600 | tf_op jit(solution)/shard_map/ppermute | solution.py:233
  428.5 42.8 %collective-permute-start.69 = (f32[128,1536]{1,0:T(8,128)}, f32[128,1536]{1,0:T(8,128)S(1)}, u32[]{:S(2)}, u32[]{:S(2)}) collective-permute-start(f32[128,1536]{1,0:T(8,128)} %collective-permute-done.68), channel_id=1, source_target_pairs={{0,1},{1,0},{2,3},{3,2},{4,5},{5,4},{6,7},{7,6},{8,9},{9,8},{10,11... | collective-permute-start | bytes 2359304 | tf_op jit(solution)/shard_map/ppermute | solution.py:233
  429.9 50.9 %collective-permute-start.67 = (f32[128,1536]{1,0:T(8,128)S(1)}, f32[128,1536]{1,0:T(8,128)S(1)}, u32[]{:S(2)}, u32[]{:S(2)}) collective-permute-start(f32[128,1536]{1,0:T(8,128)S(1)} %collective-permute-done.66), channel_id=1, source_target_pairs={{0,1},{1,0},{2,3},{3,2},{4,5},{5,4},{6,7},{7,6},{8,9},{9,8},{10,11... | collective-permute-start | bytes 2359304 | tf_op jit(solution)/shard_map/ppermute | solution.py:233
  432.6 44.6 %collective-permute-start.57 = (f32[1,4,96,384]{3,2,1,0:T(8,128)}, f32[1,4,96,384]{3,2,1,0:T(8,128)}, u32[]{:S(2)}, u32[]{:S(2)}) collective-permute-start(f32[1,4,96,384]{3,2,1,0:T(8,128)} %dynamic-slice_add_fusion.4), channel_id=1, source_target_pairs={{16,8},{18,10},{20,12},{22,14},{24,16},{26,18},{28,20},{30,22},{17... | collective-permute-start | bytes 1769480 | tf_op jit(solution)/shard_map/ppermute | solution.py:233
  471.3 42.2 %collective-permute-start.72 = (f32[128,1536]{1,0:T(8,128)}, f32[128,1536]{1,0:T(8,128)}, u32[]{:S(2)}, u32[]{:S(2)}) collective-permute-start(f32[128,1536]{1,0:T(8,128)} %constant_dynamic-update-slice_fusion.13), channel_id=1, source_target_pairs={{0,1},{1,0},{2,3},{3,2},{4,5},{5,4},{6,7},{7,6},{8,9},{9,8},{10,11... | collective-permute-start | bytes 2359304 | tf_op jit(solution)/shard_map/ppermute | solution.py:233
  480.8 44.4 %collective-permute-start.53 = (f32[1,4,96,384]{3,2,1,0:T(8,128)}, f32[1,4,96,384]{3,2,1,0:T(8,128)}, u32[]{:S(2)}, u32[]{:S(2)}) collective-permute-start(f32[1,4,96,384]{3,2,1,0:T(8,128)} %get-tuple-element.124), channel_id=1, source_target_pairs={{0,8},{2,10},{4,12},{6,14},{1,9},{3,11},{5,13},{7,15}} | collective-permute-start | bytes 1769480 | tf_op jit(solution)/shard_map/ppermute | solution.py:233
  496.6 146.9 %collective-permute-start.58 = (f32[1,4,96,384]{3,2,1,0:T(8,128)}, f32[1,4,96,384]{3,2,1,0:T(8,128)}, u32[]{:S(2)}, u32[]{:S(2)}) collective-permute-start(f32[1,4,96,384]{3,2,1,0:T(8,128)} %get-tuple-element.123), channel_id=1, source_target_pairs={{8,0},{10,2},{12,4},{14,6},{16,8},{18,10},{20,12},{22,14},{24,16},... | collective-permute-start | bytes 1769480 | tf_op jit(solution)/shard_map/ppermute | solution.py:233
  504.0 36.1 %collective-permute-start.105 = (f32[2,96,1024]{2,1,0:T(8,128)}, f32[2,96,1024]{2,1,0:T(8,128)}, u32[]{:S(2)}, u32[]{:S(2)}) collective-permute-start(f32[2,96,1024]{2,1,0:T(8,128)} %dynamic-slice_bitcast_fusion.4), channel_id=1, source_target_pairs={{0,4},{2,6},{4,0},{6,2},{8,12},{10,14},{12,8},{14,10},{16,20},{18,... | collective-permute-start | bytes 2359304 | tf_op jit(solution)/shard_map/ppermute | solution.py:233
  545.8 36.9 %collective-permute-start.41 = (f32[1,4,96,384]{3,2,1,0:T(8,128)S(1)}, f32[1,4,96,384]{3,2,1,0:T(8,128)S(1)}, u32[]{:S(2)}, u32[]{:S(2)}) collective-permute-start(f32[1,4,96,384]{3,2,1,0:T(8,128)S(1)} %copy-done.75), channel_id=1, source_target_pairs={{0,8},{2,10},{4,12},{6,14},{1,9},{3,11},{5,13},{7,15}} | collective-permute-start | bytes 1769480 | tf_op jit(solution)/shard_map/ppermute | solution.py:233
  557.9 114.3 %collective-permute-start.46 = (f32[1,4,96,384]{3,2,1,0:T(8,128)S(1)}, f32[1,4,96,384]{3,2,1,0:T(8,128)S(1)}, u32[]{:S(2)}, u32[]{:S(2)}) collective-permute-start(f32[1,4,96,384]{3,2,1,0:T(8,128)S(1)} %copy-done.74), channel_id=1, source_target_pairs={{8,0},{10,2},{12,4},{14,6},{16,8},{18,10},{20,12},{22,14},{24,16},... | collective-permute-start | bytes 1769480 | tf_op jit(solution)/shard_map/ppermute | solution.py:233
  (231 other events, 3504.0 us)

commit v2 on v1

--- a/solution.py
+++ b/solution.py
@@ -3,6 +3,7 @@
 from jax import lax
 from jax.experimental import pallas as pl
 from jax.experimental.pallas import tpu as pltpu
+from jax.sharding import PartitionSpec as P
 
 LOG2E = math.log2(math.e)
 LN2 = math.log(2.0)
@@ -169,7 +170,7 @@
     decay_ref[...] = done[-1]
 
 
-def scan_call(kernel, operands, kinds, outs, out_kinds, scratch=(), flops=0, block=None):
+def scan_call(kernel, operands, kinds, out_kinds, scratch=(), flops=0, block=None):
     streams, length, channels = operands[0].shape
     n = next(o for o, k in zip(operands, kinds) if k == "r").shape[0]
     lanes = block or pieces(channels)
@@ -196,27 +197,315 @@
         else jax.ShapeDtypeStruct(shapes[out_kinds], jnp.float32),
         scratch_shapes=[pltpu.VMEM((streams, length * n, lanes), jnp.float32) for _ in scratch],
         compiler_params=params(),
-        cost_estimate=pl.CostEstimate(flops=size * flops, bytes_accessed=4 * size // n * 4, transcendentals=size),
+        cost_estimate=spans(flops),
     )(*operands)
 
 
 def summarize(df, x, b, rate, block=None):
-    return scan_call(summary_kernel, (df, x, b, rate), "eenr", 1, "h", flops=5, block=block)
+    return scan_call(summary_kernel, (df, x, b, rate), "eenr", "h", flops=6, block=block)
 
 def run_states(df, x, b, c, rate, first, block=None):
-    return scan_call(run_kernel, (df, x, b, c, rate, first), "eennrh", 1, "e", flops=8, block=block)
+    return scan_call(run_kernel, (df, x, b, c, rate, first), "eennrh", "e", flops=12, block=block)
 
 def adjoint_summary(df, g, c, rate, block=None):
-    return scan_call(adjoint_summary_kernel, (df, g, c, rate), "eenr", 1, "h", flops=5, block=block)
+    return scan_call(adjoint_summary_kernel, (df, g, c, rate), "eenr", "h", flops=6, block=block)
 
 def adjoint_run(df, d, v, g, b, c, rate, first, last, block=None):
-    return scan_call(adjoint_run_kernel, (df, d, v, g, b, c, rate, first, last), "eeeennrhh", 5, "eennr", scratch="ab", flops=24, block=block)
-
-
-from jax.sharding import PartitionSpec as P
+    return scan_call(adjoint_run_kernel, (df, d, v, g, b, c, rate, first, last), "eeeennrhh", "eennr", scratch="ab", flops=30, block=block)
+
+
+def spans(us):
+    return pl.CostEstimate(flops=int(us * 1.1e9), bytes_accessed=int(us * 3.0e6), transcendentals=0)
+
+
+def stack_tokens(target, own_ref, more_refs):
+    own = own_ref.shape[0]
+    target[:own, :] = own_ref[...].astype(target.dtype)
+    at = own
+    for ref in more_refs:
+        rows = ref.shape[0]
+        target[at : at + rows, :] = ref[...].astype(target.dtype)
+        at += rows
+
+
+def dot(left, right):
+    return jnp.dot(left, right, preferred_element_type=jnp.float32)
+
+
+def dot_back(left, right):
+    return lax.dot_general(left, right, (((1,), (1,)), ((), ())), preferred_element_type=jnp.float32)
+
+
+def ffn_kernel(stride, more, *refs):
+    hid_own, hid_more = refs[0], refs[1 : 1 + more]
+    grad_own, grad_more = refs[1 + more], refs[2 + more : 2 + 2 * more]
+    wg, wu, wd, dg_own, du_own, act_own = refs[2 + 2 * more : 8 + 2 * more]
+    out_gate, out_up, out_down = refs[8 + 2 * more : 11 + 2 * more]
+    hid, grad, hid_cut, grad_cut, dg, du, act = refs[11 + 2 * more :]
+    own = hid_own.shape[0]
+    cut = hid_cut.shape[0]
+
+    @pl.when(pl.program_id(0) == 0)
+    def _():
+        stack_tokens(hid, hid_own, hid_more)
+        stack_tokens(grad, grad_own, grad_more)
+        at = pl.ds(pl.multiple_of((lax.axis_index("seq") // stride) * cut, 128), cut)
+        hid_cut[...] = hid[:, at].T
+        grad_cut[...] = grad[:, at].T
+
+    dg[:own, :] = dg_own[...]
+    du[:own, :] = du_own[...]
+    act[:own, :] = act_own[...]
+
+    def turn(i, _):
+        rows = pl.ds(pl.multiple_of(i * own, own), own)
+        gate = dot(hid[rows, :], wg[...])
+        up = dot(hid[rows, :], wu[...])
+        d_act = dot_back(grad[rows, :], wd[...])
+        sig = 1.0 / (1.0 + jnp.exp(-gate))
+        silu = gate * sig
+        dg[rows, :] = (d_act * up * (sig + silu * (1.0 - sig))).astype(dg.dtype)
+        du[rows, :] = (d_act * silu).astype(du.dtype)
+        act[rows, :] = (silu * up).astype(act.dtype)
+        return 0
+
+    lax.fori_loop(1, hid.shape[0] // own, turn, 0)
+    out_gate[...] = dot(hid_cut[...], dg[...])
+    out_up[...] = dot(hid_cut[...], du[...])
+    out_down[...] = dot(grad_cut[...], act[...])
+
+
+def whole(shape):
+    return pl.BlockSpec(shape, lambda i: (0,) * len(shape), pipeline_mode=pl.Buffered(1))
+
+
+def ffn_grads(stride, hid_own, hid_more, grad_own, grad_more, w_gate, w_up, w_down, d_gate, d_up, act):
+    own, width = hid_own.shape
+    units = w_gate.shape[1]
+    cut = width // SIDE
+    block = next(b for b in (256, 128) if units % b == 0)
+    tokens = own + sum(part.shape[0] for part in hid_more)
+    low = jnp.bfloat16
+    column = lambda rows: pl.BlockSpec((rows, block), lambda i: (0, i))
+    return pl.pallas_call(
+        functools.partial(ffn_kernel, stride, len(hid_more)),
+        grid=(units // block,),
+        in_specs=[whole(a.shape) for a in (hid_own, *hid_more, grad_own, *grad_more)]
+        + [column(width), column(width), pl.BlockSpec((block, width), lambda i: (i, 0))]
+        + [column(own)] * 3,
+        out_specs=[column(cut)] * 3,
+        out_shape=[jax.ShapeDtypeStruct((cut, units), jnp.float32)] * 3,
+        scratch_shapes=[pltpu.VMEM((tokens, width), low)] * 2
+        + [pltpu.VMEM((cut, tokens), low)] * 2
+        + [pltpu.VMEM((tokens, block), low)] * 3,
+        compiler_params=params(56),
+        cost_estimate=spans(24),
+    )(hid_own, *hid_more, grad_own, *grad_more, w_gate, w_up, w_down, d_gate, d_up, act)
+
+
+def mixer_kernel(more, sides, *refs):
+    at = iter(range(len(refs)))
+    take = lambda count: [refs[next(at)] for _ in range(count)]
+    (norm_own,), norm_more = take(1), take(more)
+    (mix_own,), mix_more = take(1), take(more)
+    (y_own,), y_side = take(1), take(sides)
+    wo, wm = take(2)
+    out_gate, out_mix, norm_turned = take(3)
+    norm, mix, mixed, d_out = take(4)
+    own = norm_own.shape[0]
+    half = own // 2
+
+    @pl.when(pl.program_id(0) == 0)
+    def _():
+        stack_tokens(norm, norm_own, norm_more)
+        stack_tokens(mix, mix_own, mix_more)
+
+        def finish(rows, y):
+            outgate = dot(norm[rows, :], wo[...])
+            d_mixed = dot_back(mix[rows, :], wm[...])
+            sig = 1.0 / (1.0 + jnp.exp(-outgate))
+            silu = outgate * sig
+            mixed[rows, :] = (y * silu).astype(mixed.dtype)
+            d_out[rows, :] = (d_mixed * y * (sig + silu * (1.0 - sig))).astype(d_out.dtype)
+
+        finish(slice(0, own), y_own[...])
+        for k in range(sides):
+            for s in range(2):
+                start = own + (s * sides + k) * half
+                finish(slice(start, start + half), y_side[k][s])
+
+    rows = norm_turned.shape[0]
+    span = pl.ds(pl.multiple_of(pl.program_id(0) * rows, rows), rows)
+    turned = norm[:, span].T
+    norm_turned[...] = turned
+    out_gate[...] = dot(turned, d_out[...])
+    out_mix[...] = dot(mix[:, span].T, mixed[...])
+
+
+def mixer_grads(norm_own, norm_more, mix_own, mix_more, y_own, y_side, w_out, w_mix):
+    own, width = norm_own.shape
+    cut = w_out.shape[1]
+    block = next(b for b in (256, 128) if width % b == 0)
+    tokens = own + sum(part.shape[0] for part in norm_more)
+    low = jnp.bfloat16
+    row = lambda columns: pl.BlockSpec((block, columns), lambda i: (i, 0))
+    operands = (norm_own, *norm_more, mix_own, *mix_more, y_own, *y_side, w_out, w_mix)
+    return pl.pallas_call(
+        functools.partial(mixer_kernel, len(norm_more), len(y_side)),
+        grid=(width // block,),
+        in_specs=[whole(a.shape) for a in operands],
+        out_specs=[row(cut), row(cut), row(tokens)],
+        out_shape=[
+            jax.ShapeDtypeStruct((width, cut), jnp.float32),
+            jax.ShapeDtypeStruct((width, cut), jnp.float32),
+            jax.ShapeDtypeStruct((width, tokens), low),
+        ],
+        scratch_shapes=[pltpu.VMEM((tokens, width), low)] * 2 + [pltpu.VMEM((tokens, cut), low)] * 2,
+        compiler_params=params(56),
+        cost_estimate=spans(12),
+    )(*operands)
+
+
+def inner_kernel(sides, *refs):
+    turned, d_own, d_side, out, d_all = refs[0], refs[1], refs[2 : 2 + sides], refs[2 + sides], refs[3 + sides]
+    own = d_own.shape[0]
+    half = own // 2
+
+    @pl.when(pl.program_id(0) == 0)
+    def _():
+        d_all[:own, :] = d_own[...]
+        for k in range(sides):
+            for s in range(2):
+                start = own + (s * sides + k) * half
+                d_all[start : start + half, :] = d_side[k][s].astype(d_all.dtype)
+
+    out[...] = dot(turned[...], d_all[...])
+
+
+def inner_grad(turned, d_own, d_side):
+    width, tokens = turned.shape
+    cut = d_own.shape[1]
+    block = next(b for b in (512, 256, 128) if width % b == 0)
+    return pl.pallas_call(
+        functools.partial(inner_kernel, len(d_side)),
+        grid=(width // block,),
+        in_specs=[pl.BlockSpec((block, tokens), lambda i: (i, 0))] + [whole(a.shape) for a in (d_own, *d_side)],
+        out_specs=pl.BlockSpec((block, cut), lambda i: (i, 0)),
+        out_shape=jax.ShapeDtypeStruct((width, cut), jnp.float32),
+        scratch_shapes=[pltpu.VMEM((tokens, cut), jnp.bfloat16)],
+        compiler_params=params(56),
+        cost_estimate=spans(4),
+    )(turned, d_own, *d_side)
+
+
+SIDE = 4
+MESH = pl.DeviceIdType.MESH
+
+
+def chain_kernel(
+    reverse, groups, ends_ref, total_ref, rate_ref, out_ref,
+    own, side, mine, line, back, done, side_send, side_recv, line_send, line_recv, back_send, back_recv,
+):
+    here, head = lax.axis_index("seq"), lax.axis_index("head")
+    place, group = lax.rem(here, SIDE), here // SIDE
+    streams, n, channels = ends_ref.shape
+    width = channels // SIDE
+    rows = streams * n
+    base = here - place
+    member = [base + (place ^ k) for k in range(SIDE)]
+    other = [lax.rem(group + k, groups) * SIDE + place for k in range(groups)]
+
+    barrier = pltpu.get_barrier_semaphore()
+    for device in member[1:] + other[1:]:
+        pl.semaphore_signal(barrier, inc=1, device_id=(device, head), device_id_type=MESH)
+    for q in range(SIDE):
+        cols = slice(q * width, (q + 1) * width)
+        own[q, :rows, :] = ends_ref[:, :, cols].reshape(rows, width)
+        own[q, rows : rows + streams, :] = total_ref[:, cols]
+        own[q, rows + streams :, :] = jnp.zeros((own.shape[1] - rows - streams, width), jnp.float32)
+    rate = rate_ref[:, pl.ds(pl.multiple_of(place * width, 128), width)]
+    pl.semaphore_wait(barrier, SIDE - 1 + groups - 1)
+
+    def copy(source, target, send, recv, device):
+        return pltpu.make_async_remote_copy(
+            src_ref=source, dst_ref=target, send_sem=send, recv_sem=recv,
+            device_id=(device, head), device_id_type=MESH,
+        )
+
+    sides = [copy(own.at[place ^ k], side.at[k], side_send.at[k], side_recv.at[k], member[k]) for k in range(1, SIDE)]
+    for c in sides:
+        c.start()
+    side[0] = own[place]
+    for c in sides:
+        c.wait_recv()
+
+    def through(steps):
+        return jnp.concatenate([jnp.exp2(steps[s : s + 1] * rate) for s in range(streams)], axis=0)
+
+    state, steps = jnp.zeros((rows, width), jnp.float32), jnp.zeros((streams, width), jnp.float32)
+    before, passed = [None] * SIDE, [None] * SIDE
+    for j in reversed(range(SIDE)) if reverse else range(SIDE):
+        block = side[place ^ j]
+        before[j], passed[j] = state, steps
+        step = block[rows : rows + streams]
+        state = through(step) * state + block[:rows]
+        steps = steps + step
+    mine[:rows, :] = state
+    mine[rows : rows + streams, :] = steps
+    mine[rows + streams :, :] = jnp.zeros((mine.shape[0] - rows - streams, width), jnp.float32)
+    lines = [copy(mine, line.at[k], line_send.at[k], line_recv.at[k], other[k]) for k in range(1, groups)]
+    for c in lines:
+        c.start()
+    for c in lines:
+        c.wait_recv()
+    entering = jnp.zeros((rows, width), jnp.float32)
+    for k in range(1, groups) if reverse else range(groups - 1, 0, -1):
+        counts = (k > group) if reverse else (k <= group)
+        block = line[k]
+        new = through(block[rows : rows + streams]) * entering + block[:rows]
+        entering = jnp.where(counts, new, entering)
+    for j in range(SIDE):
+        back[j] = through(passed[j]) * entering + before[j]
+    backs = [copy(back.at[place ^ k], done.at[place], back_send.at[k], back_recv.at[k], member[k]) for k in range(1, SIDE)]
+    for c in backs:
+        c.start()
+    done[place] = back[place]
+    for c in backs:
+        c.wait_recv()
+    for q in range(SIDE):
+        out_ref[:, :, q * width : (q + 1) * width] = done[q].reshape(streams, n, width)
+    for c in sides + lines + backs:
+        c.wait_send()
+
+
+def chained(ends, total, rate, reverse):
+    streams, n, channels = ends.shape
+    groups = lax.axis_size("seq") // SIDE
+    width = channels // SIDE
+    rows = streams * n
+    tall = rows + 8 * (-(-streams // 8))
+    f32 = jnp.float32
+    return pl.pallas_call(
+        functools.partial(chain_kernel, reverse, groups),
+        out_shape=jax.ShapeDtypeStruct(ends.shape, f32),
+        in_specs=[pl.BlockSpec(memory_space=pltpu.VMEM)] * 3,
+        out_specs=pl.BlockSpec(memory_space=pltpu.VMEM),
+        scratch_shapes=[
+            pltpu.VMEM((SIDE, tall, width), f32),
+            pltpu.VMEM((SIDE, tall, width), f32),
+            pltpu.VMEM((tall, width), f32),
+            pltpu.VMEM((groups, tall, width), f32),
+            pltpu.VMEM((SIDE, rows, width), f32),
+            pltpu.VMEM((SIDE, rows, width), f32),
+        ]
+        + [pltpu.SemaphoreType.DMA((m,)) for m in (SIDE, SIDE, groups, groups, SIDE, SIDE)],
+        compiler_params=pltpu.CompilerParams(
+            collective_id=1 if reverse else 0, has_side_effects=True, vmem_limit_bytes=32 * 1024 * 1024
+        ),
+    )(ends, total, rate)
+
 
 epsilon = 1e-06
-SIDE = 4
 CUT = 1e6
 
 
@@ -235,12 +524,6 @@
 
 def head_sum(part):
     return part + send(part, swaps(1, "head"), "head")
-
-
-def both_streams(mine):
-    other = send(mine, swaps(1, "head"), "head")
-    first = lax.axis_index("head") == 0
-    return jnp.where(first, mine, other), jnp.where(first, other, mine)
 
 
 def own_stream(block):
@@ -260,31 +543,18 @@
 
 def exchange(block, place):
     size = block.shape[-1] // SIDE
-    axis = block.ndim - 1
-    pieces_out = [part_of(block, place ^ k, size, axis) for k in range(SIDE)]
-    return [pieces_out[0]] + [send(pieces_out[k], swaps(k)) for k in range(1, SIDE)]
-
-
-def gather_side(block):
-    mine = own_stream(block)
-    near, far = send(mine, swaps(1)), send(mine, swaps(2))
-    half = mine.shape[0] // 2
-    top = send(far[:half], swaps(1))
-    low = send(near[half:], swaps(2))
-    return [jnp.stack(both_streams(part)) for part in (near, far, jnp.concatenate([top, low]))]
-
-
-def gather_line(block, stride):
-    mine = own_stream(block)
-    n = lax.axis_size("seq")
-    up, down, ups, downs = mine, mine, [], []
-    for turn in range(SIDE - 1):
-        up = send(up, [(i, i + stride) for i in range(turn * stride, n - stride)])
-        down = send(down, [(i, i - stride) for i in range(stride, n - turn * stride)])
-        ups.append(up)
-        downs.append(down)
-    got = [downs[k] + ups[SIDE - 2 - k] for k in range(SIDE - 1)]
-    return [jnp.stack(both_streams(part)) for part in got]
+    first = lax.axis_index("head")
+    turned = jnp.stack([lax.dynamic_index_in_dim(block, first, 0, keepdims=False), lax.dynamic_index_in_dim(block, 1 - first, 0, keepdims=False)])
+    away = [part_of(turned, place ^ k, size, 2).astype(jnp.float32) for k in range(1, SIDE)]
+    return part_of(block, place, size, 2).reshape(-1, size), [send(away[k - 1], swaps(k)) for k in range(1, SIDE)]
+
+
+def other_core(parts):
+    return [send(part, swaps(1, "head"), "head") for part in parts]
+
+
+def after(block, *earlier):
+    return lax.optimization_barrier((block,) + earlier)[0]
 
 
 def scatter_line(blocks, stride):
@@ -323,36 +593,6 @@
         out.append(low)
         low *= 2
     return out
-
-
-def chained(ends, total, rate, reverse):
-    streams, n, channels = ends.shape
-    here = lax.axis_index("seq")
-    groups = lax.axis_size("seq") // SIDE
-    place = here % SIDE
-    width = channels // SIDE
-    through = lambda d: jnp.exp2(d[:, None, :] * rate_here)
-    rate_here = part_of(rate, place, width, 1)
-    packed = jnp.concatenate([ends.reshape(streams * n, channels), total], axis=0)
-    members = unswap(exchange(packed, place), place)
-    members = [(m[: streams * n].reshape(streams, n, width), m[streams * n :]) for m in members]
-    order = range(SIDE - 1, -1, -1) if reverse else range(SIDE)
-    before, passed = {}, {}
-    state, steps = jnp.zeros((streams, n, width), jnp.float32), jnp.zeros((streams, width), jnp.float32)
-    for j in order:
-        before[j], passed[j] = state, steps
-        state = through(members[j][1]) * state + members[j][0]
-        steps = steps + members[j][1]
-    packed = jnp.concatenate([state.reshape(streams * n, width), steps], axis=0)
-    sign = -SIDE if reverse else SIDE
-    entering = jnp.zeros_like(state)
-    for k in range(groups - 1, 0, -1):
-        got = send(packed, links(sign * k))
-        entering = through(got[streams * n :]) * entering + got[: streams * n].reshape(state.shape)
-    mine = [through(passed[j]) * entering + before[j] for j in range(SIDE)]
-    mine = unswap(mine, place)
-    back = [mine[0]] + [send(mine[k], swaps(k)) for k in range(1, SIDE)]
-    return jnp.concatenate(unswap(back, place), axis=2)
 
 
 def matmul(left, right):
@@ -415,14 +655,15 @@
     z, place = here // stride, here % SIDE
     low = jnp.bfloat16
 
-    whole = (doc_ids[0, 0] >= 0).astype(jnp.float32)
-    lower = lambda part: (part * whole).astype(low)
     grad_in = out_grad.astype(jnp.float32)
     source = tokens.astype(jnp.float32)
-    line_grad = [lower(part) for part in gather_line(grad_in, stride)]
+    mine_grad = own_stream(out_grad).astype(jnp.float32)
+    line_grad = {k: send(mine_grad, links(k * stride, True)) for k in (1, 3)}
     normed, scale_mix = norm_forward(source, norm_mix)
     normed_low = normed.astype(low)
-    side_normed = [lower(part) for part in gather_side(normed_low.astype(jnp.float32))]
+    mine_normed = own_stream(normed)
+    side_normed = [send(mine_normed, swaps(k)) for k in range(1, SIDE)]
+    side_normed = side_normed + other_core(side_normed)
     inner = matmul(normed_low, w_inner)
     outgate = matmul(normed_low, w_outgate)
     rim_ids = (doc_ids[:, length - lead :] + 1).astype(jnp.float32)
@@ -457,17 +698,23 @@
     ends = summarize(fall, gain, b_wide, rate)
     total = jnp.sum(fall, axis=1)
     first = chained(ends, total, rate, False)
+    line_grad[2] = send(after(mine_grad, first), links(2 * stride, True))
+    line_grad = [line_grad[k] for k in range(1, SIDE)]
+    line_grad = line_grad + other_core(line_grad)
     outs = run_states(fall, gain, b_wide, c_wide, rate, first)
     y = outs + skip_gain * value
+    own_y, side_y = exchange(y, place)
     gate_z = jax.nn.silu(outgate)
     mixed = y * gate_z
     mixed_low = mixed.astype(low)
-    side_mixed = exchange(mixed_low.astype(jnp.float32), place)
     mix = head_sum(matmul(mixed_low, w_mixout))
     resid = source + mix
     hidden, scale_ffn = norm_forward(resid, norm_ffn)
     hidden_low = hidden.astype(low)
-    line_hidden = [lower(part) for part in gather_line(hidden_low.astype(jnp.float32), stride)]
+    mine_hidden = own_stream(hidden)
+    line_hidden = [send(mine_hidden, links(k * stride, True)) for k in (1, 3, 2)]
+    line_hidden = [line_hidden[k] for k in (0, 2, 1)]
+    line_hidden = line_hidden + other_core(line_hidden)
     gate = matmul(hidden_low, w_gate)
     up = matmul(hidden_low, w_up)
     act_low = (jax.nn.silu(gate) * up).astype(low)
@@ -480,12 +727,12 @@
     d_resid_norm, grad_norm_ffn = norm_backward(resid, scale_ffn, norm_ffn, d_hidden)
     d_resid = grad_in + d_resid_norm
     d_mix = d_resid.astype(low)
-    side_d_mix = [lower(part) for part in gather_side(d_mix.astype(jnp.float32))]
-
+    mine_d_mix = own_stream(d_resid)
+    side_d_mix = [send(mine_d_mix, swaps(k)) for k in range(1, SIDE)]
+    side_d_mix = side_d_mix + other_core(side_d_mix)
     d_mixed = matmul_back(d_mix, w_mixout)
     d_y = d_mixed * gate_z
     d_outgate = (d_mixed * y * silu_slope(outgate)).astype(low)
-    side_d_outgate = exchange(d_outgate.astype(jnp.float32), place)
     grad_skip_gain = jnp.sum(d_y * value, axis=(0, 1))
     leaving = adjoint_summary(fall, d_y, c_wide, rate)
     last = chained(leaving, total, rate, True)
@@ -493,18 +740,11 @@
         fall, step, value, d_y, b_wide, c_wide, rate, first, last
     )
 
-    more_hidden = jnp.concatenate(line_hidden).reshape(-1, width)
-    more_grad = jnp.concatenate(line_grad).reshape(-1, width)
-    more_gate = matmul(more_hidden, w_gate)
-    more_up = matmul(more_hidden, w_up)
-    more_act = matmul_back(more_grad, w_down)
     flat = lambda block: block.reshape(-1, block.shape[-1])
-    gates = jnp.concatenate([flat(d_gate), (more_act * more_up * silu_slope(more_gate)).astype(low)])
-    ups = jnp.concatenate([flat(d_up), (more_act * jax.nn.silu(more_gate)).astype(low)])
-    acts = jnp.concatenate([flat(act_low), (jax.nn.silu(more_gate) * more_up).astype(low)])
-    cut = width // SIDE
-    hidden_cut = part_of(jnp.concatenate([flat(hidden_low), more_hidden]), z, cut, 1)
-    grad_cut = part_of(jnp.concatenate([flat(out_grad), more_grad]), z, cut, 1)
+    whole_gate, whole_up, whole_down = ffn_grads(
+        stride, flat(hidden_low), line_hidden, flat(out_grad), line_grad, w_gate, w_up, w_down,
+        flat(d_gate), flat(d_up), flat(act_low),
+    )
     side_bits = bits_between(1, stride)
     orders = (side_bits, side_bits[len(side_bits) // 2 :] + side_bits[: len(side_bits) // 2])
 
@@ -515,25 +755,26 @@
             [scatter_bits(whole[..., :half], orders[0]), scatter_bits(whole[..., half:], orders[1])], axis=-1
         )
 
-    grad_w_gate = sum_side(weight_outer(hidden_cut, gates))
-    grad_w_up = sum_side(weight_outer(hidden_cut, ups))
-    grad_w_down = sum_side(weight_outer(grad_cut, acts)).T
-
-    all_normed = flat(jnp.concatenate([normed_low] + side_normed))
-    all_d_mix = flat(jnp.concatenate([d_mix] + side_d_mix))
-    joined = lambda parts: lower(flat(jnp.concatenate(parts)))
-    rest = bits_between(SIDE, stride)
+    grad_w_gate = sum_side(whole_gate)
+    grad_w_up = sum_side(whole_up)
+    grad_w_down = sum_side(whole_down).T
+
+    size = channels // SIDE
+    whole_outgate, whole_mixout, turned = mixer_grads(
+        flat(normed_low), side_normed, flat(d_mix), side_d_mix, own_y, side_y,
+        part_of(w_outgate, place, size, 1), part_of(w_mixout, place, size, 0),
+    )
+    groups = [list(range(k, count, SIDE)) for k in range(SIDE)]
 
     def sum_line(whole):
-        whole = whole.reshape(SIDE, stride // SIDE, SIDE, width // count, -1)
-        own = scatter_line(whole, stride)
-        own = scatter_bits(own, rest) if rest else own[0]
+        own = lax.psum_scatter(whole, "seq", scatter_dimension=0, axis_index_groups=groups, tiled=True)
+        own = own.reshape(SIDE, width // count, -1)
         sent = unswap([own[k] for k in range(SIDE)], place)
         got = [sent[0]] + [send(sent[k], swaps(k)) for k in range(1, SIDE)]
         return jnp.concatenate(unswap(got, place), axis=-1)
 
-    grad_w_mixout = sum_line(weight_outer(all_d_mix, joined(side_mixed))).T
-    grad_w_outgate = sum_line(weight_outer(all_normed, joined(side_d_outgate)))
+    grad_w_mixout = sum_line(whole_mixout).T
+    grad_w_outgate = sum_line(whole_outgate)
 
     d_value = d_y * skip_gain + d_scan
     d_step_pre = (d_step * jax.nn.sigmoid(step_pre)).astype(low)
@@ -568,8 +809,8 @@
     grad_conv_taps = jnp.stack(tap_grads)
     rim_grad = send(d_ext[:, :lead], links(-1))
     d_inner = (d_ext[:, lead:] + jnp.pad(rim_grad, ((0, 0), (length - lead, 0), (0, 0)))).astype(low)
-    side_d_inner = exchange(d_inner.astype(jnp.float32), place)
-    grad_w_inner = sum_line(weight_outer(all_normed, joined(side_d_inner)))
+    own_d_inner, side_d_inner = exchange(d_inner, place)
+    grad_w_inner = sum_line(inner_grad(turned, own_d_inner, side_d_inner))
     d_normed = head_sum(matmul_back(d_inner, w_inner) + matmul_back(d_outgate, w_outgate))
     d_source, grad_norm_mix = norm_backward(source, scale_mix, norm_mix, d_normed)
     tokens_grad = d_resid + d_source

time: 717 us -> 638 us (0.89)
  starting transfers between devices: 190 us -> 97.9 us
  Pallas kernels: 54.5 us -> 146 us
  matrix products: 103 us -> 48.1 us
  other arithmetic: 84.9 us -> 51.1 us
  waiting for transfers between devices: 205 us -> 225 us
  local copies, waits for them, and re-layouts: 64.7 us -> 47.6 us
  between operations: 4.79 us -> 16 us
    ppermute x115 -> x68, starting transfers between devices: 190 us -> 97.5 us  [send(): return lax.ppermute(block, axis, route)]
    pallas_call x0 -> x5, Pallas kernels: none -> 90.9 us  [the longest x2 36.9 us: chained(): pl.pallas_call(functools.partial(chain_kernel, reverse, groups), out_shap...]
    dot_general x9 -> x8, matrix products: 41.5 us -> 21.8 us  [matmul_back(): lax.dot_general(left, right, (((left.ndim - 1,), (1,)), ((), ())), prefer...]
    ppermute x115 -> x68, waiting for transfers between devices: 205 us -> 225 us  [send(): return lax.ppermute(block, axis, route)]
    add x26 -> x1, other arithmetic: 19.8 us -> 0.42 us  [body(): y = outs + skip_gain * value]
    dot_general x10 -> x8, matrix products: 44.1 us -> 25.4 us  [matmul(): return jnp.dot(left, right, preferred_element_type=jnp.float32)]
    dot_general x8 -> x2, matrix products: 17.2 us -> 0.91 us  [weight_outer(): lax.dot_general(left, right, ((axes, axes), ((), ())), preferred_element_...]
    unnamed x292 -> x208, local copies, waits for them, and re-layouts: 27.8 us -> 12.3 us
  transfers between devices with their start and end apart: 115 -> 71, of which waited for: 39 -> 26; matrix products, arithmetic and copies ran while one was open for 31% -> 14% of each run, Pallas kernels for 7% -> 9%
where the time goes in v2:
time: 638 us; the launch traced here: 631 us
  waiting for transfers between devices  225 us (35%)
  Pallas kernels  146 us (23%)
  starting transfers between devices  97.9 us (15%)
  other arithmetic  51.1 us (8%)
  matrix products  48.1 us (8%)
  local copies, waits for them, and re-layouts  47.6 us (7%)
  between operations  16 us (3%)
    ppermute x68, waiting for transfers between devices, send(): return lax.ppermute(block, axis, route)  225 us
    ppermute x68, starting transfers between devices, send(): return lax.ppermute(block, axis, route)  97.5 us
    pallas_call x4, Pallas kernels, scan_call(): pl.pallas_call(kernel, grid=(channels // lanes,), in_specs=[specs[k] for...  55 us
    pallas_call x2, Pallas kernels, chained(): pl.pallas_call(functools.partial(chain_kernel, reverse, groups), out_shap...  36.9 us
    pallas_call x1, Pallas kernels, ffn_grads(): pl.pallas_call(functools.partial(ffn_kernel, stride, len(hid_more)), grid...  32.9 us
    dot_general x8, matrix products, matmul(): return jnp.dot(left, right, preferred_element_type=jnp.float32)  25.4 us
    dot_general x8, matrix products, matmul_back(): lax.dot_general(left, right, (((left.ndim - 1,), (1,)), ((), ())), prefer...  21.8 us
    pallas_call x1, Pallas kernels, mixer_grads(): pl.pallas_call(functools.partial(mixer_kernel, len(norm_more), len(y_side...  15.6 us
  transfers between devices with their start and end apart: 71, of which 26 were waited for; matrix products, arithmetic and copies ran while one was open for 14% of the time, Pallas kernels for 9%

profile of v2, /device:TPU:0, one launch (start us, length us, event | category | flops | bytes accessed | tf_op | source)
XLA Modules:
  0.0 631.2 jit_solution(3575664616986147003)
XLA Ops:
  36.4 5.2 shard_map.322.ends_ref
  41.6 19.1 %shard_map.323.first_ref = f32[2,16,1536]{2,1,0:T(8,128)S(1)} custom-call(f32[2,16,1536]{2,1,0:T(8,128)S(1)} %shard_map.322.ends_ref, f32[2,1536]{1,0:T(2,128)S(1)} %get-tuple-element.84.total_ref, f32[16,1536]{1,0:T(8,128)S(1)} %bitcast_multiply_fusion.1.rate_ref), custom_call_target="tpu_custom_call" | custom-call | tf_op jit(solution)/shard_map/pallas_call | solution.py:488
  62.7 13.0 %shard_map.324 = f32[2,128,1536]{2,1,0:T(8,128)S(1)} custom-call(f32[2,128,1536]{2,1,0:T(8,128)S(1)} %get-tuple-element.85.df_ref, f32[2,128,1536]{2,1,0:T(8,128)S(1)} %get-tuple-element.106.x_ref, f32[2,2048,128]{2,1,0:T(8,128)} %copy-done.2, f32[2,2048,128]{2,1,0:T(8,128)} %broadcast_in_dim.25.c_ref, f32[16,1536]{1,0:T(8,128)S(1)} %bitcast_multiply_fusion.1.rate_ref, ...), custom_call_target="tpu_custom_call" | custom-call | flops 13200000000 | bytes 36000000 | tf_op jit(solution)/shard_map/pallas_call | solution.py:190
  88.0 5.4 multiply_convert_fusion.1
  93.4 5.7 fusion.4
  112.2 5.2 shard_map.325.ends_ref
  117.5 17.8 %shard_map.326.last_ref = f32[2,16,1536]{2,1,0:T(8,128)S(1)} custom-call(f32[2,16,1536]{2,1,0:T(8,128)S(1)} %shard_map.325.ends_ref, f32[2,1536]{1,0:T(2,128)S(1)} %get-tuple-element.84.total_ref, f32[16,1536]{1,0:T(8,128)S(1)} %bitcast_multiply_fusion.1.rate_ref), custom_call_target="tpu_custom_call" | custom-call | tf_op jit(solution)/shard_map/pallas_call | solution.py:488
  135.2 31.5 %shard_map.327 = (f32[2,128,1536]{2,1,0:T(8,128)S(1)}, f32[2,128,1536]{2,1,0:T(8,128)S(1)}, f32[2,2048,128]{2,1,0:T(8,128)}, f32[2,2048,128]{2,1,0:T(8,128)}, f32[16,1536]{1,0:T(8,128)S(1)}) custom-call(f32[2,128,1536]{2,1,0:T(8,128)S(1)} %get-tuple-element.85.df_ref, f32[2,128,1536]{2,1,0:T(8,128)} %get-tuple-element.104.d_ref, ...), custom_call_target="tpu_custom_call" | custom-call | flops 32999999488 | bytes 90000000 | tf_op jit(solution)/shard_map/pallas_call | solution.py:190
  207.1 10.2 %collective-permute-done.26.refs_16_ = f32[2,128,384]{2,1,0:T(8,128)S(1)} collective-permute-done((f32[2,128,384]{2,1,0:T(8,128)S(1)}, f32[2,128,384]{2,1,0:T(8,128)S(1)}, u32[]{:S(2)}, u32[]{:S(2)}) %collective-permute-start.26) | collective-permute-done | bytes 393248 | tf_op jit(solution)/shard_map/ppermute | solution.py:522
  217.7 14.1 %collective-permute-done.52.refs_10_ = f32[128,1536]{1,0:T(8,128)S(1)} collective-permute-done((f32[128,1536]{1,0:T(8,128)S(1)}, f32[128,1536]{1,0:T(8,128)S(1)}, u32[]{:S(2)}, u32[]{:S(2)}) %collective-permute-start.52) | collective-permute-done | bytes 786464 | tf_op jit(solution)/shard_map/ppermute | solution.py:522
  238.8 61.2 %collective-permute-done.51.refs_9_ = f32[128,1536]{1,0:T(8,128)S(1)} collective-permute-done((f32[128,1536]{1,0:T(8,128)S(1)}, f32[128,1536]{1,0:T(8,128)S(1)}, u32[]{:S(2)}, u32[]{:S(2)}) %collective-permute-start.51) | collective-permute-done | bytes 786464 | tf_op jit(solution)/shard_map/ppermute | solution.py:522
  303.1 13.8 %collective-permute-done.45.refs_2_ = f32[128,1536]{1,0:T(8,128)S(1)} collective-permute-done((f32[128,1536]{1,0:T(8,128)S(1)}, f32[128,1536]{1,0:T(8,128)S(1)}, u32[]{:S(2)}, u32[]{:S(2)}) %collective-permute-start.45) | collective-permute-done | bytes 786464 | tf_op jit(solution)/shard_map/ppermute | solution.py:522
  330.8 24.1 %collective-permute-done.29.refs_3_ = f32[2,128,384]{2,1,0:T(8,128)S(1)} collective-permute-done((f32[2,128,384]{2,1,0:T(8,128)S(1)}, f32[2,128,384]{2,1,0:T(8,128)S(1)}, u32[]{:S(2)}, u32[]{:S(2)}) %collective-permute-start.29) | collective-permute-done | bytes 393248 | tf_op jit(solution)/shard_map/ppermute | solution.py:522
  363.9 11.6 %collective-permute-done.13.refs_1_ = f32[128,1536]{1,0:T(8,128)} collective-permute-done((f32[128,1536]{1,0:T(8,128)S(1)}, f32[128,1536]{1,0:T(8,128)}, u32[]{:S(2)}, u32[]{:S(2)}) %collective-permute-start.13) | collective-permute-done | bytes 786464 | tf_op jit(solution)/shard_map/ppermute | solution.py:522
  375.5 12.6 %collective-permute-done.14.refs_2_ = f32[128,1536]{1,0:T(8,128)} collective-permute-done((f32[128,1536]{1,0:T(8,128)S(1)}, f32[128,1536]{1,0:T(8,128)}, u32[]{:S(2)}, u32[]{:S(2)}) %collective-permute-start.14) | collective-permute-done | bytes 786464 | tf_op jit(solution)/shard_map/ppermute | solution.py:522
  394.9 15.6 %shard_map.328 = (f32[1536,384]{1,0:T(8,128)}, f32[1536,384]{1,0:T(8,128)}, bf16[1536,1024]{1,0:T(8,128)(2,1)}) custom-call(bf16[256,1536]{1,0:T(8,128)(2,1)} %bitcast.225, f32[128,1536]{1,0:T(8,128)} %collective-permute-done.13.refs_1_, f32[128,1536]{1,0:T(8,128)} %collective-permute-done.14.refs_2_, f32[128,1536]{1,0:T(8,128)} %collective-permute-done.15.refs_3_, ...), custom_call_target="tpu_custom_call" | custom-call | flops 13200000000 | bytes 36000000 | tf_op jit(solution)/shard_map/pallas_call | solution.py:353
  410.5 5.5 shard_map.329
  417.2 32.9 %shard_map.330 = (f32[384,2048]{1,0:T(8,128)}, f32[384,2048]{1,0:T(8,128)}, f32[384,2048]{1,0:T(8,128)}) custom-call(bf16[256,1536]{1,0:T(8,128)(2,1)} %bitcast.226, f32[128,1536]{1,0:T(8,128)} %copy-done.71, f32[128,1536]{1,0:T(8,128)} %copy-done.72, f32[128,1536]{1,0:T(8,128)} %copy-done.73, f32[128,1536]{1,0:T(8,128)} %collective-permute-done.47.refs_4_, ...), custom_call_target="tpu_custom_call" | custom-call | flops 26400000000 | bytes 72000000 | tf_op jit(solution)/shard_map/pallas_call | solution.py:290
  473.4 25.3 %collective-permute-done.37 = f32[2,2,2,8,1536]{4,3,1,0,2:T(8,128)} collective-permute-done((f32[2,2,2,8,1536]{4,3,1,0,2:T(8,128)}, f32[2,2,2,8,1536]{4,3,1,0,2:T(8,128)}, u32[]{:S(2)}, u32[]{:S(2)}) %collective-permute-start.37) | collective-permute-done | bytes 393248 | tf_op jit(solution)/shard_map/ppermute | solution.py:522
  509.5 16.0 %collective-permute-start.39 = (f32[2,8,1536]{2,1,0:T(8,128)S(1)}, f32[2,8,1536]{2,1,0:T(8,128)S(1)}, u32[]{:S(2)}, u32[]{:S(2)}) collective-permute-start(f32[2,8,1536]{2,1,0:T(8,128)S(1)} %dynamic-slice_bitcast_fusion.17), channel_id=1, source_target_pairs={{0,8},{2,10},{4,12},{6,14},{8,0},{10,2},{12,4},{14,6},{16,24},{18,... | collective-permute-start | bytes 294920 | tf_op jit(solution)/shard_map/ppermute | solution.py:522
  556.0 7.6 %collective-permute-done.9 = f32[2,2,2,122,96]{4,2,1,0,3:T(2,128)S(1)} collective-permute-done((f32[2,2,2,122,96]{4,2,1,0,3:T(2,128)S(1)}, f32[2,2,2,122,96]{4,2,1,0,3:T(2,128)S(1)}, u32[]{:S(2)}, u32[]{:S(2)}) %collective-permute-start.9) | collective-permute-done | bytes 374816 | tf_op jit(solution)/shard_map/ppermute | solution.py:522
  565.8 5.0 collective-permute-done.10
  570.9 12.5 %collective-permute-start.11 = (f32[2,122,96]{2,1,0:T(8,128)S(1)}, f32[2,122,96]{2,1,0:T(8,128)S(1)}, u32[]{:S(2)}, u32[]{:S(2)}) collective-permute-start(f32[2,122,96]{2,1,0:T(8,128)S(1)} %dynamic-slice_bitcast_fusion.16), channel_id=1, source_target_pairs={{0,8},{2,10},{4,12},{6,14},{8,0},{10,2},{12,4},{14,6},{16,24},{18,... | collective-permute-start | bytes 281096 | tf_op jit(solution)/shard_map/ppermute | solution.py:522
  584.5 7.5 %collective-permute-done.11 = f32[2,122,96]{2,1,0:T(8,128)S(1)} collective-permute-done((f32[2,122,96]{2,1,0:T(8,128)S(1)}, f32[2,122,96]{2,1,0:T(8,128)S(1)}, u32[]{:S(2)}, u32[]{:S(2)}) %collective-permute-start.11) | collective-permute-done | bytes 93728 | tf_op jit(solution)/shard_map/ppermute | solution.py:522
  (503 shorter events, 236.5 us)
Async XLA Ops:
  7.2 594.9 %reduce-scatter.4.cloned.1.call-start = ((), (), s32[]{:S(2)}) async-start(), calls=%async_computation.3 | async-start | bytes 2949120 | tf_op jit(solution)/shard_map/reduce_scatter | solution.py:770
  191.7 44.1 %collective-permute-start.8 = (f32[2,128,1536]{2,1,0:T(8,128)}, f32[2,128,1536]{2,1,0:T(8,128)}, u32[]{:S(2)}, u32[]{:S(2)}) collective-permute-start(f32[2,128,1536]{2,1,0:T(8,128)} %fusion.25), channel_id=1, source_target_pairs={{0,1},{1,0},{2,3},{3,2},{4,5},{5,4},{6,7},{7,6},{8,9},{9,8},{10,11... | collective-permute-start | bytes 4718600 | tf_op jit(solution)/shard_map/ppermute | solution.py:522
  195.4 36.4 %collective-permute-start.52 = (f32[128,1536]{1,0:T(8,128)S(1)}, f32[128,1536]{1,0:T(8,128)S(1)}, u32[]{:S(2)}, u32[]{:S(2)}) collective-permute-start(f32[128,1536]{1,0:T(8,128)S(1)} %bitcast_convert_fusion), channel_id=1, source_target_pairs={{0,24},{2,26},{4,28},{6,30},{8,0},{10,2},{12,4},{14,6},{16,8},{18,... | collective-permute-start | bytes 2359304 | tf_op jit(solution)/shard_map/ppermute | solution.py:522
  217.3 82.7 %collective-permute-start.51 = (f32[128,1536]{1,0:T(8,128)S(1)}, f32[128,1536]{1,0:T(8,128)S(1)}, u32[]{:S(2)}, u32[]{:S(2)}) collective-permute-start(f32[128,1536]{1,0:T(8,128)S(1)} %bitcast_convert_fusion), channel_id=1, source_target_pairs={{0,16},{2,18},{4,20},{6,22},{8,24},{10,26},{12,28},{14,30},{16,0},... | collective-permute-start | bytes 2359304 | tf_op jit(solution)/shard_map/ppermute | solution.py:522
  217.7 83.5 %collective-permute-start.53 = (f32[128,1536]{1,0:T(8,128)S(1)}, f32[128,1536]{1,0:T(8,128)S(1)}, u32[]{:S(2)}, u32[]{:S(2)}) collective-permute-start(f32[128,1536]{1,0:T(8,128)S(1)} %collective-permute-done.50.refs_8_), channel_id=1, source_target_pairs={{0,1},{1,0},{2,3},{3,2},{4,5},{5,4},{6,7},{7,6},{8,9},{9,8},{10,11... | collective-permute-start | bytes 2359304 | tf_op jit(solution)/shard_map/ppermute | solution.py:522
  217.7 84.6 %collective-permute-start.44 = (f32[128,1536]{1,0:T(8,128)S(1)}, f32[128,1536]{1,0:T(8,128)S(1)}, u32[]{:S(2)}, u32[]{:S(2)}) collective-permute-start(f32[128,1536]{1,0:T(8,128)S(1)} %dynamic-slice_bitcast_fusion.6), channel_id=1, source_target_pairs={{0,8},{2,10},{4,12},{6,14},{8,16},{10,18},{12,20},{14,22},{16,24},... | collective-permute-start | bytes 2359304 | tf_op jit(solution)/shard_map/ppermute | solution.py:522
  231.9 85.0 %collective-permute-start.45 = (f32[128,1536]{1,0:T(8,128)S(1)}, f32[128,1536]{1,0:T(8,128)S(1)}, u32[]{:S(2)}, u32[]{:S(2)}) collective-permute-start(f32[128,1536]{1,0:T(8,128)S(1)} %dynamic-slice_bitcast_fusion.6), channel_id=1, source_target_pairs={{0,16},{2,18},{4,20},{6,22},{8,24},{10,26},{12,28},{14,30},{16,0},... | collective-permute-start | bytes 2359304 | tf_op jit(solution)/shard_map/ppermute | solution.py:522
  235.8 82.1 %collective-permute-start.46 = (f32[128,1536]{1,0:T(8,128)S(1)}, f32[128,1536]{1,0:T(8,128)S(1)}, u32[]{:S(2)}, u32[]{:S(2)}) collective-permute-start(f32[128,1536]{1,0:T(8,128)S(1)} %dynamic-slice_bitcast_fusion.6), channel_id=1, source_target_pairs={{0,24},{2,26},{4,28},{6,30},{8,0},{10,2},{12,4},{14,6},{16,8},{18,... | collective-permute-start | bytes 2359304 | tf_op jit(solution)/shard_map/ppermute | solution.py:522
  300.0 30.8 %collective-permute-start.19 = (f32[128,1536]{1,0:T(8,128)}, f32[128,1536]{1,0:T(8,128)}, u32[]{:S(2)}, u32[]{:S(2)}) collective-permute-start(f32[128,1536]{1,0:T(8,128)} %dynamic-slice_bitcast_fusion.7), channel_id=1, source_target_pairs={{0,2},{2,0},{4,6},{6,4},{8,10},{10,8},{12,14},{14,12},{16,18},{18,... | collective-permute-start | bytes 2359304 | tf_op jit(solution)/shard_map/ppermute | solution.py:522
  301.2 54.5 %collective-permute-start.20 = (f32[128,1536]{1,0:T(8,128)}, f32[128,1536]{1,0:T(8,128)}, u32[]{:S(2)}, u32[]{:S(2)}) collective-permute-start(f32[128,1536]{1,0:T(8,128)} %dynamic-slice_bitcast_fusion.7), channel_id=1, source_target_pairs={{0,4},{2,6},{4,0},{6,2},{8,12},{10,14},{12,8},{14,10},{16,20},{18,... | collective-permute-start | bytes 2359304 | tf_op jit(solution)/shard_map/ppermute | solution.py:522
  316.9 38.0 %collective-permute-start.29 = (f32[2,128,384]{2,1,0:T(8,128)S(1)}, f32[2,128,384]{2,1,0:T(8,128)S(1)}, u32[]{:S(2)}, u32[]{:S(2)}) collective-permute-start(f32[2,128,384]{2,1,0:T(8,128)S(1)} %get-tuple-element.115), channel_id=1, source_target_pairs={{0,4},{2,6},{4,0},{6,2},{8,12},{10,14},{12,8},{14,10},{16,20},{18,... | collective-permute-start | bytes 1179656 | tf_op jit(solution)/shard_map/ppermute | solution.py:522
  318.9 36.0 %collective-permute-start.30 = (f32[2,128,384]{2,1,0:T(8,128)S(1)}, f32[2,128,384]{2,1,0:T(8,128)S(1)}, u32[]{:S(2)}, u32[]{:S(2)}) collective-permute-start(f32[2,128,384]{2,1,0:T(8,128)S(1)} %get-tuple-element.113), channel_id=1, source_target_pairs={{0,6},{2,4},{4,2},{6,0},{8,14},{10,12},{12,10},{14,8},{16,22},{18,... | collective-permute-start | bytes 1179656 | tf_op jit(solution)/shard_map/ppermute | solution.py:522
  329.1 34.3 %collective-permute-start.21 = (f32[128,1536]{1,0:T(8,128)}, f32[128,1536]{1,0:T(8,128)}, u32[]{:S(2)}, u32[]{:S(2)}) collective-permute-start(f32[128,1536]{1,0:T(8,128)} %dynamic-slice_bitcast_fusion.7), channel_id=1, source_target_pairs={{0,6},{2,4},{4,2},{6,0},{8,14},{10,12},{12,10},{14,8},{16,22},{18,... | collective-permute-start | bytes 2359304 | tf_op jit(solution)/shard_map/ppermute | solution.py:522
  330.8 32.6 %collective-permute-start.22 = (f32[128,1536]{1,0:T(8,128)}, f32[128,1536]{1,0:T(8,128)}, u32[]{:S(2)}, u32[]{:S(2)}) collective-permute-start(f32[128,1536]{1,0:T(8,128)} %collective-permute-done.19.refs_8_), channel_id=1, source_target_pairs={{0,1},{1,0},{2,3},{3,2},{4,5},{5,4},{6,7},{7,6},{8,9},{9,8},{10,11... | collective-permute-start | bytes 2359304 | tf_op jit(solution)/shard_map/ppermute | solution.py:522
  354.9 33.2 %collective-permute-start.14 = (f32[128,1536]{1,0:T(8,128)S(1)}, f32[128,1536]{1,0:T(8,128)}, u32[]{:S(2)}, u32[]{:S(2)}) collective-permute-start(f32[128,1536]{1,0:T(8,128)S(1)} %dynamic-slice_bitcast_fusion.8), channel_id=1, source_target_pairs={{0,4},{2,6},{4,0},{6,2},{8,12},{10,14},{12,8},{14,10},{16,20},{18,... | collective-permute-start | bytes 2359304 | tf_op jit(solution)/shard_map/ppermute | solution.py:522
  355.8 32.3 %collective-permute-start.15 = (f32[128,1536]{1,0:T(8,128)S(1)}, f32[128,1536]{1,0:T(8,128)}, u32[]{:S(2)}, u32[]{:S(2)}) collective-permute-start(f32[128,1536]{1,0:T(8,128)S(1)} %dynamic-slice_bitcast_fusion.8), channel_id=1, source_target_pairs={{0,6},{2,4},{4,2},{6,0},{8,14},{10,12},{12,10},{14,8},{16,22},{18,... | collective-permute-start | bytes 2359304 | tf_op jit(solution)/shard_map/ppermute | solution.py:522
  363.3 30.4 %collective-permute-start.23 = (f32[128,1536]{1,0:T(8,128)}, f32[128,1536]{1,0:T(8,128)}, u32[]{:S(2)}, u32[]{:S(2)}) collective-permute-start(f32[128,1536]{1,0:T(8,128)} %collective-permute-done.20.refs_9_), channel_id=1, source_target_pairs={{0,1},{1,0},{2,3},{3,2},{4,5},{5,4},{6,7},{7,6},{8,9},{9,8},{10,11... | collective-permute-start | bytes 2359304 | tf_op jit(solution)/shard_map/ppermute | solution.py:522
  416.0 190.8 %reduce-scatter.6.cloned.1.call-start = ((), (), s32[]{:S(2)}) async-start(), calls=%async_computation.4 | async-start | bytes 2949120 | tf_op jit(solution)/shard_map/reduce_scatter | solution.py:770
  453.2 53.7 %collective-permute-start.58 = (f32[2,96,1024]{2,1,0:T(8,128)}, f32[2,96,1024]{2,1,0:T(8,128)}, u32[]{:S(2)}, u32[]{:S(2)}) collective-permute-start(f32[2,96,1024]{2,1,0:T(8,128)} %dynamic-slice_bitcast_fusion.4), channel_id=1, source_target_pairs={{0,4},{2,6},{4,0},{6,2},{8,12},{10,14},{12,8},{14,10},{16,20},{18,... | collective-permute-start | bytes 2359304 | tf_op jit(solution)/shard_map/ppermute | solution.py:522
  454.9 54.5 %collective-permute-start.56 = (f32[2,96,1024]{2,1,0:T(8,128)}, f32[2,96,1024]{2,1,0:T(8,128)}, u32[]{:S(2)}, u32[]{:S(2)}) collective-permute-start(f32[2,96,1024]{2,1,0:T(8,128)} %dynamic-slice_bitcast_fusion.5), channel_id=1, source_target_pairs={{0,2},{2,0},{4,6},{6,4},{8,10},{10,8},{12,14},{14,12},{16,18},{18,... | collective-permute-start | bytes 2359304 | tf_op jit(solution)/shard_map/ppermute | solution.py:522
  457.4 69.4 %collective-permute-start.62 = (f32[2,96,1024]{2,1,0:T(8,128)}, f32[2,96,1024]{2,1,0:T(8,128)}, u32[]{:S(2)}, u32[]{:S(2)}) collective-permute-start(f32[2,96,1024]{2,1,0:T(8,128)} %dynamic-slice_bitcast_fusion.2), channel_id=1, source_target_pairs={{0,4},{2,6},{4,0},{6,2},{8,12},{10,14},{12,8},{14,10},{16,20},{18,... | collective-permute-start | bytes 2359304 | tf_op jit(solution)/shard_map/ppermute | solution.py:522
  459.5 70.9 %collective-permute-start.60 = (f32[2,96,1024]{2,1,0:T(8,128)}, f32[2,96,1024]{2,1,0:T(8,128)}, u32[]{:S(2)}, u32[]{:S(2)}) collective-permute-start(f32[2,96,1024]{2,1,0:T(8,128)} %dynamic-slice_bitcast_fusion.3), channel_id=1, source_target_pairs={{0,2},{2,0},{4,6},{6,4},{8,10},{10,8},{12,14},{14,12},{16,18},{18,... | collective-permute-start | bytes 2359304 | tf_op jit(solution)/shard_map/ppermute | solution.py:522
  473.4 137.9 %reduce-scatter.8.cloned.1.call-start = ((), (), s32[]{:S(2)}) async-start(), calls=%async_computation.5 | async-start | bytes 2949120 | tf_op jit(solution)/shard_map/reduce_scatter | solution.py:770
  543.9 39.5 %collective-permute-start.65 = (f32[96,1024]{1,0:T(8,128)S(1)}, f32[96,1024]{1,0:T(8,128)}, u32[]{:S(2)}, u32[]{:S(2)}) collective-permute-start(f32[96,1024]{1,0:T(8,128)S(1)} %dynamic-slice_bitcast_fusion.10), channel_id=1, source_target_pairs={{0,4},{2,6},{4,0},{6,2},{8,12},{10,14},{12,8},{14,10},{16,20},{18,... | collective-permute-start | bytes 1179656 | tf_op jit(solution)/shard_map/ppermute | solution.py:522
  (146 other events, 1407.3 us)
Sparse Core Ops, SparseCore 0:
  416.1 62.5 reduce-scatter.3
  481.0 56.7 reduce-scatter.5
  544.0 58.2 reduce-scatter.7

commit v3 on v2

--- a/solution.py
+++ b/solution.py
@@ -1,5 +1,8 @@
-import functools, math
-import jax, jax.numpy as jnp
+import functools
+import math
+
+import jax
+import jax.numpy as jnp
 from jax import lax
 from jax.experimental import pallas as pl
 from jax.experimental.pallas import tpu as pltpu
@@ -22,200 +25,8 @@
     return next(w for w in (256, 128) if lanes % w == 0)
 
 
-def summary_kernel(df_ref, x_ref, b_ref, rate_ref, end_ref):
-    streams, length, lanes = df_ref.shape
-    n = rate_ref.shape[0]
-    rate = rate_ref[...]
-
-    def chunk(i, states):
-        base = pl.multiple_of(i * ROWS, ROWS)
-        out = []
-        for s in range(streams):
-            state = states[s]
-            d = df_ref[s, pl.ds(base, ROWS), :]
-            x = x_ref[s, pl.ds(base, ROWS), :]
-            for j in range(ROWS):
-                b = b_ref[s, pl.ds(pl.multiple_of((base + j) * n, n), n), :]
-                fade = jnp.exp2(d[j : j + 1] * rate)
-                state = fade * state + x[j : j + 1] * wide(b, lanes)
-            out.append(state)
-        return tuple(out)
-
-    start = tuple(jnp.zeros((n, lanes), jnp.float32) for _ in range(streams))
-    states = lax.fori_loop(0, length // ROWS, chunk, start)
-    for s in range(streams):
-        end_ref[s] = states[s]
-
-
-def run_kernel(df_ref, x_ref, b_ref, c_ref, rate_ref, first_ref, y_ref):
-    streams, length, lanes = df_ref.shape
-    n = rate_ref.shape[0]
-    rate = rate_ref[...]
-
-    def chunk(i, states):
-        base = pl.multiple_of(i * ROWS, ROWS)
-        out = []
-        for s in range(streams):
-            state = states[s]
-            d = df_ref[s, pl.ds(base, ROWS), :]
-            x = x_ref[s, pl.ds(base, ROWS), :]
-            rows = []
-            for j in range(ROWS):
-                at = pl.ds(pl.multiple_of((base + j) * n, n), n)
-                fade = jnp.exp2(d[j : j + 1] * rate)
-                state = fade * state + x[j : j + 1] * wide(b_ref[s, at, :], lanes)
-                rows.append(jnp.sum(state * wide(c_ref[s, at, :], lanes), axis=0, keepdims=True))
-            y_ref[s, pl.ds(base, ROWS), :] = jnp.concatenate(rows, axis=0)
-            out.append(state)
-        return tuple(out)
-
-    lax.fori_loop(0, length // ROWS, chunk, tuple(first_ref[s] for s in range(streams)))
-
-
-def adjoint_summary_kernel(df_ref, g_ref, c_ref, rate_ref, end_ref):
-    streams, length, lanes = df_ref.shape
-    n = rate_ref.shape[0]
-    rate = rate_ref[...]
-    chunks = length // ROWS
-
-    def chunk(i, carry):
-        base = pl.multiple_of((chunks - 1 - i) * ROWS, ROWS)
-        out = []
-        for s in range(streams):
-            carried = carry[s]
-            d = df_ref[s, pl.ds(base, ROWS), :]
-            g = g_ref[s, pl.ds(base, ROWS), :]
-            for j in reversed(range(ROWS)):
-                at = pl.ds(pl.multiple_of((base + j) * n, n), n)
-                fade = jnp.exp2(d[j : j + 1] * rate)
-                carried = fade * (g[j : j + 1] * wide(c_ref[s, at, :], lanes) + carried)
-            out.append(carried)
-        return tuple(out)
-
-    start = tuple(jnp.zeros((n, lanes), jnp.float32) for _ in range(streams))
-    last = lax.fori_loop(0, chunks, chunk, start)
-    for s in range(streams):
-        end_ref[s] = last[s]
-
-
-def adjoint_run_kernel(
-    df_ref, d_ref, v_ref, g_ref, b_ref, c_ref, rate_ref, first_ref, last_ref,
-    dstep_ref, dvalue_ref, db_ref, dc_ref, decay_ref, path_ref, fade_ref,
-):
-    streams, length, lanes = df_ref.shape
-    n = rate_ref.shape[0]
-    rate = rate_ref[...]
-    chunks = length // ROWS
-
-    @pl.when(pl.program_id(0) == 0)
-    def _():
-        db_ref[...] = jnp.zeros_like(db_ref)
-        dc_ref[...] = jnp.zeros_like(dc_ref)
-
-    def ahead(i, states):
-        base = pl.multiple_of(i * ROWS, ROWS)
-        out = []
-        for s in range(streams):
-            state = states[s]
-            d = df_ref[s, pl.ds(base, ROWS), :]
-            x = d_ref[s, pl.ds(base, ROWS), :] * v_ref[s, pl.ds(base, ROWS), :]
-            for j in range(ROWS):
-                at = pl.ds(pl.multiple_of((base + j) * n, n), n)
-                path_ref[s, at, :] = state
-                fade = jnp.exp2(d[j : j + 1] * rate)
-                fade_ref[s, at, :] = fade
-                state = fade * state + x[j : j + 1] * wide(b_ref[s, at, :], lanes)
-            out.append(state)
-        return tuple(out)
-
-    ends = lax.fori_loop(0, chunks, ahead, tuple(first_ref[s] for s in range(streams)))
-
-    def fold(tile):
-        total = tile[:, :128]
-        for k in range(1, lanes // 128):
-            total = total + tile[:, k * 128 : (k + 1) * 128]
-        return total
-
-    def back(i, carry):
-        base = pl.multiple_of((chunks - 1 - i) * ROWS, ROWS)
-        out = []
-        decay = carry[-1]
-        for s in range(streams):
-            state, carried = carry[s]
-            d = d_ref[s, pl.ds(base, ROWS), :]
-            v = v_ref[s, pl.ds(base, ROWS), :]
-            g = g_ref[s, pl.ds(base, ROWS), :]
-            x = d * v
-            weights, touches = [None] * ROWS, [None] * ROWS
-            for j in reversed(range(ROWS)):
-                at = pl.ds(pl.multiple_of((base + j) * n, n), n)
-                gj = g[j : j + 1]
-                adjoint = gj * wide(c_ref[s, at, :], lanes) + carried
-                dc_ref[s, at, :] += fold(state * gj)
-                db_ref[s, at, :] += fold(adjoint * x[j : j + 1])
-                weights[j] = jnp.sum(adjoint * wide(b_ref[s, at, :], lanes), axis=0, keepdims=True)
-                carried = adjoint * fade_ref[s, at, :]
-                state = path_ref[s, at, :]
-                touch = carried * state
-                touches[j] = jnp.sum(touch * rate, axis=0, keepdims=True)
-                decay = decay + touch * d[j : j + 1]
-            weighted = jnp.concatenate(weights, axis=0)
-            dstep_ref[s, pl.ds(base, ROWS), :] = weighted * v + jnp.concatenate(touches, axis=0) * LN2
-            dvalue_ref[s, pl.ds(base, ROWS), :] = weighted * d
-            out.append((state, carried))
-        return tuple(out) + (decay,)
-
-    start = tuple((ends[s], last_ref[s]) for s in range(streams))
-    done = lax.fori_loop(0, chunks, back, start + (jnp.zeros((n, lanes), jnp.float32),))
-    decay_ref[...] = done[-1]
-
-
-def scan_call(kernel, operands, kinds, out_kinds, scratch=(), flops=0, block=None):
-    streams, length, channels = operands[0].shape
-    n = next(o for o, k in zip(operands, kinds) if k == "r").shape[0]
-    lanes = block or pieces(channels)
-    specs = {
-        "e": pl.BlockSpec((streams, length, lanes), lambda i: (0, 0, i)),
-        "n": pl.BlockSpec((streams, length * n, 128), lambda i: (0, 0, 0)),
-        "r": pl.BlockSpec((n, lanes), lambda i: (0, i)),
-        "h": pl.BlockSpec((streams, n, lanes), lambda i: (0, 0, i)),
-    }
-    shapes = {
-        "e": (streams, length, channels),
-        "n": (streams, length * n, 128),
-        "r": (n, channels),
-        "h": (streams, n, channels),
-    }
-    size = streams * length * n * channels
-    return pl.pallas_call(
-        kernel,
-        grid=(channels // lanes,),
-        in_specs=[specs[k] for k in kinds],
-        out_specs=[specs[k] for k in out_kinds] if len(out_kinds) > 1 else specs[out_kinds],
-        out_shape=[jax.ShapeDtypeStruct(shapes[k], jnp.float32) for k in out_kinds]
-        if len(out_kinds) > 1
-        else jax.ShapeDtypeStruct(shapes[out_kinds], jnp.float32),
-        scratch_shapes=[pltpu.VMEM((streams, length * n, lanes), jnp.float32) for _ in scratch],
-        compiler_params=params(),
-        cost_estimate=spans(flops),
-    )(*operands)
-
-
-def summarize(df, x, b, rate, block=None):
-    return scan_call(summary_kernel, (df, x, b, rate), "eenr", "h", flops=6, block=block)
-
-def run_states(df, x, b, c, rate, first, block=None):
-    return scan_call(run_kernel, (df, x, b, c, rate, first), "eennrh", "e", flops=12, block=block)
-
-def adjoint_summary(df, g, c, rate, block=None):
-    return scan_call(adjoint_summary_kernel, (df, g, c, rate), "eenr", "h", flops=6, block=block)
-
-def adjoint_run(df, d, v, g, b, c, rate, first, last, block=None):
-    return scan_call(adjoint_run_kernel, (df, d, v, g, b, c, rate, first, last), "eeeennrhh", "eennr", scratch="ab", flops=30, block=block)
-
-
 def spans(us):
-    return pl.CostEstimate(flops=int(us * 1.1e9), bytes_accessed=int(us * 3.0e6), transcendentals=0)
+    return pl.CostEstimate(flops=int(us * 1.1e8), bytes_accessed=int(us * 3.0e5), transcendentals=0)
 
 
 def stack_tokens(target, own_ref, more_refs):
@@ -223,9 +34,10 @@
     target[:own, :] = own_ref[...].astype(target.dtype)
     at = own
     for ref in more_refs:
-        rows = ref.shape[0]
-        target[at : at + rows, :] = ref[...].astype(target.dtype)
-        at += rows
+        parts = [ref[k] for k in range(ref.shape[0])] if len(ref.shape) == 3 else [ref[...]]
+        for part in parts:
+            target[at : at + part.shape[0], :] = part.astype(target.dtype)
+            at += part.shape[0]
 
 
 def dot(left, right):
@@ -284,7 +96,7 @@
     units = w_gate.shape[1]
     cut = width // SIDE
     block = next(b for b in (256, 128) if units % b == 0)
-    tokens = own + sum(part.shape[0] for part in hid_more)
+    tokens = own + sum(math.prod(part.shape[:-1]) for part in hid_more)
     low = jnp.bfloat16
     column = lambda rows: pl.BlockSpec((rows, block), lambda i: (0, i))
     return pl.pallas_call(
@@ -303,12 +115,12 @@
     )(hid_own, *hid_more, grad_own, *grad_more, w_gate, w_up, w_down, d_gate, d_up, act)
 
 
-def mixer_kernel(more, sides, *refs):
+def mixer_kernel(more_norm, more_mix, *refs):
     at = iter(range(len(refs)))
     take = lambda count: [refs[next(at)] for _ in range(count)]
-    (norm_own,), norm_more = take(1), take(more)
-    (mix_own,), mix_more = take(1), take(more)
-    (y_own,), y_side = take(1), take(sides)
+    (norm_own,), norm_more = take(1), take(more_norm)
+    (mix_own,), mix_more = take(1), take(more_mix)
+    y_own, y_side = take(2)
     wo, wm = take(2)
     out_gate, out_mix, norm_turned = take(3)
     norm, mix, mixed, d_out = take(4)
@@ -329,10 +141,12 @@
             d_out[rows, :] = (d_mixed * y * (sig + silu * (1.0 - sig))).astype(d_out.dtype)
 
         finish(slice(0, own), y_own[...])
+        sides = y_side.shape[0]
+        head = lax.axis_index("head")
         for k in range(sides):
             for s in range(2):
                 start = own + (s * sides + k) * half
-                finish(slice(start, start + half), y_side[k][s])
+                finish(slice(start, start + half), y_side[k, head if s == 0 else 1 - head])
 
     rows = norm_turned.shape[0]
     span = pl.ds(pl.multiple_of(pl.program_id(0) * rows, rows), rows)
@@ -346,12 +160,12 @@
     own, width = norm_own.shape
     cut = w_out.shape[1]
     block = next(b for b in (256, 128) if width % b == 0)
-    tokens = own + sum(part.shape[0] for part in norm_more)
+    tokens = own + sum(math.prod(part.shape[:-1]) for part in norm_more)
     low = jnp.bfloat16
     row = lambda columns: pl.BlockSpec((block, columns), lambda i: (i, 0))
-    operands = (norm_own, *norm_more, mix_own, *mix_more, y_own, *y_side, w_out, w_mix)
+    operands = (norm_own, *norm_more, mix_own, *mix_more, y_own, y_side, w_out, w_mix)
     return pl.pallas_call(
-        functools.partial(mixer_kernel, len(norm_more), len(y_side)),
+        functools.partial(mixer_kernel, len(norm_more), len(mix_more)),
         grid=(width // block,),
         in_specs=[whole(a.shape) for a in operands],
         out_specs=[row(cut), row(cut), row(tokens)],
@@ -402,46 +216,154 @@
 MESH = pl.DeviceIdType.MESH
 
 
-def chain_kernel(
-    reverse, groups, ends_ref, total_ref, rate_ref, out_ref,
-    own, side, mine, line, back, done, side_send, side_recv, line_send, line_recv, back_send, back_recv,
-):
-    here, head = lax.axis_index("seq"), lax.axis_index("head")
-    place, group = lax.rem(here, SIDE), here // SIDE
-    streams, n, channels = ends_ref.shape
+def remote(source, target, sends, recvs, at, device):
+    return pltpu.make_async_remote_copy(
+        src_ref=source, dst_ref=target, send_sem=sends.at[at], recv_sem=recvs.at[at],
+        device_id=device, device_id_type=MESH,
+    )
+
+
+class Place:
+    def __init__(self, count):
+        here = lax.axis_index("seq")
+        self.head = lax.axis_index("head")
+        self.stride = count // SIDE
+        self.groups = count // SIDE
+        self.place, self.group = lax.rem(here, SIDE), here // SIDE
+        self.z = here // self.stride
+        base = here - self.place
+        self.member = [(base + (self.place ^ k), self.head) for k in range(SIDE)]
+        self.other = [
+            (lax.rem(self.group + k, self.groups) * SIDE + self.place, self.head) for k in range(self.groups)
+        ]
+        self.core = (here, 1 - self.head)
+        self.above = (lax.rem(here + self.stride, count), self.head)
+        self.below = (lax.rem(here - self.stride + count, count), self.head)
+
+    def greet(self):
+        barrier = pltpu.get_barrier_semaphore()
+        devices = self.member[1:] + self.other[1:] + [self.core]
+        for device in devices:
+            pl.semaphore_signal(barrier, inc=1, device_id=device, device_id_type=MESH)
+        pl.semaphore_wait(barrier, len(devices))
+
+
+class Line:
+    def __init__(self, where, mine, ring, rest, sends, recvs):
+        self.where, self.mine, self.ring, self.rest, self.sends, self.recvs = where, mine, ring, rest, sends, recvs
+
+    def copies(self, step):
+        w = self.where
+        up = self.mine if step == 1 else self.ring.at[SIDE - step]
+        down = self.mine if step == 1 else self.ring.at[step - 2]
+        return (
+            remote(up, self.ring.at[SIDE - 1 - step], self.sends, self.recvs, step - 1, w.above),
+            remote(down, self.ring.at[step - 1], self.sends, self.recvs, SIDE - 2 + step, w.below),
+        )
+
+    def core(self, slot):
+        return remote(self.ring.at[slot], self.rest.at[slot], self.sends, self.recvs, 2 * SIDE - 2 + slot, self.where.core)
+
+    def start(self, step):
+        up, down = self.copies(step)
+        z = self.where.z
+        pl.when((z >= step - 1) & (z < SIDE - 1))(up.start)
+        pl.when((z <= SIDE - step) & (z > 0))(down.start)
+
+    def arrive(self, step):
+        up, down = self.copies(step)
+        z = self.where.z
+
+        @pl.when(z >= step)
+        def _():
+            up.wait_recv()
+            self.core(SIDE - 1 - step).start()
+
+        @pl.when(z <= SIDE - 1 - step)
+        def _():
+            down.wait_recv()
+            self.core(step - 1).start()
+
+    def finish(self, first=1):
+        z = self.where.z
+        for step in range(first, SIDE):
+            up, down = self.copies(step)
+            pl.when((z >= step - 1) & (z < SIDE - 1))(up.wait_send)
+            pl.when((z <= SIDE - step) & (z > 0))(down.wait_send)
+        for slot in range(SIDE - 1):
+            self.core(slot).wait()
+
+
+LINE_SEMS = 3 * (SIDE - 1)
+
+
+class Side:
+    def __init__(self, where, mine, side, rest, sends, recvs):
+        self.where, self.mine, self.side, self.rest, self.sends, self.recvs = where, mine, side, rest, sends, recvs
+
+    def near(self):
+        return [
+            remote(self.mine, self.side.at[k - 1], self.sends, self.recvs, k - 1, self.where.member[k]) for k in (1, 2)
+        ]
+
+    def far(self):
+        half = self.side.shape[1] // 2
+        top, low = pl.ds(0, half), pl.ds(half, half)
+        return [
+            remote(self.side.at[1, top], self.side.at[2, top], self.sends, self.recvs, 2, self.where.member[1]),
+            remote(self.side.at[0, low], self.side.at[2, low], self.sends, self.recvs, 3, self.where.member[2]),
+        ]
+
+    def core(self, slot):
+        return remote(self.side.at[slot], self.rest.at[slot], self.sends, self.recvs, 4 + slot, self.where.core)
+
+    def start(self):
+        for c in self.near():
+            c.start()
+
+    def turn(self):
+        for c in self.near():
+            c.wait_recv()
+        for c in self.far():
+            c.start()
+        for slot in (0, 1):
+            self.core(slot).start()
+
+    def finish(self):
+        for c in self.far():
+            c.wait_recv()
+        self.core(2).start()
+        for c in self.near() + self.far():
+            c.wait_send()
+        for slot in range(3):
+            self.core(slot).wait()
+
+
+SIDE_SEMS = 7
+
+
+def chain(where, reverse, ends, total, rate_ref, out_ref, scratch, after_line, after_all):
+    own, side, mine, line, back, done, sends, recvs = scratch
+    streams, n, channels = ends.shape
     width = channels // SIDE
     rows = streams * n
-    base = here - place
-    member = [base + (place ^ k) for k in range(SIDE)]
-    other = [lax.rem(group + k, groups) * SIDE + place for k in range(groups)]
-
-    barrier = pltpu.get_barrier_semaphore()
-    for device in member[1:] + other[1:]:
-        pl.semaphore_signal(barrier, inc=1, device_id=(device, head), device_id_type=MESH)
+    place, group, groups = where.place, where.group, where.groups
     for q in range(SIDE):
         cols = slice(q * width, (q + 1) * width)
-        own[q, :rows, :] = ends_ref[:, :, cols].reshape(rows, width)
-        own[q, rows : rows + streams, :] = total_ref[:, cols]
+        own[q, :rows, :] = ends[:, :, cols].reshape(rows, width)
+        own[q, rows : rows + streams, :] = total[:, cols]
         own[q, rows + streams :, :] = jnp.zeros((own.shape[1] - rows - streams, width), jnp.float32)
-    rate = rate_ref[:, pl.ds(pl.multiple_of(place * width, 128), width)]
-    pl.semaphore_wait(barrier, SIDE - 1 + groups - 1)
-
-    def copy(source, target, send, recv, device):
-        return pltpu.make_async_remote_copy(
-            src_ref=source, dst_ref=target, send_sem=send, recv_sem=recv,
-            device_id=(device, head), device_id_type=MESH,
-        )
-
-    sides = [copy(own.at[place ^ k], side.at[k], side_send.at[k], side_recv.at[k], member[k]) for k in range(1, SIDE)]
+    sides = [remote(own.at[place ^ k], side.at[k], sends, recvs, k, where.member[k]) for k in range(1, SIDE)]
     for c in sides:
         c.start()
+    rate = rate_ref[:, pl.ds(pl.multiple_of(place * width, 128), width)]
+
+    def through(steps):
+        return jnp.concatenate([jnp.exp2(steps[s : s + 1] * rate) for s in range(streams)], axis=0)
+
     side[0] = own[place]
     for c in sides:
         c.wait_recv()
-
-    def through(steps):
-        return jnp.concatenate([jnp.exp2(steps[s : s + 1] * rate) for s in range(streams)], axis=0)
-
     state, steps = jnp.zeros((rows, width), jnp.float32), jnp.zeros((streams, width), jnp.float32)
     before, passed = [None] * SIDE, [None] * SIDE
     for j in reversed(range(SIDE)) if reverse else range(SIDE):
@@ -453,9 +375,10 @@
     mine[:rows, :] = state
     mine[rows : rows + streams, :] = steps
     mine[rows + streams :, :] = jnp.zeros((mine.shape[0] - rows - streams, width), jnp.float32)
-    lines = [copy(mine, line.at[k], line_send.at[k], line_recv.at[k], other[k]) for k in range(1, groups)]
+    lines = [remote(mine, line.at[k], sends, recvs, SIDE + k, where.other[k]) for k in range(1, groups)]
     for c in lines:
         c.start()
+    after_line()
     for c in lines:
         c.wait_recv()
     entering = jnp.zeros((rows, width), jnp.float32)
@@ -466,43 +389,380 @@
         entering = jnp.where(counts, new, entering)
     for j in range(SIDE):
         back[j] = through(passed[j]) * entering + before[j]
-    backs = [copy(back.at[place ^ k], done.at[place], back_send.at[k], back_recv.at[k], member[k]) for k in range(1, SIDE)]
+    backs = [
+        remote(back.at[place ^ k], done.at[k], sends, recvs, SIDE + groups + k, where.member[k]) for k in range(1, SIDE)
+    ]
     for c in backs:
         c.start()
-    done[place] = back[place]
+    after_all()
+    done[0] = back[place]
     for c in backs:
         c.wait_recv()
     for q in range(SIDE):
-        out_ref[:, :, q * width : (q + 1) * width] = done[q].reshape(streams, n, width)
+        out_ref[:, :, q * width : (q + 1) * width] = done[place ^ q].reshape(streams, n, width)
     for c in sides + lines + backs:
         c.wait_send()
 
 
-def chained(ends, total, rate, reverse):
-    streams, n, channels = ends.shape
-    groups = lax.axis_size("seq") // SIDE
+def chain_scratch(streams, n, channels, groups):
     width = channels // SIDE
     rows = streams * n
     tall = rows + 8 * (-(-streams // 8))
-    f32 = jnp.float32
+    sems = pltpu.SemaphoreType.DMA((2 * SIDE + groups,))
+    return [
+        pltpu.VMEM((SIDE, tall, width), jnp.float32),
+        pltpu.VMEM((SIDE, tall, width), jnp.float32),
+        pltpu.VMEM((tall, width), jnp.float32),
+        pltpu.VMEM((groups, tall, width), jnp.float32),
+        pltpu.VMEM((SIDE, rows, width), jnp.float32),
+        pltpu.VMEM((SIDE, rows, width), jnp.float32),
+        sems,
+        sems,
+    ]
+
+
+def sums(fall, total):
+    for s in range(fall.shape[0]):
+        total[s : s + 1, :] = jnp.sum(fall[s], axis=0, keepdims=True)
+
+
+def blocks_of(channels):
+    lanes = pieces(channels)
+    return lanes, channels // lanes
+
+
+def columns(i, lanes):
+    return pl.ds(pl.multiple_of(i * lanes, lanes), lanes)
+
+
+def forward_kernel(
+    count, fall, gain, b_ref, c_ref, rate_ref, grad_up, grad_down, norm_near, norm_next,
+    y_ref, first, ring, ring_rest, side_far, side_rest,
+    ends, total, line_send, line_recv, side_send, side_recv, local, *scratch,
+):
+    where = Place(count)
+    streams, length, channels = fall.shape
+    n = rate_ref.shape[0]
+    lanes, blocks = blocks_of(channels)
+    z = where.z
+    where.greet()
+    line = Line(where, None, ring, ring_rest, line_send, line_recv)
+    lift = pltpu.make_async_copy(grad_up, ring.at[SIDE - 2], local.at[0])
+    sink = pltpu.make_async_copy(grad_down, ring.at[0], local.at[1])
+    pl.when(z >= 1)(lift.start)
+    pl.when(z <= SIDE - 2)(sink.start)
+
+    def summary(i, _):
+        cols = columns(i, lanes)
+        rate = rate_ref[:, cols]
+
+        def chunk(i, states):
+            base = pl.multiple_of(i * ROWS, ROWS)
+            out = []
+            for s in range(streams):
+                state = states[s]
+                d = fall[s, pl.ds(base, ROWS), cols]
+                x = gain[s, pl.ds(base, ROWS), cols]
+                for j in range(ROWS):
+                    b = b_ref[s, pl.ds(pl.multiple_of((base + j) * n, n), n), :]
+                    fade = jnp.exp2(d[j : j + 1] * rate)
+                    state = fade * state + x[j : j + 1] * wide(b, lanes)
+                out.append(state)
+            return tuple(out)
+
+        start = tuple(jnp.zeros((n, lanes), jnp.float32) for _ in range(streams))
+        states = lax.fori_loop(0, length // ROWS, chunk, start)
+        for s in range(streams):
+            ends[s, :, cols] = states[s]
+        return 0
+
+    lax.fori_loop(0, blocks, summary, 0)
+    sums(fall, total)
+
+    half = norm_near.shape[0] // 2
+    top, low = pl.ds(0, half), pl.ds(half, half)
+    far = [
+        remote(norm_next.at[top], side_far.at[top], side_send, side_recv, 0, where.member[1]),
+        remote(norm_near.at[low], side_far.at[low], side_send, side_recv, 1, where.member[2]),
+    ]
+    cores = [
+        remote(part, side_rest.at[k], side_send, side_recv, 2 + k, where.core)
+        for k, part in enumerate((norm_near, norm_next, side_far))
+    ]
+
+    def after_line():
+        @pl.when(z >= 1)
+        def _():
+            lift.wait()
+            line.core(SIDE - 2).start()
+
+        @pl.when(z <= SIDE - 2)
+        def _():
+            sink.wait()
+            line.core(0).start()
+
+        line.start(2)
+
+    def after_all():
+        for c in far + cores[:2]:
+            c.start()
+
+    chain(where, False, ends, total, rate_ref, first, scratch, after_line, after_all)
+
+    def run(i, _):
+        cols = columns(i, lanes)
+        rate = rate_ref[:, cols]
+
+        @pl.when(i == blocks // 2)
+        def _():
+            line.arrive(2)
+            line.start(3)
+
+        def chunk(i, states):
+            base = pl.multiple_of(i * ROWS, ROWS)
+            out = []
+            for s in range(streams):
+                state = states[s]
+                d = fall[s, pl.ds(base, ROWS), cols]
+                x = gain[s, pl.ds(base, ROWS), cols]
+                rows = []
+                for j in range(ROWS):
+                    at = pl.ds(pl.multiple_of((base + j) * n, n), n)
+                    fade = jnp.exp2(d[j : j + 1] * rate)
+                    state = fade * state + x[j : j + 1] * wide(b_ref[s, at, :], lanes)
+                    rows.append(jnp.sum(state * wide(c_ref[s, at, :], lanes), axis=0, keepdims=True))
+                y_ref[s, pl.ds(base, ROWS), cols] = jnp.concatenate(rows, axis=0)
+                out.append(state)
+            return tuple(out)
+
+        lax.fori_loop(0, length // ROWS, chunk, tuple(first[s, :, cols] for s in range(streams)))
+        return 0
+
+    lax.fori_loop(0, blocks, run, 0)
+    for c in far:
+        c.wait_recv()
+    cores[2].start()
+    line.arrive(3)
+    for c in far:
+        c.wait_send()
+    for c in cores:
+        c.wait()
+    line.finish(2)
+
+
+def backward_kernel(
+    count, fall, d_ref, v_ref, g_ref, b_ref, c_ref, rate_ref, first_ref, hidden, mix, y_ref,
+    dstep_ref, dvalue_ref, db_ref, dc_ref, decay_ref, ring, ring_rest, side, side_rest, y_side,
+    ends, total, last, path, fades, line_send, line_recv, side_send, side_recv, y_send, y_recv, *scratch,
+):
+    where = Place(count)
+    streams, length, channels = fall.shape
+    n = rate_ref.shape[0]
+    lanes, blocks = blocks_of(channels)
+    chunks = length // ROWS
+    width = channels // SIDE
+    where.greet()
+    line = Line(where, hidden, ring, ring_rest, line_send, line_recv)
+    square = Side(where, mix, side, side_rest, side_send, side_recv)
+    quarters = [
+        remote(
+            y_ref.at[:, :, pl.ds(pl.multiple_of((where.place ^ k) * width, 128), width)],
+            y_side.at[k - 1], y_send, y_recv, k - 1, where.member[k],
+        )
+        for k in range(1, SIDE)
+    ]
+
+    def summary(i, _):
+        cols = columns(i, lanes)
+        rate = rate_ref[:, cols]
+
+        def chunk(i, carry):
+            base = pl.multiple_of((chunks - 1 - i) * ROWS, ROWS)
+            out = []
+            for s in range(streams):
+                carried = carry[s]
+                d = fall[s, pl.ds(base, ROWS), cols]
+                g = g_ref[s, pl.ds(base, ROWS), cols]
+                for j in reversed(range(ROWS)):
+                    at = pl.ds(pl.multiple_of((base + j) * n, n), n)
+                    fade = jnp.exp2(d[j : j + 1] * rate)
+                    carried = fade * (g[j : j + 1] * wide(c_ref[s, at, :], lanes) + carried)
+                out.append(carried)
+            return tuple(out)
+
+        start = tuple(jnp.zeros((n, lanes), jnp.float32) for _ in range(streams))
+        states = lax.fori_loop(0, chunks, chunk, start)
+        for s in range(streams):
+            ends[s, :, cols] = states[s]
+        return 0
+
+    lax.fori_loop(0, blocks, summary, 0)
+    sums(fall, total)
+
+    def after_line():
+        line.start(1)
+
+    def after_all():
+        square.start()
+
+    chain(where, True, ends, total, rate_ref, last, scratch, after_line, after_all)
+    db_ref[...] = jnp.zeros_like(db_ref)
+    dc_ref[...] = jnp.zeros_like(dc_ref)
+
+    def fold(tile):
+        out = tile[:, :128]
+        for k in range(1, lanes // 128):
+            out = out + tile[:, k * 128 : (k + 1) * 128]
+        return out
+
+    def run(i, _):
+        cols = columns(i, lanes)
+        rate = rate_ref[:, cols]
+
+        @pl.when(i == blocks // 6)
+        def _():
+            line.arrive(1)
+            line.start(2)
+
+        @pl.when(i == blocks // 2)
+        def _():
+            square.turn()
+            for c in quarters:
+                c.start()
+
+        @pl.when(i == blocks - blocks // 6)
+        def _():
+            line.arrive(2)
+            line.start(3)
+
+        def ahead(i, states):
+            base = pl.multiple_of(i * ROWS, ROWS)
+            out = []
+            for s in range(streams):
+                state = states[s]
+                d = fall[s, pl.ds(base, ROWS), cols]
+                x = d_ref[s, pl.ds(base, ROWS), cols] * v_ref[s, pl.ds(base, ROWS), cols]
+                for j in range(ROWS):
+                    at = pl.ds(pl.multiple_of((base + j) * n, n), n)
+                    path[s, at, :] = state
+                    fade = jnp.exp2(d[j : j + 1] * rate)
+                    fades[s, at, :] = fade
+                    state = fade * state + x[j : j + 1] * wide(b_ref[s, at, :], lanes)
+                out.append(state)
+            return tuple(out)
+
+        tails = lax.fori_loop(0, chunks, ahead, tuple(first_ref[s, :, cols] for s in range(streams)))
+
+        def back(i, carry):
+            base = pl.multiple_of((chunks - 1 - i) * ROWS, ROWS)
+            out = []
+            decay = carry[-1]
+            for s in range(streams):
+                state, carried = carry[s]
+                d = d_ref[s, pl.ds(base, ROWS), cols]
+                v = v_ref[s, pl.ds(base, ROWS), cols]
+                g = g_ref[s, pl.ds(base, ROWS), cols]
+                x = d * v
+                weights, touches = [None] * ROWS, [None] * ROWS
+                for j in reversed(range(ROWS)):
+                    at = pl.ds(pl.multiple_of((base + j) * n, n), n)
+                    gj = g[j : j + 1]
+                    adjoint = gj * wide(c_ref[s, at, :], lanes) + carried
+                    dc_ref[s, at, :] += fold(state * gj)
+                    db_ref[s, at, :] += fold(adjoint * x[j : j + 1])
+                    weights[j] = jnp.sum(adjoint * wide(b_ref[s, at, :], lanes), axis=0, keepdims=True)
+                    carried = adjoint * fades[s, at, :]
+                    state = path[s, at, :]
+                    touch = carried * state
+                    touches[j] = jnp.sum(touch * rate, axis=0, keepdims=True)
+                    decay = decay + touch * d[j : j + 1]
+                weighted = jnp.concatenate(weights, axis=0)
+                at = pl.ds(base, ROWS)
+                dstep_ref[s, at, cols] = weighted * v + jnp.concatenate(touches, axis=0) * LN2
+                dvalue_ref[s, at, cols] = weighted * d
+                out.append((state, carried))
+            return tuple(out) + (decay,)
+
+        start = tuple((tails[s], last[s, :, cols]) for s in range(streams))
+        done = lax.fori_loop(0, chunks, back, start + (jnp.zeros((n, lanes), jnp.float32),))
+        decay_ref[:, cols] = done[-1]
+        return 0
+
+    lax.fori_loop(0, blocks, run, 0)
+    square.finish()
+    line.arrive(3)
+    for c in quarters:
+        c.wait()
+    line.finish()
+
+
+def in_vmem():
+    return pl.BlockSpec(memory_space=pltpu.VMEM)
+
+
+def in_hbm():
+    return pl.BlockSpec(memory_space=pl.ANY)
+
+
+def shaped(*shape):
+    return jax.ShapeDtypeStruct(shape, jnp.float32)
+
+
+def sems(count):
+    return [pltpu.SemaphoreType.DMA((count,))] * 2
+
+
+def scan_forward(fall, gain, b_wide, c_wide, rate, grad_up, grad_down, norm_near, norm_next):
+    streams, length, channels = fall.shape
+    n = rate.shape[0]
+    count = lax.axis_size("seq")
+    half, width = grad_up.shape
+    three = shaped(SIDE - 1, half, width)
     return pl.pallas_call(
-        functools.partial(chain_kernel, reverse, groups),
-        out_shape=jax.ShapeDtypeStruct(ends.shape, f32),
-        in_specs=[pl.BlockSpec(memory_space=pltpu.VMEM)] * 3,
-        out_specs=pl.BlockSpec(memory_space=pltpu.VMEM),
+        functools.partial(forward_kernel, count),
+        out_shape=[shaped(streams, length, channels), shaped(streams, n, channels), three, three, shaped(half, width), three],
+        in_specs=[in_vmem()] * 5 + [in_hbm()] * 4,
+        out_specs=[in_vmem()] * 2 + [in_hbm()] * 4,
+        scratch_shapes=[pltpu.VMEM((streams, n, channels), jnp.float32), pltpu.VMEM((streams, channels), jnp.float32)]
+        + sems(LINE_SEMS) + sems(5) + [pltpu.SemaphoreType.DMA((2,))]
+        + chain_scratch(streams, n, channels, count // SIDE),
+        compiler_params=pltpu.CompilerParams(
+            collective_id=0, has_side_effects=True, vmem_limit_bytes=40 * 1024 * 1024
+        ),
+        cost_estimate=spans(40),
+    )(fall, gain, b_wide, c_wide, rate, grad_up, grad_down, norm_near, norm_next)
+
+
+def scan_backward(fall, step, value, d_y, b_wide, c_wide, rate, first, hidden, mix, y):
+    streams, length, channels = fall.shape
+    n = rate.shape[0]
+    count = lax.axis_size("seq")
+    half, width = hidden.shape
+    lanes, _ = blocks_of(channels)
+    three = shaped(SIDE - 1, half, width)
+    tall = shaped(streams, length * n, 128)
+    flat = shaped(streams, length, channels)
+    kept = pltpu.VMEM((streams, length * n, lanes), jnp.float32)
+    return pl.pallas_call(
+        functools.partial(backward_kernel, count),
+        out_shape=[flat, flat, tall, tall, shaped(n, channels), three, three, three, three,
+                   shaped(SIDE - 1, streams, length, channels // SIDE)],
+        in_specs=[in_vmem()] * 8 + [in_hbm()] * 3,
+        out_specs=[in_vmem()] * 5 + [in_hbm()] * 5,
         scratch_shapes=[
-            pltpu.VMEM((SIDE, tall, width), f32),
-            pltpu.VMEM((SIDE, tall, width), f32),
-            pltpu.VMEM((tall, width), f32),
-            pltpu.VMEM((groups, tall, width), f32),
-            pltpu.VMEM((SIDE, rows, width), f32),
-            pltpu.VMEM((SIDE, rows, width), f32),
+            pltpu.VMEM((streams, n, channels), jnp.float32),
+            pltpu.VMEM((streams, channels), jnp.float32),
+            pltpu.VMEM((streams, n, channels), jnp.float32),
+            kept,
+            kept,
         ]
-        + [pltpu.SemaphoreType.DMA((m,)) for m in (SIDE, SIDE, groups, groups, SIDE, SIDE)],
+        + sems(LINE_SEMS) + sems(SIDE_SEMS) + sems(SIDE - 1)
+        + chain_scratch(streams, n, channels, count // SIDE),
         compiler_params=pltpu.CompilerParams(
-            collective_id=1 if reverse else 0, has_side_effects=True, vmem_limit_bytes=32 * 1024 * 1024
+            collective_id=1, has_side_effects=True, vmem_limit_bytes=52 * 1024 * 1024
         ),
-    )(ends, total, rate)
+        cost_estimate=spans(62),
+    )(fall, step, value, d_y, b_wide, c_wide, rate, first, hidden, mix, y)
 
 
 epsilon = 1e-06
@@ -549,26 +809,8 @@
     return part_of(block, place, size, 2).reshape(-1, size), [send(away[k - 1], swaps(k)) for k in range(1, SIDE)]
 
 
-def other_core(parts):
-    return [send(part, swaps(1, "head"), "head") for part in parts]
-
-
 def after(block, *earlier):
     return lax.optimization_barrier((block,) + earlier)[0]
-
-
-def scatter_line(blocks, stride):
-    n = lax.axis_size("seq")
-    z = lax.axis_index("seq") // stride
-    take = lambda at: lax.dynamic_index_in_dim(blocks, jnp.clip(at, 0, SIDE - 1), 0, keepdims=False)
-    up = down = None
-    for turn in range(SIDE - 1):
-        one, two = take(SIDE - 1 - turn + z), take(z + turn - SIDE + 1)
-        if turn:
-            one, two = one + up, two + down
-        up = send(one, [(i, i + stride) for i in range(min((turn + 1) * stride, n - stride))])
-        down = send(two, [(i, i - stride) for i in range(max(n - (turn + 1) * stride, stride), n)])
-    return take(z) + (up + down)
 
 
 def scatter_bits(blocks, bits):
@@ -657,24 +899,23 @@
 
     grad_in = out_grad.astype(jnp.float32)
     source = tokens.astype(jnp.float32)
+    rim_ids = jnp.broadcast_to((doc_ids[:, length - lead :] + 1).astype(jnp.float32)[:, :, None], (streams, lead, 128))
+    rim = send(jnp.concatenate([source[:, length - lead :], rim_ids], axis=2), links(1))
     mine_grad = own_stream(out_grad).astype(jnp.float32)
-    line_grad = {k: send(mine_grad, links(k * stride, True)) for k in (1, 3)}
+    grad_up = send(mine_grad, links(stride))
+    grad_down = send(mine_grad, links(-stride))
     normed, scale_mix = norm_forward(source, norm_mix)
     normed_low = normed.astype(low)
     mine_normed = own_stream(normed)
-    side_normed = [send(mine_normed, swaps(k)) for k in range(1, SIDE)]
-    side_normed = side_normed + other_core(side_normed)
-    inner = matmul(normed_low, w_inner)
+    norm_near, norm_next = send(mine_normed, swaps(1)), send(mine_normed, swaps(2))
+    rim_normed, _ = norm_forward(rim[:, :, :width], norm_mix)
+    ext_val = matmul(jnp.concatenate([rim_normed.astype(low), normed_low], axis=1), w_inner)
     outgate = matmul(normed_low, w_outgate)
-    rim_ids = (doc_ids[:, length - lead :] + 1).astype(jnp.float32)
-    rim_val = send(inner[:, length - lead :], links(1))
-    rim_got = send(rim_ids, links(1))
-    ext_val = jnp.concatenate([rim_val, inner], axis=1)
-    ext_ids = jnp.concatenate([rim_got.astype(jnp.int32) - 1, doc_ids], axis=1)
+    ext_ids = jnp.concatenate([rim[:, :, width].astype(jnp.int32) - 1, doc_ids], axis=1)
     masks = [
         (ext_ids[:, k : k + length] == doc_ids).astype(jnp.float32)[:, :, None] for k in range(taps)
     ]
-    value_pre = jnp.zeros_like(inner) + conv_bias
+    value_pre = conv_bias
     for k in range(taps):
         value_pre = value_pre + conv_taps[k] * ext_val[:, k : k + length] * masks[k]
     value = jax.nn.silu(value_pre)
@@ -695,15 +936,10 @@
     decay_rate = -jnp.exp(log_decay).T
     rate = decay_rate * LOG2E
     b_wide, c_wide = across(bsel), across(csel)
-    ends = summarize(fall, gain, b_wide, rate)
-    total = jnp.sum(fall, axis=1)
-    first = chained(ends, total, rate, False)
-    line_grad[2] = send(after(mine_grad, first), links(2 * stride, True))
-    line_grad = [line_grad[k] for k in range(1, SIDE)]
-    line_grad = line_grad + other_core(line_grad)
-    outs = run_states(fall, gain, b_wide, c_wide, rate, first)
+    outs, first, grad_ring, grad_rest, side_far, side_rest = scan_forward(
+        fall, gain, b_wide, c_wide, rate, grad_up, grad_down, norm_near, norm_next
+    )
     y = outs + skip_gain * value
-    own_y, side_y = exchange(y, place)
     gate_z = jax.nn.silu(outgate)
     mixed = y * gate_z
     mixed_low = mixed.astype(low)
@@ -711,10 +947,6 @@
     resid = source + mix
     hidden, scale_ffn = norm_forward(resid, norm_ffn)
     hidden_low = hidden.astype(low)
-    mine_hidden = own_stream(hidden)
-    line_hidden = [send(mine_hidden, links(k * stride, True)) for k in (1, 3, 2)]
-    line_hidden = [line_hidden[k] for k in (0, 2, 1)]
-    line_hidden = line_hidden + other_core(line_hidden)
     gate = matmul(hidden_low, w_gate)
     up = matmul(hidden_low, w_up)
     act_low = (jax.nn.silu(gate) * up).astype(low)
@@ -727,22 +959,23 @@
     d_resid_norm, grad_norm_ffn = norm_backward(resid, scale_ffn, norm_ffn, d_hidden)
     d_resid = grad_in + d_resid_norm
     d_mix = d_resid.astype(low)
-    mine_d_mix = own_stream(d_resid)
-    side_d_mix = [send(mine_d_mix, swaps(k)) for k in range(1, SIDE)]
-    side_d_mix = side_d_mix + other_core(side_d_mix)
     d_mixed = matmul_back(d_mix, w_mixout)
     d_y = d_mixed * gate_z
     d_outgate = (d_mixed * y * silu_slope(outgate)).astype(low)
     grad_skip_gain = jnp.sum(d_y * value, axis=(0, 1))
-    leaving = adjoint_summary(fall, d_y, c_wide, rate)
-    last = chained(leaving, total, rate, True)
-    d_step, d_scan, db_wide, dc_wide, decay_sum = adjoint_run(
-        fall, step, value, d_y, b_wide, c_wide, rate, first, last
+    d_step, d_scan, db_wide, dc_wide, decay_sum, hid_ring, hid_rest, mix_side, mix_rest, y_side = scan_backward(
+        fall, step, value, d_y, b_wide, c_wide, rate, first, own_stream(hidden), own_stream(d_resid), y
     )
 
     flat = lambda block: block.reshape(-1, block.shape[-1])
+    size = channels // SIDE
+    whole_outgate, whole_mixout, turned = mixer_grads(
+        flat(normed_low), [norm_near, norm_next, side_far, side_rest], flat(d_mix), [mix_side, mix_rest],
+        flat(part_of(y, place, size, 2)), y_side,
+        part_of(w_outgate, place, size, 1), part_of(w_mixout, place, size, 0),
+    )
     whole_gate, whole_up, whole_down = ffn_grads(
-        stride, flat(hidden_low), line_hidden, flat(out_grad), line_grad, w_gate, w_up, w_down,
+        stride, flat(hidden_low), [hid_ring, hid_rest], flat(out_grad), [grad_ring, grad_rest], w_gate, w_up, w_down,
         flat(d_gate), flat(d_up), flat(act_low),
     )
     side_bits = bits_between(1, stride)
@@ -759,11 +992,6 @@
     grad_w_up = sum_side(whole_up)
     grad_w_down = sum_side(whole_down).T
 
-    size = channels // SIDE
-    whole_outgate, whole_mixout, turned = mixer_grads(
-        flat(normed_low), side_normed, flat(d_mix), side_d_mix, own_y, side_y,
-        part_of(w_outgate, place, size, 1), part_of(w_mixout, place, size, 0),
-    )
     groups = [list(range(k, count, SIDE)) for k in range(SIDE)]
 
     def sum_line(whole):

time: 638 us -> 522 us (0.82)
  waiting for transfers between devices: 225 us -> 99.1 us
  Pallas kernels: 146 us -> 208 us
  starting transfers between devices: 97.9 us -> 48.1 us
  local copies, waits for them, and re-layouts: 47.6 us -> 55.7 us
  matrix products: 48.1 us -> 40.7 us
    ppermute x68 -> x44, waiting for transfers between devices: 225 us -> 99 us  [send(): return lax.ppermute(block, axis, route)]
    pallas_call x7 -> x3, Pallas kernels: 107 us -> 169 us  [the longest x1 83 us: scan_backward(): pl.pallas_call(functools.partial(backward_kernel, count), out_shape=[flat...]
    ppermute x68 -> x44, starting transfers between devices: 97.5 us -> 48 us  [send(): return lax.ppermute(block, axis, route)]
    unnamed x208 -> x258, local copies, waits for them, and re-layouts: 12.3 us -> 22 us
    dot_general x8, matrix products: 25.4 us -> 17.9 us  [matmul(): return jnp.dot(left, right, preferred_element_type=jnp.float32)]
  transfers between devices with their start and end apart: 71 -> 47, of which waited for: 26 -> 22; matrix products, arithmetic and copies ran while one was open for 14% -> 19% of each run, Pallas kernels for 9% -> 8%
where the time goes in v3:
time: 522 us; the launch traced here: 514 us
  Pallas kernels  208 us (40%)
  waiting for transfers between devices  99.1 us (19%)
  local copies, waits for them, and re-layouts  55.7 us (11%)
  starting transfers between devices  48.1 us (9%)
  other arithmetic  46.7 us (9%)
  matrix products  40.7 us (8%)
  between operations  16.3 us (3%)
    ppermute x44, waiting for transfers between devices, send(): return lax.ppermute(block, axis, route)  99 us
    pallas_call x1, Pallas kernels, scan_backward(): pl.pallas_call(functools.partial(backward_kernel, count), out_shape=[flat...  83 us
    pallas_call x1, Pallas kernels, scan_forward(): pl.pallas_call(functools.partial(forward_kernel, count), out_shape=[shape...  70.3 us
    ppermute x44, starting transfers between devices, send(): return lax.ppermute(block, axis, route)  48 us
    pallas_call x1, Pallas kernels, ffn_grads(): pl.pallas_call(functools.partial(ffn_kernel, stride, len(hid_more)), grid...  33.1 us
    unnamed x258, local copies, waits for them, and re-layouts  22 us
    dot_general x8, matrix products, matmul_back(): lax.dot_general(left, right, (((left.ndim - 1,), (1,)), ((), ())), prefer...  21.9 us
    dot_general x8, matrix products, matmul(): return jnp.dot(left, right, preferred_element_type=jnp.float32)  17.9 us
  transfers between devices with their start and end apart: 47, of which 22 were waited for; matrix products, arithmetic and copies ran while one was open for 19% of the time, Pallas kernels for 8%

profile of v3, /device:TPU:0, one launch (start us, length us, event | category | flops | bytes accessed | tf_op | source)
XLA Modules:
  0.0 514.3 jit_solution(5811438439020323201)
XLA Ops:
  9.3 5.0 collective-permute-start.2
  26.6 10.1 %collective-permute-done = f32[2,3,1664]{2,1,0:T(4,128)S(1)} collective-permute-done((f32[2,3,1664]{2,1,0:T(4,128)S(1)}, f32[2,3,1664]{2,1,0:T(4,128)S(1)}, u32[]{:S(2)}, u32[]{:S(2)}) %collective-permute-start) | collective-permute-done | bytes 39968 | tf_op jit(solution)/shard_map/ppermute | solution.py:782
  45.0 4.6 compare_select_fusion
  54.2 70.3 %shard_map.322 = (f32[2,128,1536]{2,1,0:T(8,128)S(1)}, f32[2,16,1536]{2,1,0:T(8,128)S(1)}, f32[3,128,1536]{2,1,0:T(8,128)}, f32[3,128,1536]{2,1,0:T(8,128)}, f32...) custom-call(f32[2,128,1536]{2,1,0:T(8,128)S(1)} %get-tuple-element.118.fall, f32[2,128,1536]{2,1,0:T(8,128)S(1)} %get-tuple-element.119.gain, ...), custom_call_target="tpu_custom_call" | custom-call | flops 4400000000 | bytes 12000000 | tf_op jit(solution)/shard_map/pallas_call | solution.py:721
  141.5 3.0 fusion.27
  144.9 3.0 fusion.2
  157.9 4.6 fusion.87
  163.3 4.0 multiply_reduce_fusion.1
  168.3 83.0 %shard_map.323 = (f32[2,128,1536]{2,1,0:T(8,128)}, f32[2,128,1536]{2,1,0:T(8,128)}, f32[2,2048,128]{2,1,0:T(8,128)}, f32[2,2048,128]{2,1,0:T(8,128)}, f32[16,153...) custom-call(f32[2,128,1536]{2,1,0:T(8,128)} %copy-done.9, ...), custom_call_target="tpu_custom_call" | custom-call | flops 6819999744 | bytes 18600000 | tf_op jit(solution)/shard_map/pallas_call | solution.py:746
  251.3 15.6 %shard_map.324 = (f32[1536,384]{1,0:T(8,128)}, f32[1536,384]{1,0:T(8,128)}, bf16[1536,1024]{1,0:T(8,128)(2,1)}) custom-call(bf16[256,1536]{1,0:T(8,128)(2,1)} %bitcast.229, f32[128,1536]{1,0:T(8,128)} %copy-done.3, f32[128,1536]{1,0:T(8,128)} %copy-done.4, f32[128,1536]{1,0:T(8,128)} %copy-done.6, f32[3,128,1536]{2,1,0:T(8,128)} %get-tuple-element.48.refs_4_, ...), custom_call_target="tpu_custom_call" | custom-call | flops 1320000000 | bytes 3600000 | tf_op jit(solution)/shard_map/pallas_call | solution.py:167
  276.8 33.1 %shard_map.326 = (f32[384,2048]{1,0:T(8,128)}, f32[384,2048]{1,0:T(8,128)}, f32[384,2048]{1,0:T(8,128)}) custom-call(bf16[256,1536]{1,0:T(8,128)(2,1)} %bitcast.233, f32[3,128,1536]{2,1,0:T(8,128)} %get-tuple-element.55.refs_1_, f32[3,128,1536]{2,1,0:T(8,128)} %get-tuple-element.56.refs_2_, bf16[256,1536]{1,0:T(8,128)(2,1)} %bitcast.226, ...), custom_call_target="tpu_custom_call" | custom-call | flops 2640000000 | bytes 7200000 | tf_op jit(solution)/shard_map/pallas_call | solution.py:102
  323.6 5.2 %fusion.16 = f32[2,128,1536]{2,1,0:T(8,128)} fusion(bf16[1536,1536]{1,0:T(8,128)(2,1)} %param.24, f32[2,128,1536]{2,1,0:T(8,128)S(1)} %copy-done.111, f32[2,128,1536]{2,1,0:T(8,128)S(1)} %copy-done.54, f32[2,128,1536]{2,1,0:T(8,128)S(1)} %copy-done.110), kind=kOutput, calls=%fused_computation.16 | convolution fusion | flops 1211891712 | bytes 11010048 | tf_op jit(solution)/shard_map/dot_general | solution.py:845
  331.9 4.2 multiply_reduce_fusion.2
  358.3 3.1 collective-permute-done.16.refs_2_
  361.6 8.5 %collective-permute-done.17.refs_3_ = f32[2,128,384]{2,1,0:T(8,128)S(1)} collective-permute-done((f32[2,128,384]{2,1,0:T(8,128)S(1)}, f32[2,128,384]{2,1,0:T(8,128)S(1)}, u32[]{:S(2)}, u32[]{:S(2)}) %collective-permute-start.17) | collective-permute-done | bytes 393248 | tf_op jit(solution)/shard_map/ppermute | solution.py:782
  373.2 5.8 %shard_map.325 = f32[1536,384]{1,0:T(8,128)} custom-call(bf16[1536,1024]{1,0:T(8,128)(2,1)} %get-tuple-element.52.refs_0_, bf16[256,384]{1,0:T(8,128)(2,1)} %bitcast.240, f32[2,128,384]{2,1,0:T(8,128)} %copy-done.61, f32[2,128,384]{2,1,0:T(8,128)} %copy-done.62, f32[2,128,384]{2,1,0:T(8,128)} %copy-done.63), custom_call_target="tpu_custom_call" | custom-call | flops 440000000 | bytes 1200000 | tf_op jit(solution)/shard_map/pallas_call | solution.py:203
  382.0 9.1 %collective-permute-done.32 = f32[2,96,1024]{2,1,0:T(8,128)} collective-permute-done((f32[2,96,1024]{2,1,0:T(8,128)}, f32[2,96,1024]{2,1,0:T(8,128)}, u32[]{:S(2)}, u32[]{:S(2)}) %collective-permute-start.32) | collective-permute-done | bytes 786464 | tf_op jit(solution)/shard_map/ppermute | solution.py:782
  393.8 14.1 %collective-permute-done.36 = f32[2,96,1024]{2,1,0:T(8,128)} collective-permute-done((f32[2,96,1024]{2,1,0:T(8,128)}, f32[2,96,1024]{2,1,0:T(8,128)}, u32[]{:S(2)}, u32[]{:S(2)}) %collective-permute-start.36) | collective-permute-done | bytes 786464 | tf_op jit(solution)/shard_map/ppermute | solution.py:782
  411.5 13.2 %collective-permute-done.40 = f32[2,96,1024]{2,1,0:T(8,128)S(1)} collective-permute-done((f32[2,96,1024]{2,1,0:T(8,128)}, f32[2,96,1024]{2,1,0:T(8,128)S(1)}, u32[]{:S(2)}, u32[]{:S(2)}) %collective-permute-start.40) | collective-permute-done | bytes 786464 | tf_op jit(solution)/shard_map/ppermute | solution.py:782
  426.7 4.3 collective-permute-done.28
  436.6 5.0 collective-permute-done.39
  455.5 5.8 %collective-permute-done.12 = f32[2,2,2,122,96]{4,2,1,0,3:T(2,128)S(1)} collective-permute-done((f32[2,2,2,122,96]{4,2,1,0,3:T(2,128)S(1)}, f32[2,2,2,122,96]{4,2,1,0,3:T(2,128)S(1)}, u32[]{:S(2)}, u32[]{:S(2)}) %collective-permute-start.12) | collective-permute-done | bytes 374816 | tf_op jit(solution)/shard_map/ppermute | solution.py:782
  463.8 4.8 collective-permute-done.13
  468.8 4.9 collective-permute-done.14
  (505 shorter events, 173.9 us)
Async XLA Ops:
  7.2 474.7 %reduce-scatter.6.cloned.1.call-start = ((), (), s32[]{:S(2)}) async-start(), calls=%async_computation.4 | async-start | bytes 2949120 | tf_op jit(solution)/shard_map/reduce_scatter | solution.py:998
  9.3 40.3 %collective-permute-start.2 = (f32[128,1536]{1,0:T(8,128)}, f32[128,1536]{1,0:T(8,128)S(1)}, u32[]{:S(2)}, u32[]{:S(2)}) collective-permute-start(f32[128,1536]{1,0:T(8,128)} %bitcast_convert_fusion), channel_id=1, source_target_pairs={{0,8},{2,10},{4,12},{6,14},{8,16},{10,18},{12,20},{14,22},{16,24},... | collective-permute-start | bytes 2359304 | tf_op jit(solution)/shard_map/ppermute | solution.py:782
  14.3 36.2 %collective-permute-start.3 = (f32[128,1536]{1,0:T(8,128)}, f32[128,1536]{1,0:T(8,128)}, u32[]{:S(2)}, u32[]{:S(2)}) collective-permute-start(f32[128,1536]{1,0:T(8,128)} %bitcast_convert_fusion), channel_id=1, source_target_pairs={{8,0},{10,2},{12,4},{14,6},{16,8},{18,10},{20,12},{22,14},{24,16},... | collective-permute-start | bytes 2359304 | tf_op jit(solution)/shard_map/ppermute | solution.py:782
  17.4 33.2 %collective-permute-start.4 = (f32[128,1536]{1,0:T(8,128)}, f32[128,1536]{1,0:T(8,128)S(1)}, u32[]{:S(2)}, u32[]{:S(2)}) collective-permute-start(f32[128,1536]{1,0:T(8,128)} %dynamic-slice_bitcast_fusion.8), channel_id=1, source_target_pairs={{0,2},{2,0},{4,6},{6,4},{8,10},{10,8},{12,14},{14,12},{16,18},{18,... | collective-permute-start | bytes 2359304 | tf_op jit(solution)/shard_map/ppermute | solution.py:782
  18.8 31.7 %collective-permute-start.5 = (f32[128,1536]{1,0:T(8,128)}, f32[128,1536]{1,0:T(8,128)S(1)}, u32[]{:S(2)}, u32[]{:S(2)}) collective-permute-start(f32[128,1536]{1,0:T(8,128)} %dynamic-slice_bitcast_fusion.8), channel_id=1, source_target_pairs={{0,4},{2,6},{4,0},{6,2},{8,12},{10,14},{12,8},{14,10},{16,20},{18,... | collective-permute-start | bytes 2359304 | tf_op jit(solution)/shard_map/ppermute | solution.py:782
  266.9 219.8 %reduce-scatter.8.cloned.1.call-start = ((), (), s32[]{:S(2)}) async-start(), calls=%async_computation.5 | async-start | bytes 2949120 | tf_op jit(solution)/shard_map/reduce_scatter | solution.py:998
  274.8 56.4 %collective-permute-start.9 = (f32[2,128,128]{1,2,0:T(8,128)S(1)}, f32[2,128,128]{1,2,0:T(8,128)S(1)}, u32[]{:S(2)}, u32[]{:S(2)}) collective-permute-start(f32[2,128,128]{1,2,0:T(8,128)S(1)} %pad_maximum_fusion.4), channel_id=1, source_target_pairs={{0,1},{1,0},{2,3},{3,2},{4,5},{5,4},{6,7},{7,6},{8,9},{9,8},{10,11... | collective-permute-start | bytes 393224 | tf_op jit(solution)/shard_map/ppermute | solution.py:782
  313.0 66.7 %collective-permute-start.34 = (f32[2,96,1024]{2,1,0:T(8,128)}, f32[2,96,1024]{2,1,0:T(8,128)}, u32[]{:S(2)}, u32[]{:S(2)}) collective-permute-start(f32[2,96,1024]{2,1,0:T(8,128)} %dynamic-slice_bitcast_fusion.4), channel_id=1, source_target_pairs={{0,4},{2,6},{4,0},{6,2},{8,12},{10,14},{12,8},{14,10},{16,20},{18,... | collective-permute-start | bytes 2359304 | tf_op jit(solution)/shard_map/ppermute | solution.py:782
  328.9 168.6 %reduce-scatter.4.cloned.1.call-start = ((), (), s32[]{:S(2)}) async-start(), calls=%async_computation.3 | async-start | bytes 2949120 | tf_op jit(solution)/shard_map/reduce_scatter | solution.py:998
  349.6 20.5 %collective-permute-start.17 = (f32[2,128,384]{2,1,0:T(8,128)S(1)}, f32[2,128,384]{2,1,0:T(8,128)S(1)}, u32[]{:S(2)}, u32[]{:S(2)}) collective-permute-start(f32[2,128,384]{2,1,0:T(8,128)S(1)} %get-tuple-element.129), channel_id=1, source_target_pairs={{0,4},{2,6},{4,0},{6,2},{8,12},{10,14},{12,8},{14,10},{16,20},{18,... | collective-permute-start | bytes 1179656 | tf_op jit(solution)/shard_map/ppermute | solution.py:782
  351.4 20.4 %collective-permute-start.18 = (f32[2,128,384]{2,1,0:T(8,128)S(1)}, f32[2,128,384]{2,1,0:T(8,128)S(1)}, u32[]{:S(2)}, u32[]{:S(2)}) collective-permute-start(f32[2,128,384]{2,1,0:T(8,128)S(1)} %get-tuple-element.127), channel_id=1, source_target_pairs={{0,6},{2,4},{4,2},{6,0},{8,14},{10,12},{12,10},{14,8},{16,22},{18,... | collective-permute-start | bytes 1179656 | tf_op jit(solution)/shard_map/ppermute | solution.py:782
  354.0 25.0 %collective-permute-start.26 = (f32[2,2,8,1536]{3,2,1,0:T(8,128)S(1)}, f32[2,2,8,1536]{3,2,1,0:T(8,128)S(1)}, u32[]{:S(2)}, u32[]{:S(2)}) collective-permute-start(f32[2,2,8,1536]{3,2,1,0:T(8,128)S(1)} %dynamic-slice_bitcast_fusion.15), channel_id=1, source_target_pairs={{0,2},{2,0},{4,6},{6,4},{8,10},{10,8},{12,14},{14,12},{16,18},{18,... | collective-permute-start | bytes 589832 | tf_op jit(solution)/shard_map/ppermute | solution.py:782
  361.4 29.6 %collective-permute-start.32 = (f32[2,96,1024]{2,1,0:T(8,128)}, f32[2,96,1024]{2,1,0:T(8,128)}, u32[]{:S(2)}, u32[]{:S(2)}) collective-permute-start(f32[2,96,1024]{2,1,0:T(8,128)} %dynamic-slice_bitcast_fusion.5), channel_id=1, source_target_pairs={{0,2},{2,0},{4,6},{6,4},{8,10},{10,8},{12,14},{14,12},{16,18},{18,... | collective-permute-start | bytes 2359304 | tf_op jit(solution)/shard_map/ppermute | solution.py:782
  370.1 22.2 %collective-permute-start.38 = (f32[2,96,1024]{2,1,0:T(8,128)}, f32[2,96,1024]{2,1,0:T(8,128)}, u32[]{:S(2)}, u32[]{:S(2)}) collective-permute-start(f32[2,96,1024]{2,1,0:T(8,128)} %dynamic-slice_bitcast_fusion.2), channel_id=1, source_target_pairs={{0,4},{2,6},{4,0},{6,2},{8,12},{10,14},{12,8},{14,10},{16,20},{18,... | collective-permute-start | bytes 2359304 | tf_op jit(solution)/shard_map/ppermute | solution.py:782
  371.9 36.1 %collective-permute-start.36 = (f32[2,96,1024]{2,1,0:T(8,128)}, f32[2,96,1024]{2,1,0:T(8,128)}, u32[]{:S(2)}, u32[]{:S(2)}) collective-permute-start(f32[2,96,1024]{2,1,0:T(8,128)} %dynamic-slice_bitcast_fusion.3), channel_id=1, source_target_pairs={{0,2},{2,0},{4,6},{6,4},{8,10},{10,8},{12,14},{14,12},{16,18},{18,... | collective-permute-start | bytes 2359304 | tf_op jit(solution)/shard_map/ppermute | solution.py:782
  379.0 30.4 %collective-permute-start.42 = (f32[2,96,1024]{2,1,0:T(8,128)}, f32[2,96,1024]{2,1,0:T(8,128)S(1)}, u32[]{:S(2)}, u32[]{:S(2)}) collective-permute-start(f32[2,96,1024]{2,1,0:T(8,128)} %dynamic-slice_bitcast_fusion), channel_id=1, source_target_pairs={{0,4},{2,6},{4,0},{6,2},{8,12},{10,14},{12,8},{14,10},{16,20},{18,... | collective-permute-start | bytes 2359304 | tf_op jit(solution)/shard_map/ppermute | solution.py:782
  379.7 45.0 %collective-permute-start.40 = (f32[2,96,1024]{2,1,0:T(8,128)}, f32[2,96,1024]{2,1,0:T(8,128)S(1)}, u32[]{:S(2)}, u32[]{:S(2)}) collective-permute-start(f32[2,96,1024]{2,1,0:T(8,128)} %dynamic-slice_bitcast_fusion.1), channel_id=1, source_target_pairs={{0,2},{2,0},{4,6},{6,4},{8,10},{10,8},{12,14},{14,12},{16,18},{18,... | collective-permute-start | bytes 2359304 | tf_op jit(solution)/shard_map/ppermute | solution.py:782
  391.1 53.0 %collective-permute-start.11 = (f32[2,128,1536]{2,1,0:T(8,128)S(1)}, f32[2,128,1536]{2,1,0:T(8,128)S(1)}, u32[]{:S(2)}, u32[]{:S(2)}) collective-permute-start(f32[2,128,1536]{2,1,0:T(8,128)S(1)} %fusion.24), channel_id=1, source_target_pairs={{0,1},{1,0},{2,3},{3,2},{4,5},{5,4},{6,7},{7,6},{8,9},{9,8},{10,11... | collective-permute-start | bytes 4718600 | tf_op jit(solution)/shard_map/ppermute | solution.py:782
  392.4 33.5 %collective-permute-start.27 = (f32[2,8,1536]{2,1,0:T(8,128)S(1)}, f32[2,8,1536]{2,1,0:T(8,128)S(1)}, u32[]{:S(2)}, u32[]{:S(2)}) collective-permute-start(f32[2,8,1536]{2,1,0:T(8,128)S(1)} %dynamic-slice_bitcast_fusion.17), channel_id=1, source_target_pairs={{0,8},{2,10},{4,12},{6,14},{8,0},{10,2},{12,4},{14,6},{16,24},{18,... | collective-permute-start | bytes 294920 | tf_op jit(solution)/shard_map/ppermute | solution.py:782
  407.9 25.5 %collective-permute-start.35 = (f32[96,1024]{1,0:T(8,128)S(1)}, f32[96,1024]{1,0:T(8,128)S(1)}, u32[]{:S(2)}, u32[]{:S(2)}) collective-permute-start(f32[96,1024]{1,0:T(8,128)S(1)} %dynamic-slice_bitcast_fusion.13), channel_id=1, source_target_pairs={{0,2},{2,0},{4,6},{6,4},{8,10},{10,8},{12,14},{14,12},{16,18},{18,... | collective-permute-start | bytes 1179656 | tf_op jit(solution)/shard_map/ppermute | solution.py:782
  409.4 24.1 %collective-permute-start.33 = (f32[96,1024]{1,0:T(8,128)S(1)}, f32[96,1024]{1,0:T(8,128)S(1)}, u32[]{:S(2)}, u32[]{:S(2)}) collective-permute-start(f32[96,1024]{1,0:T(8,128)S(1)} %dynamic-slice_bitcast_fusion.14), channel_id=1, source_target_pairs={{0,4},{2,6},{4,0},{6,2},{8,12},{10,14},{12,8},{14,10},{16,20},{18,... | collective-permute-start | bytes 1179656 | tf_op jit(solution)/shard_map/ppermute | solution.py:782
  424.7 16.9 %collective-permute-start.39 = (f32[96,1024]{1,0:T(8,128)S(1)}, f32[96,1024]{1,0:T(8,128)S(1)}, u32[]{:S(2)}, u32[]{:S(2)}) collective-permute-start(f32[96,1024]{1,0:T(8,128)S(1)} %dynamic-slice_bitcast_fusion.11), channel_id=1, source_target_pairs={{0,2},{2,0},{4,6},{6,4},{8,10},{10,8},{12,14},{14,12},{16,18},{18,... | collective-permute-start | bytes 1179656 | tf_op jit(solution)/shard_map/ppermute | solution.py:782
  433.4 20.0 %collective-permute-start.43 = (f32[96,1024]{1,0:T(8,128)}, f32[96,1024]{1,0:T(8,128)}, u32[]{:S(2)}, u32[]{:S(2)}) collective-permute-start(f32[96,1024]{1,0:T(8,128)} %dynamic-slice_bitcast_fusion.9), channel_id=1, source_target_pairs={{0,2},{2,0},{4,6},{6,4},{8,10},{10,8},{12,14},{14,12},{16,18},{18,... | collective-permute-start | bytes 1179656 | tf_op jit(solution)/shard_map/ppermute | solution.py:782
  433.5 20.9 %collective-permute-start.41 = (f32[96,1024]{1,0:T(8,128)}, f32[96,1024]{1,0:T(8,128)}, u32[]{:S(2)}, u32[]{:S(2)}) collective-permute-start(f32[96,1024]{1,0:T(8,128)} %dynamic-slice_bitcast_fusion.10), channel_id=1, source_target_pairs={{0,4},{2,6},{4,0},{6,2},{8,12},{10,14},{12,8},{14,10},{16,20},{18,... | collective-permute-start | bytes 1179656 | tf_op jit(solution)/shard_map/ppermute | solution.py:782
  (147 other events, 1264.3 us)
Sparse Core Ops, SparseCore 0:
  267.1 46.4 reduce-scatter.5
  328.9 47.3 reduce-scatter.7
  379.1 48.3 reduce-scatter.3

commit v4 on v3

--- a/solution.py
+++ b/solution.py
@@ -48,71 +48,8 @@
     return lax.dot_general(left, right, (((1,), (1,)), ((), ())), preferred_element_type=jnp.float32)
 
 
-def ffn_kernel(stride, more, *refs):
-    hid_own, hid_more = refs[0], refs[1 : 1 + more]
-    grad_own, grad_more = refs[1 + more], refs[2 + more : 2 + 2 * more]
-    wg, wu, wd, dg_own, du_own, act_own = refs[2 + 2 * more : 8 + 2 * more]
-    out_gate, out_up, out_down = refs[8 + 2 * more : 11 + 2 * more]
-    hid, grad, hid_cut, grad_cut, dg, du, act = refs[11 + 2 * more :]
-    own = hid_own.shape[0]
-    cut = hid_cut.shape[0]
-
-    @pl.when(pl.program_id(0) == 0)
-    def _():
-        stack_tokens(hid, hid_own, hid_more)
-        stack_tokens(grad, grad_own, grad_more)
-        at = pl.ds(pl.multiple_of((lax.axis_index("seq") // stride) * cut, 128), cut)
-        hid_cut[...] = hid[:, at].T
-        grad_cut[...] = grad[:, at].T
-
-    dg[:own, :] = dg_own[...]
-    du[:own, :] = du_own[...]
-    act[:own, :] = act_own[...]
-
-    def turn(i, _):
-        rows = pl.ds(pl.multiple_of(i * own, own), own)
-        gate = dot(hid[rows, :], wg[...])
-        up = dot(hid[rows, :], wu[...])
-        d_act = dot_back(grad[rows, :], wd[...])
-        sig = 1.0 / (1.0 + jnp.exp(-gate))
-        silu = gate * sig
-        dg[rows, :] = (d_act * up * (sig + silu * (1.0 - sig))).astype(dg.dtype)
-        du[rows, :] = (d_act * silu).astype(du.dtype)
-        act[rows, :] = (silu * up).astype(act.dtype)
-        return 0
-
-    lax.fori_loop(1, hid.shape[0] // own, turn, 0)
-    out_gate[...] = dot(hid_cut[...], dg[...])
-    out_up[...] = dot(hid_cut[...], du[...])
-    out_down[...] = dot(grad_cut[...], act[...])
-
-
 def whole(shape):
     return pl.BlockSpec(shape, lambda i: (0,) * len(shape), pipeline_mode=pl.Buffered(1))
-
-
-def ffn_grads(stride, hid_own, hid_more, grad_own, grad_more, w_gate, w_up, w_down, d_gate, d_up, act):
-    own, width = hid_own.shape
-    units = w_gate.shape[1]
-    cut = width // SIDE
-    block = next(b for b in (256, 128) if units % b == 0)
-    tokens = own + sum(math.prod(part.shape[:-1]) for part in hid_more)
-    low = jnp.bfloat16
-    column = lambda rows: pl.BlockSpec((rows, block), lambda i: (0, i))
-    return pl.pallas_call(
-        functools.partial(ffn_kernel, stride, len(hid_more)),
-        grid=(units // block,),
-        in_specs=[whole(a.shape) for a in (hid_own, *hid_more, grad_own, *grad_more)]
-        + [column(width), column(width), pl.BlockSpec((block, width), lambda i: (i, 0))]
-        + [column(own)] * 3,
-        out_specs=[column(cut)] * 3,
-        out_shape=[jax.ShapeDtypeStruct((cut, units), jnp.float32)] * 3,
-        scratch_shapes=[pltpu.VMEM((tokens, width), low)] * 2
-        + [pltpu.VMEM((cut, tokens), low)] * 2
-        + [pltpu.VMEM((tokens, block), low)] * 3,
-        compiler_params=params(56),
-        cost_estimate=spans(24),
-    )(hid_own, *hid_more, grad_own, *grad_more, w_gate, w_up, w_down, d_gate, d_up, act)
 
 
 def mixer_kernel(more_norm, more_mix, *refs):
@@ -121,16 +58,26 @@
     (norm_own,), norm_more = take(1), take(more_norm)
     (mix_own,), mix_more = take(1), take(more_mix)
     y_own, y_side = take(2)
-    wo, wm = take(2)
-    out_gate, out_mix, norm_turned = take(3)
-    norm, mix, mixed, d_out = take(4)
+    w_out, w_mix = take(2)
+    out, norm_turned = take(2)
+    norm, mix, mixed, d_out, wo, wm, local = take(7)
     own = norm_own.shape[0]
     half = own // 2
 
     @pl.when(pl.program_id(0) == 0)
     def _():
+        size = wo.shape[1]
+        at = pl.ds(pl.multiple_of(lax.rem(lax.axis_index("seq"), SIDE) * size, 128), size)
+        loads = [
+            pltpu.make_async_copy(w_out.at[:, at], wo, local.at[0]),
+            pltpu.make_async_copy(w_mix.at[at], wm, local.at[1]),
+        ]
+        for c in loads:
+            c.start()
         stack_tokens(norm, norm_own, norm_more)
         stack_tokens(mix, mix_own, mix_more)
+        for c in loads:
+            c.wait()
 
         def finish(rows, y):
             outgate = dot(norm[rows, :], wo[...])
@@ -152,13 +99,13 @@
     span = pl.ds(pl.multiple_of(pl.program_id(0) * rows, rows), rows)
     turned = norm[:, span].T
     norm_turned[...] = turned
-    out_gate[...] = dot(turned, d_out[...])
-    out_mix[...] = dot(mix[:, span].T, mixed[...])
+    out[0] = dot(turned, d_out[...])
+    out[1] = dot(mix[:, span].T, mixed[...])
 
 
 def mixer_grads(norm_own, norm_more, mix_own, mix_more, y_own, y_side, w_out, w_mix):
     own, width = norm_own.shape
-    cut = w_out.shape[1]
+    cut = w_out.shape[1] // SIDE
     block = next(b for b in (256, 128) if width % b == 0)
     tokens = own + sum(math.prod(part.shape[:-1]) for part in norm_more)
     low = jnp.bfloat16
@@ -167,49 +114,18 @@
     return pl.pallas_call(
         functools.partial(mixer_kernel, len(norm_more), len(mix_more)),
         grid=(width // block,),
-        in_specs=[whole(a.shape) for a in operands],
-        out_specs=[row(cut), row(cut), row(tokens)],
+        in_specs=[whole(a.shape) for a in operands[:-2]] + [pl.BlockSpec(memory_space=pl.ANY)] * 2,
+        out_specs=[pl.BlockSpec((2, block, cut), lambda i: (0, i, 0)), row(tokens)],
         out_shape=[
-            jax.ShapeDtypeStruct((width, cut), jnp.float32),
-            jax.ShapeDtypeStruct((width, cut), jnp.float32),
+            jax.ShapeDtypeStruct((2, width, cut), jnp.float32),
             jax.ShapeDtypeStruct((width, tokens), low),
         ],
-        scratch_shapes=[pltpu.VMEM((tokens, width), low)] * 2 + [pltpu.VMEM((tokens, cut), low)] * 2,
+        scratch_shapes=[pltpu.VMEM((tokens, width), low)] * 2
+        + [pltpu.VMEM((tokens, cut), low)] * 2
+        + [pltpu.VMEM((width, cut), low), pltpu.VMEM((cut, width), low), pltpu.SemaphoreType.DMA((2,))],
         compiler_params=params(56),
         cost_estimate=spans(12),
     )(*operands)
-
-
-def inner_kernel(sides, *refs):
-    turned, d_own, d_side, out, d_all = refs[0], refs[1], refs[2 : 2 + sides], refs[2 + sides], refs[3 + sides]
-    own = d_own.shape[0]
-    half = own // 2
-
-    @pl.when(pl.program_id(0) == 0)
-    def _():
-        d_all[:own, :] = d_own[...]
-        for k in range(sides):
-            for s in range(2):
-                start = own + (s * sides + k) * half
-                d_all[start : start + half, :] = d_side[k][s].astype(d_all.dtype)
-
-    out[...] = dot(turned[...], d_all[...])
-
-
-def inner_grad(turned, d_own, d_side):
-    width, tokens = turned.shape
-    cut = d_own.shape[1]
-    block = next(b for b in (512, 256, 128) if width % b == 0)
-    return pl.pallas_call(
-        functools.partial(inner_kernel, len(d_side)),
-        grid=(width // block,),
-        in_specs=[pl.BlockSpec((block, tokens), lambda i: (i, 0))] + [whole(a.shape) for a in (d_own, *d_side)],
-        out_specs=pl.BlockSpec((block, cut), lambda i: (i, 0)),
-        out_shape=jax.ShapeDtypeStruct((width, cut), jnp.float32),
-        scratch_shapes=[pltpu.VMEM((tokens, cut), jnp.bfloat16)],
-        compiler_params=params(56),
-        cost_estimate=spans(4),
-    )(turned, d_own, *d_side)
 
 
 SIDE = 4
@@ -249,13 +165,14 @@
 
 
 class Line:
-    def __init__(self, where, mine, ring, rest, sends, recvs):
-        self.where, self.mine, self.ring, self.rest, self.sends, self.recvs = where, mine, ring, rest, sends, recvs
+    def __init__(self, where, up_one, down_one, ring, rest, sends, recvs):
+        self.where, self.up_one, self.down_one = where, up_one, down_one
+        self.ring, self.rest, self.sends, self.recvs = ring, rest, sends, recvs
 
     def copies(self, step):
         w = self.where
-        up = self.mine if step == 1 else self.ring.at[SIDE - step]
-        down = self.mine if step == 1 else self.ring.at[step - 2]
+        up = self.up_one if step == 2 else self.ring.at[SIDE - step]
+        down = self.down_one if step == 2 else self.ring.at[step - 2]
         return (
             remote(up, self.ring.at[SIDE - 1 - step], self.sends, self.recvs, step - 1, w.above),
             remote(down, self.ring.at[step - 1], self.sends, self.recvs, SIDE - 2 + step, w.below),
@@ -284,9 +201,20 @@
             down.wait_recv()
             self.core(step - 1).start()
 
-    def finish(self, first=1):
+    def cores_of_one(self):
+        return (
+            remote(self.up_one, self.rest.at[SIDE - 2], self.sends, self.recvs, 2 * SIDE - 2 + SIDE - 2, self.where.core),
+            remote(self.down_one, self.rest.at[0], self.sends, self.recvs, 2 * SIDE - 2, self.where.core),
+        )
+
+    def start_cores_of_one(self):
+        up, down = self.cores_of_one()
+        pl.when(self.where.z >= 1)(up.start)
+        pl.when(self.where.z <= SIDE - 2)(down.start)
+
+    def finish(self):
         z = self.where.z
-        for step in range(first, SIDE):
+        for step in range(2, SIDE):
             up, down = self.copies(step)
             pl.when((z >= step - 1) & (z < SIDE - 1))(up.wait_send)
             pl.when((z <= SIDE - step) & (z > 0))(down.wait_send)
@@ -378,9 +306,9 @@
     lines = [remote(mine, line.at[k], sends, recvs, SIDE + k, where.other[k]) for k in range(1, groups)]
     for c in lines:
         c.start()
-    after_line()
     for c in lines:
         c.wait_recv()
+    after_line()
     entering = jnp.zeros((rows, width), jnp.float32)
     for k in range(1, groups) if reverse else range(groups - 1, 0, -1):
         counts = (k > group) if reverse else (k <= group)
@@ -436,9 +364,9 @@
 
 
 def forward_kernel(
-    count, fall, gain, b_ref, c_ref, rate_ref, grad_up, grad_down, norm_near, norm_next,
+    count, fall, gain, b_ref, c_ref, rate_ref, up_one, down_one, norm_near, norm_next,
     y_ref, first, ring, ring_rest, side_far, side_rest,
-    ends, total, line_send, line_recv, side_send, side_recv, local, *scratch,
+    ends, total, line_send, line_recv, side_send, side_recv, *scratch,
 ):
     where = Place(count)
     streams, length, channels = fall.shape
@@ -446,11 +374,7 @@
     lanes, blocks = blocks_of(channels)
     z = where.z
     where.greet()
-    line = Line(where, None, ring, ring_rest, line_send, line_recv)
-    lift = pltpu.make_async_copy(grad_up, ring.at[SIDE - 2], local.at[0])
-    sink = pltpu.make_async_copy(grad_down, ring.at[0], local.at[1])
-    pl.when(z >= 1)(lift.start)
-    pl.when(z <= SIDE - 2)(sink.start)
+    line = Line(where, up_one, down_one, ring, ring_rest, line_send, line_recv)
 
     def summary(i, _):
         cols = columns(i, lanes)
@@ -491,16 +415,7 @@
     ]
 
     def after_line():
-        @pl.when(z >= 1)
-        def _():
-            lift.wait()
-            line.core(SIDE - 2).start()
-
-        @pl.when(z <= SIDE - 2)
-        def _():
-            sink.wait()
-            line.core(0).start()
-
+        line.start_cores_of_one()
         line.start(2)
 
     def after_all():
@@ -547,11 +462,11 @@
         c.wait_send()
     for c in cores:
         c.wait()
-    line.finish(2)
+    line.finish()
 
 
 def backward_kernel(
-    count, fall, d_ref, v_ref, g_ref, b_ref, c_ref, rate_ref, first_ref, hidden, mix, y_ref,
+    count, fall, d_ref, v_ref, g_ref, b_ref, c_ref, rate_ref, first_ref, up_one, down_one, mix, y_ref,
     dstep_ref, dvalue_ref, db_ref, dc_ref, decay_ref, ring, ring_rest, side, side_rest, y_side,
     ends, total, last, path, fades, line_send, line_recv, side_send, side_recv, y_send, y_recv, *scratch,
 ):
@@ -562,7 +477,7 @@
     chunks = length // ROWS
     width = channels // SIDE
     where.greet()
-    line = Line(where, hidden, ring, ring_rest, line_send, line_recv)
+    line = Line(where, up_one, down_one, ring, ring_rest, line_send, line_recv)
     square = Side(where, mix, side, side_rest, side_send, side_recv)
     quarters = [
         remote(
@@ -600,10 +515,13 @@
     sums(fall, total)
 
     def after_line():
-        line.start(1)
+        line.start_cores_of_one()
+        line.start(2)
 
     def after_all():
         square.start()
+        for c in quarters:
+            c.start()
 
     chain(where, True, ends, total, rate_ref, last, scratch, after_line, after_all)
     db_ref[...] = jnp.zeros_like(db_ref)
@@ -619,21 +537,14 @@
         cols = columns(i, lanes)
         rate = rate_ref[:, cols]
 
-        @pl.when(i == blocks // 6)
+        @pl.when(i == blocks // 3)
         def _():
-            line.arrive(1)
-            line.start(2)
+            line.arrive(2)
+            line.start(3)
 
         @pl.when(i == blocks // 2)
         def _():
             square.turn()
-            for c in quarters:
-                c.start()
-
-        @pl.when(i == blocks - blocks // 6)
-        def _():
-            line.arrive(2)
-            line.start(3)
 
         def ahead(i, states):
             base = pl.multiple_of(i * ROWS, ROWS)
@@ -712,11 +623,11 @@
     return [pltpu.SemaphoreType.DMA((count,))] * 2
 
 
-def scan_forward(fall, gain, b_wide, c_wide, rate, grad_up, grad_down, norm_near, norm_next):
+def scan_forward(fall, gain, b_wide, c_wide, rate, line, norm_near, norm_next):
     streams, length, channels = fall.shape
     n = rate.shape[0]
     count = lax.axis_size("seq")
-    half, width = grad_up.shape
+    half, width = norm_near.shape
     three = shaped(SIDE - 1, half, width)
     return pl.pallas_call(
         functools.partial(forward_kernel, count),
@@ -724,20 +635,20 @@
         in_specs=[in_vmem()] * 5 + [in_hbm()] * 4,
         out_specs=[in_vmem()] * 2 + [in_hbm()] * 4,
         scratch_shapes=[pltpu.VMEM((streams, n, channels), jnp.float32), pltpu.VMEM((streams, channels), jnp.float32)]
-        + sems(LINE_SEMS) + sems(5) + [pltpu.SemaphoreType.DMA((2,))]
+        + sems(LINE_SEMS) + sems(5)
         + chain_scratch(streams, n, channels, count // SIDE),
         compiler_params=pltpu.CompilerParams(
             collective_id=0, has_side_effects=True, vmem_limit_bytes=40 * 1024 * 1024
         ),
         cost_estimate=spans(40),
-    )(fall, gain, b_wide, c_wide, rate, grad_up, grad_down, norm_near, norm_next)
-
-
-def scan_backward(fall, step, value, d_y, b_wide, c_wide, rate, first, hidden, mix, y):
+    )(fall, gain, b_wide, c_wide, rate, *line, norm_near, norm_next)
+
+
+def scan_backward(fall, step, value, d_y, b_wide, c_wide, rate, first, line, mix, y):
     streams, length, channels = fall.shape
     n = rate.shape[0]
     count = lax.axis_size("seq")
-    half, width = hidden.shape
+    half, width = mix.shape
     lanes, _ = blocks_of(channels)
     three = shaped(SIDE - 1, half, width)
     tall = shaped(streams, length * n, 128)
@@ -747,7 +658,7 @@
         functools.partial(backward_kernel, count),
         out_shape=[flat, flat, tall, tall, shaped(n, channels), three, three, three, three,
                    shaped(SIDE - 1, streams, length, channels // SIDE)],
-        in_specs=[in_vmem()] * 8 + [in_hbm()] * 3,
+        in_specs=[in_vmem()] * 8 + [in_hbm()] * 4,
         out_specs=[in_vmem()] * 5 + [in_hbm()] * 5,
         scratch_shapes=[
             pltpu.VMEM((streams, n, channels), jnp.float32),
@@ -762,7 +673,439 @@
             collective_id=1, has_side_effects=True, vmem_limit_bytes=52 * 1024 * 1024
         ),
         cost_estimate=spans(62),
-    )(fall, step, value, d_y, b_wide, c_wide, rate, first, hidden, mix, y)
+    )(fall, step, value, d_y, b_wide, c_wide, rate, first, *line, mix, y)
+
+
+CHUNKS = 4
+
+
+def place_step_one(target, own, z, up, down):
+    rows = up.shape[0]
+
+    @pl.when(z >= 1)
+    def _():
+        target[own + (SIDE - 2) * rows : own + (SIDE - 1) * rows, :] = up[...].astype(target.dtype)
+
+    @pl.when(z <= SIDE - 2)
+    def _():
+        target[own : own + rows, :] = down[...].astype(target.dtype)
+
+
+def ffn_kernel(
+    count, hid_own, hid_ring, hid_rest, hid_up, hid_down, grad_own, grad_ring, grad_rest, grad_up, grad_down, wg, wu, wd, dg_own, du_own, act_own,
+    got, inner, mixer,
+    out, passed, d_side, near,
+    hid, grad, hid_cut, grad_cut, dg, du, act, sent, stash, sends, recvs, local,
+):
+    own, cut = hid_own.shape[0], hid_cut.shape[0]
+    where = Place(count)
+    z, place = where.z, where.place
+    width = d_side.shape[-1]
+    first = pl.program_id(0) == 0
+    last = pl.program_id(0) == pl.num_programs(0) - 1
+    quarters = [
+        remote(
+            inner.at[:, :, pl.ds(pl.multiple_of((place ^ k) * width, 128), width)],
+            d_side.at[k - 1], sends, recvs, k - 1, where.member[k],
+        )
+        for k in range(1, SIDE)
+    ]
+    rising = z < SIDE // 2
+    step = remote(
+        sent, passed.at[jnp.where(rising, 0, 1)], sends, recvs, jnp.where(rising, SIDE - 1, SIDE),
+        (jnp.where(rising, where.above[0], where.below[0]), where.head),
+    )
+    from_below = remote(sent, passed.at[0], sends, recvs, SIDE - 1, where.above)
+    from_above = remote(sent, passed.at[1], sends, recvs, SIDE, where.below)
+    middle = (z > 0) & (z < SIDE - 1)
+    odd, far = lax.rem(place, 2), place // 2
+    early = [
+        remote(stash.at[0, :, :, :, 1 - odd], near.at[0], sends, recvs, SIDE + 1, where.member[1]),
+        remote(stash.at[1, :, :, 1 - far], near.at[1], sends, recvs, SIDE + 2, where.member[2]),
+    ]
+    turns = pl.num_programs(0) // CHUNKS
+
+    @pl.when(first)
+    def _():
+        where.greet()
+        for c in quarters:
+            c.start()
+        fetch = pltpu.make_async_copy(mixer.at[:, lax.rem(z + 2, SIDE)], sent, local.at[0])
+        fetch.start()
+        stack_tokens(hid, hid_own, [hid_ring, hid_rest])
+        place_step_one(hid, own, z, hid_up, hid_down)
+        fetch.wait()
+
+        @pl.when(middle)
+        def _():
+            sent[...] += got[...]
+
+        step.start()
+        stack_tokens(grad, grad_own, [grad_ring, grad_rest])
+        place_step_one(grad, own, z, grad_up, grad_down)
+        at = pl.ds(pl.multiple_of(z * cut, 128), cut)
+        hid_cut[...] = hid[:, at].T
+        grad_cut[...] = grad[:, at].T
+
+    dg[:own, :] = dg_own[...]
+    du[:own, :] = du_own[...]
+    act[:own, :] = act_own[...]
+
+    def turn(i, _):
+        rows = pl.ds(pl.multiple_of(i * own, own), own)
+        gate = dot(hid[rows, :], wg[...])
+        up = dot(hid[rows, :], wu[...])
+        d_act = dot_back(grad[rows, :], wd[...])
+        sig = 1.0 / (1.0 + jnp.exp(-gate))
+        silu = gate * sig
+        dg[rows, :] = (d_act * up * (sig + silu * (1.0 - sig))).astype(dg.dtype)
+        du[rows, :] = (d_act * silu).astype(du.dtype)
+        act[rows, :] = (silu * up).astype(act.dtype)
+        return 0
+
+    lax.fori_loop(1, hid.shape[0] // own, turn, 0)
+    out[0] = dot(hid_cut[...], dg[...])
+    out[1] = dot(hid_cut[...], du[...])
+    out[2] = dot(grad_cut[...], act[...])
+
+    @pl.when(pl.program_id(0) < 2 * turns)
+    def _():
+        block = out.shape[2]
+        at = pl.ds(pl.multiple_of(lax.rem(pl.program_id(0), turns) * block, block), block)
+        for m in range(3):
+            stash[pl.program_id(0) // turns, m, :, :, :, :, at] = out[m].reshape(stash.shape[2:6] + (block,))
+
+    for c in range(2):
+        pl.when(pl.program_id(0) == (c + 1) * turns - 1)(early[c].start)
+
+    @pl.when(last)
+    def _():
+        for c in quarters + early:
+            c.wait()
+        step.wait_send()
+
+        @pl.when(middle)
+        def _():
+            from_below.wait_recv()
+            from_above.wait_recv()
+
+
+def ffn_grads(hid_own, hid_ring, hid_rest, hid_one, grad_own, grad_ring, grad_rest, grad_one, w_gate, w_up, w_down, d_gate, d_up, act, got, inner, mixer):
+    own, width = hid_own.shape
+    units = w_gate.shape[1]
+    count = lax.axis_size("seq")
+    cut = width // SIDE
+    streams, length, channels = inner.shape
+    block = next(b for b in (256, 128) if units % (b * CHUNKS) == 0)
+    more = count // SIDE // SIDE
+    rows = cut // (more * SIDE)
+    tokens = own * SIDE
+    low = jnp.bfloat16
+    column = lambda rows: pl.BlockSpec((rows, block), lambda i: (0, i))
+    tokens_in = (hid_own, hid_ring, hid_rest, *hid_one, grad_own, grad_ring, grad_rest, *grad_one)
+    return pl.pallas_call(
+        functools.partial(ffn_kernel, count),
+        grid=(units // block,),
+        in_specs=[whole(a.shape) for a in tokens_in]
+        + [column(width), column(width), pl.BlockSpec((block, width), lambda i: (i, 0))]
+        + [column(own)] * 3
+        + [whole(got.shape), in_hbm(), in_hbm()],
+        out_specs=[pl.BlockSpec((3, cut, block), lambda i: (0, 0, i))] + [in_hbm()] * 3,
+        out_shape=[
+            shaped(3, cut, units), shaped(2, *got.shape), shaped(SIDE - 1, streams, length, channels // SIDE),
+            shaped(2, 3, more, 2, rows, units // CHUNKS),
+        ],
+        scratch_shapes=[pltpu.VMEM((tokens, width), low)] * 2
+        + [pltpu.VMEM((cut, tokens), low)] * 2
+        + [pltpu.VMEM((tokens, block), low)] * 3
+        + [pltpu.VMEM(got.shape, jnp.float32), pltpu.VMEM((2, 3, more, 2, 2, rows, units // CHUNKS), jnp.float32)]
+        + sems(SIDE + 3) + [pltpu.SemaphoreType.DMA((1,))],
+        compiler_params=pltpu.CompilerParams(
+            collective_id=2, has_side_effects=True, vmem_limit_bytes=56 * 1024 * 1024
+        ),
+        cost_estimate=spans(36),
+    )(*tokens_in, w_gate, w_up, w_down, d_gate, d_up, act, got, inner, mixer)
+
+
+class Reduce:
+    def __init__(self, where, blocks, got, passed, arrived, sends, recvs):
+        self.where, self.blocks, self.got, self.passed, self.arrived = where, blocks, got, passed, arrived
+        self.sends, self.recvs = sends, recvs
+
+    def out(self, source, target, at, rising):
+        w = self.where
+        return remote(source, target, self.sends, self.recvs, at, (jnp.where(rising, w.above[0], w.below[0]), w.head))
+
+    def one(self):
+        return self.out(self.blocks.at[:, SIDE - 1 - self.where.z], self.got, 0, self.where.z == 0)
+
+    def start_one(self):
+        pl.when((self.where.z == 0) | (self.where.z == SIDE - 1))(self.one().start)
+
+    def middle(self):
+        return (self.where.z > 0) & (self.where.z < SIDE - 1)
+
+    def two(self, source):
+        rising = self.where.z < SIDE // 2
+        return self.out(source, self.passed.at[jnp.where(rising, 0, 1)], jnp.where(rising, 1, 2), rising)
+
+    def start_two(self):
+        z = self.where.z
+
+        @pl.when(self.middle())
+        def _():
+            self.one().wait_recv()
+            self.got[...] += self.blocks[:, lax.rem(z + 2, SIDE)]
+            self.two(self.got).start()
+
+        @pl.when(jnp.logical_not(self.middle()))
+        def _():
+            self.two(self.blocks.at[:, lax.rem(z + 2, SIDE)]).start()
+
+    def three(self, source, way):
+        return self.out(source, self.arrived.at[way], 3 + way, way == 0)
+
+    def start_three(self, wait):
+        z = self.where.z
+
+        @pl.when(self.middle())
+        def _():
+            for way in (0, 1):
+                if wait:
+                    self.two_from(way).wait_recv()
+                self.passed[way] += self.blocks[:, z + 1 - 2 * way]
+                self.three(self.passed.at[way], way).start()
+
+        pl.when(z == 0)(self.three(self.blocks.at[:, 1], 0).start)
+        pl.when(z == SIDE - 1)(self.three(self.blocks.at[:, SIDE - 2], 1).start)
+
+    def two_from(self, way):
+        return self.out(self.passed.at[way], self.passed.at[way], 1 + way, way == 0)
+
+    def result(self, done):
+        z = self.where.z
+        done[...] = self.blocks[:, z].reshape(done.shape)
+        for way in (0, 1):
+
+            @pl.when((z >= 1) if way == 0 else (z <= SIDE - 2))
+            def _():
+                self.three(self.passed.at[way], way).wait_recv()
+                done[...] += self.arrived[way].reshape(done.shape)
+
+    def finish(self, first):
+        z = self.where.z
+        if first <= 1:
+            pl.when((z == 0) | (z == SIDE - 1))(self.one().wait_send)
+        if first <= 2:
+            self.two(self.got).wait_send()
+        pl.when(z <= SIDE - 2)(self.three(self.passed.at[0], 0).wait_send)
+        pl.when(z >= 1)(self.three(self.passed.at[1], 1).wait_send)
+
+
+REDUCE_SEMS = 5
+
+
+def sum_kernel(
+    count, ffn, mixer_in, passed_in, near_in, turned, d_own, d_side, small,
+    ffn_out, mixer_out, inner_out, small_out,
+    d_all, kept, near, next_, mixer, m_passed, m_arrived, inner, i_got, i_passed, i_arrived, m_done, m_back, i_done, i_back, s_near, s_next, s_done, s_line,
+    ffn_send, ffn_recv, m_send, m_recv, i_send, i_recv, back_send, back_recv, s_send, s_recv, local,
+):
+    where = Place(count)
+    place = where.place
+    more = where.stride // SIDE
+    span = near.shape[5]
+    odd, far = lax.rem(place, 2), place // 2
+    cols = [pl.ds(c * span, span) for c in range(CHUNKS)]
+    loads = [pltpu.make_async_copy(mixer_in, mixer, local.at[0]), pltpu.make_async_copy(passed_in, m_passed, local.at[1])]
+    keeps = [
+        pltpu.make_async_copy(
+            ffn.at[:, :, :, odd, :, cols[c]] if c % 2 == 0 else ffn.at[:, :, far, :, :, cols[c]], kept.at[c], local.at[2 + c]
+        )
+        for c in range(CHUNKS)
+    ]
+    nears = [pltpu.make_async_copy(near_in.at[c], near.at[c], local.at[2 + CHUNKS + c]) for c in range(2)]
+    for c in loads + nears + keeps:
+        c.start()
+    where.greet()
+    first = {
+        c: remote(
+            ffn.at[:, :, :, 1 - odd, :, cols[c]] if c % 2 == 0 else ffn.at[:, :, 1 - far, :, :, cols[c]],
+            near.at[c], ffn_send, ffn_recv, c, where.member[1 + c % 2],
+        )
+        for c in range(2, CHUNKS)
+    }
+    for c in first.values():
+        c.start()
+    groups, half = where.groups, s_near.shape[3]
+    s_rows = [pl.ds(0, half), pl.ds(half, half)]
+    s_first = [
+        remote(small.at[:, :, 1 - odd, s_rows[0]], s_near.at[0], s_send, s_recv, 0, where.member[1]),
+        remote(small.at[:, 1 - far, :, s_rows[1]], s_near.at[1], s_send, s_recv, 1, where.member[2]),
+    ]
+    for c in s_first:
+        c.start()
+    second = {}
+
+    def again(c):
+        kept[c] += near[c]
+        bit = far if c % 2 == 0 else odd
+        second[c] = remote(
+            kept.at[c, :, :, 1 - bit], next_.at[c], ffn_send, ffn_recv, CHUNKS + c, where.member[2 - c % 2]
+        )
+        second[c].start()
+
+    line = Reduce(where, mixer, None, m_passed, m_arrived, m_send, m_recv)
+    for c in loads:
+        c.wait()
+    line.start_three(False)
+    for c in range(2):
+        nears[c].wait()
+        keeps[c].wait()
+        again(c)
+    own = d_own.shape[0]
+    part = own // 2
+    d_all[:own, :] = d_own[...]
+    for k in range(SIDE - 1):
+        for s in range(2):
+            start = own + (s * (SIDE - 1) + k) * part
+            d_all[start : start + part, :] = d_side[k, where.head if s == 0 else 1 - where.head].astype(d_all.dtype)
+    for k in range(SIDE):
+        at = slice(k * inner.shape[2], (k + 1) * inner.shape[2])
+        inner[0, k] = dot(turned[at, :], d_all[...])
+    other = Reduce(where, inner, i_got, i_passed, i_arrived, i_send, i_recv)
+    other.start_one()
+    other.start_two()
+    for c in s_first:
+        c.wait_recv()
+    s_near[0] += small[:, :, odd, s_rows[0]]
+    s_near[1] += small[:, far, :, s_rows[1]]
+    s_second = [
+        remote(s_near.at[0, :, 1 - far], s_next.at[0], s_send, s_recv, 2, where.member[2]),
+        remote(s_near.at[1, :, 1 - odd], s_next.at[1], s_send, s_recv, 3, where.member[1]),
+    ]
+    for c in s_second:
+        c.start()
+    for c in range(2, CHUNKS):
+        keeps[c].wait()
+        first[c].wait_recv()
+        again(c)
+    for c in s_second:
+        c.wait_recv()
+    s_done[:, :half] = s_near[0, :, far] + s_next[0]
+    s_done[:, half:] = s_near[1, :, odd] + s_next[1]
+    s_last = [
+        remote(s_done.at[lax.rem(where.group + k, groups)], s_line.at[k], s_send, s_recv, 3 + k, where.other[k])
+        for k in range(1, groups)
+    ]
+    for c in s_last:
+        c.start()
+    other.start_three(True)
+
+    def spread(reduced, done, back, at):
+        reduced.result(done)
+        copies = [
+            remote(done.at[:, :, place ^ k], back.at[k], back_send, back_recv, at + k, where.member[k])
+            for k in range(1, SIDE)
+        ]
+        for c in copies:
+            c.start()
+        back[0] = done[:, :, place]
+        return copies
+
+    spreads = spread(line, m_done, m_back, 0)
+    for c in range(CHUNKS):
+        second[c].wait_recv()
+        bit = far if c % 2 == 0 else odd
+        ffn_out[:, :, :, c * span : (c + 1) * span] = kept[c, :, :, bit] + next_[c]
+    spreads += spread(other, i_done, i_back, SIDE)
+    for c in spreads:
+        c.wait_recv()
+    width = inner.shape[3]
+    for q in range(SIDE):
+        cols = slice(q * width, (q + 1) * width)
+        mixer_out[:, :, :, cols] = m_back[place ^ q]
+        inner_out[:, :, :, cols] = i_back[place ^ q]
+    total = s_done[where.group]
+    for k in range(1, groups):
+        s_last[k - 1].wait_recv()
+        total = total + s_line[k]
+    small_out[...] = total
+    for c in list(first.values()) + list(second.values()) + spreads + s_first + s_second + s_last:
+        c.wait_send()
+    line.finish(3)
+    other.finish(1)
+
+
+def sum_grads(ffn, mixer, passed, near, turned, d_own, d_side, small):
+    count = lax.axis_size("seq")
+    more = count // SIDE // SIDE
+    cut, units = ffn.shape[1:]
+    rows = cut // (more * SIDE)
+    size = mixer.shape[-1]
+    f32 = jnp.float32
+    v = lambda *shape: pltpu.VMEM(shape, f32)
+    groups, tall = count // SIDE, small.shape[1]
+    return pl.pallas_call(
+        functools.partial(sum_kernel, count),
+        out_shape=[shaped(3, more, rows, units), shaped(2, more, rows, size * SIDE), shaped(1, more, rows, size * SIDE),
+                   shaped(tall, LANES)],
+        in_specs=[in_hbm()] * 4 + [in_vmem()] * 4,
+        out_specs=[in_vmem()] * 4,
+        scratch_shapes=[
+            pltpu.VMEM((turned.shape[1], size), jnp.bfloat16),
+            v(CHUNKS, 3, more, 2, rows, units // CHUNKS),
+            v(CHUNKS, 3, more, 2, rows, units // CHUNKS),
+            v(CHUNKS, 3, more, rows, units // CHUNKS),
+            v(2, SIDE, cut, size), v(2, 2, cut, size), v(2, 2, cut, size),
+            v(1, SIDE, cut, size), v(1, cut, size), v(2, 1, cut, size), v(2, 1, cut, size),
+            v(2, more, SIDE, rows, size), v(SIDE, 2, more, rows, size),
+            v(1, more, SIDE, rows, size), v(SIDE, 1, more, rows, size),
+            v(2, groups, 2, tall // 2, LANES), v(2, groups, tall // 2, LANES), v(groups, tall, LANES), v(groups, tall, LANES),
+        ]
+        + sems(2 * CHUNKS) + sems(REDUCE_SEMS) + sems(REDUCE_SEMS) + sems(2 * SIDE) + sems(3 + groups) + [pltpu.SemaphoreType.DMA((4 + CHUNKS,))],
+        compiler_params=pltpu.CompilerParams(
+            collective_id=3, has_side_effects=True, vmem_limit_bytes=58 * 1024 * 1024
+        ),
+        cost_estimate=spans(100),
+    )(ffn.reshape(3, more, 2, 2, rows, units), mixer, passed, near, turned, d_own, d_side, small.reshape(groups, 2, 2, tall, LANES))
+
+
+LANES = 128
+
+
+def gather_kernel(places, w_step, log_decay, taps, rows, select, out):
+    ranks, states, taps_n = w_step.shape[0], log_decay.shape[0], taps.shape[0]
+    size = w_step.shape[1] // places
+    high = select.shape[0] // places
+    low = ranks + states + 16
+    out[...] = jnp.zeros_like(out)
+    for p in range(places):
+        cols = slice(p * size, (p + 1) * size)
+        out[p, :ranks, :size] = w_step[:, cols]
+        out[p, ranks : ranks + states, :size] = log_decay[:, cols]
+        at = ranks + states
+        out[p, at : at + 8, :size] = jnp.concatenate([taps[:, cols], rows[: 8 - taps_n, cols]], axis=0)
+        out[p, at + 8 : at + 16, :size] = rows[8 - taps_n : 16 - taps_n, cols]
+        for b in range(select.shape[1] // LANES):
+            out[p, low + b * high : low + (b + 1) * high, :] = select[
+                p * high : (p + 1) * high, b * LANES : (b + 1) * LANES
+            ]
+
+
+def gather_small(w_step, log_decay, taps, rows, select):
+    places = lax.axis_size("seq")
+    channels = w_step.shape[1]
+    tall = w_step.shape[0] + log_decay.shape[0] + 16 + select.shape[0] // places * (channels // LANES)
+    tall = -(-tall // 16) * 16
+    return pl.pallas_call(
+        functools.partial(gather_kernel, places),
+        out_shape=shaped(places, tall, LANES),
+        in_specs=[in_vmem()] * 5,
+        out_specs=in_vmem(),
+        compiler_params=params(24),
+        cost_estimate=spans(4),
+    )(w_step, log_decay, taps, rows, select)
 
 
 epsilon = 1e-06
@@ -790,51 +1133,12 @@
     return lax.dynamic_index_in_dim(block, lax.axis_index("head"), 0, keepdims=False)
 
 
-def unswap(parts, place):
-    odd, far = (place & 1) == 1, (place & 2) == 2
-    p = list(parts)
-    p = [jnp.where(odd, p[k ^ 1], p[k]) for k in range(4)]
-    return [jnp.where(far, p[k ^ 2], p[k]) for k in range(4)]
-
-
 def part_of(block, index, size, axis):
     return lax.dynamic_slice_in_dim(block, index * size, size, axis)
 
 
-def exchange(block, place):
-    size = block.shape[-1] // SIDE
-    first = lax.axis_index("head")
-    turned = jnp.stack([lax.dynamic_index_in_dim(block, first, 0, keepdims=False), lax.dynamic_index_in_dim(block, 1 - first, 0, keepdims=False)])
-    away = [part_of(turned, place ^ k, size, 2).astype(jnp.float32) for k in range(1, SIDE)]
-    return part_of(block, place, size, 2).reshape(-1, size), [send(away[k - 1], swaps(k)) for k in range(1, SIDE)]
-
-
 def after(block, *earlier):
     return lax.optimization_barrier((block,) + earlier)[0]
-
-
-def scatter_bits(blocks, bits):
-    here = lax.axis_index("seq")
-    order = sorted(bits)
-    shape = blocks.shape[1:]
-    left = list(order)
-    blocks = blocks.reshape((2,) * len(order) + shape)
-    for bit in bits:
-        axis = len(left) - 1 - left.index(bit)
-        mine = (here // bit) % 2
-        keep = lax.dynamic_index_in_dim(blocks, mine, axis, keepdims=False)
-        away = lax.dynamic_index_in_dim(blocks, 1 - mine, axis, keepdims=False)
-        blocks = keep + send(away, swaps(bit))
-        left.remove(bit)
-    return blocks
-
-
-def bits_between(low, high):
-    out = []
-    while low < high:
-        out.append(low)
-        low *= 2
-    return out
 
 
 def matmul(left, right):
@@ -901,9 +1205,8 @@
     source = tokens.astype(jnp.float32)
     rim_ids = jnp.broadcast_to((doc_ids[:, length - lead :] + 1).astype(jnp.float32)[:, :, None], (streams, lead, 128))
     rim = send(jnp.concatenate([source[:, length - lead :], rim_ids], axis=2), links(1))
-    mine_grad = own_stream(out_grad).astype(jnp.float32)
-    grad_up = send(mine_grad, links(stride))
-    grad_down = send(mine_grad, links(-stride))
+    mine_grad, source, rim = lax.optimization_barrier((own_stream(out_grad).astype(jnp.float32), source, rim))
+    line_grad = [send(mine_grad, links(stride)), send(mine_grad, links(-stride))]
     normed, scale_mix = norm_forward(source, norm_mix)
     normed_low = normed.astype(low)
     mine_normed = own_stream(normed)
@@ -937,7 +1240,7 @@
     rate = decay_rate * LOG2E
     b_wide, c_wide = across(bsel), across(csel)
     outs, first, grad_ring, grad_rest, side_far, side_rest = scan_forward(
-        fall, gain, b_wide, c_wide, rate, grad_up, grad_down, norm_near, norm_next
+        fall, gain, b_wide, c_wide, rate, line_grad, norm_near, norm_next
     )
     y = outs + skip_gain * value
     gate_z = jax.nn.silu(outgate)
@@ -947,6 +1250,8 @@
     resid = source + mix
     hidden, scale_ffn = norm_forward(resid, norm_ffn)
     hidden_low = hidden.astype(low)
+    mine_hidden = own_stream(hidden)
+    line_hidden = [send(mine_hidden, links(stride)), send(mine_hidden, links(-stride))]
     gate = matmul(hidden_low, w_gate)
     up = matmul(hidden_low, w_up)
     act_low = (jax.nn.silu(gate) * up).astype(low)
@@ -964,45 +1269,21 @@
     d_outgate = (d_mixed * y * silu_slope(outgate)).astype(low)
     grad_skip_gain = jnp.sum(d_y * value, axis=(0, 1))
     d_step, d_scan, db_wide, dc_wide, decay_sum, hid_ring, hid_rest, mix_side, mix_rest, y_side = scan_backward(
-        fall, step, value, d_y, b_wide, c_wide, rate, first, own_stream(hidden), own_stream(d_resid), y
+        fall, step, value, d_y, b_wide, c_wide, rate, first, line_hidden, own_stream(d_resid), y
     )
 
     flat = lambda block: block.reshape(-1, block.shape[-1])
     size = channels // SIDE
-    whole_outgate, whole_mixout, turned = mixer_grads(
+    mixer, turned = mixer_grads(
         flat(normed_low), [norm_near, norm_next, side_far, side_rest], flat(d_mix), [mix_side, mix_rest],
         flat(part_of(y, place, size, 2)), y_side,
-        part_of(w_outgate, place, size, 1), part_of(w_mixout, place, size, 0),
-    )
-    whole_gate, whole_up, whole_down = ffn_grads(
-        stride, flat(hidden_low), [hid_ring, hid_rest], flat(out_grad), [grad_ring, grad_rest], w_gate, w_up, w_down,
-        flat(d_gate), flat(d_up), flat(act_low),
-    )
-    side_bits = bits_between(1, stride)
-    orders = (side_bits, side_bits[len(side_bits) // 2 :] + side_bits[: len(side_bits) // 2])
-
-    def sum_side(whole):
-        whole = whole.reshape(stride, width // count, -1)
-        half = whole.shape[2] // 2
-        return jnp.concatenate(
-            [scatter_bits(whole[..., :half], orders[0]), scatter_bits(whole[..., half:], orders[1])], axis=-1
-        )
-
-    grad_w_gate = sum_side(whole_gate)
-    grad_w_up = sum_side(whole_up)
-    grad_w_down = sum_side(whole_down).T
-
-    groups = [list(range(k, count, SIDE)) for k in range(SIDE)]
-
-    def sum_line(whole):
-        own = lax.psum_scatter(whole, "seq", scatter_dimension=0, axis_index_groups=groups, tiled=True)
-        own = own.reshape(SIDE, width // count, -1)
-        sent = unswap([own[k] for k in range(SIDE)], place)
-        got = [sent[0]] + [send(sent[k], swaps(k)) for k in range(1, SIDE)]
-        return jnp.concatenate(unswap(got, place), axis=-1)
-
-    grad_w_mixout = sum_line(whole_mixout).T
-    grad_w_outgate = sum_line(whole_outgate)
+        w_outgate, w_mixout,
+    )
+    mixer = mixer.reshape(2, SIDE, width // SIDE, size)
+    got = send(mixer[:, SIDE - 1], [(i, i + stride) for i in range(stride)]) + send(
+        mixer[:, 0], [(i, i - stride) for i in range(count - stride, count)]
+    )
+    d_step = after(d_step, mixer)
 
     d_value = d_y * skip_gain + d_scan
     d_step_pre = (d_step * jax.nn.sigmoid(step_pre)).astype(low)
@@ -1037,50 +1318,54 @@
     grad_conv_taps = jnp.stack(tap_grads)
     rim_grad = send(d_ext[:, :lead], links(-1))
     d_inner = (d_ext[:, lead:] + jnp.pad(rim_grad, ((0, 0), (length - lead, 0), (0, 0)))).astype(low)
-    own_d_inner, side_d_inner = exchange(d_inner, place)
-    grad_w_inner = sum_line(inner_grad(turned, own_d_inner, side_d_inner))
     d_normed = head_sum(matmul_back(d_inner, w_inner) + matmul_back(d_outgate, w_outgate))
     d_source, grad_norm_mix = norm_backward(source, scale_mix, norm_mix, d_normed)
     tokens_grad = d_resid + d_source
 
     pad = lambda v: jnp.pad(v, (0, channels - v.shape[0]))
-    selects = grad_select_gain.reshape(count, -1)
-    tall = jnp.concatenate(
-        [
-            grad_w_step,
-            decay_sum * decay_rate,
-            grad_conv_taps,
-            jnp.stack([grad_conv_bias, grad_step_bias, grad_skip_gain, grad_norm_mix, grad_norm_ffn]),
-        ]
-    )
-    tall = jnp.swapaxes(tall.reshape(tall.shape[0], count, -1), 0, 1)
-    selects = jnp.pad(selects, ((0, 0), (0, tall.shape[2] - selects.shape[1])))
-    tall = jnp.concatenate([tall, selects[:, None]], axis=1)
-    broad = grad_w_select.reshape(count, -1, channels)
-    every = bits_between(1, count)
-    turned = every[1:2] + every[:1] + every[2:]
-    tall = scatter_bits(tall, every)
-    broad = scatter_bits(broad, turned)
+    rows = [grad_conv_bias, grad_step_bias, grad_skip_gain, pad(grad_norm_mix), pad(grad_norm_ffn)]
+    gains = grad_select_gain.reshape(count, -1)
+    rows.append(jnp.pad(gains, ((0, 0), (0, channels // count - gains.shape[1]))).reshape(channels))
+    rows = jnp.stack(rows + [jnp.zeros_like(grad_conv_bias)] * (16 - taps - len(rows)))
+    small = gather_small(grad_w_step, decay_sum * decay_rate, grad_conv_taps, rows, grad_w_select)
+    ffn, passed, d_side, near = ffn_grads(
+        flat(hidden_low), hid_ring, hid_rest, line_hidden, flat(out_grad), grad_ring, grad_rest, line_grad, w_gate, w_up, w_down,
+        flat(d_gate), flat(d_up), flat(act_low), got, d_inner.astype(jnp.float32), mixer,
+    )
+    ffn, mixer, inner, tall = sum_grads(
+        ffn, mixer, passed, near, turned, flat(part_of(d_inner, place, size, 2)), d_side, small
+    )
+    if count > SIDE * SIDE:
+        groups = [[a * stride + b + SIDE * k for k in range(stride // SIDE)] for a in range(SIDE) for b in range(SIDE)]
+        ffn, mixer, inner = (
+            lax.psum_scatter(part, "seq", scatter_dimension=1, axis_index_groups=groups) for part in (ffn, mixer, inner)
+        )
+    else:
+        ffn, mixer, inner = (part[:, 0] for part in (ffn, mixer, inner))
     at = rank + states
+    high = grad_w_select.shape[0] // count
+    broad = tall[at + 16 : at + 16 + high * channels // LANES].reshape(channels // LANES, high, LANES)
+    broad = jnp.swapaxes(broad, 0, 1).reshape(high, channels)
+    tall = tall[:, : channels // count]
     return (
         output,
         tokens_grad,
         tall[at + taps + 3],
-        grad_w_inner,
-        grad_w_outgate,
+        inner[0],
+        mixer[0],
         tall[at : at + taps],
         tall[at + taps],
         broad.T,
-        tall[at + taps + 5, : grad_select_gain.shape[0] // count],
+        tall[at + taps + 5, : gains.shape[1]],
         tall[:rank],
         tall[at + taps + 1],
         tall[rank:at].T,
         tall[at + taps + 2],
-        grad_w_mixout,
+        mixer[1].T,
         tall[at + taps + 4],
-        grad_w_gate,
-        grad_w_up,
-        grad_w_down,
+        ffn[0],
+        ffn[1],
+        ffn[2].T,
     )
 
 

time: 522 us -> 468 us (0.90)
  Pallas kernels: 208 us -> 308 us
  waiting for transfers between devices: 99.1 us -> 15.3 us
  starting transfers between devices: 48.1 us -> 22.6 us
  local copies, waits for them, and re-layouts: 55.7 us -> 41.2 us
  between operations: 16.3 us -> 2.39 us
  other arithmetic: 46.7 us -> 33.4 us
    pallas_call x2 -> x3, Pallas kernels: 38.9 us -> 162 us  [the longest x1 97.8 us: sum_grads(): pl.pallas_call(functools.partial(sum_kernel, count), out_shape=[shaped(3,...]
    ppermute x44 -> x16, waiting for transfers between devices: 99 us -> 15.3 us  [send(): return lax.ppermute(block, axis, route)]
    ppermute x44 -> x16, starting transfers between devices: 48 us -> 22.6 us  [send(): return lax.ppermute(block, axis, route)]
    pallas_call x1, Pallas kernels: 70.3 us -> 55.5 us  [scan_forward(): pl.pallas_call(functools.partial(forward_kernel, count), out_shape=[shape...]
    pallas_call x1, Pallas kernels: 83 us -> 73.5 us  [scan_backward(): pl.pallas_call(functools.partial(backward_kernel, count), out_shape=[flat...]
    unnamed x258 -> x197, local copies, waits for them, and re-layouts: 22 us -> 12.8 us
    concatenate x5 -> x0, other arithmetic: 6.42 us -> none  [the longest x1 2.81 us: body(): tall = jnp.concatenate([tall, selects[:, None]], axis=1)]
    add x19 -> x1, other arithmetic: 8.16 us -> 2.75 us  [body(): send(mixer[:, SIDE - 1], [(i, i + stride) for i in range(stride)])]
  transfers between devices with their start and end apart: 47 -> 16, of which waited for: 22 -> 8; matrix products, arithmetic and copies ran while one was open for 19% -> 12% of each run, Pallas kernels for 8% -> 14%
where the time goes in v4:
time: 468 us; the launch traced here: 461 us
  Pallas kernels  308 us (66%)
  local copies, waits for them, and re-layouts  41.2 us (9%)
  matrix products  37.4 us (8%)
  other arithmetic  33.4 us (7%)
  starting transfers between devices  22.6 us (5%)
  waiting for transfers between devices  15.3 us (3%)
    pallas_call x1, Pallas kernels, sum_grads(): pl.pallas_call(functools.partial(sum_kernel, count), out_shape=[shaped(3,...  97.8 us
    pallas_call x1, Pallas kernels, scan_backward(): pl.pallas_call(functools.partial(backward_kernel, count), out_shape=[flat...  73.5 us
    pallas_call x1, Pallas kernels, ffn_grads(): pl.pallas_call(functools.partial(ffn_kernel, count), grid=(units // block...  64.1 us
    pallas_call x1, Pallas kernels, scan_forward(): pl.pallas_call(functools.partial(forward_kernel, count), out_shape=[shape...  55.5 us
    ppermute x16, starting transfers between devices, send(): return lax.ppermute(block, axis, route)  22.6 us
    dot_general x8, matrix products, matmul_back(): lax.dot_general(left, right, (((left.ndim - 1,), (1,)), ((), ())), prefer...  17.9 us
    dot_general x8, matrix products, matmul(): return jnp.dot(left, right, preferred_element_type=jnp.float32)  17.8 us
    pallas_call x1, Pallas kernels, mixer_grads(): pl.pallas_call(functools.partial(mixer_kernel, len(norm_more), len(mix_mo...  17 us
  transfers between devices with their start and end apart: 16, of which 8 were waited for; matrix products, arithmetic and copies ran while one was open for 12% of the time, Pallas kernels for 14%

profile of v4, /device:TPU:0, one launch (start us, length us, event | category | flops | bytes accessed | tf_op | source)
XLA Modules:
  0.0 460.7 jit_solution(4870199803412210774)
XLA Ops:
  2.4 4.8 %collective-permute-start = (f32[2,3,1664]{2,1,0:T(4,128)S(1)}, f32[2,3,1664]{2,1,0:T(4,128)S(1)}, u32[]{:S(2)}, u32[]{:S(2)}) collective-permute-start(f32[2,3,1664]{2,1,0:T(4,128)S(1)} %pad_maximum_fusion.2), channel_id=1, source_target_pairs={{0,2},{2,4},{4,6},{6,8},{8,10},{10,12},{12,14},{14,16},{16,18},{18... | collective-permute-start | bytes 119816 | tf_op jit(solution)/shard_map/ppermute | solution.py:1125
  12.1 3.5 collective-permute-start.2
  24.0 2.5 fusion.32
  27.6 2.5 fusion.18
  30.8 4.6 compare_select_fusion
  42.4 55.5 %shard_map.322 = (f32[2,128,1536]{2,1,0:T(8,128)S(1)}, f32[2,16,1536]{2,1,0:T(8,128)S(1)}, f32[3,128,1536]{2,1,0:T(8,128)}, f32[3,128,1536]{2,1,0:T(8,128)}, f32...) custom-call(f32[2,128,1536]{2,1,0:T(8,128)S(1)} %get-tuple-element.128.fall, f32[2,128,1536]{2,1,0:T(8,128)S(1)} %get-tuple-element.129.gain, ...), custom_call_target="tpu_custom_call" | custom-call | flops 4400000000 | bytes 12000000 | tf_op jit(solution)/shard_map/pallas_call | solution.py:632
  109.3 2.5 multiply_convert_fusion.1
  113.8 3.0 fusion.27
  117.2 2.9 fusion.2
  128.4 4.6 %fusion.66 = (bf16[2,128,1536]{2,1,0:T(8,128)(2,1)S(1)}, f32[2,128,1536]{2,1,0:T(8,128)S(1)}, bf16[2,128,1536]{2,1,0:T(8,128)(2,1)}) fusion(f32[2,128]{1,0:T(2,128)S(1)} %broadcast_multiply_fusion.5, f32[2,128,1536]{2,1,0:T(8,128)S(1)} %get-tuple-element.112, f32[1536]{0:T(1024)S(1)} %copy-done.45, f32[2,128,1536]{2,1,0:T(8,128)} %fusion.27, ...), kind=kLoop, calls=%fused_computation.170 | loop fusion | flops 5505024 | bytes 11804672 | tf_op jit(solution)/shard_map/convert_element_type | solution.py:1266
  133.8 3.0 multiply_reduce_fusion.2
  138.5 2.8 fusion.16
  142.1 4.2 collective-permute-done.10.down_one.hid_down
  146.3 73.5 %shard_map.323 = (f32[2,128,1536]{2,1,0:T(8,128)}, f32[2,128,1536]{2,1,0:T(8,128)}, f32[2,2048,128]{2,1,0:T(8,128)}, f32[2,2048,128]{2,1,0:T(8,128)}, f32[16,153...) custom-call(f32[2,128,1536]{2,1,0:T(8,128)} %copy-done.12, ...), custom_call_target="tpu_custom_call" | custom-call | flops 6819999744 | bytes 18600000 | tf_op jit(solution)/shard_map/pallas_call | solution.py:657
  224.6 17.0 %shard_map.324 = (f32[2,1536,384]{2,1,0:T(8,128)}, bf16[1536,1024]{1,0:T(8,128)(2,1)}) custom-call(bf16[256,1536]{1,0:T(8,128)(2,1)} %bitcast.158, f32[128,1536]{1,0:T(8,128)} %copy-done.4, f32[128,1536]{1,0:T(8,128)} %copy-done.5, f32[128,1536]{1,0:T(8,128)} %copy-done.7, f32[3,128,1536]{2,1,0:T(8,128)} %get-tuple-element.56.refs_4_, ...), custom_call_target="tpu_custom_call" | custom-call | flops 1320000000 | bytes 3600000 | tf_op jit(solution)/shard_map/pallas_call | solution.py:114
  241.6 3.4 slice_bitcast_fusion
  246.1 2.6 collective-permute-start.14
  257.9 4.2 collective-permute-done.12
  263.6 2.7 fusion.24
  270.4 3.5 collective-permute-done.14
  273.9 2.8 add.241.got
  276.6 64.1 %shard_map.325 = (f32[3,384,2048]{2,1,0:T(8,128)}, f32[2,2,384,384]{3,2,1,0:T(8,128)}, f32[3,2,128,384]{3,2,1,0:T(8,128)}, f32[2,3,1,2,96,512]{5,4,3,2,1,0:T(8,128)}) custom-call(bf16[256,1536]{1,0:T(8,128)(2,1)} %bitcast.159, f32[3,128,1536]{2,1,0:T(8,128)} %get-tuple-element.64.hid_ring, f32[3,128,1536]{2,1,0:T(8,128)} %get-tuple-element.65.hid_rest, ...), custom_call_target="tpu_custom_call" | custom-call | flops 3960000000 | bytes 10800000 | tf_op jit(solution)/shard_map/pallas_call | solution.py:806
  345.1 97.8 %shard_map.327 = (f32[3,1,96,2048]{3,2,1,0:T(8,128)}, f32[2,1,96,1536]{3,2,1,0:T(8,128)}, f32[1,1,96,1536]{3,2,1,0:T(8,128)}, f32[224,128]{1,0:T(8,128)}) custom-call(f32[3,1,2,2,96,2048]{5,4,3,2,1,0:T(8,128)} %bitcast.170, f32[2,4,384,384]{3,2,1,0:T(8,128)} %bitcast.141, f32[2,2,384,384]{3,2,1,0:T(8,128)} %get-tuple-element.69.passed_in, ...), custom_call_target="tpu_custom_call" | custom-call | flops 11000000512 | bytes 30000000 | tf_op jit(solution)/shard_map/pallas_call | solution.py:1049
  456.0 3.6 subtract_add_fusion
  (329 shorter events, 86.8 us)
Async XLA Ops:
  2.4 9.4 %collective-permute-start = (f32[2,3,1664]{2,1,0:T(4,128)S(1)}, f32[2,3,1664]{2,1,0:T(4,128)S(1)}, u32[]{:S(2)}, u32[]{:S(2)}) collective-permute-start(f32[2,3,1664]{2,1,0:T(4,128)S(1)} %pad_maximum_fusion.2), channel_id=1, source_target_pairs={{0,2},{2,4},{4,6},{6,8},{8,10},{10,12},{12,14},{14,16},{16,18},{18... | collective-permute-start | bytes 119816 | tf_op jit(solution)/shard_map/ppermute | solution.py:1125
  12.1 23.3 %collective-permute-start.2 = (f32[128,1536]{1,0:T(8,128)}, f32[128,1536]{1,0:T(8,128)S(1)}, u32[]{:S(2)}, u32[]{:S(2)}) collective-permute-start(f32[128,1536]{1,0:T(8,128)} %bitcast_convert_fusion), channel_id=1, source_target_pairs={{0,8},{2,10},{4,12},{6,14},{8,16},{10,18},{12,20},{14,22},{16,24},... | collective-permute-start | bytes 2359304 | tf_op jit(solution)/shard_map/ppermute | solution.py:1125
  15.6 20.9 %collective-permute-start.3 = (f32[128,1536]{1,0:T(8,128)}, f32[128,1536]{1,0:T(8,128)}, u32[]{:S(2)}, u32[]{:S(2)}) collective-permute-start(f32[128,1536]{1,0:T(8,128)} %bitcast_convert_fusion), channel_id=1, source_target_pairs={{8,0},{10,2},{12,4},{14,6},{16,8},{18,10},{20,12},{22,14},{24,16},... | collective-permute-start | bytes 2359304 | tf_op jit(solution)/shard_map/ppermute | solution.py:1125
  18.6 18.9 %collective-permute-start.4 = (f32[128,1536]{1,0:T(8,128)}, f32[128,1536]{1,0:T(8,128)S(1)}, u32[]{:S(2)}, u32[]{:S(2)}) collective-permute-start(f32[128,1536]{1,0:T(8,128)} %dynamic-slice_bitcast_fusion.2), channel_id=1, source_target_pairs={{0,2},{2,0},{4,6},{6,4},{8,10},{10,8},{12,14},{14,12},{16,18},{18,... | collective-permute-start | bytes 2359304 | tf_op jit(solution)/shard_map/ppermute | solution.py:1125
  20.1 18.7 %collective-permute-start.5 = (f32[128,1536]{1,0:T(8,128)}, f32[128,1536]{1,0:T(8,128)S(1)}, u32[]{:S(2)}, u32[]{:S(2)}) collective-permute-start(f32[128,1536]{1,0:T(8,128)} %dynamic-slice_bitcast_fusion.2), channel_id=1, source_target_pairs={{0,4},{2,6},{4,0},{6,2},{8,12},{10,14},{12,8},{14,10},{16,20},{18,... | collective-permute-start | bytes 2359304 | tf_op jit(solution)/shard_map/ppermute | solution.py:1125
  27.6 2.6 collective-permute-start.1
  40.2 57.6 %copy-start.1 = (f32[2,2048,128]{2,1,0:T(8,128)}, f32[2,2048,128]{2,1,0:T(8,128)S(1)}, u32[]{:S(2)}) copy-start(f32[2,2048,128]{2,1,0:T(8,128)S(1)} %broadcast_in_dim.22.b_ref) | copy-start | bytes 6291460
  40.3 59.7 %slice-start.6 = ((s8[4718592]{0:T(1024)(128)(4,1)}), s8[4194304]{0:T(1024)(128)(4,1)S(1)}, s32[]{:S(2)}) async-start(s8[4718592]{0:T(1024)(128)(4,1)} %bitcast.149), calls=%async_computation.6 | async-start | bytes 8388608
  42.4 57.6 %slice-start.7 = ((s8[4718592]{0:T(1024)(128)(4,1)}), s8[524288]{0:T(1024)(128)(4,1)S(1)}, s32[]{:S(2)}) async-start(s8[4718592]{0:T(1024)(128)(4,1)} %bitcast.149), calls=%async_computation.7 | async-start | bytes 1048576
  42.4 57.6 %copy-start.78 = (f32[2,128,1536]{2,1,0:T(8,128)S(1)}, f32[2,128,1536]{2,1,0:T(8,128)}, u32[]{:S(2)}) copy-start(f32[2,128,1536]{2,1,0:T(8,128)} %fusion.18) | copy-start | bytes 4718596
  101.5 3.5 collective-permute-start.6
  116.8 9.2 %collective-permute-start.8 = (f32[2,128,1536]{2,1,0:T(8,128)}, f32[2,128,1536]{2,1,0:T(8,128)}, u32[]{:S(2)}, u32[]{:S(2)}) collective-permute-start(f32[2,128,1536]{2,1,0:T(8,128)} %fusion.27), channel_id=1, source_target_pairs={{0,1},{1,0},{2,3},{3,2},{4,5},{5,4},{6,7},{7,6},{8,9},{9,8},{10,11... | collective-permute-start | bytes 4718600 | tf_op jit(solution)/shard_map/ppermute | solution.py:1125
  120.1 8.3 %collective-permute-start.7 = (f32[2,128,1536]{2,1,0:T(8,128)}, f32[2,128,1536]{2,1,0:T(8,128)}, u32[]{:S(2)}, u32[]{:S(2)}) collective-permute-start(f32[2,128,1536]{2,1,0:T(8,128)} %fusion.2), channel_id=1, source_target_pairs={{0,1},{1,0},{2,3},{3,2},{4,5},{5,4},{6,7},{7,6},{8,9},{9,8},{10,11... | collective-permute-start | bytes 4718600 | tf_op jit(solution)/shard_map/ppermute | solution.py:1125
  123.2 18.9 %collective-permute-start.9 = (f32[128,1536]{1,0:T(8,128)S(1)}, f32[128,1536]{1,0:T(8,128)S(1)}, u32[]{:S(2)}, u32[]{:S(2)}) collective-permute-start(f32[128,1536]{1,0:T(8,128)S(1)} %dynamic-slice_bitcast_fusion.1), channel_id=1, source_target_pairs={{0,8},{2,10},{4,12},{6,14},{8,16},{10,18},{12,20},{14,22},{16,24},... | collective-permute-start | bytes 2359304 | tf_op jit(solution)/shard_map/ppermute | solution.py:1125
  124.6 21.7 %collective-permute-start.10 = (f32[128,1536]{1,0:T(8,128)S(1)}, f32[128,1536]{1,0:T(8,128)S(1)}, u32[]{:S(2)}, u32[]{:S(2)}) collective-permute-start(f32[128,1536]{1,0:T(8,128)S(1)} %dynamic-slice_bitcast_fusion.1), channel_id=1, source_target_pairs={{8,0},{10,2},{12,4},{14,6},{16,8},{18,10},{20,12},{22,14},{24,16},... | collective-permute-start | bytes 2359304 | tf_op jit(solution)/shard_map/ppermute | solution.py:1125
  142.1 77.7 %copy-start.10 = (f32[128,1536]{1,0:T(8,128)}, f32[128,1536]{1,0:T(8,128)S(1)}, u32[]{:S(2)}) copy-start(f32[128,1536]{1,0:T(8,128)S(1)} %collective-permute-done.9.up_one.hid_up) | copy-start | bytes 2359300
  146.3 73.5 %copy-start.11 = (f32[128,1536]{1,0:T(8,128)}, f32[128,1536]{1,0:T(8,128)S(1)}, u32[]{:S(2)}) copy-start(f32[128,1536]{1,0:T(8,128)S(1)} %collective-permute-done.10.down_one.hid_down) | copy-start | bytes 2359300
  245.9 6.5 %collective-permute-start.11 = (f32[2,128,128]{1,2,0:T(8,128)S(1)}, f32[2,128,128]{1,2,0:T(8,128)S(1)}, u32[]{:S(2)}, u32[]{:S(2)}) collective-permute-start(f32[2,128,128]{1,2,0:T(8,128)S(1)} %pad_maximum_fusion), channel_id=1, source_target_pairs={{0,1},{1,0},{2,3},{3,2},{4,5},{5,4},{6,7},{7,6},{8,9},{9,8},{10,11... | collective-permute-start | bytes 393224 | tf_op jit(solution)/shard_map/ppermute | solution.py:1125
  246.1 27.8 %collective-permute-start.14 = (f32[2,384,384]{2,1,0:T(8,128)}, f32[2,384,384]{2,1,0:T(8,128)}, u32[]{:S(2)}, u32[]{:S(2)}) collective-permute-start(f32[2,384,384]{2,1,0:T(8,128)} %get-tuple-element.116), channel_id=1, source_target_pairs={{0,8},{2,10},{4,12},{6,14},{1,9},{3,11},{5,13},{7,15}} | collective-permute-start | bytes 3538952 | tf_op jit(solution)/shard_map/ppermute | solution.py:1125
  248.7 25.2 %collective-permute-start.15 = (f32[2,384,384]{2,1,0:T(8,128)}, f32[2,384,384]{2,1,0:T(8,128)}, u32[]{:S(2)}, u32[]{:S(2)}) collective-permute-start(f32[2,384,384]{2,1,0:T(8,128)} %get-tuple-element.115), channel_id=1, source_target_pairs={{24,16},{26,18},{28,20},{30,22},{25,17},{27,19},{29,21},{31,23}} | collective-permute-start | bytes 3538952 | tf_op jit(solution)/shard_map/ppermute | solution.py:1125
  255.4 6.7 %collective-permute-start.12 = (f32[2,3,1536]{2,1,0:T(4,128)S(1)}, f32[2,3,1536]{2,1,0:T(4,128)S(1)}, u32[]{:S(2)}, u32[]{:S(2)}) collective-permute-start(f32[2,3,1536]{2,1,0:T(4,128)S(1)} %pad_add_fusion.1), channel_id=1, source_target_pairs={{2,0},{4,2},{6,4},{8,6},{10,8},{12,10},{14,12},{16,14},{18,16},{20... | collective-permute-start | bytes 110600 | tf_op jit(solution)/shard_map/ppermute | solution.py:1125
  266.3 74.5 %collective-permute-start.13 = (f32[2,128,1536]{2,1,0:T(8,128)}, f32[2,128,1536]{2,1,0:T(8,128)}, u32[]{:S(2)}, u32[]{:S(2)}) collective-permute-start(f32[2,128,1536]{2,1,0:T(8,128)} %fusion.24), channel_id=1, source_target_pairs={{0,1},{1,0},{2,3},{3,2},{4,5},{5,4},{6,7},{7,6},{8,9},{9,8},{10,11... | collective-permute-start | bytes 4718600 | tf_op jit(solution)/shard_map/ppermute | solution.py:1125
  276.6 64.2 %copy-start.17 = (f32[2,128,1536]{2,1,0:T(8,128)S(1)}, f32[2,128,1536]{2,1,0:T(8,128)}, u32[]{:S(2)}) copy-start(f32[2,128,1536]{2,1,0:T(8,128)} %copy-done.15) | copy-start | bytes 4718596
  276.6 64.2 %copy-start.59 = (f32[2,128]{1,0:T(2,128)S(1)}, f32[2,128]{1,0:T(2,128)}, u32[]{:S(2)}) copy-start(f32[2,128]{1,0:T(2,128)} %copy-done.58) | copy-start | bytes 3076
  (90 other events, 584.1 us)

commit v5 on v4

--- a/solution.py
+++ b/solution.py
@@ -114,7 +114,7 @@
     return pl.pallas_call(
         functools.partial(mixer_kernel, len(norm_more), len(mix_more)),
         grid=(width // block,),
-        in_specs=[whole(a.shape) for a in operands[:-2]] + [pl.BlockSpec(memory_space=pl.ANY)] * 2,
+        in_specs=[whole(a.shape) for a in operands[:-2]] + [in_hbm()] * 2,
         out_specs=[pl.BlockSpec((2, block, cut), lambda i: (0, i, 0)), row(tokens)],
         out_shape=[
             jax.ShapeDtypeStruct((2, width, cut), jnp.float32),
@@ -123,7 +123,7 @@
         scratch_shapes=[pltpu.VMEM((tokens, width), low)] * 2
         + [pltpu.VMEM((tokens, cut), low)] * 2
         + [pltpu.VMEM((width, cut), low), pltpu.VMEM((cut, width), low), pltpu.SemaphoreType.DMA((2,))],
-        compiler_params=params(56),
+        compiler_params=params(40),
         cost_estimate=spans(12),
     )(*operands)
 
@@ -211,6 +211,15 @@
         up, down = self.cores_of_one()
         pl.when(self.where.z >= 1)(up.start)
         pl.when(self.where.z <= SIDE - 2)(down.start)
+
+    def finish_two(self):
+        z = self.where.z
+        up, down = self.copies(2)
+        pl.when((z >= 1) & (z < SIDE - 1))(up.wait_send)
+        pl.when((z <= SIDE - 2) & (z > 0))(down.wait_send)
+        self.core(1).wait()
+        pl.when(z >= 1)(self.core(SIDE - 2).wait)
+        pl.when(z <= SIDE - 2)(self.core(0).wait)
 
     def finish(self):
         z = self.where.z
@@ -428,11 +437,6 @@
         cols = columns(i, lanes)
         rate = rate_ref[:, cols]
 
-        @pl.when(i == blocks // 2)
-        def _():
-            line.arrive(2)
-            line.start(3)
-
         def chunk(i, states):
             base = pl.multiple_of(i * ROWS, ROWS)
             out = []
@@ -457,18 +461,18 @@
     for c in far:
         c.wait_recv()
     cores[2].start()
-    line.arrive(3)
+    line.arrive(2)
     for c in far:
         c.wait_send()
     for c in cores:
         c.wait()
-    line.finish()
+    line.finish_two()
 
 
 def backward_kernel(
-    count, fall, d_ref, v_ref, g_ref, b_ref, c_ref, rate_ref, first_ref, up_one, down_one, mix, y_ref,
-    dstep_ref, dvalue_ref, db_ref, dc_ref, decay_ref, ring, ring_rest, side, side_rest, y_side,
-    ends, total, last, path, fades, line_send, line_recv, side_send, side_recv, y_send, y_recv, *scratch,
+    count, fall, d_ref, v_ref, g_ref, b_ref, c_ref, rate_ref, first_ref, up_one, down_one, mix, grad_middle,
+    dstep_ref, dvalue_ref, db_ref, dc_ref, decay_ref, ring, ring_rest, side, side_rest, grad_end, grad_rest,
+    ends, total, last, path, fades, line_send, line_recv, side_send, side_recv, *scratch,
 ):
     where = Place(count)
     streams, length, channels = fall.shape
@@ -478,14 +482,13 @@
     width = channels // SIDE
     where.greet()
     line = Line(where, up_one, down_one, ring, ring_rest, line_send, line_recv)
+    z = where.z
+    rise = remote(grad_middle, grad_end, line_send, line_recv, LINE_SEMS, where.above)
+    sink = remote(grad_middle, grad_end, line_send, line_recv, LINE_SEMS + 1, where.below)
+    core = remote(grad_end, grad_rest, line_send, line_recv, LINE_SEMS + 2, where.core)
     square = Side(where, mix, side, side_rest, side_send, side_recv)
-    quarters = [
-        remote(
-            y_ref.at[:, :, pl.ds(pl.multiple_of((where.place ^ k) * width, 128), width)],
-            y_side.at[k - 1], y_send, y_recv, k - 1, where.member[k],
-        )
-        for k in range(1, SIDE)
-    ]
+    line.start(2)
+    line.start_cores_of_one()
 
     def summary(i, _):
         cols = columns(i, lanes)
@@ -515,13 +518,11 @@
     sums(fall, total)
 
     def after_line():
-        line.start_cores_of_one()
-        line.start(2)
+        line.arrive(2)
+        line.start(3)
 
     def after_all():
         square.start()
-        for c in quarters:
-            c.start()
 
     chain(where, True, ends, total, rate_ref, last, scratch, after_line, after_all)
     db_ref[...] = jnp.zeros_like(db_ref)
@@ -539,8 +540,8 @@
 
         @pl.when(i == blocks // 3)
         def _():
-            line.arrive(2)
-            line.start(3)
+            pl.when(z == SIDE - 2)(rise.start)
+            pl.when(z == 1)(sink.start)
 
         @pl.when(i == blocks // 2)
         def _():
@@ -602,9 +603,13 @@
     lax.fori_loop(0, blocks, run, 0)
     square.finish()
     line.arrive(3)
-    for c in quarters:
-        c.wait()
+    pl.when(z == SIDE - 1)(rise.wait_recv)
+    pl.when(z == 0)(sink.wait_recv)
+    pl.when((z == 0) | (z == SIDE - 1))(core.start)
     line.finish()
+    pl.when(z == SIDE - 2)(rise.wait_send)
+    pl.when(z == 1)(sink.wait_send)
+    pl.when((z == 0) | (z == SIDE - 1))(core.wait)
 
 
 def in_vmem():
@@ -638,13 +643,13 @@
         + sems(LINE_SEMS) + sems(5)
         + chain_scratch(streams, n, channels, count // SIDE),
         compiler_params=pltpu.CompilerParams(
-            collective_id=0, has_side_effects=True, vmem_limit_bytes=40 * 1024 * 1024
+            collective_id=0, has_side_effects=True, vmem_limit_bytes=24 * 1024 * 1024
         ),
         cost_estimate=spans(40),
     )(fall, gain, b_wide, c_wide, rate, *line, norm_near, norm_next)
 
 
-def scan_backward(fall, step, value, d_y, b_wide, c_wide, rate, first, line, mix, y):
+def scan_backward(fall, step, value, d_y, b_wide, c_wide, rate, first, line, mix, grad_middle):
     streams, length, channels = fall.shape
     n = rate.shape[0]
     count = lax.axis_size("seq")
@@ -656,10 +661,9 @@
     kept = pltpu.VMEM((streams, length * n, lanes), jnp.float32)
     return pl.pallas_call(
         functools.partial(backward_kernel, count),
-        out_shape=[flat, flat, tall, tall, shaped(n, channels), three, three, three, three,
-                   shaped(SIDE - 1, streams, length, channels // SIDE)],
+        out_shape=[flat, flat, tall, tall, shaped(n, channels), three, three, three, three, shaped(half, width), shaped(half, width)],
         in_specs=[in_vmem()] * 8 + [in_hbm()] * 4,
-        out_specs=[in_vmem()] * 5 + [in_hbm()] * 5,
+        out_specs=[in_vmem()] * 5 + [in_hbm()] * 6,
         scratch_shapes=[
             pltpu.VMEM((streams, n, channels), jnp.float32),
             pltpu.VMEM((streams, channels), jnp.float32),
@@ -667,82 +671,92 @@
             kept,
             kept,
         ]
-        + sems(LINE_SEMS) + sems(SIDE_SEMS) + sems(SIDE - 1)
+        + sems(LINE_SEMS + 3) + sems(SIDE_SEMS)
         + chain_scratch(streams, n, channels, count // SIDE),
         compiler_params=pltpu.CompilerParams(
-            collective_id=1, has_side_effects=True, vmem_limit_bytes=52 * 1024 * 1024
+            collective_id=1, has_side_effects=True, vmem_limit_bytes=40 * 1024 * 1024
         ),
         cost_estimate=spans(62),
-    )(fall, step, value, d_y, b_wide, c_wide, rate, first, *line, mix, y)
-
-
-CHUNKS = 4
-
-
-def place_step_one(target, own, z, up, down):
-    rows = up.shape[0]
+    )(fall, step, value, d_y, b_wide, c_wide, rate, first, *line, mix, grad_middle)
+
+
+CHUNKS = 8
+EARLY = 6
+
+
+def stack_line(target, own, z, up, down, middle, first, last, rest, rest_first, rest_last):
+    rows = own.shape[0]
+    size = up.shape[0]
+    target[:rows, :] = own[...].astype(target.dtype)
+
+    def put(slot, block):
+        target[rows + slot * size : rows + (slot + 1) * size, :] = block[...].astype(target.dtype)
+
+    put(1, middle)
+    put(4, rest.at[1])
 
     @pl.when(z >= 1)
     def _():
-        target[own + (SIDE - 2) * rows : own + (SIDE - 1) * rows, :] = up[...].astype(target.dtype)
+        put(2, up)
+        put(5, rest.at[2])
+
+    @pl.when(z < 1)
+    def _():
+        put(2, last)
+        put(5, rest_last)
 
     @pl.when(z <= SIDE - 2)
     def _():
-        target[own : own + rows, :] = down[...].astype(target.dtype)
+        put(0, down)
+        put(3, rest.at[0])
+
+    @pl.when(z > SIDE - 2)
+    def _():
+        put(0, first)
+        put(3, rest_first)
 
 
 def ffn_kernel(
-    count, hid_own, hid_ring, hid_rest, hid_up, hid_down, grad_own, grad_ring, grad_rest, grad_up, grad_down, wg, wu, wd, dg_own, du_own, act_own,
-    got, inner, mixer,
-    out, passed, d_side, near,
-    hid, grad, hid_cut, grad_cut, dg, du, act, sent, stash, sends, recvs, local,
+    count, hid_own, hid_up, hid_down, hid_ring, hid_rest, grad_own, grad_up, grad_down, grad_middle, grad_rest, grad_end, grad_rest_end, wg, wu, wd, dg_own, du_own, act_own,
+    mixer, out, near, passed,
+    hid, grad, hid_cut, grad_cut, dg, du, act, stash, got, sent, sends, recvs, local,
 ):
     own, cut = hid_own.shape[0], hid_cut.shape[0]
     where = Place(count)
     z, place = where.z, where.place
-    width = d_side.shape[-1]
     first = pl.program_id(0) == 0
     last = pl.program_id(0) == pl.num_programs(0) - 1
-    quarters = [
-        remote(
-            inner.at[:, :, pl.ds(pl.multiple_of((place ^ k) * width, 128), width)],
-            d_side.at[k - 1], sends, recvs, k - 1, where.member[k],
-        )
-        for k in range(1, SIDE)
-    ]
-    rising = z < SIDE // 2
-    step = remote(
-        sent, passed.at[jnp.where(rising, 0, 1)], sends, recvs, jnp.where(rising, SIDE - 1, SIDE),
-        (jnp.where(rising, where.above[0], where.below[0]), where.head),
-    )
-    from_below = remote(sent, passed.at[0], sends, recvs, SIDE - 1, where.above)
-    from_above = remote(sent, passed.at[1], sends, recvs, SIDE, where.below)
-    middle = (z > 0) & (z < SIDE - 1)
     odd, far = lax.rem(place, 2), place // 2
     early = [
-        remote(stash.at[0, :, :, :, 1 - odd], near.at[0], sends, recvs, SIDE + 1, where.member[1]),
-        remote(stash.at[1, :, :, 1 - far], near.at[1], sends, recvs, SIDE + 2, where.member[2]),
+        remote(
+            stash.at[c, :, :, :, 1 - odd] if c % 2 == 0 else stash.at[c, :, :, 1 - far],
+            near.at[c], sends, recvs, c, where.member[1 + c % 2],
+        )
+        for c in range(EARLY)
     ]
-    turns = pl.num_programs(0) // CHUNKS
+    tips, rising = (z == 0) | (z == SIDE - 1), z < SIDE // 2
+
+    def along(source, target, at, up):
+        return remote(source, target, sends, recvs, at, (jnp.where(up, where.above[0], where.below[0]), where.head))
+
+    one = along(mixer.at[:, SIDE - 1 - z], got, EARLY, z == 0)
+    fetch = pltpu.make_async_copy(mixer.at[:, lax.rem(z + 2, SIDE)], sent, local.at[0])
+    way = jnp.where(rising, 0, 1)
+    two = along(sent, passed.at[way], EARLY + 1 + way, rising)
+    from_below = along(sent, passed.at[0], EARLY + 1, True)
+    from_above = along(sent, passed.at[1], EARLY + 2, False)
 
     @pl.when(first)
     def _():
         where.greet()
-        for c in quarters:
-            c.start()
-        fetch = pltpu.make_async_copy(mixer.at[:, lax.rem(z + 2, SIDE)], sent, local.at[0])
         fetch.start()
-        stack_tokens(hid, hid_own, [hid_ring, hid_rest])
-        place_step_one(hid, own, z, hid_up, hid_down)
+        pl.when(tips)(one.start)
         fetch.wait()
-
-        @pl.when(middle)
-        def _():
-            sent[...] += got[...]
-
-        step.start()
-        stack_tokens(grad, grad_own, [grad_ring, grad_rest])
-        place_step_one(grad, own, z, grad_up, grad_down)
+        pl.when(tips)(two.start)
+        ring, rest = hid_ring, hid_rest
+        stack_line(hid, hid_own, z, hid_up, hid_down, ring.at[1], ring.at[0], ring.at[2], rest, rest.at[0], rest.at[2])
+        ends = (grad_middle, grad_end, grad_end, grad_rest, grad_rest_end, grad_rest_end)
+        stack_line(grad, grad_own, z, grad_up, grad_down, *ends)
         at = pl.ds(pl.multiple_of(z * cut, 128), cut)
         hid_cut[...] = hid[:, at].T
         grad_cut[...] = grad[:, at].T
@@ -768,63 +782,66 @@
     out[1] = dot(hid_cut[...], du[...])
     out[2] = dot(grad_cut[...], act[...])
 
-    @pl.when(pl.program_id(0) < 2 * turns)
+    for c in range(EARLY):
+
+        @pl.when(pl.program_id(0) == c)
+        def _():
+            for m in range(3):
+                stash[c, m] = out[m].reshape(stash.shape[2:])
+            early[c].start()
+
+    @pl.when((pl.program_id(0) == pl.num_programs(0) // 2 + 1) & jnp.logical_not(tips))
     def _():
-        block = out.shape[2]
-        at = pl.ds(pl.multiple_of(lax.rem(pl.program_id(0), turns) * block, block), block)
-        for m in range(3):
-            stash[pl.program_id(0) // turns, m, :, :, :, :, at] = out[m].reshape(stash.shape[2:6] + (block,))
-
-    for c in range(2):
-        pl.when(pl.program_id(0) == (c + 1) * turns - 1)(early[c].start)
+        one.wait_recv()
+        sent[...] += got[...]
+        two.start()
 
     @pl.when(last)
     def _():
-        for c in quarters + early:
+        for c in early:
             c.wait()
-        step.wait_send()
-
-        @pl.when(middle)
+        pl.when(tips)(one.wait_send)
+        two.wait_send()
+
+        @pl.when(jnp.logical_not(tips))
         def _():
             from_below.wait_recv()
             from_above.wait_recv()
 
 
-def ffn_grads(hid_own, hid_ring, hid_rest, hid_one, grad_own, grad_ring, grad_rest, grad_one, w_gate, w_up, w_down, d_gate, d_up, act, got, inner, mixer):
+def ffn_grads(hidden, out_grad, w_gate, w_up, w_down, d_gate, d_up, act, mixer):
+    hid_own = hidden[0]
     own, width = hid_own.shape
     units = w_gate.shape[1]
     count = lax.axis_size("seq")
     cut = width // SIDE
-    streams, length, channels = inner.shape
-    block = next(b for b in (256, 128) if units % (b * CHUNKS) == 0)
+    block = units // CHUNKS
     more = count // SIDE // SIDE
     rows = cut // (more * SIDE)
     tokens = own * SIDE
     low = jnp.bfloat16
     column = lambda rows: pl.BlockSpec((rows, block), lambda i: (0, i))
-    tokens_in = (hid_own, hid_ring, hid_rest, *hid_one, grad_own, grad_ring, grad_rest, *grad_one)
+    tokens_in = (*hidden, *out_grad)
     return pl.pallas_call(
         functools.partial(ffn_kernel, count),
         grid=(units // block,),
         in_specs=[whole(a.shape) for a in tokens_in]
         + [column(width), column(width), pl.BlockSpec((block, width), lambda i: (i, 0))]
         + [column(own)] * 3
-        + [whole(got.shape), in_hbm(), in_hbm()],
-        out_specs=[pl.BlockSpec((3, cut, block), lambda i: (0, 0, i))] + [in_hbm()] * 3,
-        out_shape=[
-            shaped(3, cut, units), shaped(2, *got.shape), shaped(SIDE - 1, streams, length, channels // SIDE),
-            shaped(2, 3, more, 2, rows, units // CHUNKS),
-        ],
+        + [in_hbm()],
+        out_specs=[pl.BlockSpec((3, cut, block), lambda i: (0, 0, i))] + [in_hbm()] * 2,
+        out_shape=[shaped(3, cut, units), shaped(EARLY, 3, more, 2, rows, block), shaped(2, 2, *mixer.shape[2:])],
         scratch_shapes=[pltpu.VMEM((tokens, width), low)] * 2
         + [pltpu.VMEM((cut, tokens), low)] * 2
         + [pltpu.VMEM((tokens, block), low)] * 3
-        + [pltpu.VMEM(got.shape, jnp.float32), pltpu.VMEM((2, 3, more, 2, 2, rows, units // CHUNKS), jnp.float32)]
-        + sems(SIDE + 3) + [pltpu.SemaphoreType.DMA((1,))],
+        + [pltpu.VMEM((EARLY, 3, more, 2, 2, rows, block), jnp.float32)]
+        + [pltpu.VMEM((2, *mixer.shape[2:]), jnp.float32)] * 2
+        + sems(EARLY + 3) + [pltpu.SemaphoreType.DMA((1,))],
         compiler_params=pltpu.CompilerParams(
             collective_id=2, has_side_effects=True, vmem_limit_bytes=56 * 1024 * 1024
         ),
         cost_estimate=spans(36),
-    )(*tokens_in, w_gate, w_up, w_down, d_gate, d_up, act, got, inner, mixer)
+    )(*tokens_in, w_gate, w_up, w_down, d_gate, d_up, act, mixer)
 
 
 class Reduce:
@@ -906,10 +923,10 @@
 
 
 def sum_kernel(
-    count, ffn, mixer_in, passed_in, near_in, turned, d_own, d_side, small,
+    count, ffn, mixer_in, passed_in, d_inner, near_in, turned, d_own, small,
     ffn_out, mixer_out, inner_out, small_out,
-    d_all, kept, near, next_, mixer, m_passed, m_arrived, inner, i_got, i_passed, i_arrived, m_done, m_back, i_done, i_back, s_near, s_next, s_done, s_line,
-    ffn_send, ffn_recv, m_send, m_recv, i_send, i_recv, back_send, back_recv, s_send, s_recv, local,
+    d_all, kept, near, next_, mixer, m_passed, m_arrived, d_side, inner, i_got, i_passed, i_arrived, m_done, m_back, i_done, i_back, s_near, s_next, s_done, s_line,
+    ffn_send, ffn_recv, m_send, m_recv, i_send, i_recv, back_send, back_recv, s_send, s_recv, d_send, d_recv, local,
 ):
     where = Place(count)
     place = where.place
@@ -920,11 +937,11 @@
     loads = [pltpu.make_async_copy(mixer_in, mixer, local.at[0]), pltpu.make_async_copy(passed_in, m_passed, local.at[1])]
     keeps = [
         pltpu.make_async_copy(
-            ffn.at[:, :, :, odd, :, cols[c]] if c % 2 == 0 else ffn.at[:, :, far, :, :, cols[c]], kept.at[c], local.at[2 + c]
+            ffn.at[:, :, :, odd, :, cols[c]] if c % 2 == 0 else ffn.at[:, :, far, :, :, cols[c]], kept.at[c], local.at[3 + c]
         )
         for c in range(CHUNKS)
     ]
-    nears = [pltpu.make_async_copy(near_in.at[c], near.at[c], local.at[2 + CHUNKS + c]) for c in range(2)]
+    nears = [pltpu.make_async_copy(near_in.at[c], near.at[c], local.at[3 + CHUNKS + c]) for c in range(EARLY)]
     for c in loads + nears + keeps:
         c.start()
     where.greet()
@@ -933,8 +950,18 @@
             ffn.at[:, :, :, 1 - odd, :, cols[c]] if c % 2 == 0 else ffn.at[:, :, 1 - far, :, :, cols[c]],
             near.at[c], ffn_send, ffn_recv, c, where.member[1 + c % 2],
         )
-        for c in range(2, CHUNKS)
+        for c in range(EARLY, CHUNKS)
     }
+    size = inner.shape[3]
+    quarters = [
+        remote(
+            d_inner.at[:, :, pl.ds(pl.multiple_of((place ^ k) * size, 128), size)], d_side.at[k - 1],
+            d_send, d_recv, k - 1, where.member[k],
+        )
+        for k in range(1, SIDE)
+    ]
+    for c in quarters:
+        c.start()
     for c in first.values():
         c.start()
     groups, half = where.groups, s_near.shape[3]
@@ -959,10 +986,12 @@
     for c in loads:
         c.wait()
     line.start_three(False)
-    for c in range(2):
+    for c in range(EARLY):
         nears[c].wait()
         keeps[c].wait()
         again(c)
+    for c in quarters:
+        c.wait_recv()
     own = d_own.shape[0]
     part = own // 2
     d_all[:own, :] = d_own[...]
@@ -986,7 +1015,7 @@
     ]
     for c in s_second:
         c.start()
-    for c in range(2, CHUNKS):
+    for c in range(EARLY, CHUNKS):
         keeps[c].wait()
         first[c].wait_recv()
         again(c)
@@ -1033,11 +1062,13 @@
     small_out[...] = total
     for c in list(first.values()) + list(second.values()) + spreads + s_first + s_second + s_last:
         c.wait_send()
+    for c in quarters:
+        c.wait_send()
     line.finish(3)
     other.finish(1)
 
 
-def sum_grads(ffn, mixer, passed, near, turned, d_own, d_side, small):
+def sum_grads(ffn, mixer, passed, d_inner, near, turned, d_own, small):
     count = lax.axis_size("seq")
     more = count // SIDE // SIDE
     cut, units = ffn.shape[1:]
@@ -1050,7 +1081,7 @@
         functools.partial(sum_kernel, count),
         out_shape=[shaped(3, more, rows, units), shaped(2, more, rows, size * SIDE), shaped(1, more, rows, size * SIDE),
                    shaped(tall, LANES)],
-        in_specs=[in_hbm()] * 4 + [in_vmem()] * 4,
+        in_specs=[in_hbm()] * 5 + [in_vmem()] * 3,
         out_specs=[in_vmem()] * 4,
         scratch_shapes=[
             pltpu.VMEM((turned.shape[1], size), jnp.bfloat16),
@@ -1058,24 +1089,100 @@
             v(CHUNKS, 3, more, 2, rows, units // CHUNKS),
             v(CHUNKS, 3, more, rows, units // CHUNKS),
             v(2, SIDE, cut, size), v(2, 2, cut, size), v(2, 2, cut, size),
+            v(SIDE - 1, *d_inner.shape[:2], size),
             v(1, SIDE, cut, size), v(1, cut, size), v(2, 1, cut, size), v(2, 1, cut, size),
             v(2, more, SIDE, rows, size), v(SIDE, 2, more, rows, size),
             v(1, more, SIDE, rows, size), v(SIDE, 1, more, rows, size),
             v(2, groups, 2, tall // 2, LANES), v(2, groups, tall // 2, LANES), v(groups, tall, LANES), v(groups, tall, LANES),
         ]
-        + sems(2 * CHUNKS) + sems(REDUCE_SEMS) + sems(REDUCE_SEMS) + sems(2 * SIDE) + sems(3 + groups) + [pltpu.SemaphoreType.DMA((4 + CHUNKS,))],
+        + sems(2 * CHUNKS) + sems(REDUCE_SEMS) + sems(REDUCE_SEMS) + sems(2 * SIDE) + sems(3 + groups) + sems(SIDE) + [pltpu.SemaphoreType.DMA((3 + CHUNKS + EARLY,))],
         compiler_params=pltpu.CompilerParams(
             collective_id=3, has_side_effects=True, vmem_limit_bytes=58 * 1024 * 1024
         ),
         cost_estimate=spans(100),
-    )(ffn.reshape(3, more, 2, 2, rows, units), mixer, passed, near, turned, d_own, d_side, small.reshape(groups, 2, 2, tall, LANES))
+    )(ffn.reshape(3, more, 2, 2, rows, units), mixer, passed, d_inner, near, turned, d_own, small.reshape(groups, 2, 2, tall, LANES))
+
+
+def middle_kernel(
+    count, hid, grad, wg, wu, wd, hidden, y,
+    dg, du, act, ffn, d_hid, up_one, down_one, y_side, sends, recvs,
+):
+    where = Place(count)
+    z, place = where.z, where.place
+    width = y_side.shape[-1]
+    quarters = [
+        remote(
+            y.at[:, :, pl.ds(pl.multiple_of((place ^ k) * width, 128), width)], y_side.at[k - 1],
+            sends, recvs, k - 1, where.member[k],
+        )
+        for k in range(1, SIDE)
+    ]
+    mine = hidden.at[where.head]
+    up = remote(mine, up_one, sends, recvs, SIDE - 1, where.above)
+    down = remote(mine, down_one, sends, recvs, SIDE, where.below)
+
+    @pl.when(pl.program_id(0) == 0)
+    def _():
+        where.greet()
+        pl.when(z < SIDE - 1)(up.start)
+        pl.when(z > 0)(down.start)
+        for c in quarters:
+            c.start()
+        ffn[...] = jnp.zeros_like(ffn)
+        d_hid[...] = jnp.zeros_like(d_hid)
+
+    gate = dot(hid[...], wg[...])
+    raised = dot(hid[...], wu[...])
+    d_act = dot_back(grad[...], wd[...])
+    sig = 1.0 / (1.0 + jnp.exp(-gate))
+    silu = gate * sig
+    dg[...] = (d_act * raised * (sig + silu * (1.0 - sig))).astype(dg.dtype)
+    du[...] = (d_act * silu).astype(du.dtype)
+    act[...] = (silu * raised).astype(act.dtype)
+    ffn[...] += dot(act[...], wd[...])
+    d_hid[...] += dot_back(dg[...], wg[...]) + dot_back(du[...], wu[...])
+
+    @pl.when(pl.program_id(0) == pl.num_programs(0) - 1)
+    def _():
+        for c in quarters:
+            c.wait()
+        pl.when(z < SIDE - 1)(up.wait_send)
+        pl.when(z > 0)(down.wait_send)
+        pl.when(z > 0)(up.wait_recv)
+        pl.when(z < SIDE - 1)(down.wait_recv)
+
+
+def feed_forward(hid, grad, w_gate, w_up, w_down, hidden, y):
+    own, width = hid.shape
+    units = w_gate.shape[1]
+    count = lax.axis_size("seq")
+    streams, length, channels = y.shape
+    block = next(b for b in (256, 128) if units % b == 0)
+    column = lambda rows: pl.BlockSpec((rows, block), lambda i: (0, i))
+    low = jax.ShapeDtypeStruct((own, units), jnp.bfloat16)
+    flat = shaped(own, width)
+    one = shaped(length, width)
+    return pl.pallas_call(
+        functools.partial(middle_kernel, count),
+        grid=(units // block,),
+        in_specs=[whole(hid.shape), whole(grad.shape), column(width), column(width),
+                  pl.BlockSpec((block, width), lambda i: (i, 0)), in_hbm(), in_hbm()],
+        out_specs=[column(own)] * 3 + [whole(flat.shape)] * 2 + [in_hbm()] * 3,
+        out_shape=[low, low, low, flat, flat, one, one, shaped(SIDE - 1, streams, length, channels // SIDE)],
+        scratch_shapes=sems(SIDE + 1),
+        compiler_params=pltpu.CompilerParams(
+            collective_id=4, has_side_effects=True, vmem_limit_bytes=24 * 1024 * 1024
+        ),
+        cost_estimate=spans(20),
+    )(hid, grad, w_gate, w_up, w_down, hidden, y)
 
 
 LANES = 128
 
 
-def gather_kernel(places, w_step, log_decay, taps, rows, select, out):
-    ranks, states, taps_n = w_step.shape[0], log_decay.shape[0], taps.shape[0]
+def gather_kernel(places, w_step, log_decay, select, *refs):
+    rows, out = refs[:-1], refs[-1]
+    ranks, states = w_step.shape[0], log_decay.shape[0]
     size = w_step.shape[1] // places
     high = select.shape[0] // places
     low = ranks + states + 16
@@ -1084,16 +1191,15 @@
         cols = slice(p * size, (p + 1) * size)
         out[p, :ranks, :size] = w_step[:, cols]
         out[p, ranks : ranks + states, :size] = log_decay[:, cols]
-        at = ranks + states
-        out[p, at : at + 8, :size] = jnp.concatenate([taps[:, cols], rows[: 8 - taps_n, cols]], axis=0)
-        out[p, at + 8 : at + 16, :size] = rows[8 - taps_n : 16 - taps_n, cols]
+        for k, row in enumerate(rows):
+            out[p, ranks + states + k : ranks + states + k + 1, :size] = row[:, cols]
         for b in range(select.shape[1] // LANES):
             out[p, low + b * high : low + (b + 1) * high, :] = select[
                 p * high : (p + 1) * high, b * LANES : (b + 1) * LANES
             ]
 
 
-def gather_small(w_step, log_decay, taps, rows, select):
+def gather_small(w_step, log_decay, select, rows):
     places = lax.axis_size("seq")
     channels = w_step.shape[1]
     tall = w_step.shape[0] + log_decay.shape[0] + 16 + select.shape[0] // places * (channels // LANES)
@@ -1101,11 +1207,48 @@
     return pl.pallas_call(
         functools.partial(gather_kernel, places),
         out_shape=shaped(places, tall, LANES),
-        in_specs=[in_vmem()] * 5,
+        in_specs=[in_vmem()] * (3 + len(rows)),
         out_specs=in_vmem(),
-        compiler_params=params(24),
+        compiler_params=params(12),
         cost_estimate=spans(4),
-    )(w_step, log_decay, taps, rows, select)
+    )(w_step, log_decay, select, *[row.reshape(1, -1) for row in rows])
+
+
+def place_kernel(rank, states, taps, high, size, gains, ffn, mixer, inner, small, *outs):
+    gate, up, down, mixout, outgate, w_in, w_step, log_decay, conv_taps, w_select = outs[:10]
+    gate[...] = ffn[0]
+    up[...] = ffn[1]
+    down[...] = ffn[2]
+    outgate[...] = mixer[0]
+    mixout[...] = mixer[1]
+    w_in[...] = inner[0]
+    w_step[...] = small[:rank, :size]
+    at = rank + states
+    log_decay[...] = small[rank:at, :size]
+    conv_taps[...] = small[at : at + taps, :size]
+    at += taps
+    for k, row in enumerate(outs[10:15]):
+        row[...] = small[at + k : at + k + 1, :size]
+    outs[15][...] = small[at + 5 : at + 6, :gains]
+    at = rank + states + 16
+    for b in range(w_select.shape[1] // LANES):
+        w_select[:, b * LANES : (b + 1) * LANES] = small[at + b * high : at + (b + 1) * high, :]
+
+
+def place_all(rank, states, taps, high, gains, channels, ffn, mixer, inner, small):
+    rows, units = ffn.shape[1:]
+    size = channels // lax.axis_size("seq")
+    width = mixer.shape[2]
+    shapes = [(rows, units), (rows, units), (rows, units), (rows, width), (rows, width), (rows, width), (rank, size),
+              (states, size), (taps, size), (high, channels)] + [(1, size)] * 5 + [(1, gains)]
+    return pl.pallas_call(
+        functools.partial(place_kernel, rank, states, taps, high, size, gains),
+        out_shape=[shaped(*shape) for shape in shapes],
+        in_specs=[in_vmem()] * 4,
+        out_specs=[in_vmem()] * len(shapes),
+        compiler_params=params(40),
+        cost_estimate=spans(6),
+    )(ffn, mixer, inner, small)
 
 
 epsilon = 1e-06
@@ -1199,6 +1342,7 @@
     stride = count // SIDE
     here = lax.axis_index("seq")
     z, place = here // stride, here % SIDE
+    size = channels // SIDE
     low = jnp.bfloat16
 
     grad_in = out_grad.astype(jnp.float32)
@@ -1250,17 +1394,13 @@
     resid = source + mix
     hidden, scale_ffn = norm_forward(resid, norm_ffn)
     hidden_low = hidden.astype(low)
-    mine_hidden = own_stream(hidden)
-    line_hidden = [send(mine_hidden, links(stride)), send(mine_hidden, links(-stride))]
-    gate = matmul(hidden_low, w_gate)
-    up = matmul(hidden_low, w_up)
-    act_low = (jax.nn.silu(gate) * up).astype(low)
-    ffn = head_sum(matmul(act_low, w_down))
-    output = (resid + ffn).astype(low)
-    d_act = matmul_back(out_grad, w_down)
-    d_gate = (d_act * up * silu_slope(gate)).astype(low)
-    d_up = (d_act * jax.nn.silu(gate)).astype(low)
-    d_hidden = head_sum(matmul_back(d_gate, w_gate) + matmul_back(d_up, w_up))
+    flat = lambda block: block.reshape(-1, block.shape[-1])
+    like = lambda block: block.reshape(streams, length, -1)
+    d_gate, d_up, act_low, ffn, d_hidden, *line_hidden, y_side = feed_forward(
+        flat(hidden_low), flat(out_grad), w_gate, w_up, w_down, hidden, y
+    )
+    output = (resid + head_sum(like(ffn))).astype(low)
+    d_hidden = head_sum(like(d_hidden))
     d_resid_norm, grad_norm_ffn = norm_backward(resid, scale_ffn, norm_ffn, d_hidden)
     d_resid = grad_in + d_resid_norm
     d_mix = d_resid.astype(low)
@@ -1268,22 +1408,24 @@
     d_y = d_mixed * gate_z
     d_outgate = (d_mixed * y * silu_slope(outgate)).astype(low)
     grad_skip_gain = jnp.sum(d_y * value, axis=(0, 1))
-    d_step, d_scan, db_wide, dc_wide, decay_sum, hid_ring, hid_rest, mix_side, mix_rest, y_side = scan_backward(
-        fall, step, value, d_y, b_wide, c_wide, rate, first, line_hidden, own_stream(d_resid), y
-    )
-
-    flat = lambda block: block.reshape(-1, block.shape[-1])
-    size = channels // SIDE
+    (
+        d_step, d_scan, db_wide, dc_wide, decay_sum, hid_ring, hid_rest, mix_side, mix_rest, grad_end, grad_rest_end,
+    ) = scan_backward(
+        fall, step, value, d_y, b_wide, c_wide, rate, first, line_hidden, own_stream(d_resid), grad_ring[1]
+    )
+
     mixer, turned = mixer_grads(
         flat(normed_low), [norm_near, norm_next, side_far, side_rest], flat(d_mix), [mix_side, mix_rest],
         flat(part_of(y, place, size, 2)), y_side,
         w_outgate, w_mixout,
     )
     mixer = mixer.reshape(2, SIDE, width // SIDE, size)
-    got = send(mixer[:, SIDE - 1], [(i, i + stride) for i in range(stride)]) + send(
-        mixer[:, 0], [(i, i - stride) for i in range(count - stride, count)]
-    )
-    d_step = after(d_step, mixer)
+    ffn, near, passed = ffn_grads(
+        (flat(hidden_low), *line_hidden, hid_ring, hid_rest),
+        (flat(out_grad), *line_grad, grad_ring[1], grad_rest, grad_end, grad_rest_end),
+        w_gate, w_up, w_down, d_gate, d_up, act_low, mixer,
+    )
+    d_step = after(d_step, ffn)
 
     d_value = d_y * skip_gain + d_scan
     d_step_pre = (d_step * jax.nn.sigmoid(step_pre)).astype(low)
@@ -1315,25 +1457,22 @@
         masked = d_value_pre * masks[k]
         tap_grads.append(jnp.sum(masked * ext_val[:, k : k + length], axis=(0, 1)))
         d_ext = d_ext + jnp.pad(masked * conv_taps[k], ((0, 0), (k, lead - k), (0, 0)))
-    grad_conv_taps = jnp.stack(tap_grads)
     rim_grad = send(d_ext[:, :lead], links(-1))
     d_inner = (d_ext[:, lead:] + jnp.pad(rim_grad, ((0, 0), (length - lead, 0), (0, 0)))).astype(low)
     d_normed = head_sum(matmul_back(d_inner, w_inner) + matmul_back(d_outgate, w_outgate))
     d_source, grad_norm_mix = norm_backward(source, scale_mix, norm_mix, d_normed)
     tokens_grad = d_resid + d_source
 
+    gains = grad_select_gain.reshape(count, -1)
+    spread = jnp.pad(gains, ((0, 0), (0, channels // count - gains.shape[1]))).reshape(channels)
     pad = lambda v: jnp.pad(v, (0, channels - v.shape[0]))
-    rows = [grad_conv_bias, grad_step_bias, grad_skip_gain, pad(grad_norm_mix), pad(grad_norm_ffn)]
-    gains = grad_select_gain.reshape(count, -1)
-    rows.append(jnp.pad(gains, ((0, 0), (0, channels // count - gains.shape[1]))).reshape(channels))
-    rows = jnp.stack(rows + [jnp.zeros_like(grad_conv_bias)] * (16 - taps - len(rows)))
-    small = gather_small(grad_w_step, decay_sum * decay_rate, grad_conv_taps, rows, grad_w_select)
-    ffn, passed, d_side, near = ffn_grads(
-        flat(hidden_low), hid_ring, hid_rest, line_hidden, flat(out_grad), grad_ring, grad_rest, line_grad, w_gate, w_up, w_down,
-        flat(d_gate), flat(d_up), flat(act_low), got, d_inner.astype(jnp.float32), mixer,
-    )
+    rows = tap_grads + [
+        grad_conv_bias, grad_step_bias, grad_skip_gain, pad(grad_norm_mix), pad(grad_norm_ffn), spread
+    ]
+    grad_w_step = after(grad_w_step, tokens_grad)
+    small = gather_small(grad_w_step, decay_sum * decay_rate, grad_w_select, rows)
     ffn, mixer, inner, tall = sum_grads(
-        ffn, mixer, passed, near, turned, flat(part_of(d_inner, place, size, 2)), d_side, small
+        ffn, mixer, passed, d_inner.astype(jnp.float32), near, turned, flat(part_of(d_inner, place, size, 2)), small
     )
     if count > SIDE * SIDE:
         groups = [[a * stride + b + SIDE * k for k in range(stride // SIDE)] for a in range(SIDE) for b in range(SIDE)]
@@ -1342,30 +1481,30 @@
         )
     else:
         ffn, mixer, inner = (part[:, 0] for part in (ffn, mixer, inner))
-    at = rank + states
-    high = grad_w_select.shape[0] // count
-    broad = tall[at + 16 : at + 16 + high * channels // LANES].reshape(channels // LANES, high, LANES)
-    broad = jnp.swapaxes(broad, 0, 1).reshape(high, channels)
-    tall = tall[:, : channels // count]
+    outs = place_all(
+        rank, states, taps, grad_w_select.shape[0] // count, gains.shape[1], channels, ffn, mixer, inner, tall
+    )
+    gate, up, down, mixout, outgate, w_in, d_w_step, d_log_decay, d_taps, d_select = outs[:10]
+    conv, bias, skip, mix_gain, ffn_gain, select_gains = (row[0] for row in outs[10:])
     return (
         output,
         tokens_grad,
-        tall[at + taps + 3],
-        inner[0],
-        mixer[0],
-        tall[at : at + taps],
-        tall[at + taps],
-        broad.T,
-        tall[at + taps + 5, : gains.shape[1]],
-        tall[:rank],
-        tall[at + taps + 1],
-        tall[rank:at].T,
-        tall[at + taps + 2],
-        mixer[1].T,
-        tall[at + taps + 4],
-        ffn[0],
-        ffn[1],
-        ffn[2].T,
+        mix_gain,
+        w_in,
+        outgate,
+        d_taps,
+        conv,
+        d_select.T,
+        select_gains,
+        d_w_step,
+        bias,
+        d_log_decay.T,
+        skip,
+        mixout.T,
+        ffn_gain,
+        gate,
+        up,
+        down.T,
     )
 
 

time: 468 us -> 458 us (0.979)
  matrix products: 37.4 us -> 26.4 us
  Pallas kernels: 308 us -> 316 us
  starting transfers between devices: 22.6 us -> 16.4 us
  waiting for transfers between devices: 15.3 us -> 9.9 us
    pallas_call x0 -> x2, Pallas kernels: none -> 25.9 us  [the longest x1 23.6 us: feed_forward(): pl.pallas_call(functools.partial(middle_kernel, count), grid=(units // bl...]
    unnamed x197 -> x244, local copies, waits for them, and re-layouts: 12.8 us -> 29.9 us
    pallas_call x1, Pallas kernels: 55.5 us -> 39.9 us  [scan_forward(): pl.pallas_call(functools.partial(forward_kernel, count), out_shape=[shape...]
    dot_general x8 -> x5, matrix products: 17.8 us -> 10.7 us  [matmul(): return jnp.dot(left, right, preferred_element_type=jnp.float32)]
    pallas_call x1, Pallas kernels: 97.8 us -> 105 us  [sum_grads(): pl.pallas_call(functools.partial(sum_kernel, count), out_shape=[shaped(3,...]
    transpose x4 -> x0, local copies, waits for them, and re-layouts: 6.49 us -> none  [the longest x1 2.33 us: body(): mixer[1]]
    ppermute x16 -> x12, starting transfers between devices: 22.6 us -> 16.4 us  [send(): return lax.ppermute(block, axis, route)]
    ppermute x16 -> x12, waiting for transfers between devices: 15.3 us -> 9.9 us  [send(): return lax.ppermute(block, axis, route)]
  transfers between devices with their start and end apart: 16 -> 12, of which waited for: 8 -> 3; matrix products, arithmetic and copies ran while one was open for 12% -> 9% of each run, Pallas kernels for 14% -> 0%
where the time goes in v5:
time: 458 us; the launch traced here: 449 us
  Pallas kernels  316 us (69%)
  local copies, waits for them, and re-layouts  45 us (10%)
  other arithmetic  32.4 us (7%)
  matrix products  26.4 us (6%)
  starting transfers between devices  16.4 us (4%)
  waiting for transfers between devices  9.9 us (2%)
    pallas_call x1, Pallas kernels, sum_grads(): pl.pallas_call(functools.partial(sum_kernel, count), out_shape=[shaped(3,...  105 us
    pallas_call x1, Pallas kernels, scan_backward(): pl.pallas_call(functools.partial(backward_kernel, count), out_shape=[flat...  69.8 us
    pallas_call x1, Pallas kernels, ffn_grads(): pl.pallas_call(functools.partial(ffn_kernel, count), grid=(units // block...  62.4 us
    pallas_call x1, Pallas kernels, scan_forward(): pl.pallas_call(functools.partial(forward_kernel, count), out_shape=[shape...  39.9 us
    unnamed x244, local copies, waits for them, and re-layouts  29.9 us
    pallas_call x1, Pallas kernels, feed_forward(): pl.pallas_call(functools.partial(middle_kernel, count), grid=(units // bl...  23.6 us
    ppermute x12, starting transfers between devices, send(): return lax.ppermute(block, axis, route)  16.4 us
    dot_general x5, matrix products, matmul_back(): lax.dot_general(left, right, (((left.ndim - 1,), (1,)), ((), ())), prefer...  13.2 us
  transfers between devices with their start and end apart: 12, of which 3 were waited for; matrix products, arithmetic and copies ran while one was open for 9% of the time, Pallas kernels for 0%

profile of v5, /device:TPU:0, one launch (start us, length us, event | category | flops | bytes accessed | tf_op | source)
XLA Modules:
  0.0 448.7 jit_solution(12677019787376479375)
XLA Ops:
  2.4 4.8 %collective-permute-start = (f32[2,3,1664]{2,1,0:T(4,128)S(1)}, f32[2,3,1664]{2,1,0:T(4,128)S(1)}, u32[]{:S(2)}, u32[]{:S(2)}) collective-permute-start(f32[2,3,1664]{2,1,0:T(4,128)S(1)} %pad_maximum_fusion.2), channel_id=1, source_target_pairs={{0,2},{2,4},{4,6},{6,8},{8,10},{10,12},{12,14},{14,16},{16,18},{18... | collective-permute-start | bytes 119816 | tf_op jit(solution)/shard_map/ppermute | solution.py:1268
  14.4 4.6 %collective-permute-start.2 = (f32[128,1536]{1,0:T(8,128)}, f32[128,1536]{1,0:T(8,128)S(1)}, u32[]{:S(2)}, u32[]{:S(2)}) collective-permute-start(f32[128,1536]{1,0:T(8,128)} %bitcast_convert_fusion), channel_id=1, source_target_pairs={{0,8},{2,10},{4,12},{6,14},{8,16},{10,18},{12,20},{14,22},{16,24},... | collective-permute-start | bytes 2359304 | tf_op jit(solution)/shard_map/ppermute | solution.py:1268
  26.1 2.5 fusion.16
  29.3 2.5 fusion.6
  40.9 4.7 %compare_select_fusion = (f32[2,128,1536]{2,1,0:T(8,128)}, f32[2,128,1536]{2,1,0:T(8,128)S(1)}, f32[2,128,1536]{2,1,0:T(8,128)S(1)}, f32[2,128,1536]{2,1,0:T(8,128)}) fusion(pred[2,128]{1,0:T(4,128)(4,1)} %get-tuple-element.178, f32[2,128,1536]{2,1,0:T(8,128)} %copy-done.61, f32[1536]{0:T(1024)} %param.30, bf16[96,1536]{1,0:T(8,128)(2,1)} %param.29, ...), kind=kOutput, calls=%fused_computation.12 | convolution fusion | flops 80683008 | bytes 8267776 | tf_op jit(solution)/shard_map/dot_general | solution.py:1288
  47.4 39.9 %shard_map.322 = (f32[2,128,1536]{2,1,0:T(8,128)S(1)}, f32[2,16,1536]{2,1,0:T(8,128)S(1)}, f32[3,128,1536]{2,1,0:T(8,128)S(1)}, f32[3,128,1536]{2,1,0:T(8,128)S(...) custom-call(f32[2,128,1536]{2,1,0:T(8,128)S(1)} %get-tuple-element.170.fall, ...), custom_call_target="tpu_custom_call" | custom-call | flops 4400000000 | bytes 12000000 | tf_op jit(solution)/shard_map/pallas_call | solution.py:637
  96.3 3.0 collective-permute-done.6
  101.3 23.6 %shard_map.323 = (bf16[256,2048]{1,0:T(8,128)(2,1)S(1)}, bf16[256,2048]{1,0:T(8,128)(2,1)S(1)}, bf16[256,2048]{1,0:T(8,128)(2,1)S(1)}, f32[256,1536]{1,0:T(8,128...) custom-call(bf16[256,1536]{1,0:T(8,128)(2,1)S(1)} %bitcast.93, ...), custom_call_target="tpu_custom_call" | custom-call | flops 2200000000 | bytes 6000000 | tf_op jit(solution)/shard_map/pallas_call | solution.py:1165
  133.5 2.9 collective-permute-done.8
  138.6 4.2 fusion.50
  144.8 3.0 multiply_reduce_fusion.2
  147.9 69.8 %shard_map.324 = (f32[2,128,1536]{2,1,0:T(8,128)S(1)}, f32[2,128,1536]{2,1,0:T(8,128)S(1)}, f32[2,2048,128]{2,1,0:T(8,128)}, f32[2,2048,128]{2,1,0:T(8,128)}, f3...) custom-call(f32[2,128,1536]{2,1,0:T(8,128)S(1)} %copy-done.45, ...), custom_call_target="tpu_custom_call" | custom-call | flops 6819999744 | bytes 18600000 | tf_op jit(solution)/shard_map/pallas_call | solution.py:662
  217.9 2.7 copy-done.12
  222.3 12.4 %shard_map.325 = (f32[2,1536,384]{2,1,0:T(8,128)}, bf16[1536,1024]{1,0:T(8,128)(2,1)}) custom-call(bf16[256,1536]{1,0:T(8,128)(2,1)S(1)} %bitcast.96, f32[128,1536]{1,0:T(8,128)S(1)} %copy-done.27, f32[128,1536]{1,0:T(8,128)S(1)} %copy-done.25, f32[128,1536]{1,0:T(8,128)S(1)} %copy-done.29, f32[3,128,1536]{2,1,0:T(8,128)S(1)} %copy-done.11, ...), custom_call_target="tpu_custom_call" | custom-call | flops 1320000000 | bytes 3600000 | tf_op jit(solution)/shard_map/pallas_call | solution.py:114
  234.7 62.4 %shard_map.326 = (f32[3,384,2048]{2,1,0:T(8,128)}, f32[6,3,1,2,96,256]{5,4,3,2,1,0:T(8,128)}, f32[2,2,384,384]{3,2,1,0:T(8,128)}) custom-call(bf16[256,1536]{1,0:T(8,128)(2,1)} %bitcast.94, f32[128,1536]{1,0:T(8,128)} %copy-done.32, f32[128,1536]{1,0:T(8,128)} %copy-done.34, f32[3,128,1536]{2,1,0:T(8,128)} %get-tuple-element.85.hid_ring, ...), custom_call_target="tpu_custom_call" | custom-call | flops 3960000000 | bytes 10800000 | tf_op jit(solution)/shard_map/pallas_call | solution.py:825
  297.1 2.2 reduce_sum.232
  305.0 5.0 %fusion.4 = f32[2,128,1536]{2,1,0:T(8,128)S(1)} fusion(bf16[1536,1536]{1,0:T(8,128)(2,1)} %refs_10_.1, f32[2,128,1536]{2,1,0:T(8,128)} %get-tuple-element.184, f32[2,128,1536]{2,1,0:T(8,128)S(1)} %copy-done.3, f32[2,128,1536]{2,1,0:T(8,128)} %fusion.6), kind=kOutput, calls=%fused_computation.4 | convolution fusion | flops 1211891712 | bytes 11010048 | tf_op jit(solution)/shard_map/dot_general | solution.py:1292
  310.8 2.2 multiply_reduce_fusion.3
  315.4 3.9 collective-permute-done.10
  320.7 2.6 fusion.12
  328.4 2.4 multiply_reduce_fusion.1
  330.9 3.6 subtract_add_fusion
  336.3 104.8 %shard_map.328 = (f32[3,1,96,2048]{3,2,1,0:T(8,128)}, f32[2,1,96,1536]{3,2,1,0:T(8,128)}, f32[1,1,96,1536]{3,2,1,0:T(8,128)}, f32[224,128]{1,0:T(8,128)}) custom-call(f32[3,1,2,2,96,2048]{5,4,3,2,1,0:T(8,128)} %bitcast.115, f32[2,4,384,384]{3,2,1,0:T(8,128)} %bitcast.103, f32[2,2,384,384]{3,2,1,0:T(8,128)} %get-tuple-element.103.passed_in, ...), custom_call_target="tpu_custom_call" | custom-call | flops 11000000512 | bytes 30000000 | tf_op jit(solution)/shard_map/pallas_call | solution.py:1080
  446.0 2.3 shard_map.329
  (348 shorter events, 73.7 us)
Async XLA Ops:
  2.4 10.0 %collective-permute-start = (f32[2,3,1664]{2,1,0:T(4,128)S(1)}, f32[2,3,1664]{2,1,0:T(4,128)S(1)}, u32[]{:S(2)}, u32[]{:S(2)}) collective-permute-start(f32[2,3,1664]{2,1,0:T(4,128)S(1)} %pad_maximum_fusion.2), channel_id=1, source_target_pairs={{0,2},{2,4},{4,6},{6,8},{8,10},{10,12},{12,14},{14,16},{16,18},{18... | collective-permute-start | bytes 119816 | tf_op jit(solution)/shard_map/ppermute | solution.py:1268
  13.1 32.5 %collective-permute-start.3 = (f32[128,1536]{1,0:T(8,128)}, f32[128,1536]{1,0:T(8,128)S(1)}, u32[]{:S(2)}, u32[]{:S(2)}) collective-permute-start(f32[128,1536]{1,0:T(8,128)} %bitcast_convert_fusion), channel_id=1, source_target_pairs={{8,0},{10,2},{12,4},{14,6},{16,8},{18,10},{20,12},{22,14},{24,16},... | collective-permute-start | bytes 2359304 | tf_op jit(solution)/shard_map/ppermute | solution.py:1268
  14.4 31.2 %collective-permute-start.2 = (f32[128,1536]{1,0:T(8,128)}, f32[128,1536]{1,0:T(8,128)S(1)}, u32[]{:S(2)}, u32[]{:S(2)}) collective-permute-start(f32[128,1536]{1,0:T(8,128)} %bitcast_convert_fusion), channel_id=1, source_target_pairs={{0,8},{2,10},{4,12},{6,14},{8,16},{10,18},{12,20},{14,22},{16,24},... | collective-permute-start | bytes 2359304 | tf_op jit(solution)/shard_map/ppermute | solution.py:1268
  20.7 25.0 %collective-permute-start.5 = (f32[128,1536]{1,0:T(8,128)}, f32[128,1536]{1,0:T(8,128)S(1)}, u32[]{:S(2)}, u32[]{:S(2)}) collective-permute-start(f32[128,1536]{1,0:T(8,128)} %dynamic-slice_bitcast_fusion.1), channel_id=1, source_target_pairs={{0,4},{2,6},{4,0},{6,2},{8,12},{10,14},{12,8},{14,10},{16,20},{18,... | collective-permute-start | bytes 2359304 | tf_op jit(solution)/shard_map/ppermute | solution.py:1268
  22.3 23.5 %collective-permute-start.4 = (f32[128,1536]{1,0:T(8,128)}, f32[128,1536]{1,0:T(8,128)S(1)}, u32[]{:S(2)}, u32[]{:S(2)}) collective-permute-start(f32[128,1536]{1,0:T(8,128)} %dynamic-slice_bitcast_fusion.1), channel_id=1, source_target_pairs={{0,2},{2,0},{4,6},{6,4},{8,10},{10,8},{12,14},{14,12},{16,18},{18,... | collective-permute-start | bytes 2359304 | tf_op jit(solution)/shard_map/ppermute | solution.py:1268
  29.2 2.7 collective-permute-start.1
  46.4 47.9 %slice-start.4 = ((s8[4718592]{0:T(1024)(128)(4,1)}), s8[4194304]{0:T(1024)(128)(4,1)S(1)}, s32[]{:S(2)}) async-start(s8[4718592]{0:T(1024)(128)(4,1)} %bitcast.104), calls=%async_computation.4 | async-start | bytes 8388608
  47.4 46.0 %copy-start.62 = (f32[2,128,1536]{2,1,0:T(8,128)S(1)}, f32[2,128,1536]{2,1,0:T(8,128)}, u32[]{:S(2)}) copy-start(f32[2,128,1536]{2,1,0:T(8,128)} %copy-done.61) | copy-start | bytes 4718596
  47.4 46.0 %copy-start.94 = (f32[1536]{0:T(1024)S(1)}, f32[1536]{0:T(1024)}, u32[]{:S(2)}) copy-start(f32[1536]{0:T(1024)} %param.32) | copy-start | bytes 18436
  47.4 46.9 %slice-start.5 = ((s8[4718592]{0:T(1024)(128)(4,1)}), s8[524288]{0:T(1024)(128)(4,1)S(1)}, s32[]{:S(2)}) async-start(s8[4718592]{0:T(1024)(128)(4,1)} %bitcast.104), calls=%async_computation.5 | async-start | bytes 1048576
  47.4 46.9 %copy-start.108 = (f32[2,128,1536]{2,1,0:T(8,128)S(1)}, f32[2,128,1536]{2,1,0:T(8,128)}, u32[]{:S(2)}) copy-start(f32[2,128,1536]{2,1,0:T(8,128)} %fusion.6) | copy-start | bytes 4718596
  95.8 3.5 collective-permute-start.6
  130.6 5.8 %collective-permute-start.8 = (f32[2,128,1536]{2,1,0:T(8,128)S(1)}, f32[2,128,1536]{2,1,0:T(8,128)}, u32[]{:S(2)}, u32[]{:S(2)}) collective-permute-start(f32[2,128,1536]{2,1,0:T(8,128)S(1)} %bitcast.89), channel_id=1, source_target_pairs={{0,1},{1,0},{2,3},{3,2},{4,5},{5,4},{6,7},{7,6},{8,9},{9,8},{10,11... | collective-permute-start | bytes 4718600 | tf_op jit(solution)/shard_map/ppermute | solution.py:1268
  130.7 7.9 %collective-permute-start.7 = (f32[2,128,1536]{2,1,0:T(8,128)}, f32[2,128,1536]{2,1,0:T(8,128)}, u32[]{:S(2)}, u32[]{:S(2)}) collective-permute-start(f32[2,128,1536]{2,1,0:T(8,128)} %bitcast.10), channel_id=1, source_target_pairs={{0,1},{1,0},{2,3},{3,2},{4,5},{5,4},{6,7},{7,6},{8,9},{9,8},{10,11... | collective-permute-start | bytes 4718600 | tf_op jit(solution)/shard_map/ppermute | solution.py:1268
  147.8 70.0 %copy-start.46 = (f32[2,128,1536]{2,1,0:T(8,128)}, f32[2,128,1536]{2,1,0:T(8,128)S(1)}, u32[]{:S(2)}) copy-start(f32[2,128,1536]{2,1,0:T(8,128)S(1)} %get-tuple-element.150.g_ref) | copy-start | bytes 4718596
  147.9 69.9 %copy-start.6 = (bf16[2,128,1536]{2,1,0:T(8,128)(2,1)S(1)}, bf16[2,128,1536]{2,1,0:T(8,128)(2,1)}, u32[]{:S(2)}) copy-start(bf16[2,128,1536]{2,1,0:T(8,128)(2,1)} %copy-done.5) | copy-start | bytes 2359300
  147.9 69.9 %copy-start.11 = (f32[3,128,1536]{2,1,0:T(8,128)S(1)}, f32[3,128,1536]{2,1,0:T(8,128)}, u32[]{:S(2)}) copy-start(f32[3,128,1536]{2,1,0:T(8,128)} %copy-done.10) | copy-start | bytes 7077892
  147.9 69.9 %copy-start.20 = (f32[3,2,128,384]{3,2,1,0:T(8,128)S(1)}, f32[3,2,128,384]{3,2,1,0:T(8,128)}, u32[]{:S(2)}) copy-start(f32[3,2,128,384]{3,2,1,0:T(8,128)} %copy-done.19) | copy-start | bytes 3538948
  147.9 69.9 %copy-start.25 = (f32[128,1536]{1,0:T(8,128)S(1)}, f32[128,1536]{1,0:T(8,128)}, u32[]{:S(2)}) copy-start(f32[128,1536]{1,0:T(8,128)} %copy-done.24) | copy-start | bytes 2359300
  147.9 69.9 %copy-start.27 = (f32[128,1536]{1,0:T(8,128)S(1)}, f32[128,1536]{1,0:T(8,128)}, u32[]{:S(2)}) copy-start(f32[128,1536]{1,0:T(8,128)} %copy-done.26) | copy-start | bytes 2359300
  147.9 69.9 %copy-start.29 = (f32[128,1536]{1,0:T(8,128)S(1)}, f32[128,1536]{1,0:T(8,128)}, u32[]{:S(2)}) copy-start(f32[128,1536]{1,0:T(8,128)} %copy-done.28) | copy-start | bytes 2359300
  304.2 5.8 %collective-permute-start.9 = (f32[2,128,128]{1,2,0:T(8,128)S(1)}, f32[2,128,128]{1,2,0:T(8,128)S(1)}, u32[]{:S(2)}, u32[]{:S(2)}) collective-permute-start(f32[2,128,128]{1,2,0:T(8,128)S(1)} %pad_maximum_fusion), channel_id=1, source_target_pairs={{0,1},{1,0},{2,3},{3,2},{4,5},{5,4},{6,7},{7,6},{8,9},{9,8},{10,11... | collective-permute-start | bytes 393224 | tf_op jit(solution)/shard_map/ppermute | solution.py:1268
  313.1 6.2 %collective-permute-start.10 = (f32[2,3,1536]{2,1,0:T(4,128)S(1)}, f32[2,3,1536]{2,1,0:T(4,128)S(1)}, u32[]{:S(2)}, u32[]{:S(2)}) collective-permute-start(f32[2,3,1536]{2,1,0:T(4,128)S(1)} %pad_add_fusion.1), channel_id=1, source_target_pairs={{2,0},{4,2},{6,4},{8,6},{10,8},{12,10},{14,12},{16,14},{18,16},{20... | collective-permute-start | bytes 110600 | tf_op jit(solution)/shard_map/ppermute | solution.py:1268
  323.4 5.1 %collective-permute-start.11 = (f32[2,128,1536]{2,1,0:T(8,128)}, f32[2,128,1536]{2,1,0:T(8,128)}, u32[]{:S(2)}, u32[]{:S(2)}) collective-permute-start(f32[2,128,1536]{2,1,0:T(8,128)} %fusion.12), channel_id=1, source_target_pairs={{0,1},{1,0},{2,3},{3,2},{4,5},{5,4},{6,7},{7,6},{8,9},{9,8},{10,11... | collective-permute-start | bytes 4718600 | tf_op jit(solution)/shard_map/ppermute | solution.py:1268
  (110 other events, 594.2 us)

commit v6 on v5

--- a/solution.py
+++ b/solution.py
@@ -29,15 +29,23 @@
     return pl.CostEstimate(flops=int(us * 1.1e8), bytes_accessed=int(us * 3.0e5), transcendentals=0)
 
 
-def stack_tokens(target, own_ref, more_refs):
-    own = own_ref.shape[0]
-    target[:own, :] = own_ref[...].astype(target.dtype)
-    at = own
-    for ref in more_refs:
-        parts = [ref[k] for k in range(ref.shape[0])] if len(ref.shape) == 3 else [ref[...]]
-        for part in parts:
-            target[at : at + part.shape[0], :] = part.astype(target.dtype)
-            at += part.shape[0]
+def fetch_tokens(blocks, stage, arrived):
+    copies = [pltpu.make_async_copy(block, stage.at[k], arrived.at[k]) for k, block in enumerate(blocks)]
+    for c in copies:
+        c.start()
+
+    def put(target, own):
+        rows, size = own.shape[0], stage.shape[1]
+        target[:rows, :] = own[...].astype(target.dtype)
+        for k, c in enumerate(copies):
+            c.wait()
+            target[rows + k * size : rows + (k + 1) * size, :] = stage[k].astype(target.dtype)
+
+    return put
+
+
+def parts_of(refs):
+    return [part for ref in refs for part in ([ref.at[k] for k in range(ref.shape[0])] if len(ref.shape) == 3 else [ref])]
 
 
 def dot(left, right):
@@ -60,7 +68,7 @@
     y_own, y_side = take(2)
     w_out, w_mix = take(2)
     out, norm_turned = take(2)
-    norm, mix, mixed, d_out, wo, wm, local = take(7)
+    norm, mix, mixed, d_out, wo, wm, local, norm_stage, mix_stage, norm_got, mix_got = take(11)
     own = norm_own.shape[0]
     half = own // 2
 
@@ -74,8 +82,10 @@
         ]
         for c in loads:
             c.start()
-        stack_tokens(norm, norm_own, norm_more)
-        stack_tokens(mix, mix_own, mix_more)
+        put_norm = fetch_tokens(parts_of(norm_more), norm_stage, norm_got)
+        put_mix = fetch_tokens(parts_of(mix_more), mix_stage, mix_got)
+        put_norm(norm, norm_own)
+        put_mix(mix, mix_own)
         for c in loads:
             c.wait()
 
@@ -114,7 +124,8 @@
     return pl.pallas_call(
         functools.partial(mixer_kernel, len(norm_more), len(mix_more)),
         grid=(width // block,),
-        in_specs=[whole(a.shape) for a in operands[:-2]] + [in_hbm()] * 2,
+        in_specs=[whole(norm_own.shape)] + [in_hbm()] * len(norm_more) + [whole(mix_own.shape)] + [in_hbm()] * len(mix_more)
+        + [whole(y_own.shape), whole(y_side.shape)] + [in_hbm()] * 2,
         out_specs=[pl.BlockSpec((2, block, cut), lambda i: (0, i, 0)), row(tokens)],
         out_shape=[
             jax.ShapeDtypeStruct((2, width, cut), jnp.float32),
@@ -122,7 +133,9 @@
         ],
         scratch_shapes=[pltpu.VMEM((tokens, width), low)] * 2
         + [pltpu.VMEM((tokens, cut), low)] * 2
-        + [pltpu.VMEM((width, cut), low), pltpu.VMEM((cut, width), low), pltpu.SemaphoreType.DMA((2,))],
+        + [pltpu.VMEM((width, cut), low), pltpu.VMEM((cut, width), low), pltpu.SemaphoreType.DMA((2,))]
+        + [pltpu.VMEM((2 * SIDE - 2, own // 2, width), jnp.float32)] * 2
+        + [pltpu.SemaphoreType.DMA((2 * SIDE - 2,))] * 2,
         compiler_params=params(40),
         cost_estimate=spans(12),
     )(*operands)
@@ -221,12 +234,11 @@
         pl.when(z >= 1)(self.core(SIDE - 2).wait)
         pl.when(z <= SIDE - 2)(self.core(0).wait)
 
-    def finish(self):
+    def finish_three(self):
         z = self.where.z
-        for step in range(2, SIDE):
-            up, down = self.copies(step)
-            pl.when((z >= step - 1) & (z < SIDE - 1))(up.wait_send)
-            pl.when((z <= SIDE - step) & (z > 0))(down.wait_send)
+        up, down = self.copies(3)
+        pl.when(z == SIDE - 2)(up.wait_send)
+        pl.when(z == 1)(down.wait_send)
         for slot in range(SIDE - 1):
             self.core(slot).wait()
 
@@ -279,26 +291,31 @@
 SIDE_SEMS = 7
 
 
-def chain(where, reverse, ends, total, rate_ref, out_ref, scratch, after_line, after_all):
+def chain(where, reverse, summary, fall, rate_ref, out_ref, scratch, after_line, after_all):
     own, side, mine, line, back, done, sends, recvs = scratch
-    streams, n, channels = ends.shape
+    streams, n, channels = out_ref.shape
     width = channels // SIDE
     rows = streams * n
     place, group, groups = where.place, where.group, where.groups
-    for q in range(SIDE):
-        cols = slice(q * width, (q + 1) * width)
-        own[q, :rows, :] = ends[:, :, cols].reshape(rows, width)
-        own[q, rows : rows + streams, :] = total[:, cols]
-        own[q, rows + streams :, :] = jnp.zeros((own.shape[1] - rows - streams, width), jnp.float32)
-    sides = [remote(own.at[place ^ k], side.at[k], sends, recvs, k, where.member[k]) for k in range(1, SIDE)]
-    for c in sides:
-        c.start()
+    sides = [remote(own.at[k], side.at[k], sends, recvs, k, where.member[k]) for k in range(1, SIDE)]
+
+    def quarter(k, target):
+        cols = pl.ds(pl.multiple_of((place ^ k) * width, 128), width)
+        states = summary(cols)
+        for s in range(streams):
+            target[k, s * n : (s + 1) * n, :] = states[s]
+            target[k, rows + s : rows + s + 1, :] = jnp.sum(fall[s, :, cols], axis=0, keepdims=True)
+        target[k, rows + streams :, :] = jnp.zeros((target.shape[1] - rows - streams, width), jnp.float32)
+
+    for k in range(1, SIDE):
+        quarter(k, own)
+        sides[k - 1].start()
+    quarter(0, side)
     rate = rate_ref[:, pl.ds(pl.multiple_of(place * width, 128), width)]
 
     def through(steps):
         return jnp.concatenate([jnp.exp2(steps[s : s + 1] * rate) for s in range(streams)], axis=0)
 
-    side[0] = own[place]
     for c in sides:
         c.wait_recv()
     state, steps = jnp.zeros((rows, width), jnp.float32), jnp.zeros((streams, width), jnp.float32)
@@ -358,11 +375,6 @@
     ]
 
 
-def sums(fall, total):
-    for s in range(fall.shape[0]):
-        total[s : s + 1, :] = jnp.sum(fall[s], axis=0, keepdims=True)
-
-
 def blocks_of(channels):
     lanes = pieces(channels)
     return lanes, channels // lanes
@@ -375,7 +387,7 @@
 def forward_kernel(
     count, fall, gain, b_ref, c_ref, rate_ref, up_one, down_one, norm_near, norm_next,
     y_ref, first, ring, ring_rest, side_far, side_rest,
-    ends, total, line_send, line_recv, side_send, side_recv, *scratch,
+    line_send, line_recv, side_send, side_recv, *scratch,
 ):
     where = Place(count)
     streams, length, channels = fall.shape
@@ -385,9 +397,9 @@
     where.greet()
     line = Line(where, up_one, down_one, ring, ring_rest, line_send, line_recv)
 
-    def summary(i, _):
-        cols = columns(i, lanes)
+    def summary(cols):
         rate = rate_ref[:, cols]
+        span = rate.shape[1]
 
         def chunk(i, states):
             base = pl.multiple_of(i * ROWS, ROWS)
@@ -399,18 +411,12 @@
                 for j in range(ROWS):
                     b = b_ref[s, pl.ds(pl.multiple_of((base + j) * n, n), n), :]
                     fade = jnp.exp2(d[j : j + 1] * rate)
-                    state = fade * state + x[j : j + 1] * wide(b, lanes)
+                    state = fade * state + x[j : j + 1] * wide(b, span)
                 out.append(state)
             return tuple(out)
 
-        start = tuple(jnp.zeros((n, lanes), jnp.float32) for _ in range(streams))
-        states = lax.fori_loop(0, length // ROWS, chunk, start)
-        for s in range(streams):
-            ends[s, :, cols] = states[s]
-        return 0
-
-    lax.fori_loop(0, blocks, summary, 0)
-    sums(fall, total)
+        start = tuple(jnp.zeros((n, span), jnp.float32) for _ in range(streams))
+        return lax.fori_loop(0, length // ROWS, chunk, start)
 
     half = norm_near.shape[0] // 2
     top, low = pl.ds(0, half), pl.ds(half, half)
@@ -431,7 +437,7 @@
         for c in far + cores[:2]:
             c.start()
 
-    chain(where, False, ends, total, rate_ref, first, scratch, after_line, after_all)
+    chain(where, False, summary, fall, rate_ref, first, scratch, after_line, after_all)
 
     def run(i, _):
         cols = columns(i, lanes)
@@ -472,7 +478,7 @@
 def backward_kernel(
     count, fall, d_ref, v_ref, g_ref, b_ref, c_ref, rate_ref, first_ref, up_one, down_one, mix, grad_middle,
     dstep_ref, dvalue_ref, db_ref, dc_ref, decay_ref, ring, ring_rest, side, side_rest, grad_end, grad_rest,
-    ends, total, last, path, fades, line_send, line_recv, side_send, side_recv, *scratch,
+    db_wide, dc_wide, last, path, fades, line_send, line_recv, side_send, side_recv, *scratch,
 ):
     where = Place(count)
     streams, length, channels = fall.shape
@@ -487,12 +493,28 @@
     sink = remote(grad_middle, grad_end, line_send, line_recv, LINE_SEMS + 1, where.below)
     core = remote(grad_end, grad_rest, line_send, line_recv, LINE_SEMS + 2, where.core)
     square = Side(where, mix, side, side_rest, side_send, side_recv)
-    line.start(2)
+    half = ring.shape[1] // 2
+    steps = []
+    for part in range(2):
+        at = pl.ds(part * half, half)
+        steps.append(
+            (
+                remote(up_one.at[at], ring.at[1, at], line_send, line_recv, LINE_SEMS + 3 + 2 * part, where.above),
+                remote(down_one.at[at], ring.at[1, at], line_send, line_recv, LINE_SEMS + 4 + 2 * part, where.below),
+            )
+        )
+
+    def start_half(part):
+        up, down = steps[part]
+        pl.when((z >= 1) & (z < SIDE - 1))(up.start)
+        pl.when((z <= SIDE - 2) & (z > 0))(down.start)
+
+    start_half(0)
     line.start_cores_of_one()
 
-    def summary(i, _):
-        cols = columns(i, lanes)
+    def summary(cols):
         rate = rate_ref[:, cols]
+        span = rate.shape[1]
 
         def chunk(i, carry):
             base = pl.multiple_of((chunks - 1 - i) * ROWS, ROWS)
@@ -504,29 +526,24 @@
                 for j in reversed(range(ROWS)):
                     at = pl.ds(pl.multiple_of((base + j) * n, n), n)
                     fade = jnp.exp2(d[j : j + 1] * rate)
-                    carried = fade * (g[j : j + 1] * wide(c_ref[s, at, :], lanes) + carried)
+                    carried = fade * (g[j : j + 1] * wide(c_ref[s, at, :], span) + carried)
                 out.append(carried)
             return tuple(out)
 
-        start = tuple(jnp.zeros((n, lanes), jnp.float32) for _ in range(streams))
-        states = lax.fori_loop(0, chunks, chunk, start)
-        for s in range(streams):
-            ends[s, :, cols] = states[s]
-        return 0
-
-    lax.fori_loop(0, blocks, summary, 0)
-    sums(fall, total)
+        start = tuple(jnp.zeros((n, span), jnp.float32) for _ in range(streams))
+        return lax.fori_loop(0, chunks, chunk, start)
 
     def after_line():
-        line.arrive(2)
-        line.start(3)
+        start_half(1)
+        pl.when(z == SIDE - 2)(rise.start)
+        pl.when(z == 1)(sink.start)
 
     def after_all():
         square.start()
 
-    chain(where, True, ends, total, rate_ref, last, scratch, after_line, after_all)
-    db_ref[...] = jnp.zeros_like(db_ref)
-    dc_ref[...] = jnp.zeros_like(dc_ref)
+    chain(where, True, summary, fall, rate_ref, last, scratch, after_line, after_all)
+    db_wide[...] = jnp.zeros_like(db_wide)
+    dc_wide[...] = jnp.zeros_like(dc_wide)
 
     def fold(tile):
         out = tile[:, :128]
@@ -540,8 +557,11 @@
 
         @pl.when(i == blocks // 3)
         def _():
-            pl.when(z == SIDE - 2)(rise.start)
-            pl.when(z == 1)(sink.start)
+            for up, down in steps:
+                pl.when(z >= 2)(up.wait_recv)
+                pl.when(z <= SIDE - 3)(down.wait_recv)
+            line.core(1).start()
+            line.start(3)
 
         @pl.when(i == blocks // 2)
         def _():
@@ -580,8 +600,8 @@
                     at = pl.ds(pl.multiple_of((base + j) * n, n), n)
                     gj = g[j : j + 1]
                     adjoint = gj * wide(c_ref[s, at, :], lanes) + carried
-                    dc_ref[s, at, :] += fold(state * gj)
-                    db_ref[s, at, :] += fold(adjoint * x[j : j + 1])
+                    dc_wide[s, at, :] += fold(state * gj)
+                    db_wide[s, at, :] += fold(adjoint * x[j : j + 1])
                     weights[j] = jnp.sum(adjoint * wide(b_ref[s, at, :], lanes), axis=0, keepdims=True)
                     carried = adjoint * fades[s, at, :]
                     state = path[s, at, :]
@@ -601,12 +621,18 @@
         return 0
 
     lax.fori_loop(0, blocks, run, 0)
+    for s in range(streams):
+        db_ref[s] = jnp.sum(db_wide[s].reshape(length, n, 128), axis=-1)
+        dc_ref[s] = jnp.sum(dc_wide[s].reshape(length, n, 128), axis=-1)
     square.finish()
     line.arrive(3)
     pl.when(z == SIDE - 1)(rise.wait_recv)
     pl.when(z == 0)(sink.wait_recv)
     pl.when((z == 0) | (z == SIDE - 1))(core.start)
-    line.finish()
+    line.finish_three()
+    for up, down in steps:
+        pl.when((z >= 1) & (z < SIDE - 1))(up.wait_send)
+        pl.when((z <= SIDE - 2) & (z > 0))(down.wait_send)
     pl.when(z == SIDE - 2)(rise.wait_send)
     pl.when(z == 1)(sink.wait_send)
     pl.when((z == 0) | (z == SIDE - 1))(core.wait)
@@ -639,11 +665,10 @@
         out_shape=[shaped(streams, length, channels), shaped(streams, n, channels), three, three, shaped(half, width), three],
         in_specs=[in_vmem()] * 5 + [in_hbm()] * 4,
         out_specs=[in_vmem()] * 2 + [in_hbm()] * 4,
-        scratch_shapes=[pltpu.VMEM((streams, n, channels), jnp.float32), pltpu.VMEM((streams, channels), jnp.float32)]
-        + sems(LINE_SEMS) + sems(5)
+        scratch_shapes=sems(LINE_SEMS) + sems(5)
         + chain_scratch(streams, n, channels, count // SIDE),
         compiler_params=pltpu.CompilerParams(
-            collective_id=0, has_side_effects=True, vmem_limit_bytes=24 * 1024 * 1024
+            collective_id=0, has_side_effects=True, vmem_limit_bytes=56 * 1024 * 1024
         ),
         cost_estimate=spans(40),
     )(fall, gain, b_wide, c_wide, rate, *line, norm_near, norm_next)
@@ -656,7 +681,7 @@
     half, width = mix.shape
     lanes, _ = blocks_of(channels)
     three = shaped(SIDE - 1, half, width)
-    tall = shaped(streams, length * n, 128)
+    tall = shaped(streams, length, n)
     flat = shaped(streams, length, channels)
     kept = pltpu.VMEM((streams, length * n, lanes), jnp.float32)
     return pl.pallas_call(
@@ -665,16 +690,16 @@
         in_specs=[in_vmem()] * 8 + [in_hbm()] * 4,
         out_specs=[in_vmem()] * 5 + [in_hbm()] * 6,
         scratch_shapes=[
-            pltpu.VMEM((streams, n, channels), jnp.float32),
-            pltpu.VMEM((streams, channels), jnp.float32),
+            pltpu.VMEM((streams, length * n, 128), jnp.float32),
+            pltpu.VMEM((streams, length * n, 128), jnp.float32),
             pltpu.VMEM((streams, n, channels), jnp.float32),
             kept,
             kept,
         ]
-        + sems(LINE_SEMS + 3) + sems(SIDE_SEMS)
+        + sems(LINE_SEMS + 7) + sems(SIDE_SEMS)
         + chain_scratch(streams, n, channels, count // SIDE),
         compiler_params=pltpu.CompilerParams(
-            collective_id=1, has_side_effects=True, vmem_limit_bytes=40 * 1024 * 1024
+            collective_id=1, has_side_effects=True, vmem_limit_bytes=56 * 1024 * 1024
         ),
         cost_estimate=spans(62),
     )(fall, step, value, d_y, b_wide, c_wide, rate, first, *line, mix, grad_middle)
@@ -684,42 +709,47 @@
 EARLY = 6
 
 
-def stack_line(target, own, z, up, down, middle, first, last, rest, rest_first, rest_last):
-    rows = own.shape[0]
-    size = up.shape[0]
-    target[:rows, :] = own[...].astype(target.dtype)
-
-    def put(slot, block):
-        target[rows + slot * size : rows + (slot + 1) * size, :] = block[...].astype(target.dtype)
-
-    put(1, middle)
-    put(4, rest.at[1])
+def fetch_line(z, up, down, middle, first, last, rest, rest_first, rest_last, stage, arrived):
+    def copy(block, k):
+        return pltpu.make_async_copy(block, stage.at[k], arrived.at[k])
+
+    copy(middle, 1).start()
+    copy(rest.at[1], 4).start()
 
     @pl.when(z >= 1)
     def _():
-        put(2, up)
-        put(5, rest.at[2])
+        copy(up, 2).start()
+        copy(rest.at[2], 5).start()
 
     @pl.when(z < 1)
     def _():
-        put(2, last)
-        put(5, rest_last)
+        copy(last, 2).start()
+        copy(rest_last, 5).start()
 
     @pl.when(z <= SIDE - 2)
     def _():
-        put(0, down)
-        put(3, rest.at[0])
+        copy(down, 0).start()
+        copy(rest.at[0], 3).start()
 
     @pl.when(z > SIDE - 2)
     def _():
-        put(0, first)
-        put(3, rest_first)
+        copy(first, 0).start()
+        copy(rest_first, 3).start()
+
+    def put(target, own):
+        rows, size = own.shape[0], stage.shape[1]
+        target[:rows, :] = own[...].astype(target.dtype)
+        for k in range(2 * SIDE - 2):
+            copy(middle, k).wait()
+            target[rows + k * size : rows + (k + 1) * size, :] = stage[k].astype(target.dtype)
+
+    return put
 
 
 def ffn_kernel(
     count, hid_own, hid_up, hid_down, hid_ring, hid_rest, grad_own, grad_up, grad_down, grad_middle, grad_rest, grad_end, grad_rest_end, wg, wu, wd, dg_own, du_own, act_own,
     mixer, out, near, passed,
-    hid, grad, hid_cut, grad_cut, dg, du, act, stash, got, sent, sends, recvs, local,
+    hid, grad, hid_cut, grad_cut, dg, du, act, stash, got, sent, sends, recvs, local, hid_stage, grad_stage, hid_got, grad_got,
 ):
     own, cut = hid_own.shape[0], hid_cut.shape[0]
     where = Place(count)
@@ -748,15 +778,19 @@
 
     @pl.when(first)
     def _():
+        ring, rest = hid_ring, hid_rest
+        put_hid = fetch_line(
+            z, hid_up, hid_down, ring.at[1], ring.at[0], ring.at[2], rest, rest.at[0], rest.at[2], hid_stage, hid_got
+        )
+        ends = (grad_middle, grad_end, grad_end, grad_rest, grad_rest_end, grad_rest_end)
+        put_grad = fetch_line(z, grad_up, grad_down, *ends, grad_stage, grad_got)
         where.greet()
         fetch.start()
         pl.when(tips)(one.start)
         fetch.wait()
         pl.when(tips)(two.start)
-        ring, rest = hid_ring, hid_rest
-        stack_line(hid, hid_own, z, hid_up, hid_down, ring.at[1], ring.at[0], ring.at[2], rest, rest.at[0], rest.at[2])
-        ends = (grad_middle, grad_end, grad_end, grad_rest, grad_rest_end, grad_rest_end)
-        stack_line(grad, grad_own, z, grad_up, grad_down, *ends)
+        put_hid(hid, hid_own)
+        put_grad(grad, grad_own)
         at = pl.ds(pl.multiple_of(z * cut, 128), cut)
         hid_cut[...] = hid[:, at].T
         grad_cut[...] = grad[:, at].T
@@ -825,7 +859,7 @@
     return pl.pallas_call(
         functools.partial(ffn_kernel, count),
         grid=(units // block,),
-        in_specs=[whole(a.shape) for a in tokens_in]
+        in_specs=[whole(a.shape) if a is hid_own or a is out_grad[0] else in_hbm() for a in tokens_in]
         + [column(width), column(width), pl.BlockSpec((block, width), lambda i: (i, 0))]
         + [column(own)] * 3
         + [in_hbm()],
@@ -836,7 +870,9 @@
         + [pltpu.VMEM((tokens, block), low)] * 3
         + [pltpu.VMEM((EARLY, 3, more, 2, 2, rows, block), jnp.float32)]
         + [pltpu.VMEM((2, *mixer.shape[2:]), jnp.float32)] * 2
-        + sems(EARLY + 3) + [pltpu.SemaphoreType.DMA((1,))],
+        + sems(EARLY + 3) + [pltpu.SemaphoreType.DMA((1,))]
+        + [pltpu.VMEM((2 * SIDE - 2, own // 2, width), jnp.float32)] * 2
+        + [pltpu.SemaphoreType.DMA((2 * SIDE - 2,))] * 2,
         compiler_params=pltpu.CompilerParams(
             collective_id=2, has_side_effects=True, vmem_limit_bytes=56 * 1024 * 1024
         ),
@@ -1171,7 +1207,7 @@
         out_shape=[low, low, low, flat, flat, one, one, shaped(SIDE - 1, streams, length, channels // SIDE)],
         scratch_shapes=sems(SIDE + 1),
         compiler_params=pltpu.CompilerParams(
-            collective_id=4, has_side_effects=True, vmem_limit_bytes=24 * 1024 * 1024
+            collective_id=4, has_side_effects=True, vmem_limit_bytes=56 * 1024 * 1024
         ),
         cost_estimate=spans(20),
     )(hid, grad, w_gate, w_up, w_down, hidden, y)
@@ -1321,11 +1357,6 @@
 def across(small):
     streams, length, n = small.shape
     return jnp.broadcast_to(small.reshape(streams, length * n, 1), (streams, length * n, 128))
-
-
-def along(wide_sum, n):
-    streams, rows, _ = wide_sum.shape
-    return jnp.sum(wide_sum, axis=-1).reshape(streams, rows // n, n)
 
 
 def body(
@@ -1409,7 +1440,7 @@
     d_outgate = (d_mixed * y * silu_slope(outgate)).astype(low)
     grad_skip_gain = jnp.sum(d_y * value, axis=(0, 1))
     (
-        d_step, d_scan, db_wide, dc_wide, decay_sum, hid_ring, hid_rest, mix_side, mix_rest, grad_end, grad_rest_end,
+        d_step, d_scan, d_bsel, d_csel, decay_sum, hid_ring, hid_rest, mix_side, mix_rest, grad_end, grad_rest_end,
     ) = scan_backward(
         fall, step, value, d_y, b_wide, c_wide, rate, first, line_hidden, own_stream(d_resid), grad_ring[1]
     )
@@ -1433,7 +1464,7 @@
     grad_w_step = weight_outer(step_low, d_step_pre)
     d_small = head_sum(
         jnp.concatenate(
-            [matmul_back(d_step_pre, w_step), along(db_wide, states), along(dc_wide, states)], axis=-1
+            [matmul_back(d_step_pre, w_step), d_bsel, d_csel], axis=-1
         )
     )
     d_raw_step, gain_step = norm_backward(

time: 458 us -> 440 us (0.961)
  local copies, waits for them, and re-layouts: 45 us -> 30.7 us
  other arithmetic: 32.4 us -> 27.6 us
    unnamed x244 -> x192, local copies, waits for them, and re-layouts: 29.9 us -> 14.6 us
    pallas_call x1, Pallas kernels: 62.4 us -> 57.3 us  [ffn_grads(): pl.pallas_call(functools.partial(ffn_kernel, count), grid=(units // block...]
  transfers between devices with their start and end apart: 12 -> 12, of which waited for: 3 -> 4; matrix products, arithmetic and copies ran while one was open for 9% -> 8% of each run, Pallas kernels for 0% -> 0%
where the time goes in v6:
time: 440 us; the launch traced here: 433 us
  Pallas kernels  315 us (72%)
  local copies, waits for them, and re-layouts  30.7 us (7%)
  matrix products  30.3 us (7%)
  other arithmetic  27.6 us (6%)
  starting transfers between devices  17.2 us (4%)
  waiting for transfers between devices  9.08 us (2%)
    pallas_call x1, Pallas kernels, sum_grads(): pl.pallas_call(functools.partial(sum_kernel, count), out_shape=[shaped(3,...  106 us
    pallas_call x1, Pallas kernels, scan_backward(): pl.pallas_call(functools.partial(backward_kernel, count), out_shape=[flat...  70.5 us
    pallas_call x1, Pallas kernels, ffn_grads(): pl.pallas_call(functools.partial(ffn_kernel, count), grid=(units // block...  57.3 us
    pallas_call x1, Pallas kernels, scan_forward(): pl.pallas_call(functools.partial(forward_kernel, count), out_shape=[shape...  39.4 us
    pallas_call x1, Pallas kernels, feed_forward(): pl.pallas_call(functools.partial(middle_kernel, count), grid=(units // bl...  26.5 us
    ppermute x12, starting transfers between devices, send(): return lax.ppermute(block, axis, route)  17.2 us
    unnamed x192, local copies, waits for them, and re-layouts  14.6 us
    dot_general x5, matrix products, matmul(): return jnp.dot(left, right, preferred_element_type=jnp.float32)  14.5 us
  transfers between devices with their start and end apart: 12, of which 4 were waited for; matrix products, arithmetic and copies ran while one was open for 8% of the time, Pallas kernels for 0%

profile of v6, /device:TPU:0, one launch (start us, length us, event | category | flops | bytes accessed | tf_op | source)
XLA Modules:
  0.0 432.6 jit_solution(2295638117424300990)
XLA Ops:
  2.4 4.8 %collective-permute-start = (f32[2,3,1664]{2,1,0:T(4,128)S(1)}, f32[2,3,1664]{2,1,0:T(4,128)S(1)}, u32[]{:S(2)}, u32[]{:S(2)}) collective-permute-start(f32[2,3,1664]{2,1,0:T(4,128)S(1)} %pad_maximum_fusion.2), channel_id=1, source_target_pairs={{0,2},{2,4},{4,6},{6,8},{8,10},{10,12},{12,14},{14,16},{16,18},{18... | collective-permute-start | bytes 119816 | tf_op jit(solution)/shard_map/ppermute | solution.py:1304
  13.5 5.5 %collective-permute-start.2 = (f32[128,1536]{1,0:T(8,128)}, f32[128,1536]{1,0:T(8,128)}, u32[]{:S(2)}, u32[]{:S(2)}) collective-permute-start(f32[128,1536]{1,0:T(8,128)} %bitcast_convert_fusion), channel_id=1, source_target_pairs={{0,8},{2,10},{4,12},{6,14},{8,16},{10,18},{12,20},{14,22},{16,24},... | collective-permute-start | bytes 2359304 | tf_op jit(solution)/shard_map/ppermute | solution.py:1304
  25.5 2.5 fusion.16
  29.2 2.6 fusion.6
  33.0 5.5 %compare_select_fusion = (f32[2,128,1536]{2,1,0:T(8,128)}, f32[2,128,1536]{2,1,0:T(8,128)}, f32[2,128,1536]{2,1,0:T(8,128)}, f32[2,128,1536]{2,1,0:T(8,128)}) fusion(pred[2,128]{1,0:T(4,128)(4,1)S(1)} %get-tuple-element.178, f32[2,128,1536]{2,1,0:T(8,128)} %copy-done.26, f32[1536]{0:T(1024)S(1)} %copy-done.83, bf16[96,1536]{1,0:T(8,128)(2,1)S(1)} %copy-done.37, ...), kind=kOutput, calls=%fused_computation.12 | convolution fusion | flops 80683008 | bytes 8267776 | tf_op jit(solution)/shard_map/dot_general | solution.py:1324
  44.5 39.4 %shard_map.322 = (f32[2,128,1536]{2,1,0:T(8,128)}, f32[2,16,1536]{2,1,0:T(8,128)}, f32[3,128,1536]{2,1,0:T(8,128)}, f32[3,128,1536]{2,1,0:T(8,128)}, f32[128,1536]{1,0:T(8,128)}, /*index=5*/f32[3,128,1536]{2,1,0:T(8,128)}) custom-call(f32[2,128,1536]{2,1,0:T(8,128)} %get-tuple-element.170.fall, f32[2,128,1536]{2,1,0:T(8,128)} %get-tuple-element.171.gain, ...), custom_call_target="tpu_custom_call" | custom-call | flops 4400000000 | bytes 12000000 | tf_op jit(solution)/shard_map/pallas_call | solution.py:663
  85.9 4.3 %fusion.2 = f32[2,128,1536]{2,1,0:T(8,128)S(1)} fusion(bf16[1536,1536]{1,0:T(8,128)(2,1)} %refs_11_.1, f32[2,128,1536]{2,1,0:T(8,128)S(1)} %multiply_add_fusion.y, f32[2,128,1536]{2,1,0:T(8,128)S(1)} %copy-done.84), kind=kOutput, calls=%fused_computation.2 | convolution fusion | flops 1210318848 | bytes 9437184 | tf_op jit(solution)/shard_map/dot_general | solution.py:1324
  90.8 3.0 collective-permute-done.6
  95.8 26.5 %shard_map.323 = (bf16[256,2048]{1,0:T(8,128)(2,1)}, bf16[256,2048]{1,0:T(8,128)(2,1)}, bf16[256,2048]{1,0:T(8,128)(2,1)}, f32[256,1536]{1,0:T(8,128)}, f32[256,...) custom-call(bf16[256,1536]{1,0:T(8,128)(2,1)} %bitcast.96, ...), custom_call_target="tpu_custom_call" | custom-call | flops 2200000000 | bytes 6000000 | tf_op jit(solution)/shard_map/pallas_call | solution.py:1201
  124.0 2.1 slice_bitcast_fusion.grad_middle
  126.1 2.6 multiply_reduce_fusion
  128.7 3.7 fusion.50
  134.7 4.1 multiply_reduce_fusion.2
  138.8 70.5 %shard_map.324 = (f32[2,128,1536]{2,1,0:T(8,128)}, f32[2,128,1536]{2,1,0:T(8,128)}, f32[2,128,16]{2,1,0:T(8,128)}, f32[2,128,16]{2,1,0:T(8,128)}, f32[16,1536]{1...) custom-call(f32[2,128,1536]{2,1,0:T(8,128)} %get-tuple-element.170.f, ...), custom_call_target="tpu_custom_call" | custom-call | flops 6819999744 | bytes 18600000 | tf_op jit(solution)/shard_map/pallas_call | solution.py:687
  212.7 12.6 %shard_map.325 = (f32[2,1536,384]{2,1,0:T(8,128)}, bf16[1536,1024]{1,0:T(8,128)(2,1)}) custom-call(bf16[256,1536]{1,0:T(8,128)(2,1)S(1)} %bitcast.86, f32[128,1536]{1,0:T(8,128)S(1)} %copy-done.11, f32[128,1536]{1,0:T(8,128)S(1)} %copy-done.9, f32[128,1536]{1,0:T(8,128)S(1)} %copy-done.12, f32[3,128,1536]{2,1,0:T(8,128)S(1)} %copy-done.2, ...), custom_call_target="tpu_custom_call" | custom-call | flops 1320000000 | bytes 3600000 | tf_op jit(solution)/shard_map/pallas_call | solution.py:124
  225.2 57.3 %shard_map.326 = (f32[3,384,2048]{2,1,0:T(8,128)}, f32[6,3,1,2,96,256]{5,4,3,2,1,0:T(8,128)}, f32[2,2,384,384]{3,2,1,0:T(8,128)}) custom-call(bf16[256,1536]{1,0:T(8,128)(2,1)} %bitcast.97, f32[128,1536]{1,0:T(8,128)} %get-tuple-element.80.up_one.hid_up, f32[128,1536]{1,0:T(8,128)} %get-tuple-element.81.down_one.hid_down, ...), custom_call_target="tpu_custom_call" | custom-call | flops 3960000000 | bytes 10800000 | tf_op jit(solution)/shard_map/pallas_call | solution.py:859
  287.8 4.2 fusion.4
  292.7 2.9 multiply_reduce_fusion.3
  297.9 3.9 collective-permute-done.10
  303.3 2.6 fusion.12
  310.8 2.5 multiply_reduce_fusion.1
  313.3 3.6 subtract_add_fusion
  318.8 106.2 %shard_map.328 = (f32[3,1,96,2048]{3,2,1,0:T(8,128)}, f32[2,1,96,1536]{3,2,1,0:T(8,128)}, f32[1,1,96,1536]{3,2,1,0:T(8,128)}, f32[224,128]{1,0:T(8,128)}) custom-call(f32[3,1,2,2,96,2048]{5,4,3,2,1,0:T(8,128)} %bitcast.111, f32[2,4,384,384]{3,2,1,0:T(8,128)} %bitcast.99, f32[2,2,384,384]{3,2,1,0:T(8,128)} %get-tuple-element.103.passed_in, ...), custom_call_target="tpu_custom_call" | custom-call | flops 11000000512 | bytes 30000000 | tf_op jit(solution)/shard_map/pallas_call | solution.py:1116
  429.9 2.3 shard_map.329
  (289 shorter events, 55.1 us)
Async XLA Ops:
  0.7 27.4 %copy-start = (bf16[1536,128]{1,0:T(8,128)(2,1)S(1)}, bf16[1536,128]{1,0:T(8,128)(2,1)}, u32[]{:S(2)}) copy-start(bf16[1536,128]{1,0:T(8,128)(2,1)} %param.27) | copy-start | bytes 1179652
  2.4 9.5 %collective-permute-start = (f32[2,3,1664]{2,1,0:T(4,128)S(1)}, f32[2,3,1664]{2,1,0:T(4,128)S(1)}, u32[]{:S(2)}, u32[]{:S(2)}) collective-permute-start(f32[2,3,1664]{2,1,0:T(4,128)S(1)} %pad_maximum_fusion.2), channel_id=1, source_target_pairs={{0,2},{2,4},{4,6},{6,8},{8,10},{10,12},{12,14},{14,16},{16,18},{18... | collective-permute-start | bytes 119816 | tf_op jit(solution)/shard_map/ppermute | solution.py:1304
  8.1 23.8 %copy-start.67 = (f32[16]{0:T(128)}, f32[16]{0:T(128)S(1)}, u32[]{:S(2)}) copy-start(f32[16]{0:T(128)S(1)} %get-tuple-element.181) | copy-start | bytes 196
  8.1 23.8 %copy-start.69 = (f32[16]{0:T(128)}, f32[16]{0:T(128)S(1)}, u32[]{:S(2)}) copy-start(f32[16]{0:T(128)S(1)} %get-tuple-element.182) | copy-start | bytes 196
  12.2 26.3 %collective-permute-start.3 = (f32[128,1536]{1,0:T(8,128)}, f32[128,1536]{1,0:T(8,128)}, u32[]{:S(2)}, u32[]{:S(2)}) collective-permute-start(f32[128,1536]{1,0:T(8,128)} %bitcast_convert_fusion), channel_id=1, source_target_pairs={{8,0},{10,2},{12,4},{14,6},{16,8},{18,10},{20,12},{22,14},{24,16},... | collective-permute-start | bytes 2359304 | tf_op jit(solution)/shard_map/ppermute | solution.py:1304
  13.5 25.0 %collective-permute-start.2 = (f32[128,1536]{1,0:T(8,128)}, f32[128,1536]{1,0:T(8,128)}, u32[]{:S(2)}, u32[]{:S(2)}) collective-permute-start(f32[128,1536]{1,0:T(8,128)} %bitcast_convert_fusion), channel_id=1, source_target_pairs={{0,8},{2,10},{4,12},{6,14},{8,16},{10,18},{12,20},{14,22},{16,24},... | collective-permute-start | bytes 2359304 | tf_op jit(solution)/shard_map/ppermute | solution.py:1304
  20.7 18.7 %collective-permute-start.5 = (f32[128,1536]{1,0:T(8,128)}, f32[128,1536]{1,0:T(8,128)S(1)}, u32[]{:S(2)}, u32[]{:S(2)}) collective-permute-start(f32[128,1536]{1,0:T(8,128)} %dynamic-slice_bitcast_fusion.1), channel_id=1, source_target_pairs={{0,4},{2,6},{4,0},{6,2},{8,12},{10,14},{12,8},{14,10},{16,20},{18,... | collective-permute-start | bytes 2359304 | tf_op jit(solution)/shard_map/ppermute | solution.py:1304
  22.2 18.4 %collective-permute-start.4 = (f32[128,1536]{1,0:T(8,128)}, f32[128,1536]{1,0:T(8,128)S(1)}, u32[]{:S(2)}, u32[]{:S(2)}) collective-permute-start(f32[128,1536]{1,0:T(8,128)} %dynamic-slice_bitcast_fusion.1), channel_id=1, source_target_pairs={{0,2},{2,0},{4,6},{6,4},{8,10},{10,8},{12,14},{14,12},{16,18},{18,... | collective-permute-start | bytes 2359304 | tf_op jit(solution)/shard_map/ppermute | solution.py:1304
  29.2 2.6 collective-permute-start.1
  44.5 39.4 %copy-start.27 = (f32[2,128,1536]{2,1,0:T(8,128)S(1)}, f32[2,128,1536]{2,1,0:T(8,128)}, u32[]{:S(2)}) copy-start(f32[2,128,1536]{2,1,0:T(8,128)} %copy-done.26) | copy-start | bytes 4718596
  44.5 39.4 %copy-start.65 = (f32[1536]{0:T(1024)S(1)}, f32[1536]{0:T(1024)}, u32[]{:S(2)}) copy-start(f32[1536]{0:T(1024)} %param.32) | copy-start | bytes 18436
  90.3 3.5 collective-permute-start.6
  122.3 3.8 collective-permute-start.8
  122.3 6.4 %collective-permute-start.7 = (f32[2,128,1536]{2,1,0:T(8,128)}, f32[2,128,1536]{2,1,0:T(8,128)}, u32[]{:S(2)}, u32[]{:S(2)}) collective-permute-start(f32[2,128,1536]{2,1,0:T(8,128)} %bitcast.104), channel_id=1, source_target_pairs={{0,1},{1,0},{2,3},{3,2},{4,5},{5,4},{6,7},{7,6},{8,9},{9,8},{10,11... | collective-permute-start | bytes 4718600 | tf_op jit(solution)/shard_map/ppermute | solution.py:1304
  138.8 70.5 %copy-start.2 = (f32[3,128,1536]{2,1,0:T(8,128)S(1)}, f32[3,128,1536]{2,1,0:T(8,128)}, u32[]{:S(2)}) copy-start(f32[3,128,1536]{2,1,0:T(8,128)} %get-tuple-element.94.refs_4_) | copy-start | bytes 7077892
  138.8 70.5 %copy-start.7 = (f32[3,2,128,384]{3,2,1,0:T(8,128)S(1)}, f32[3,2,128,384]{3,2,1,0:T(8,128)}, u32[]{:S(2)}) copy-start(f32[3,2,128,384]{3,2,1,0:T(8,128)} %get-tuple-element.97.refs_9_) | copy-start | bytes 3538948
  138.8 70.5 %copy-start.9 = (f32[128,1536]{1,0:T(8,128)S(1)}, f32[128,1536]{1,0:T(8,128)}, u32[]{:S(2)}) copy-start(f32[128,1536]{1,0:T(8,128)} %copy-done.8) | copy-start | bytes 2359300
  138.8 70.5 %copy-start.11 = (f32[128,1536]{1,0:T(8,128)S(1)}, f32[128,1536]{1,0:T(8,128)}, u32[]{:S(2)}) copy-start(f32[128,1536]{1,0:T(8,128)} %copy-done.10) | copy-start | bytes 2359300
  138.8 70.5 %copy-start.12 = (f32[128,1536]{1,0:T(8,128)S(1)}, f32[128,1536]{1,0:T(8,128)}, u32[]{:S(2)}) copy-start(f32[128,1536]{1,0:T(8,128)} %get-tuple-element.93.refs_3_) | copy-start | bytes 2359300
  225.2 59.9 %copy-start.32 = (f32[2,128,1536]{2,1,0:T(8,128)S(1)}, f32[2,128,1536]{2,1,0:T(8,128)}, u32[]{:S(2)}) copy-start(f32[2,128,1536]{2,1,0:T(8,128)} %get-tuple-element.183) | copy-start | bytes 4718596
  225.2 59.9 %copy-start.33 = (f32[2,128,1536]{2,1,0:T(8,128)S(1)}, f32[2,128,1536]{2,1,0:T(8,128)}, u32[]{:S(2)}) copy-start(f32[2,128,1536]{2,1,0:T(8,128)} %get-tuple-element.100) | copy-start | bytes 4718596
  286.5 5.5 %collective-permute-start.9 = (f32[2,128,128]{1,2,0:T(8,128)S(1)}, f32[2,128,128]{1,2,0:T(8,128)S(1)}, u32[]{:S(2)}, u32[]{:S(2)}) collective-permute-start(f32[2,128,128]{1,2,0:T(8,128)S(1)} %pad_maximum_fusion), channel_id=1, source_target_pairs={{0,1},{1,0},{2,3},{3,2},{4,5},{5,4},{6,7},{7,6},{8,9},{9,8},{10,11... | collective-permute-start | bytes 393224 | tf_op jit(solution)/shard_map/ppermute | solution.py:1304
  295.6 6.2 %collective-permute-start.10 = (f32[2,3,1536]{2,1,0:T(4,128)S(1)}, f32[2,3,1536]{2,1,0:T(4,128)S(1)}, u32[]{:S(2)}, u32[]{:S(2)}) collective-permute-start(f32[2,3,1536]{2,1,0:T(4,128)S(1)} %pad_add_fusion.1), channel_id=1, source_target_pairs={{2,0},{4,2},{6,4},{8,6},{10,8},{12,10},{14,12},{16,14},{18,16},{20... | collective-permute-start | bytes 110600 | tf_op jit(solution)/shard_map/ppermute | solution.py:1304
  305.9 4.9 %collective-permute-start.11 = (f32[2,128,1536]{2,1,0:T(8,128)}, f32[2,128,1536]{2,1,0:T(8,128)}, u32[]{:S(2)}, u32[]{:S(2)}) collective-permute-start(f32[2,128,1536]{2,1,0:T(8,128)} %fusion.12), channel_id=1, source_target_pairs={{0,1},{1,0},{2,3},{3,2},{4,5},{5,4},{6,7},{7,6},{8,9},{9,8},{10,11... | collective-permute-start | bytes 4718600 | tf_op jit(solution)/shard_map/ppermute | solution.py:1304
  (84 other events, 354.1 us)

commit v7 on v6

--- a/solution.py
+++ b/solution.py
@@ -959,7 +959,7 @@
 
 
 def sum_kernel(
-    count, ffn, mixer_in, passed_in, d_inner, near_in, turned, d_own, small,
+    count, ffn, mixer_in, passed_in, d_inner, near_in, turned, small,
     ffn_out, mixer_out, inner_out, small_out,
     d_all, kept, near, next_, mixer, m_passed, m_arrived, d_side, inner, i_got, i_passed, i_arrived, m_done, m_back, i_done, i_back, s_near, s_next, s_done, s_line,
     ffn_send, ffn_recv, m_send, m_recv, i_send, i_recv, back_send, back_recv, s_send, s_recv, d_send, d_recv, local,
@@ -996,6 +996,10 @@
         )
         for k in range(1, SIDE)
     ]
+    own_quarter = pltpu.make_async_copy(
+        d_inner.at[:, :, pl.ds(pl.multiple_of(place * size, 128), size)], d_side.at[SIDE - 1], local.at[local.shape[0] - 1]
+    )
+    own_quarter.start()
     for c in quarters:
         c.start()
     for c in first.values():
@@ -1028,9 +1032,10 @@
         again(c)
     for c in quarters:
         c.wait_recv()
-    own = d_own.shape[0]
-    part = own // 2
-    d_all[:own, :] = d_own[...]
+    part = d_side.shape[2]
+    own = 2 * part
+    own_quarter.wait()
+    d_all[:own, :] = d_side[SIDE - 1].reshape(own, size).astype(d_all.dtype)
     for k in range(SIDE - 1):
         for s in range(2):
             start = own + (s * (SIDE - 1) + k) * part
@@ -1104,7 +1109,7 @@
     other.finish(1)
 
 
-def sum_grads(ffn, mixer, passed, d_inner, near, turned, d_own, small):
+def sum_grads(ffn, mixer, passed, d_inner, near, turned, small):
     count = lax.axis_size("seq")
     more = count // SIDE // SIDE
     cut, units = ffn.shape[1:]
@@ -1117,7 +1122,7 @@
         functools.partial(sum_kernel, count),
         out_shape=[shaped(3, more, rows, units), shaped(2, more, rows, size * SIDE), shaped(1, more, rows, size * SIDE),
                    shaped(tall, LANES)],
-        in_specs=[in_hbm()] * 5 + [in_vmem()] * 3,
+        in_specs=[in_hbm()] * 5 + [in_vmem()] * 2,
         out_specs=[in_vmem()] * 4,
         scratch_shapes=[
             pltpu.VMEM((turned.shape[1], size), jnp.bfloat16),
@@ -1125,18 +1130,18 @@
             v(CHUNKS, 3, more, 2, rows, units // CHUNKS),
             v(CHUNKS, 3, more, rows, units // CHUNKS),
             v(2, SIDE, cut, size), v(2, 2, cut, size), v(2, 2, cut, size),
-            v(SIDE - 1, *d_inner.shape[:2], size),
+            v(SIDE, *d_inner.shape[:2], size),
             v(1, SIDE, cut, size), v(1, cut, size), v(2, 1, cut, size), v(2, 1, cut, size),
             v(2, more, SIDE, rows, size), v(SIDE, 2, more, rows, size),
             v(1, more, SIDE, rows, size), v(SIDE, 1, more, rows, size),
             v(2, groups, 2, tall // 2, LANES), v(2, groups, tall // 2, LANES), v(groups, tall, LANES), v(groups, tall, LANES),
         ]
-        + sems(2 * CHUNKS) + sems(REDUCE_SEMS) + sems(REDUCE_SEMS) + sems(2 * SIDE) + sems(3 + groups) + sems(SIDE) + [pltpu.SemaphoreType.DMA((3 + CHUNKS + EARLY,))],
+        + sems(2 * CHUNKS) + sems(REDUCE_SEMS) + sems(REDUCE_SEMS) + sems(2 * SIDE) + sems(3 + groups) + sems(SIDE) + [pltpu.SemaphoreType.DMA((4 + CHUNKS + EARLY,))],
         compiler_params=pltpu.CompilerParams(
             collective_id=3, has_side_effects=True, vmem_limit_bytes=58 * 1024 * 1024
         ),
         cost_estimate=spans(100),
-    )(ffn.reshape(3, more, 2, 2, rows, units), mixer, passed, d_inner, near, turned, d_own, small.reshape(groups, 2, 2, tall, LANES))
+    )(ffn.reshape(3, more, 2, 2, rows, units), mixer, passed, d_inner, near, turned, small.reshape(groups, 2, 2, tall, LANES))
 
 
 def middle_kernel(
@@ -1503,7 +1508,7 @@
     grad_w_step = after(grad_w_step, tokens_grad)
     small = gather_small(grad_w_step, decay_sum * decay_rate, grad_w_select, rows)
     ffn, mixer, inner, tall = sum_grads(
-        ffn, mixer, passed, d_inner.astype(jnp.float32), near, turned, flat(part_of(d_inner, place, size, 2)), small
+        ffn, mixer, passed, d_inner.astype(jnp.float32), near, turned, small
     )
     if count > SIDE * SIDE:
         groups = [[a * stride + b + SIDE * k for k in range(stride // SIDE)] for a in range(SIDE) for b in range(SIDE)]

time: 440 us -> 439 us (level)
    unnamed x192 -> x186, local copies, waits for them, and re-layouts: 14.6 us -> 14.5 us
where the time goes in v7:
time: 439 us; the launch traced here: 432 us
  Pallas kernels  317 us (72%)
  matrix products  30.4 us (7%)
  local copies, waits for them, and re-layouts  28.6 us (7%)
  other arithmetic  27.4 us (6%)
  starting transfers between devices  17.2 us (4%)
  waiting for transfers between devices  9.02 us (2%)
    pallas_call x1, Pallas kernels, sum_grads(): pl.pallas_call(functools.partial(sum_kernel, count), out_shape=[shaped(3,...  108 us
    pallas_call x1, Pallas kernels, scan_backward(): pl.pallas_call(functools.partial(backward_kernel, count), out_shape=[flat...  70.5 us
    pallas_call x1, Pallas kernels, ffn_grads(): pl.pallas_call(functools.partial(ffn_kernel, count), grid=(units // block...  57.3 us
    pallas_call x1, Pallas kernels, scan_forward(): pl.pallas_call(functools.partial(forward_kernel, count), out_shape=[shape...  39.4 us
    pallas_call x1, Pallas kernels, feed_forward(): pl.pallas_call(functools.partial(middle_kernel, count), grid=(units // bl...  26.5 us
    ppermute x12, starting transfers between devices, send(): return lax.ppermute(block, axis, route)  17.2 us
    dot_general x5, matrix products, matmul(): return jnp.dot(left, right, preferred_element_type=jnp.float32)  14.6 us
    unnamed x186, local copies, waits for them, and re-layouts  14.5 us
  transfers between devices with their start and end apart: 12, of which 4 were waited for; matrix products, arithmetic and copies ran while one was open for 8% of the time, Pallas kernels for 0%

profile of v7, /device:TPU:0, one launch (start us, length us, event | category | flops | bytes accessed | tf_op | source)
XLA Modules:
  0.0 431.9 jit_solution(12867962675371950226)
XLA Ops:
  2.4 4.8 %collective-permute-start = (f32[2,3,1664]{2,1,0:T(4,128)S(1)}, f32[2,3,1664]{2,1,0:T(4,128)S(1)}, u32[]{:S(2)}, u32[]{:S(2)}) collective-permute-start(f32[2,3,1664]{2,1,0:T(4,128)S(1)} %pad_maximum_fusion.2), channel_id=1, source_target_pairs={{0,2},{2,4},{4,6},{6,8},{8,10},{10,12},{12,14},{14,16},{16,18},{18... | collective-permute-start | bytes 119816 | tf_op jit(solution)/shard_map/ppermute | solution.py:1309
  13.5 5.5 %collective-permute-start.2 = (f32[128,1536]{1,0:T(8,128)}, f32[128,1536]{1,0:T(8,128)}, u32[]{:S(2)}, u32[]{:S(2)}) collective-permute-start(f32[128,1536]{1,0:T(8,128)} %bitcast_convert_fusion), channel_id=1, source_target_pairs={{0,8},{2,10},{4,12},{6,14},{8,16},{10,18},{12,20},{14,22},{16,24},... | collective-permute-start | bytes 2359304 | tf_op jit(solution)/shard_map/ppermute | solution.py:1309
  25.5 2.5 fusion.16
  29.2 2.6 fusion.6
  33.0 5.6 %compare_select_fusion = (f32[2,128,1536]{2,1,0:T(8,128)}, f32[2,128,1536]{2,1,0:T(8,128)}, f32[2,128,1536]{2,1,0:T(8,128)}, f32[2,128,1536]{2,1,0:T(8,128)}) fusion(pred[2,128]{1,0:T(4,128)(4,1)S(1)} %get-tuple-element.176, f32[2,128,1536]{2,1,0:T(8,128)} %copy-done.26, f32[1536]{0:T(1024)S(1)} %copy-done.80, bf16[96,1536]{1,0:T(8,128)(2,1)S(1)} %copy-done.37, ...), kind=kOutput, calls=%fused_computation.12 | convolution fusion | flops 80683008 | bytes 8267776 | tf_op jit(solution)/shard_map/dot_general | solution.py:1329
  44.5 39.4 %shard_map.322 = (f32[2,128,1536]{2,1,0:T(8,128)}, f32[2,16,1536]{2,1,0:T(8,128)}, f32[3,128,1536]{2,1,0:T(8,128)}, f32[3,128,1536]{2,1,0:T(8,128)}, f32[128,1536]{1,0:T(8,128)}, /*index=5*/f32[3,128,1536]{2,1,0:T(8,128)}) custom-call(f32[2,128,1536]{2,1,0:T(8,128)} %get-tuple-element.168.fall, f32[2,128,1536]{2,1,0:T(8,128)} %get-tuple-element.169.gain, ...), custom_call_target="tpu_custom_call" | custom-call | flops 4400000000 | bytes 12000000 | tf_op jit(solution)/shard_map/pallas_call | solution.py:663
  85.9 4.4 %fusion.2 = f32[2,128,1536]{2,1,0:T(8,128)S(1)} fusion(bf16[1536,1536]{1,0:T(8,128)(2,1)} %refs_11_.1, f32[2,128,1536]{2,1,0:T(8,128)S(1)} %multiply_add_fusion.y, f32[2,128,1536]{2,1,0:T(8,128)S(1)} %copy-done.81), kind=kOutput, calls=%fused_computation.2 | convolution fusion | flops 1210318848 | bytes 9437184 | tf_op jit(solution)/shard_map/dot_general | solution.py:1329
  90.7 3.0 collective-permute-done.6
  95.7 26.5 %shard_map.323 = (bf16[256,2048]{1,0:T(8,128)(2,1)}, bf16[256,2048]{1,0:T(8,128)(2,1)}, bf16[256,2048]{1,0:T(8,128)(2,1)}, f32[256,1536]{1,0:T(8,128)}, f32[256,...) custom-call(bf16[256,1536]{1,0:T(8,128)(2,1)} %bitcast.94, ...), custom_call_target="tpu_custom_call" | custom-call | flops 2200000000 | bytes 6000000 | tf_op jit(solution)/shard_map/pallas_call | solution.py:1206
  124.0 2.1 slice_bitcast_fusion.grad_middle
  126.1 2.6 multiply_reduce_fusion
  128.8 3.7 fusion.51
  134.8 4.0 multiply_reduce_fusion.2
  138.8 70.5 %shard_map.324 = (f32[2,128,1536]{2,1,0:T(8,128)}, f32[2,128,1536]{2,1,0:T(8,128)}, f32[2,128,16]{2,1,0:T(8,128)}, f32[2,128,16]{2,1,0:T(8,128)}, f32[16,1536]{1...) custom-call(f32[2,128,1536]{2,1,0:T(8,128)} %get-tuple-element.168.f, ...), custom_call_target="tpu_custom_call" | custom-call | flops 6819999744 | bytes 18600000 | tf_op jit(solution)/shard_map/pallas_call | solution.py:687
  212.7 12.5 %shard_map.325 = (f32[2,1536,384]{2,1,0:T(8,128)}, bf16[1536,1024]{1,0:T(8,128)(2,1)}) custom-call(bf16[256,1536]{1,0:T(8,128)(2,1)S(1)} %bitcast.84, f32[128,1536]{1,0:T(8,128)S(1)} %copy-done.11, f32[128,1536]{1,0:T(8,128)S(1)} %copy-done.9, f32[128,1536]{1,0:T(8,128)S(1)} %copy-done.12, f32[3,128,1536]{2,1,0:T(8,128)S(1)} %copy-done.2, ...), custom_call_target="tpu_custom_call" | custom-call | flops 1320000000 | bytes 3600000 | tf_op jit(solution)/shard_map/pallas_call | solution.py:124
  225.3 57.3 %shard_map.326 = (f32[3,384,2048]{2,1,0:T(8,128)}, f32[6,3,1,2,96,256]{5,4,3,2,1,0:T(8,128)}, f32[2,2,384,384]{3,2,1,0:T(8,128)}) custom-call(bf16[256,1536]{1,0:T(8,128)(2,1)} %bitcast.95, f32[128,1536]{1,0:T(8,128)} %get-tuple-element.80.up_one.hid_up, f32[128,1536]{1,0:T(8,128)} %get-tuple-element.81.down_one.hid_down, ...), custom_call_target="tpu_custom_call" | custom-call | flops 3960000000 | bytes 10800000 | tf_op jit(solution)/shard_map/pallas_call | solution.py:859
  287.9 4.2 fusion.4
  292.8 2.3 multiply_reduce_fusion.3
  297.4 3.9 collective-permute-done.10
  301.4 2.6 fusion.12
  308.7 2.4 multiply_reduce_fusion.1
  311.1 3.6 subtract_add_fusion
  316.6 107.7 %shard_map.328 = (f32[3,1,96,2048]{3,2,1,0:T(8,128)}, f32[2,1,96,1536]{3,2,1,0:T(8,128)}, f32[1,1,96,1536]{3,2,1,0:T(8,128)}, f32[224,128]{1,0:T(8,128)}) custom-call(f32[3,1,2,2,96,2048]{5,4,3,2,1,0:T(8,128)} %bitcast.108, f32[2,4,384,384]{3,2,1,0:T(8,128)} %bitcast.97, f32[2,2,384,384]{3,2,1,0:T(8,128)} %get-tuple-element.103.passed_in, ...), custom_call_target="tpu_custom_call" | custom-call | flops 11000000512 | bytes 30000000 | tf_op jit(solution)/shard_map/pallas_call | solution.py:1121
  429.2 2.3 shard_map.329
  (282 shorter events, 53.5 us)
Async XLA Ops:
  0.7 27.4 %copy-start = (bf16[1536,128]{1,0:T(8,128)(2,1)S(1)}, bf16[1536,128]{1,0:T(8,128)(2,1)}, u32[]{:S(2)}) copy-start(bf16[1536,128]{1,0:T(8,128)(2,1)} %param.27) | copy-start | bytes 1179652
  2.4 9.5 %collective-permute-start = (f32[2,3,1664]{2,1,0:T(4,128)S(1)}, f32[2,3,1664]{2,1,0:T(4,128)S(1)}, u32[]{:S(2)}, u32[]{:S(2)}) collective-permute-start(f32[2,3,1664]{2,1,0:T(4,128)S(1)} %pad_maximum_fusion.2), channel_id=1, source_target_pairs={{0,2},{2,4},{4,6},{6,8},{8,10},{10,12},{12,14},{14,16},{16,18},{18... | collective-permute-start | bytes 119816 | tf_op jit(solution)/shard_map/ppermute | solution.py:1309
  8.1 23.8 %copy-start.67 = (f32[16]{0:T(128)}, f32[16]{0:T(128)S(1)}, u32[]{:S(2)}) copy-start(f32[16]{0:T(128)S(1)} %get-tuple-element.179) | copy-start | bytes 196
  8.1 23.8 %copy-start.69 = (f32[16]{0:T(128)}, f32[16]{0:T(128)S(1)}, u32[]{:S(2)}) copy-start(f32[16]{0:T(128)S(1)} %get-tuple-element.180) | copy-start | bytes 196
  12.2 26.3 %collective-permute-start.3 = (f32[128,1536]{1,0:T(8,128)}, f32[128,1536]{1,0:T(8,128)}, u32[]{:S(2)}, u32[]{:S(2)}) collective-permute-start(f32[128,1536]{1,0:T(8,128)} %bitcast_convert_fusion), channel_id=1, source_target_pairs={{8,0},{10,2},{12,4},{14,6},{16,8},{18,10},{20,12},{22,14},{24,16},... | collective-permute-start | bytes 2359304 | tf_op jit(solution)/shard_map/ppermute | solution.py:1309
  13.5 25.0 %collective-permute-start.2 = (f32[128,1536]{1,0:T(8,128)}, f32[128,1536]{1,0:T(8,128)}, u32[]{:S(2)}, u32[]{:S(2)}) collective-permute-start(f32[128,1536]{1,0:T(8,128)} %bitcast_convert_fusion), channel_id=1, source_target_pairs={{0,8},{2,10},{4,12},{6,14},{8,16},{10,18},{12,20},{14,22},{16,24},... | collective-permute-start | bytes 2359304 | tf_op jit(solution)/shard_map/ppermute | solution.py:1309
  20.7 18.7 %collective-permute-start.5 = (f32[128,1536]{1,0:T(8,128)}, f32[128,1536]{1,0:T(8,128)S(1)}, u32[]{:S(2)}, u32[]{:S(2)}) collective-permute-start(f32[128,1536]{1,0:T(8,128)} %dynamic-slice_bitcast_fusion.1), channel_id=1, source_target_pairs={{0,4},{2,6},{4,0},{6,2},{8,12},{10,14},{12,8},{14,10},{16,20},{18,... | collective-permute-start | bytes 2359304 | tf_op jit(solution)/shard_map/ppermute | solution.py:1309
  22.2 18.4 %collective-permute-start.4 = (f32[128,1536]{1,0:T(8,128)}, f32[128,1536]{1,0:T(8,128)S(1)}, u32[]{:S(2)}, u32[]{:S(2)}) collective-permute-start(f32[128,1536]{1,0:T(8,128)} %dynamic-slice_bitcast_fusion.1), channel_id=1, source_target_pairs={{0,2},{2,0},{4,6},{6,4},{8,10},{10,8},{12,14},{14,12},{16,18},{18,... | collective-permute-start | bytes 2359304 | tf_op jit(solution)/shard_map/ppermute | solution.py:1309
  29.2 2.6 collective-permute-start.1
  44.5 39.4 %copy-start.27 = (f32[2,128,1536]{2,1,0:T(8,128)S(1)}, f32[2,128,1536]{2,1,0:T(8,128)}, u32[]{:S(2)}) copy-start(f32[2,128,1536]{2,1,0:T(8,128)} %copy-done.26) | copy-start | bytes 4718596
  44.5 39.4 %copy-start.65 = (f32[1536]{0:T(1024)S(1)}, f32[1536]{0:T(1024)}, u32[]{:S(2)}) copy-start(f32[1536]{0:T(1024)} %param.32) | copy-start | bytes 18436
  90.3 3.5 collective-permute-start.6
  122.3 3.8 collective-permute-start.8
  122.4 6.4 %collective-permute-start.7 = (f32[2,128,1536]{2,1,0:T(8,128)}, f32[2,128,1536]{2,1,0:T(8,128)}, u32[]{:S(2)}, u32[]{:S(2)}) collective-permute-start(f32[2,128,1536]{2,1,0:T(8,128)} %bitcast.102), channel_id=1, source_target_pairs={{0,1},{1,0},{2,3},{3,2},{4,5},{5,4},{6,7},{7,6},{8,9},{9,8},{10,11... | collective-permute-start | bytes 4718600 | tf_op jit(solution)/shard_map/ppermute | solution.py:1309
  138.8 70.5 %copy-start.2 = (f32[3,128,1536]{2,1,0:T(8,128)S(1)}, f32[3,128,1536]{2,1,0:T(8,128)}, u32[]{:S(2)}) copy-start(f32[3,128,1536]{2,1,0:T(8,128)} %get-tuple-element.94.refs_4_) | copy-start | bytes 7077892
  138.8 70.5 %copy-start.7 = (f32[3,2,128,384]{3,2,1,0:T(8,128)S(1)}, f32[3,2,128,384]{3,2,1,0:T(8,128)}, u32[]{:S(2)}) copy-start(f32[3,2,128,384]{3,2,1,0:T(8,128)} %get-tuple-element.97.refs_9_) | copy-start | bytes 3538948
  138.8 70.6 %copy-start.9 = (f32[128,1536]{1,0:T(8,128)S(1)}, f32[128,1536]{1,0:T(8,128)}, u32[]{:S(2)}) copy-start(f32[128,1536]{1,0:T(8,128)} %copy-done.8) | copy-start | bytes 2359300
  138.8 70.6 %copy-start.11 = (f32[128,1536]{1,0:T(8,128)S(1)}, f32[128,1536]{1,0:T(8,128)}, u32[]{:S(2)}) copy-start(f32[128,1536]{1,0:T(8,128)} %copy-done.10) | copy-start | bytes 2359300
  138.8 70.6 %copy-start.12 = (f32[128,1536]{1,0:T(8,128)S(1)}, f32[128,1536]{1,0:T(8,128)}, u32[]{:S(2)}) copy-start(f32[128,1536]{1,0:T(8,128)} %get-tuple-element.93.refs_3_) | copy-start | bytes 2359300
  225.3 59.9 %copy-start.32 = (f32[2,128,1536]{2,1,0:T(8,128)S(1)}, f32[2,128,1536]{2,1,0:T(8,128)}, u32[]{:S(2)}) copy-start(f32[2,128,1536]{2,1,0:T(8,128)} %get-tuple-element.181) | copy-start | bytes 4718596
  225.3 59.9 %copy-start.33 = (f32[2,128,1536]{2,1,0:T(8,128)S(1)}, f32[2,128,1536]{2,1,0:T(8,128)}, u32[]{:S(2)}) copy-start(f32[2,128,1536]{2,1,0:T(8,128)} %get-tuple-element.100) | copy-start | bytes 4718596
  286.5 5.5 %collective-permute-start.9 = (f32[2,128,128]{1,2,0:T(8,128)S(1)}, f32[2,128,128]{1,2,0:T(8,128)S(1)}, u32[]{:S(2)}, u32[]{:S(2)}) collective-permute-start(f32[2,128,128]{1,2,0:T(8,128)S(1)} %pad_maximum_fusion), channel_id=1, source_target_pairs={{0,1},{1,0},{2,3},{3,2},{4,5},{5,4},{6,7},{7,6},{8,9},{9,8},{10,11... | collective-permute-start | bytes 393224 | tf_op jit(solution)/shard_map/ppermute | solution.py:1309
  295.1 6.2 %collective-permute-start.10 = (f32[2,3,1536]{2,1,0:T(4,128)S(1)}, f32[2,3,1536]{2,1,0:T(4,128)S(1)}, u32[]{:S(2)}, u32[]{:S(2)}) collective-permute-start(f32[2,3,1536]{2,1,0:T(4,128)S(1)} %pad_add_fusion.1), channel_id=1, source_target_pairs={{2,0},{4,2},{6,4},{8,6},{10,8},{12,10},{14,12},{16,14},{18,16},{20... | collective-permute-start | bytes 110600 | tf_op jit(solution)/shard_map/ppermute | solution.py:1309
  304.0 4.1 collective-permute-start.11
  (81 other events, 359.3 us)
